TPU v7x, 32 devices: a whole 2x2x4 slice. The times are simulated.
32 devices in a mesh: grp: 2 (over y), shot: 16 (over z, x, core), depth: 1.
Axes of the slice: x: 2, y: 2, z: 4, core: 2. Of those that a mesh axis runs over, the one named last changes fastest.
Arguments:
- velocity_p: bfloat16 [128, 8, 8, 128], P(('grp', 'shot'), None, None, 'depth'), parts along dimension 0, may hold values from 0.5 to 0.8984375
- velocity_s: bfloat16 [128, 8, 8, 128], P(('grp', 'shot'), None, None, 'depth'), parts along dimension 0, may hold values from 0.19921875 to 0.5
- density: bfloat16 [128, 8, 8, 128], P(('grp', 'shot'), None, None, 'depth'), parts along dimension 0, may hold values from 1 to 2
- perturbation: bfloat16 [128, 8, 8, 128], P(('grp', 'shot'), None, None, 'depth'), parts along dimension 0, may hold values from -4 to 4
- seafloor: int32 [128, 8, 8], P(('grp', 'shot')), parts along dimension 0, may hold values from 16 to 63
- owner_ids: int32 [128], P(('grp', 'shot')), parts along dimension 0, may hold values from 0 to 63, each once
- corner_x: int32 [32], P(('grp', 'shot')), parts along dimension 0, may hold values from 0 to 4
- corner_y: int32 [32], P(('grp', 'shot')), parts along dimension 0, may hold values from 0 to 4
- wave_prev: bfloat16 [32, 32, 32, 128], P(('grp', 'shot'), None, None, 'depth'), parts along dimension 0, may hold values from -6 to 6
- wave_now: bfloat16 [32, 32, 32, 128], P(('grp', 'shot'), None, None, 'depth'), parts along dimension 0, may hold values from -6 to 6
Outputs:
- hessian_vec: float32 [128, 8, 8, 128], P(('grp', 'shot'), None, None, 'depth'), parts along dimension 0
There are 2 independent parts, one for each index of `grp`. A program takes and returns all parts, laid end to end along the dimension named above; each array names one. Nothing has to cross between parts.
Inputs may be any that keep to these rules, and one draw needn't show every extreme that they name: `owner_ids`: each lateral block is held by exactly one slot. Shot s images the block rows corner_x[s] to corner_x[s] + 3. Shot s images the block columns corner_y[s] to corner_y[s] + 3.
All inputs are finite; a program needn't handle non-finite values.
Results may differ from a plain program's by a relative error of at most 0.0048.
Values may be sent and summed in bfloat16 or wider, within the bound.
No kernel may reach another device: no remote copies, remote signals or barrier semaphores. Data moves between devices by JAX's collectives and lax.ppermute only.
A program may use at most 64 MiB of HBM per device.

v0:
```python
import functools

import jax
import jax.numpy as jnp
from jax import lax
from jax.experimental import pallas as pl
from jax.experimental.pallas import tpu as pltpu
from jax.sharding import PartitionSpec as P

APX = 4
APY = 4
STEPS = 4
GRID_COLS = 8
LANES = 8

speed_factor = 0.28
image_scale = 0.01


def with_halo(block, sides, width):
    for axis, dim in sides:
        count = lax.axis_size(axis)
        forward = [(i, i + 1) for i in range(count - 1)]
        backward = [(target, source) for source, target in forward]
        low = lax.ppermute(
            lax.slice_in_dim(block, block.shape[dim] - width, None, axis=dim), axis, forward
        )
        high = lax.ppermute(lax.slice_in_dim(block, 0, width, axis=dim), axis, backward)
        block = jnp.concatenate([low, block, high], axis=dim)
    return block


def laplace_many(fields):
    stacked = jnp.stack(fields)
    padded = with_halo(stacked.astype(jnp.bfloat16), (("depth", 3),), 1).astype(stacked.dtype)
    padded = jnp.pad(padded, ((0, 0), (1, 1), (1, 1), (0, 0)))
    beside = padded[:, 2:, 1:-1, 1:-1] + padded[:, :-2, 1:-1, 1:-1]
    beside = beside + padded[:, 1:-1, 2:, 1:-1] + padded[:, 1:-1, :-2, 1:-1]
    beside = beside + padded[:, 1:-1, 1:-1, 2:] + padded[:, 1:-1, 1:-1, :-2]
    result = beside - 6.0 * stacked
    return [result[index] for index in range(len(fields))]


def propagate(kappa, contrast, before, current, apply):
    grads = []
    datas = []
    grad_now = apply([current])[0]
    delta_prev = jnp.zeros_like(current)
    delta_now = contrast * grad_now
    grads.append(grad_now)
    datas.append(delta_now)
    before, current = (current, 2.0 * current - before + kappa * grad_now)
    for step in range(1, STEPS):
        grad_now, spread = apply([current, delta_now])
        delta_next = 2.0 * delta_now - delta_prev + kappa * spread + contrast * grad_now
        grads.append(grad_now)
        datas.append(delta_next)
        delta_prev, delta_now = (delta_now, delta_next)
        if step + 1 < STEPS:
            before, current = (current, 2.0 * current - before + kappa * grad_now)
    back = datas[STEPS - 1]
    back_after = jnp.zeros_like(back)
    image = grads[STEPS - 1] * back
    for step in range(STEPS - 2, -1, -1):
        spread = apply([kappa * back])
        back_new = 2.0 * back - back_after + spread[0] + datas[step]
        image = image + grads[step] * back_new
        back_after, back = (back, back_new)
    return image


def limit(mebibytes):
    return pltpu.CompilerParams(vmem_limit_bytes=mebibytes * 2**20)


def vmem():
    return pl.BlockSpec(memory_space=pltpu.VMEM)


def smem():
    return pl.BlockSpec(memory_space=pltpu.SMEM)


def prepare_kernel(
    row_ref, col_ref, ids_hbm, floor_hbm, p_hbm, s_hbm, rho_hbm, pert_hbm, out_ref,
    ids, floors, p, s, rho, pert, sems,
):
    slots, block_x, block_y, depth = p.shape
    near = block_x
    copies = [
        pltpu.make_async_copy(source, target, sems.at[index])
        for index, (source, target) in enumerate(
            [(p_hbm, p), (s_hbm, s), (rho_hbm, rho), (floor_hbm, floors), (pert_hbm, pert),
             (ids_hbm, ids)]
        )
    ]
    for copy in copies:
        copy.start()
    shape = (block_y, depth)
    deep = lax.broadcasted_iota(jnp.int32, shape, 1).astype(jnp.float32)
    lane = lax.broadcasted_iota(jnp.int32, shape, 1)
    same = lax.broadcasted_iota(jnp.int32, (block_y, block_y), 0) == (
        lax.broadcasted_iota(jnp.int32, (block_y, block_y), 1)
    )
    for copy in copies:
        copy.wait()
    for slot in range(slots):
        lines = floors[slot].astype(jnp.float32)
        for x in range(block_x):
            line = jnp.broadcast_to(lines[x:x + 1], (block_y, block_y))
            floor = jnp.sum(jnp.where(same, line, 0.0), axis=1, keepdims=True)
            primary = p[slot, x].astype(jnp.float32)
            shear = s[slot, x].astype(jnp.float32)
            square = primary * primary
            stiffness = jnp.where(deep >= floor, square + shear * shear, square)
            coef = speed_factor * stiffness / rho[slot, x].astype(jnp.float32)
            coef = coef.astype(out_ref.dtype)
            for piece in range(x, out_ref.shape[0], near):
                out_ref[piece, 2 * slot] = coef
                out_ref[piece, 2 * slot + 1] = pert[slot, x]
    facts = jnp.where(lane == slots, row_ref[0], 0)
    facts = jnp.where(lane == slots + 1, col_ref[0], facts)
    for slot in range(slots):
        facts = jnp.where(lane == slot, ids[slot], facts)
    facts = facts.astype(jnp.float32).astype(out_ref.dtype)
    for piece in range(out_ref.shape[0]):
        out_ref[piece, 2 * slots] = facts


def pick_kernel(slots, pieces_ref, out_ref, facts_ref, facts, spots, sem):
    count = facts_ref.shape[0]
    tiles = 2 * slots + 1
    near = out_ref.shape[0] // (2 * APX * APY)
    for piece in range(count):
        tile = pieces_ref[piece * tiles + 2 * slots].astype(jnp.float32)
        facts_ref[piece:piece + 1] = tile.astype(jnp.int32)[0:1]
    copy = pltpu.make_async_copy(facts_ref, facts, sem)
    copy.start()
    base = lax.axis_index("shot") // near * near
    copy.wait()
    for piece in range(count):
        for slot in range(slots):
            spots[facts[piece, slot]] = piece * tiles + 2 * slot

    def one(shot, carry):
        first = facts[base + shot, slots] * GRID_COLS + facts[base + shot, slots + 1]
        for x in range(APX):
            found = []
            for y in range(APY):
                spot = spots[first + x * GRID_COLS + y]
                found += [pieces_ref[spot], pieces_ref[spot + 1]]
            for index, tile in enumerate(found):
                out_ref[(shot * APX + x) * APY * 2 + index] = tile
        return carry

    lax.fori_loop(0, near, one, 0, unroll=2)


def ends(shape):
    lane = lax.broadcasted_iota(jnp.int32, shape, 1)
    row = lax.broadcasted_iota(jnp.int32, shape, 0)
    return lane == 0, lane == shape[1] - 1, row == 0, row == shape[0] - 1


def laplace(before, here, after, masks):
    lane_0, lane_n, row_0, row_n = masks
    many = len(here)
    depth = here[0].shape[1]
    low = [jnp.where(row_0, 0.0, pltpu.roll(here[-1], 1, 0))] + here[:-1]
    high = here[1:] + [jnp.where(row_n, 0.0, pltpu.roll(here[0], LANES - 1, 0))]
    result = []
    for v in range(many):
        up = jnp.where(lane_0, 0.0, pltpu.roll(here[v], 1, 1))
        down = jnp.where(lane_n, 0.0, pltpu.roll(here[v], depth - 1, 1))
        total = (before[v] + after[v]) + (low[v] + high[v]) + (up + down)
        result.append(total - 6.0 * here[v])
    return result


def registers(ref, x):
    return [ref[x, v] for v in range(ref.shape[1])]


def strided(ref, x):
    many = ref.shape[1] // LANES
    return [ref[x, pl.ds(v, LANES, stride=many)] for v in range(many)]


def sweep(count, fields, body, unroll):
    many = fields[0].shape[1]
    zero = [jnp.zeros(fields[0].shape[2:], jnp.float32)] * many
    first = [(zero, registers(field, 0)) for field in fields]

    def step(x, carry):
        rows = [
            (before, here, registers(field, x + 1))
            for (before, here), field in zip(carry, fields)
        ]
        body(x, rows)
        return [(here, after) for _, here, after in rows]

    lax.fori_loop(0, count, step, first, unroll=unroll)


def start_kernel(prev_ref, now_ref, wave_ref, grad_ref, next_ref, flat, flat_prev, field):
    span_x, span_y, depth = now_ref.shape
    many = span_y // LANES
    masks = ends((LANES, depth))

    def load(x, carry):
        flat[x] = now_ref[x].astype(jnp.float32)
        flat_prev[x] = prev_ref[x].astype(jnp.float32)
        return carry

    lax.fori_loop(0, span_x, load, 0, unroll=2)

    def order(x, carry):
        rows = strided(flat, x)
        older = strided(flat_prev, x)
        for v in range(many):
            field[x, v] = rows[v]
            wave_ref[x, v] = rows[v]
            next_ref[x, v] = 2.0 * rows[v] - older[v]
        return carry

    lax.fori_loop(0, span_x, order, 0, unroll=2)
    for v in range(many):
        field[span_x, v] = jnp.zeros((LANES, depth), jnp.float32)

    def body(x, rows):
        grads = laplace(*rows[0], masks)
        for v in range(many):
            grad_ref[x, v] = grads[v]

    sweep(span_x, [field], body, 16)


def start(before, current):
    span_x, span_y, depth = before.shape
    many = span_y // LANES
    out = jax.ShapeDtypeStruct((span_x, many, LANES, depth), jnp.float32)
    flat = pltpu.VMEM((span_x, span_y, depth), jnp.float32)
    return pl.pallas_call(
        start_kernel,
        out_shape=(out, out, out),
        in_specs=[vmem()] * 2,
        out_specs=(vmem(),) * 3,
        scratch_shapes=[flat, flat, pltpu.VMEM((span_x + 1, many, LANES, depth), jnp.float32)],
        compiler_params=limit(8),
        cost_estimate=pl.CostEstimate(
            flops=20 * before.size, bytes_accessed=16 * before.size, transcendentals=0
        ),
        name="start",
    )(before, current)


def wave_kernel(
    model_ref, u_0, g_0, next_ref, out_ref,
    kap, con, u_1, u_2, u_3, d_0, d_1, d_2, kb_3, kb_2, kb_1, g_1, g_2, d_3, b_2, b_1, image,
):
    span_x, many = u_0.shape[:2]
    depth = u_0.shape[3]
    block_y = model_ref.shape[2]
    block_x = span_x // APX
    masks = ends((LANES, depth))
    each = range(many)
    for field in (u_1, u_2, u_3, d_0, d_1, d_2, kb_3, kb_2, kb_1):
        for v in each:
            field[span_x, v] = jnp.zeros((LANES, depth), jnp.float32)

    def load(piece, carry):
        for x in range(APX):
            for y in range(APY):
                rows = pl.ds(y * block_y, block_y)
                at = x * block_x + piece
                tile = 2 * (x * APY + y)
                kap[at, rows] = model_ref[piece, tile].astype(jnp.float32)
                con[at, rows] = speed_factor * model_ref[piece, tile + 1].astype(jnp.float32)
        return carry

    lax.fori_loop(0, block_x, load, 0, unroll=4)

    def forward_0(x, carry):
        kaps, cons, grads = strided(kap, x), strided(con, x), registers(g_0, x)
        older = registers(next_ref, x)
        for v in each:
            d_0[x, v] = cons[v] * grads[v]
            u_1[x, v] = older[v] + kaps[v] * grads[v]
        return carry

    lax.fori_loop(0, span_x, forward_0, 0, unroll=16)

    def forward(u_now, u_prev, d_now, d_prev, u_next, d_next, g_now):
        def body(x, rows):
            waves, deltas = rows
            grads = laplace(*waves, masks)
            spread = laplace(*deltas, masks)
            kaps, cons = strided(kap, x), strided(con, x)
            for v in each:
                value = 2.0 * deltas[1][v] + kaps[v] * spread[v] + cons[v] * grads[v]
                if d_prev is not None:
                    value = value - d_prev[x, v]
                d_next[x, v] = value
                if u_next is None:
                    image[x, v] = grads[v] * value
                    kb_3[x, v] = kaps[v] * value
                else:
                    g_now[x, v] = grads[v]
                    u_next[x, v] = 2.0 * waves[1][v] - u_prev[x, v] + kaps[v] * grads[v]

        sweep(span_x, [u_now, d_now], body, 16)

    forward(u_1, u_0, d_0, None, u_2, d_1, g_1)
    forward(u_2, u_1, d_1, d_0, u_3, d_2, g_2)
    forward(u_3, u_2, d_2, d_1, None, d_3, None)

    def adjoint(kb, b_now, b_after, data, grad, kb_next, b_next):
        def body(x, rows):
            spread = laplace(*rows[0], masks)
            kaps = None if kb_next is None else strided(kap, x)
            for v in each:
                back = 2.0 * b_now[x, v] + spread[v] + data[x, v]
                if b_after is not None:
                    back = back - b_after[x, v]
                total = image[x, v] + grad[x, v] * back
                if kb_next is None:
                    total = (image_scale * total).astype(out_ref.dtype)
                    out_ref[x % block_x, x // block_x * many + v] = total
                else:
                    image[x, v] = total
                    b_next[x, v] = back
                    kb_next[x, v] = kaps[v] * back

        sweep(span_x, [kb], body, 16)

    adjoint(kb_3, d_3, None, d_2, g_2, kb_2, b_2)
    adjoint(kb_2, b_2, d_3, d_1, g_1, kb_1, b_1)
    adjoint(kb_1, b_1, b_2, d_0, g_0, None, None)


def wave(model, started):
    span_x, many, _, depth = started[0].shape
    near, tiles, _, _ = model.shape
    flat = pltpu.VMEM((span_x, many * LANES, depth), jnp.float32)
    field = pltpu.VMEM((span_x + 1, many, LANES, depth), jnp.float32)
    plain = pltpu.VMEM((span_x, many, LANES, depth), jnp.float32)
    return pl.pallas_call(
        wave_kernel,
        out_shape=jax.ShapeDtypeStruct((near, APX * many, LANES, depth), jnp.bfloat16),
        in_specs=[vmem()] * 4,
        out_specs=vmem(),
        scratch_shapes=[flat] * 2 + [field] * 9 + [plain] * 6,
        compiler_params=limit(20),
        name="wave",
    )(model, *started)


def wave_split_depth(model, before, current):
    span_x, span_y, depth = before.shape
    block_x, tiles, block_y, _ = model.shape
    grids = model.reshape(block_x, APX, APY, 2, block_y, depth).transpose(3, 1, 0, 2, 4, 5)
    grids = grids.reshape(2, span_x, span_y, depth).astype(jnp.float32)
    image = image_scale * propagate(
        grids[0],
        speed_factor * grids[1],
        before.astype(jnp.float32),
        current.astype(jnp.float32),
        laplace_many,
    )
    many = span_y // LANES
    image = image.reshape(APX, block_x, LANES, many, depth).transpose(1, 0, 3, 2, 4)
    return image.reshape(block_x, APX * many, LANES, depth).astype(jnp.bfloat16)


def stack_kernel(slots, facts_ref, terms_ref, out_ref, facts, total, lined, sem):
    shots, tiles = terms_ref.shape[:2]
    wide = tiles // APX
    width = LANES // APY
    grid_rows = total.shape[0] // wide
    copy = pltpu.make_async_copy(facts_ref, facts, sem)
    copy.start()
    base = lax.axis_index("shot") // shots * shots

    def clear(index, carry):
        total[index] = jnp.zeros(total.shape[1:], total.dtype)
        return carry

    lax.fori_loop(0, total.shape[0], clear, 0, unroll=8)
    copy.wait()

    def add(shot, carry):
        first = facts[base + shot, slots] * wide
        rows = pl.ds(facts[base + shot, slots + 1] * width, LANES)
        sums = [
            total[first + tile, rows] + terms_ref[shot, tile].astype(jnp.float32)
            for tile in range(tiles)
        ]
        for tile in range(tiles):
            total[first + tile, rows] = sums[tile]
        return carry

    lax.fori_loop(0, shots, add, 0, unroll=2)

    for row in range(grid_rows):
        for part in range(wide):
            for tile in range(total.shape[1] // LANES):
                at = pl.ds(tile * LANES * wide + part, LANES, stride=wide)
                lined[row, at] = total[row * wide + part, tile * LANES:(tile + 1) * LANES]

    def give(owner, carry):
        found = []
        for slot in range(slots):
            block = facts[owner, slot]
            rows = pl.ds(pl.multiple_of(block % GRID_COLS * LANES, LANES), LANES)
            found.append(lined[block // GRID_COLS, rows])
        for slot in range(slots):
            out_ref[owner, slot] = found[slot].astype(out_ref.dtype)
        return carry

    lax.fori_loop(0, out_ref.shape[0], give, 0, unroll=4)


def finish_kernel(sums_ref, out_ref):
    slots, block_x = out_ref.shape[:2]
    for x in range(block_x):
        for slot in range(slots):
            result = sums_ref[x, slot].astype(jnp.float32)
            for piece in range(x + block_x, sums_ref.shape[0], block_x):
                result = result + sums_ref[piece, slot].astype(jnp.float32)
            out_ref[slot, x] = result


def per_device(
    velocity_p,
    velocity_s,
    density,
    perturbation,
    seafloor,
    owner_ids,
    corner_x,
    corner_y,
    wave_prev,
    wave_now,
):
    slots, block_x, block_y, depth = velocity_p.shape
    count = lax.axis_size("shot")
    assert count == 2 * block_x and block_y == LANES
    patch = APX * APY
    split = lax.axis_size("depth") > 1
    if split:
        seafloor = seafloor - lax.axis_index("depth") * depth

    near = block_x
    groups = [list(range(first, first + near)) for first in range(0, count, near)]
    sent = pl.pallas_call(
        prepare_kernel,
        out_shape=jax.ShapeDtypeStruct((count, 2 * slots + 1, block_y, depth), jnp.bfloat16),
        in_specs=[smem()] * 2 + [pl.BlockSpec(memory_space=pltpu.HBM)] * 6,
        out_specs=vmem(),
        scratch_shapes=[
            pltpu.SMEM(owner_ids.shape, jnp.int32),
            pltpu.VMEM(seafloor.shape, jnp.int32),
            *[pltpu.VMEM(velocity_p.shape, jnp.bfloat16) for _ in range(4)],
            pltpu.SemaphoreType.DMA((6,)),
        ],
        name="prepare",
    )(
        corner_x, corner_y, owner_ids, seafloor,
        velocity_p, velocity_s, density, perturbation,
    )
    pieces = lax.all_to_all(sent, "shot", 0, 0, tiled=True)

    if not split:
        started = start(wave_prev[0], wave_now[0])
        pieces, started = lax.optimization_barrier((pieces, started))
    picked, facts = pl.pallas_call(
        functools.partial(pick_kernel, slots),
        out_shape=(
            jax.ShapeDtypeStruct((near * patch * 2, block_y, depth), jnp.bfloat16),
            jax.ShapeDtypeStruct((count, depth), jnp.int32),
        ),
        in_specs=[vmem()],
        out_specs=(vmem(), vmem()),
        scratch_shapes=[
            pltpu.SMEM((count, depth), jnp.int32),
            pltpu.SMEM((count * slots,), jnp.int32),
            pltpu.SemaphoreType.DMA,
        ],
        compiler_params=limit(3),
        name="pick",
    )(pieces.reshape(count * (2 * slots + 1), block_y, depth))
    model = lax.all_to_all(
        picked.reshape(near, patch * 2, block_y, depth), "shot", 0, 0,
        axis_index_groups=groups, tiled=True,
    )

    if split:
        terms = wave_split_depth(model, wave_prev[0], wave_now[0])
    else:
        terms = wave(model, started)
    terms = lax.all_to_all(terms, "shot", 0, 0, axis_index_groups=groups, tiled=True)

    grid_rows = count * slots // GRID_COLS
    wide = terms.shape[1] // APX
    sums = pl.pallas_call(
        functools.partial(stack_kernel, slots),
        out_shape=jax.ShapeDtypeStruct((count, slots, block_y, depth), jnp.bfloat16),
        in_specs=[vmem(), vmem()],
        out_specs=vmem(),
        scratch_shapes=[
            pltpu.SMEM(facts.shape, jnp.int32),
            pltpu.VMEM((grid_rows * wide, GRID_COLS * LANES // APY, depth), jnp.float32),
            pltpu.VMEM((grid_rows, GRID_COLS * block_y, depth), jnp.float32),
            pltpu.SemaphoreType.DMA,
        ],
        compiler_params=limit(3),
        name="stack",
    )(facts, terms)
    sums = lax.all_to_all(sums, "shot", 0, 0, tiled=True)
    return pl.pallas_call(
        finish_kernel,
        out_shape=jax.ShapeDtypeStruct(velocity_p.shape, jnp.float32),
        in_specs=[vmem()],
        out_specs=vmem(),
        compiler_params=limit(2),
        name="finish",
    )(sums)


def solution(mesh):
    in_specs = (
        P(("grp", "shot"), None, None, "depth"),
        P(("grp", "shot"), None, None, "depth"),
        P(("grp", "shot"), None, None, "depth"),
        P(("grp", "shot"), None, None, "depth"),
        P(("grp", "shot"), None, None),
        P(("grp", "shot")),
        P(("grp", "shot")),
        P(("grp", "shot")),
        P(("grp", "shot"), None, None, "depth"),
        P(("grp", "shot"), None, None, "depth"),
    )
    out_specs = P(("grp", "shot"), None, None, "depth")
    return jax.shard_map(
        per_device, mesh=mesh, in_specs=in_specs, out_specs=out_specs, check_vma=False
    )
```

profile of v0, /device:TPU:0, one launch (start us, length us, event | category | flops | bytes accessed | tf_op | source)
XLA Modules:
  0.0 58.8 jit_solution(16435193077348856559)
XLA Ops:
  1.3 1.8 %prepare.1 = bf16[16,9,8,128]{3,2,1,0:T(8,128)(2,1)} custom-call(s32[1]{0:T(128)S(6)} %copy.11.row_ref, s32[1]{0:T(128)S(6)} %copy.12.col_ref, s32[4]{0:T(128)} %ids_hbm.1, s32[4,8,8]{2,1,0:T(8,128)} %floor_hbm.1, bf16[4,8,8,128]{3,2,1,0:T(8,128)(2,1)} %p_hbm.1, bf16[4,8,8,128]{3,2,1,0:T(8,128)(2,1)} %s_hbm.1, bf16[4,8,8,128]{3,2,1,0:T(8,128)(2,1)} %rho_hbm.1, ...), custom_call_target="tpu_custom_call" | custom-call | tf_op jit(solution)/shard_map/prepare/pallas_call | solution.py:455
  3.1 0.0 copy-start
  3.2 0.0 copy-start.1
  3.2 7.5 %all-to-all-start = ((bf16[16,9,8,128]{3,2,1,0:T(8,128)(2,1)}), bf16[16,9,8,128]{3,2,1,0:T(8,128)(2,1)S(1)}, u32[]{:S(2)}, u32[]{:S(2)}) async-start(bf16[16,9,8,128]{3,2,1,0:T(8,128)(2,1)} %prepare.1), calls=%async_computation | async-start | bytes 589824 | tf_op jit(solution)/shard_map/all_to_all | solution.py:471
  10.7 0.0 copy-done
  10.7 0.0 copy-done.1
  10.7 0.7 %start.1 = (f32[32,4,8,128]{3,2,1,0:T(8,128)S(1)}, f32[32,4,8,128]{3,2,1,0:T(8,128)S(1)}, f32[32,4,8,128]{3,2,1,0:T(8,128)S(1)}) custom-call(bf16[32,32,128]{2,1,0:T(8,128)(2,1)S(1)} %bitcast.6, bf16[32,32,128]{2,1,0:T(8,128)(2,1)S(1)} %bitcast.7), custom_call_target="tpu_custom_call" | custom-call | flops 2621440 | bytes 2097152 | tf_op jit(solution)/shard_map/start/pallas_call | solution.py:243
  11.4 9.9 %all-to-all-done = bf16[16,9,8,128]{3,2,1,0:T(8,128)(2,1)S(1)} async-done(((bf16[16,9,8,128]{3,2,1,0:T(8,128)(2,1)}), bf16[16,9,8,128]{3,2,1,0:T(8,128)(2,1)S(1)}, u32[]{:S(2)}, u32[]{:S(2)}) %all-to-all-start) | async-done | bytes 294944 | tf_op jit(solution)/shard_map/all_to_all | solution.py:471
  21.2 0.9 %pick.1 = (bf16[256,8,128]{2,1,0:T(8,128)(2,1)S(1)}, s32[16,128]{1,0:T(8,128)S(1)}) custom-call(bf16[144,8,128]{2,1,0:T(8,128)(2,1)S(1)} %bitcast.4), custom_call_target="tpu_custom_call" | custom-call | tf_op jit(solution)/shard_map/pick/pallas_call | solution.py:476
  22.2 11.3 %all_to_all.20.model_ref = bf16[8,32,8,128]{3,2,1,0:T(8,128)(2,1)S(1)} all-to-all(bf16[8,32,8,128]{3,2,1,0:T(8,128)(2,1)S(1)} %bitcast.5), channel_id=1, replica_groups={{0,1,2,3,4,5,6,7},{8,9,10,11,12,13,14,15},{16,17,18,19,20,21,22,23},{24..., dimensions={0} | all-to-all | bytes 1048576 | tf_op jit(solution)/shard_map/all_to_all | solution.py:492
  33.5 3.5 %wave.1 = bf16[8,16,8,128]{3,2,1,0:T(8,128)(2,1)S(1)} custom-call(bf16[8,32,8,128]{3,2,1,0:T(8,128)(2,1)S(1)} %all_to_all.20.model_ref, f32[32,4,8,128]{3,2,1,0:T(8,128)S(1)} %get-tuple-element.20.u_0, f32[32,4,8,128]{3,2,1,0:T(8,128)S(1)} %get-tuple-element.21.g_0, f32[32,4,8,128]{3,2,1,0:T(8,128)S(1)} %get-tuple-element.22.next_ref), custom_call_target="tpu_custom_call" | custom-call | tf_op jit(solution)/shard_map/wave/pallas_call | solution.py:347
  37.0 8.6 %all_to_all.21.terms_ref = bf16[8,16,8,128]{3,2,1,0:T(8,128)(2,1)S(1)} all-to-all(bf16[8,16,8,128]{3,2,1,0:T(8,128)(2,1)S(1)} %wave.1), channel_id=1, replica_groups={{0,1,2,3,4,5,6,7},{8,9,10,11,12,13,14,15},{16,17,18,19,20,21,22,23},{24..., dimensions={0} | all-to-all | bytes 524288 | tf_op jit(solution)/shard_map/all_to_all | solution.py:501
  45.7 1.2 %stack.1 = bf16[16,4,8,128]{3,2,1,0:T(8,128)(2,1)S(1)} custom-call(s32[16,128]{1,0:T(8,128)S(1)} %get-tuple-element.18.facts_ref, bf16[8,16,8,128]{3,2,1,0:T(8,128)(2,1)S(1)} %all_to_all.21.terms_ref), custom_call_target="tpu_custom_call" | custom-call | tf_op jit(solution)/shard_map/stack/pallas_call | solution.py:505
  46.9 11.3 %all_to_all.22.sums_ref = bf16[16,4,8,128]{3,2,1,0:T(8,128)(2,1)S(1)} all-to-all(bf16[16,4,8,128]{3,2,1,0:T(8,128)(2,1)S(1)} %stack.1), channel_id=1, replica_groups=mesh['grp'=2,'shot'=16,'depth'=1] {'shot'}, dimensions={0} | all-to-all | bytes 262144 | tf_op jit(solution)/shard_map/all_to_all | solution.py:519
  58.2 0.7 %finish.1 = f32[4,8,8,128]{3,2,1,0:T(8,128)} custom-call(bf16[16,4,8,128]{3,2,1,0:T(8,128)(2,1)S(1)} %all_to_all.22.sums_ref), custom_call_target="tpu_custom_call" | custom-call | tf_op jit(solution)/shard_map/finish/pallas_call | solution.py:520
Async XLA Ops:
  3.1 7.5 %copy-start = (bf16[1,32,32,128]{3,2,1,0:T(8,128)(2,1)S(1)}, bf16[1,32,32,128]{3,2,1,0:T(8,128)(2,1)}, u32[]{:S(2)}) copy-start(bf16[1,32,32,128]{3,2,1,0:T(8,128)(2,1)} %param.18) | copy-start | bytes 786436
  3.2 7.5 %copy-start.1 = (bf16[1,32,32,128]{3,2,1,0:T(8,128)(2,1)S(1)}, bf16[1,32,32,128]{3,2,1,0:T(8,128)(2,1)}, u32[]{:S(2)}) copy-start(bf16[1,32,32,128]{3,2,1,0:T(8,128)(2,1)} %param.19) | copy-start | bytes 786436
  3.2 18.1 %all-to-all-start = ((bf16[16,9,8,128]{3,2,1,0:T(8,128)(2,1)}), bf16[16,9,8,128]{3,2,1,0:T(8,128)(2,1)S(1)}, u32[]{:S(2)}, u32[]{:S(2)}) async-start(bf16[16,9,8,128]{3,2,1,0:T(8,128)(2,1)} %prepare.1), calls=%async_computation | async-start | bytes 589824 | tf_op jit(solution)/shard_map/all_to_all | solution.py:471
where the time goes:
time: 59.2 us; the launch traced here: 58.8 us
  blocking collectives  31.2 us (53%)
  waiting for transfers between devices  9.85 us (17%)
  Pallas kernels  8.88 us (15%)
  starting transfers between devices  7.5 us (13%)
  between operations  1.38 us (2%)
    all_to_all x1, blocking collectives, per_device(): lax.all_to_all(picked.reshape(near, patch * 2, block_y, depth), 'shot', 0...  11.3 us
    all_to_all x1, blocking collectives, per_device(): sums = lax.all_to_all(sums, 'shot', 0, 0, tiled=True)  11.3 us
    all_to_all x1, waiting for transfers between devices, per_device(): pieces = lax.all_to_all(sent, 'shot', 0, 0, tiled=True)  9.85 us
    all_to_all x1, blocking collectives, per_device(): lax.all_to_all(terms, 'shot', 0, 0, axis_index_groups=groups, tiled=True)  8.62 us
    all_to_all x1, starting transfers between devices, per_device(): pieces = lax.all_to_all(sent, 'shot', 0, 0, tiled=True)  7.5 us
    pallas_call x1, Pallas kernels, wave(): pl.pallas_call(wave_kernel, out_shape=jax.ShapeDtypeStruct((near, APX * m...  3.55 us
    pallas_call x1, Pallas kernels, per_device(): pl.pallas_call(prepare_kernel, out_shape=jax.ShapeDtypeStruct((count, 2 *...  1.84 us
    pallas_call x1, Pallas kernels, per_device(): pl.pallas_call(functools.partial(stack_kernel, slots), out_shape=jax.Shap...  1.21 us
  transfers between devices with their start and end apart: 1, of which 1 were waited for; matrix products, arithmetic and copies ran while one was open for 0% of the time, Pallas kernels for 1%

commit v1 on v0

--- a/solution.py
+++ b/solution.py
@@ -82,7 +82,7 @@
 
 
 def prepare_kernel(
-    row_ref, col_ref, ids_hbm, floor_hbm, p_hbm, s_hbm, rho_hbm, pert_hbm, out_ref,
+    row_ref, col_ref, ids_hbm, floor_hbm, p_hbm, s_hbm, rho_hbm, pert_hbm, out_ref, pert_ref,
     ids, floors, p, s, rho, pert, sems,
 ):
     slots, block_x, block_y, depth = p.shape
@@ -116,44 +116,49 @@
             coef = speed_factor * stiffness / rho[slot, x].astype(jnp.float32)
             coef = coef.astype(out_ref.dtype)
             for piece in range(x, out_ref.shape[0], near):
-                out_ref[piece, 2 * slot] = coef
-                out_ref[piece, 2 * slot + 1] = pert[slot, x]
+                out_ref[piece, slot] = coef
+                pert_ref[piece, slot] = pert[slot, x]
     facts = jnp.where(lane == slots, row_ref[0], 0)
     facts = jnp.where(lane == slots + 1, col_ref[0], facts)
     for slot in range(slots):
         facts = jnp.where(lane == slot, ids[slot], facts)
     facts = facts.astype(jnp.float32).astype(out_ref.dtype)
     for piece in range(out_ref.shape[0]):
-        out_ref[piece, 2 * slots] = facts
-
-
-def pick_kernel(slots, pieces_ref, out_ref, facts_ref, facts, spots, sem):
+        out_ref[piece, slots] = facts
+
+
+def pick_tiles(slots, stride, pieces_ref, facts_ref, out_ref, facts, spots, sem):
     count = facts_ref.shape[0]
-    tiles = 2 * slots + 1
-    near = out_ref.shape[0] // (2 * APX * APY)
-    for piece in range(count):
-        tile = pieces_ref[piece * tiles + 2 * slots].astype(jnp.float32)
-        facts_ref[piece:piece + 1] = tile.astype(jnp.int32)[0:1]
+    near = out_ref.shape[0] // (APX * APY)
     copy = pltpu.make_async_copy(facts_ref, facts, sem)
     copy.start()
     base = lax.axis_index("shot") // near * near
     copy.wait()
     for piece in range(count):
         for slot in range(slots):
-            spots[facts[piece, slot]] = piece * tiles + 2 * slot
+            spots[facts[piece, slot]] = piece * stride + slot
 
     def one(shot, carry):
         first = facts[base + shot, slots] * GRID_COLS + facts[base + shot, slots + 1]
-        for x in range(APX):
-            found = []
-            for y in range(APY):
-                spot = spots[first + x * GRID_COLS + y]
-                found += [pieces_ref[spot], pieces_ref[spot + 1]]
-            for index, tile in enumerate(found):
-                out_ref[(shot * APX + x) * APY * 2 + index] = tile
+        found = [
+            pieces_ref[spots[first + x * GRID_COLS + y]] for x in range(APX) for y in range(APY)
+        ]
+        for index, tile in enumerate(found):
+            out_ref[shot * APX * APY + index] = tile
         return carry
 
     lax.fori_loop(0, near, one, 0, unroll=2)
+
+
+def pick_kernel(slots, pieces_ref, out_ref, facts_ref, facts, spots, sem):
+    for piece in range(facts_ref.shape[0]):
+        tile = pieces_ref[piece * (slots + 1) + slots].astype(jnp.float32)
+        facts_ref[piece:piece + 1] = tile.astype(jnp.int32)[0:1]
+    pick_tiles(slots, slots + 1, pieces_ref, facts_ref, out_ref, facts, spots, sem)
+
+
+def pick_more_kernel(slots, facts_ref, pieces_ref, out_ref, facts, spots, sem):
+    pick_tiles(slots, slots, pieces_ref, facts_ref, out_ref, facts, spots, sem)
 
 
 def ends(shape):
@@ -254,65 +259,113 @@
     )(before, current)
 
 
-def wave_kernel(
-    model_ref, u_0, g_0, next_ref, out_ref,
-    kap, con, u_1, u_2, u_3, d_0, d_1, d_2, kb_3, kb_2, kb_1, g_1, g_2, d_3, b_2, b_1, image,
-):
-    span_x, many = u_0.shape[:2]
-    depth = u_0.shape[3]
-    block_y = model_ref.shape[2]
-    block_x = span_x // APX
-    masks = ends((LANES, depth))
-    each = range(many)
-    for field in (u_1, u_2, u_3, d_0, d_1, d_2, kb_3, kb_2, kb_1):
-        for v in each:
-            field[span_x, v] = jnp.zeros((LANES, depth), jnp.float32)
+def flatten(model_ref, flat, factor):
+    block_x, _, block_y, _ = model_ref.shape
 
     def load(piece, carry):
         for x in range(APX):
             for y in range(APY):
-                rows = pl.ds(y * block_y, block_y)
-                at = x * block_x + piece
-                tile = 2 * (x * APY + y)
-                kap[at, rows] = model_ref[piece, tile].astype(jnp.float32)
-                con[at, rows] = speed_factor * model_ref[piece, tile + 1].astype(jnp.float32)
+                tile = model_ref[piece, x * APY + y].astype(jnp.float32)
+                tile = tile if factor is None else factor * tile
+                flat[x * block_x + piece, pl.ds(y * block_y, block_y)] = tile
         return carry
 
     lax.fori_loop(0, block_x, load, 0, unroll=4)
 
+
+def close(*fields):
+    for field in fields:
+        for v in range(field.shape[1]):
+            field[field.shape[0] - 1, v] = jnp.zeros(field.shape[2:], jnp.float32)
+
+
+def background_kernel(model_ref, u_0, g_0, next_ref, kap, g_1, g_2, g_3, u_1, u_2, u_3):
+    span_x, many, _, depth = u_0.shape
+    masks = ends((LANES, depth))
+    each = range(many)
+    close(u_1, u_2, u_3)
+    flatten(model_ref, kap, None)
+
     def forward_0(x, carry):
-        kaps, cons, grads = strided(kap, x), strided(con, x), registers(g_0, x)
-        older = registers(next_ref, x)
+        kaps, grads, older = strided(kap, x), registers(g_0, x), registers(next_ref, x)
+        for v in each:
+            u_1[x, v] = older[v] + kaps[v] * grads[v]
+        return carry
+
+    lax.fori_loop(0, span_x, forward_0, 0, unroll=16)
+
+    def forward(u_now, u_prev, u_next, g_now):
+        def body(x, rows):
+            grads = laplace(*rows[0], masks)
+            kaps = None if u_next is None else strided(kap, x)
+            for v in each:
+                g_now[x, v] = grads[v]
+                if u_next is not None:
+                    u_next[x, v] = 2.0 * rows[0][1][v] - u_prev[x, v] + kaps[v] * grads[v]
+
+        sweep(span_x, [u_now], body, 16)
+
+    forward(u_1, u_0, u_2, g_1)
+    forward(u_2, u_1, u_3, g_2)
+    forward(u_3, u_2, None, g_3)
+
+
+def background(model, started):
+    span_x, many, _, depth = started[0].shape
+    flat = (span_x, many * LANES, depth)
+    plain = jax.ShapeDtypeStruct(started[0].shape, jnp.float32)
+    field = pltpu.VMEM((span_x + 1, many, LANES, depth), jnp.float32)
+    return pl.pallas_call(
+        background_kernel,
+        out_shape=(jax.ShapeDtypeStruct(flat, jnp.float32), plain, plain, plain),
+        in_specs=[vmem()] * 4,
+        out_specs=(vmem(),) * 4,
+        scratch_shapes=[field] * 3,
+        compiler_params=limit(8),
+        cost_estimate=pl.CostEstimate(
+            flops=50 * plain.size, bytes_accessed=32 * plain.size, transcendentals=0
+        ),
+        name="background",
+    )(model, *started)
+
+
+def wave_kernel(
+    model_ref, kap, g_0, g_1, g_2, g_3, out_ref,
+    con, d_0, d_1, d_2, kb_3, kb_2, kb_1, d_3, b_2, b_1, image,
+):
+    span_x, many, _, depth = g_0.shape
+    block_x = model_ref.shape[0]
+    masks = ends((LANES, depth))
+    each = range(many)
+    close(d_0, d_1, d_2, kb_3, kb_2, kb_1)
+    flatten(model_ref, con, speed_factor)
+
+    def forward_0(x, carry):
+        cons, grads = strided(con, x), registers(g_0, x)
         for v in each:
             d_0[x, v] = cons[v] * grads[v]
-            u_1[x, v] = older[v] + kaps[v] * grads[v]
         return carry
 
     lax.fori_loop(0, span_x, forward_0, 0, unroll=16)
 
-    def forward(u_now, u_prev, d_now, d_prev, u_next, d_next, g_now):
+    def forward(d_now, d_prev, d_next, grad, last):
         def body(x, rows):
-            waves, deltas = rows
-            grads = laplace(*waves, masks)
-            spread = laplace(*deltas, masks)
-            kaps, cons = strided(kap, x), strided(con, x)
+            spread = laplace(*rows[0], masks)
+            kaps, cons, grads = strided(kap, x), strided(con, x), registers(grad, x)
             for v in each:
-                value = 2.0 * deltas[1][v] + kaps[v] * spread[v] + cons[v] * grads[v]
+                value = 2.0 * rows[0][1][v] + kaps[v] * spread[v] + cons[v] * grads[v]
                 if d_prev is not None:
                     value = value - d_prev[x, v]
                 d_next[x, v] = value
-                if u_next is None:
+                if last:
                     image[x, v] = grads[v] * value
                     kb_3[x, v] = kaps[v] * value
-                else:
-                    g_now[x, v] = grads[v]
-                    u_next[x, v] = 2.0 * waves[1][v] - u_prev[x, v] + kaps[v] * grads[v]
-
-        sweep(span_x, [u_now, d_now], body, 16)
-
-    forward(u_1, u_0, d_0, None, u_2, d_1, g_1)
-    forward(u_2, u_1, d_1, d_0, u_3, d_2, g_2)
-    forward(u_3, u_2, d_2, d_1, None, d_3, None)
+
+        sweep(span_x, [d_now], body, 16)
+
+    forward(d_0, None, d_1, g_1, False)
+    forward(d_1, d_0, d_2, g_2, False)
+    forward(d_2, d_1, d_3, g_3, True)
 
     def adjoint(kb, b_now, b_after, data, grad, kb_next, b_next):
         def body(x, rows):
@@ -338,31 +391,34 @@
     adjoint(kb_1, b_1, b_2, d_0, g_0, None, None)
 
 
-def wave(model, started):
-    span_x, many, _, depth = started[0].shape
-    near, tiles, _, _ = model.shape
+def wave(model, g_0, kap, *grads):
+    span_x, many, _, depth = g_0.shape
+    near = model.shape[0]
     flat = pltpu.VMEM((span_x, many * LANES, depth), jnp.float32)
     field = pltpu.VMEM((span_x + 1, many, LANES, depth), jnp.float32)
     plain = pltpu.VMEM((span_x, many, LANES, depth), jnp.float32)
     return pl.pallas_call(
         wave_kernel,
         out_shape=jax.ShapeDtypeStruct((near, APX * many, LANES, depth), jnp.bfloat16),
-        in_specs=[vmem()] * 4,
+        in_specs=[vmem()] * 6,
         out_specs=vmem(),
-        scratch_shapes=[flat] * 2 + [field] * 9 + [plain] * 6,
-        compiler_params=limit(20),
+        scratch_shapes=[flat] + [field] * 6 + [plain] * 4,
+        compiler_params=limit(16),
         name="wave",
-    )(model, *started)
-
-
-def wave_split_depth(model, before, current):
+    )(model, kap, g_0, *grads)
+
+
+def wave_split_depth(coef, pert, before, current):
     span_x, span_y, depth = before.shape
-    block_x, tiles, block_y, _ = model.shape
-    grids = model.reshape(block_x, APX, APY, 2, block_y, depth).transpose(3, 1, 0, 2, 4, 5)
-    grids = grids.reshape(2, span_x, span_y, depth).astype(jnp.float32)
+    block_x, _, block_y, _ = coef.shape
+
+    def grid(model):
+        model = model.reshape(block_x, APX, APY, block_y, depth).transpose(1, 0, 2, 3, 4)
+        return model.reshape(span_x, span_y, depth).astype(jnp.float32)
+
     image = image_scale * propagate(
-        grids[0],
-        speed_factor * grids[1],
+        grid(coef),
+        speed_factor * grid(pert),
         before.astype(jnp.float32),
         current.astype(jnp.float32),
         laplace_many,
@@ -452,11 +508,14 @@
 
     near = block_x
     groups = [list(range(first, first + near)) for first in range(0, count, near)]
-    sent = pl.pallas_call(
+    sent, sent_pert = pl.pallas_call(
         prepare_kernel,
-        out_shape=jax.ShapeDtypeStruct((count, 2 * slots + 1, block_y, depth), jnp.bfloat16),
+        out_shape=(
+            jax.ShapeDtypeStruct((count, slots + 1, block_y, depth), jnp.bfloat16),
+            jax.ShapeDtypeStruct((count, slots, block_y, depth), jnp.bfloat16),
+        ),
         in_specs=[smem()] * 2 + [pl.BlockSpec(memory_space=pltpu.HBM)] * 6,
-        out_specs=vmem(),
+        out_specs=(vmem(), vmem()),
         scratch_shapes=[
             pltpu.SMEM(owner_ids.shape, jnp.int32),
             pltpu.VMEM(seafloor.shape, jnp.int32),
@@ -469,35 +528,46 @@
         velocity_p, velocity_s, density, perturbation,
     )
     pieces = lax.all_to_all(sent, "shot", 0, 0, tiled=True)
-
+    pieces_pert = lax.all_to_all(sent_pert, "shot", 0, 0, tiled=True)
     if not split:
         started = start(wave_prev[0], wave_now[0])
         pieces, started = lax.optimization_barrier((pieces, started))
+    picked_shape = jax.ShapeDtypeStruct((near * patch, block_y, depth), jnp.bfloat16)
+    pick_scratch = [
+        pltpu.SMEM((count, depth), jnp.int32),
+        pltpu.SMEM((count * slots,), jnp.int32),
+        pltpu.SemaphoreType.DMA,
+    ]
     picked, facts = pl.pallas_call(
         functools.partial(pick_kernel, slots),
-        out_shape=(
-            jax.ShapeDtypeStruct((near * patch * 2, block_y, depth), jnp.bfloat16),
-            jax.ShapeDtypeStruct((count, depth), jnp.int32),
-        ),
+        out_shape=(picked_shape, jax.ShapeDtypeStruct((count, depth), jnp.int32)),
         in_specs=[vmem()],
         out_specs=(vmem(), vmem()),
-        scratch_shapes=[
-            pltpu.SMEM((count, depth), jnp.int32),
-            pltpu.SMEM((count * slots,), jnp.int32),
-            pltpu.SemaphoreType.DMA,
-        ],
+        scratch_shapes=pick_scratch,
         compiler_params=limit(3),
         name="pick",
-    )(pieces.reshape(count * (2 * slots + 1), block_y, depth))
-    model = lax.all_to_all(
-        picked.reshape(near, patch * 2, block_y, depth), "shot", 0, 0,
-        axis_index_groups=groups, tiled=True,
-    )
+    )(pieces.reshape(count * (slots + 1), block_y, depth))
+    picked_pert = pl.pallas_call(
+        functools.partial(pick_more_kernel, slots),
+        out_shape=picked_shape,
+        in_specs=[vmem()] * 2,
+        out_specs=vmem(),
+        scratch_shapes=pick_scratch,
+        compiler_params=limit(3),
+        name="pick_more",
+    )(facts, pieces_pert.reshape(count * slots, block_y, depth))
+    coef, pert = [
+        lax.all_to_all(
+            tiles.reshape(near, patch, block_y, depth), "shot", 0, 0,
+            axis_index_groups=groups, tiled=True,
+        )
+        for tiles in (picked, picked_pert)
+    ]
 
     if split:
-        terms = wave_split_depth(model, wave_prev[0], wave_now[0])
+        terms = wave_split_depth(coef, pert, wave_prev[0], wave_now[0])
     else:
-        terms = wave(model, started)
+        terms = wave(pert, started[1], *background(coef, started))
     terms = lax.all_to_all(terms, "shot", 0, 0, axis_index_groups=groups, tiled=True)
 
     grid_rows = count * slots // GRID_COLS

time: 59.2 us -> 76 us (1.28)
  blocking collectives: 31.2 us -> 35.2 us
  local copies, waits for them, and re-layouts: 0.01 us -> 3.67 us
  waiting for transfers between devices: 9.85 us -> 12.9 us
  Pallas kernels: 8.88 us -> 11.8 us
  starting transfers between devices: 7.5 us -> 10.3 us
    all_to_all x1, blocking collectives: 11.3 us -> 16 us  [per_device(): pieces = lax.all_to_all(sent, 'shot', 0, 0, tiled=True)]
    pallas_call x2 -> x4, Pallas kernels: 2.76 us -> 6.44 us  [the longest x1 1.79 us: per_device(): pl.pallas_call(prepare_kernel, out_shape=(jax.ShapeDtypeStruct((count, sl...]
    unnamed x4 -> x12, local copies, waits for them, and re-layouts: 0.01 us -> 3.67 us
    all_to_all x1 -> x3, waiting for transfers between devices: 9.85 us -> 12.9 us  [the longest x2 7.33 us: per_device(): lax.all_to_all(tiles.reshape(near, patch, block_y, depth), 'shot', 0, 0,...]
    all_to_all x1 -> x3, starting transfers between devices: 7.5 us -> 10.3 us  [the longest x2 6.82 us: per_device(): lax.all_to_all(tiles.reshape(near, patch, block_y, depth), 'shot', 0, 0,...]
    pallas_call x1, Pallas kernels: 3.55 us -> 2.76 us  [wave(): pl.pallas_call(wave_kernel, out_shape=jax.ShapeDtypeStruct((near, APX * m...]
  transfers between devices with their start and end apart: 1 -> 3, of which waited for: 1 -> 3; matrix products, arithmetic and copies ran while one was open for 0% -> 0% of each run, Pallas kernels for 1% -> 7%
where the time goes in v1:
time: 76 us; the launch traced here: 75.3 us
  blocking collectives  35.2 us (46%)
  waiting for transfers between devices  12.9 us (17%)
  Pallas kernels  11.8 us (16%)
  starting transfers between devices  10.3 us (14%)
  local copies, waits for them, and re-layouts  3.67 us (5%)
  between operations  1.42 us (2%)
    all_to_all x1, blocking collectives, per_device(): pieces = lax.all_to_all(sent, 'shot', 0, 0, tiled=True)  16 us
    all_to_all x1, blocking collectives, per_device(): sums = lax.all_to_all(sums, 'shot', 0, 0, tiled=True)  10.6 us
    all_to_all x1, blocking collectives, per_device(): lax.all_to_all(terms, 'shot', 0, 0, axis_index_groups=groups, tiled=True)  8.62 us
    all_to_all x2, waiting for transfers between devices, per_device(): lax.all_to_all(tiles.reshape(near, patch, block_y, depth), 'shot', 0, 0,...  7.33 us
    all_to_all x2, starting transfers between devices, per_device(): lax.all_to_all(tiles.reshape(near, patch, block_y, depth), 'shot', 0, 0,...  6.82 us
    all_to_all x1, waiting for transfers between devices, per_device(): pieces_pert = lax.all_to_all(sent_pert, 'shot', 0, 0, tiled=True)  5.54 us
    unnamed x12, local copies, waits for them, and re-layouts  3.67 us
    all_to_all x1, starting transfers between devices, per_device(): pieces_pert = lax.all_to_all(sent_pert, 'shot', 0, 0, tiled=True)  3.51 us
  transfers between devices with their start and end apart: 3, of which 3 were waited for; matrix products, arithmetic and copies ran while one was open for 0% of the time, Pallas kernels for 7%

profile of v1, /device:TPU:0, one launch (start us, length us, event | category | flops | bytes accessed | tf_op | source)
XLA Modules:
  0.0 75.3 jit_solution(12561811576657394658)
XLA Ops:
  1.3 1.8 %prepare.1 = (bf16[16,5,8,128]{3,2,1,0:T(8,128)(2,1)}, bf16[16,4,8,128]{3,2,1,0:T(8,128)(2,1)}) custom-call(s32[1]{0:T(128)S(6)} %copy.11.row_ref, s32[1]{0:T(128)S(6)} %copy.12.col_ref, s32[4]{0:T(128)} %ids_hbm.1, s32[4,8,8]{2,1,0:T(8,128)} %floor_hbm.1, bf16[4,8,8,128]{3,2,1,0:T(8,128)(2,1)} %p_hbm.1, bf16[4,8,8,128]{3,2,1,0:T(8,128)(2,1)} %s_hbm.1, ...), custom_call_target="tpu_custom_call" | custom-call | tf_op jit(solution)/shard_map/prepare/pallas_call | solution.py:511
  3.1 0.0 copy-start.4
  3.1 0.0 copy-start.5
  3.1 16.0 %all_to_all.30 = bf16[16,5,8,128]{3,2,1,0:T(8,128)(2,1)S(1)} all-to-all(bf16[16,5,8,128]{3,2,1,0:T(8,128)(2,1)} %get-tuple-element.20), channel_id=1, replica_groups=mesh['grp'=2,'shot'=16,'depth'=1] {'shot'}, dimensions={0} | all-to-all | bytes 327680 | tf_op jit(solution)/shard_map/all_to_all | solution.py:530
  19.1 3.5 %all-to-all-start.1 = ((bf16[16,4,8,128]{3,2,1,0:T(8,128)(2,1)}), bf16[16,4,8,128]{3,2,1,0:T(8,128)(2,1)S(1)}, u32[]{:S(2)}, u32[]{:S(2)}) async-start(bf16[16,4,8,128]{3,2,1,0:T(8,128)(2,1)} %get-tuple-element.26), calls=%async_computation.1 | async-start | bytes 262144 | tf_op jit(solution)/shard_map/all_to_all | solution.py:531
  22.6 0.0 copy-done.4
  22.6 0.0 copy-done.5
  22.6 0.7 start.1
  23.3 1.6 %pick.1 = (bf16[128,8,128]{2,1,0:T(8,128)(2,1)}, s32[16,128]{1,0:T(8,128)S(1)}) custom-call(bf16[80,8,128]{2,1,0:T(8,128)(2,1)S(1)} %bitcast.6), custom_call_target="tpu_custom_call" | custom-call | tf_op jit(solution)/shard_map/pick/pallas_call | solution.py:541
  25.0 5.5 %all-to-all-done.1 = bf16[16,4,8,128]{3,2,1,0:T(8,128)(2,1)S(1)} async-done(((bf16[16,4,8,128]{3,2,1,0:T(8,128)(2,1)}), bf16[16,4,8,128]{3,2,1,0:T(8,128)(2,1)S(1)}, u32[]{:S(2)}, u32[]{:S(2)}) %all-to-all-start.1) | async-done | bytes 131104 | tf_op jit(solution)/shard_map/all_to_all | solution.py:531
  30.5 3.4 %all-to-all-start.3 = ((bf16[8,16,8,128]{3,2,1,0:T(8,128)(2,1)}), bf16[8,16,8,128]{3,2,1,0:T(8,128)(2,1)S(1)}, u32[]{:S(2)}, u32[]{:S(2)}) async-start(bf16[8,16,8,128]{3,2,1,0:T(8,128)(2,1)} %bitcast.5), calls=%async_computation.3 | async-start | bytes 524288 | tf_op jit(solution)/shard_map/all_to_all | solution.py:560
  33.9 1.6 %pick_more.1 = bf16[128,8,128]{2,1,0:T(8,128)(2,1)} custom-call(s32[16,128]{1,0:T(8,128)S(1)} %get-tuple-element.25.facts_ref, bf16[64,8,128]{2,1,0:T(8,128)(2,1)S(1)} %bitcast.7), custom_call_target="tpu_custom_call" | custom-call | tf_op jit(solution)/shard_map/pick_more/pallas_call | solution.py:550
  35.6 4.3 %all-to-all-done.3.model_ref = bf16[8,16,8,128]{3,2,1,0:T(8,128)(2,1)S(1)} async-done(((bf16[8,16,8,128]{3,2,1,0:T(8,128)(2,1)}), bf16[8,16,8,128]{3,2,1,0:T(8,128)(2,1)S(1)}, u32[]{:S(2)}, u32[]{:S(2)}) %all-to-all-start.3) | async-done | bytes 262176 | tf_op jit(solution)/shard_map/all_to_all | solution.py:560
  39.9 3.4 %all-to-all-start.2 = ((bf16[8,16,8,128]{3,2,1,0:T(8,128)(2,1)}), bf16[8,16,8,128]{3,2,1,0:T(8,128)(2,1)S(1)}, u32[]{:S(2)}, u32[]{:S(2)}) async-start(bf16[8,16,8,128]{3,2,1,0:T(8,128)(2,1)} %bitcast.4), calls=%async_computation.2 | async-start | bytes 524288 | tf_op jit(solution)/shard_map/all_to_all | solution.py:560
  43.3 1.4 %background.1 = (f32[32,32,128]{2,1,0:T(8,128)S(1)}, f32[32,4,8,128]{3,2,1,0:T(8,128)S(1)}, f32[32,4,8,128]{3,2,1,0:T(8,128)S(1)}, f32[32,4,8,128]{3,2,1,0:T(8,128)S(1)}) custom-call(bf16[8,16,8,128]{3,2,1,0:T(8,128)(2,1)S(1)} %all-to-all-done.3.model_ref, f32[32,4,8,128]{3,2,1,0:T(8,128)S(1)} %get-tuple-element.28.u_0, ...), custom_call_target="tpu_custom_call" | custom-call | flops 6553600 | bytes 4194304 | tf_op jit(solution)/shard_map/background/pallas_call | solution.py:318
  44.7 0.0 copy-start
  44.7 0.8 %copy-done = f32[32,4,8,128]{3,2,1,0:T(8,128)} copy-done((f32[32,4,8,128]{3,2,1,0:T(8,128)}, f32[32,4,8,128]{3,2,1,0:T(8,128)S(1)}, u32[]{:S(2)}) %copy-start) | copy-done | bytes 524312
  45.5 0.0 copy-start.2
  45.5 0.8 %copy-done.2 = f32[32,4,8,128]{3,2,1,0:T(8,128)} copy-done((f32[32,4,8,128]{3,2,1,0:T(8,128)}, f32[32,4,8,128]{3,2,1,0:T(8,128)S(1)}, u32[]{:S(2)}) %copy-start.2) | copy-done | bytes 524312
  46.3 3.0 %all-to-all-done.2.model_ref = bf16[8,16,8,128]{3,2,1,0:T(8,128)(2,1)S(1)} async-done(((bf16[8,16,8,128]{3,2,1,0:T(8,128)(2,1)}), bf16[8,16,8,128]{3,2,1,0:T(8,128)(2,1)S(1)}, u32[]{:S(2)}, u32[]{:S(2)}) %all-to-all-start.2) | async-done | bytes 262176 | tf_op jit(solution)/shard_map/all_to_all | solution.py:560
  49.3 0.0 copy-start.1
  49.3 1.0 %copy-done.1 = f32[32,4,8,128]{3,2,1,0:T(8,128)S(1)} copy-done((f32[32,4,8,128]{3,2,1,0:T(8,128)S(1)}, f32[32,4,8,128]{3,2,1,0:T(8,128)}, u32[]{:S(2)}) %copy-start.1) | copy-done | bytes 524312
  50.3 0.0 copy-start.3
  50.3 1.0 %copy-done.3 = f32[32,4,8,128]{3,2,1,0:T(8,128)S(1)} copy-done((f32[32,4,8,128]{3,2,1,0:T(8,128)S(1)}, f32[32,4,8,128]{3,2,1,0:T(8,128)}, u32[]{:S(2)}) %copy-start.3) | copy-done | bytes 524312
  51.4 2.8 %wave.1 = bf16[8,16,8,128]{3,2,1,0:T(8,128)(2,1)S(1)} custom-call(bf16[8,16,8,128]{3,2,1,0:T(8,128)(2,1)S(1)} %all-to-all-done.2.model_ref, f32[32,32,128]{2,1,0:T(8,128)S(1)} %get-tuple-element.31.kap, f32[32,4,8,128]{3,2,1,0:T(8,128)S(1)} %get-tuple-element.29.g_0, f32[32,4,8,128]{3,2,1,0:T(8,128)S(1)} %get-tuple-element.32.g_1, ...), custom_call_target="tpu_custom_call" | custom-call | tf_op jit(solution)/shard_map/wave/pallas_call | solution.py:400
  54.1 8.6 %all_to_all.31.terms_ref = bf16[8,16,8,128]{3,2,1,0:T(8,128)(2,1)S(1)} all-to-all(bf16[8,16,8,128]{3,2,1,0:T(8,128)(2,1)S(1)} %wave.1), channel_id=1, replica_groups={{0,1,2,3,4,5,6,7},{8,9,10,11,12,13,14,15},{16,17,18,19,20,21,22,23},{24..., dimensions={0} | all-to-all | bytes 524288 | tf_op jit(solution)/shard_map/all_to_all | solution.py:571
  62.8 1.2 %stack.1 = bf16[16,4,8,128]{3,2,1,0:T(8,128)(2,1)S(1)} custom-call(s32[16,128]{1,0:T(8,128)S(1)} %get-tuple-element.25.facts_ref, bf16[8,16,8,128]{3,2,1,0:T(8,128)(2,1)S(1)} %all_to_all.31.terms_ref), custom_call_target="tpu_custom_call" | custom-call | tf_op jit(solution)/shard_map/stack/pallas_call | solution.py:575
  64.0 10.6 %all_to_all.32.sums_ref = bf16[16,4,8,128]{3,2,1,0:T(8,128)(2,1)S(1)} all-to-all(bf16[16,4,8,128]{3,2,1,0:T(8,128)(2,1)S(1)} %stack.1), channel_id=1, replica_groups=mesh['grp'=2,'shot'=16,'depth'=1] {'shot'}, dimensions={0} | all-to-all | bytes 262144 | tf_op jit(solution)/shard_map/all_to_all | solution.py:589
  74.6 0.7 finish.1
Async XLA Ops:
  3.1 19.5 %copy-start.4 = (bf16[1,32,32,128]{3,2,1,0:T(8,128)(2,1)S(1)}, bf16[1,32,32,128]{3,2,1,0:T(8,128)(2,1)}, u32[]{:S(2)}) copy-start(bf16[1,32,32,128]{3,2,1,0:T(8,128)(2,1)} %param.18) | copy-start | bytes 786436
  3.1 19.5 %copy-start.5 = (bf16[1,32,32,128]{3,2,1,0:T(8,128)(2,1)S(1)}, bf16[1,32,32,128]{3,2,1,0:T(8,128)(2,1)}, u32[]{:S(2)}) copy-start(bf16[1,32,32,128]{3,2,1,0:T(8,128)(2,1)} %param.19) | copy-start | bytes 786436
  19.1 11.4 %all-to-all-start.1 = ((bf16[16,4,8,128]{3,2,1,0:T(8,128)(2,1)}), bf16[16,4,8,128]{3,2,1,0:T(8,128)(2,1)S(1)}, u32[]{:S(2)}, u32[]{:S(2)}) async-start(bf16[16,4,8,128]{3,2,1,0:T(8,128)(2,1)} %get-tuple-element.26), calls=%async_computation.1 | async-start | bytes 262144 | tf_op jit(solution)/shard_map/all_to_all | solution.py:531
  30.5 9.4 %all-to-all-start.3 = ((bf16[8,16,8,128]{3,2,1,0:T(8,128)(2,1)}), bf16[8,16,8,128]{3,2,1,0:T(8,128)(2,1)S(1)}, u32[]{:S(2)}, u32[]{:S(2)}) async-start(bf16[8,16,8,128]{3,2,1,0:T(8,128)(2,1)} %bitcast.5), calls=%async_computation.3 | async-start | bytes 524288 | tf_op jit(solution)/shard_map/all_to_all | solution.py:560
  39.9 9.4 %all-to-all-start.2 = ((bf16[8,16,8,128]{3,2,1,0:T(8,128)(2,1)}), bf16[8,16,8,128]{3,2,1,0:T(8,128)(2,1)S(1)}, u32[]{:S(2)}, u32[]{:S(2)}) async-start(bf16[8,16,8,128]{3,2,1,0:T(8,128)(2,1)} %bitcast.4), calls=%async_computation.2 | async-start | bytes 524288 | tf_op jit(solution)/shard_map/all_to_all | solution.py:560
  44.7 0.8 %copy-start = (f32[32,4,8,128]{3,2,1,0:T(8,128)}, f32[32,4,8,128]{3,2,1,0:T(8,128)S(1)}, u32[]{:S(2)}) copy-start(f32[32,4,8,128]{3,2,1,0:T(8,128)S(1)} %get-tuple-element.33.g_2) | copy-start | bytes 1572868
  45.5 0.8 %copy-start.2 = (f32[32,4,8,128]{3,2,1,0:T(8,128)}, f32[32,4,8,128]{3,2,1,0:T(8,128)S(1)}, u32[]{:S(2)}) copy-start(f32[32,4,8,128]{3,2,1,0:T(8,128)S(1)} %get-tuple-element.34.g_3) | copy-start | bytes 1572868
  49.3 1.0 %copy-start.1 = (f32[32,4,8,128]{3,2,1,0:T(8,128)S(1)}, f32[32,4,8,128]{3,2,1,0:T(8,128)}, u32[]{:S(2)}) copy-start(f32[32,4,8,128]{3,2,1,0:T(8,128)} %copy-done) | copy-start | bytes 1572868
  50.3 1.0 %copy-start.3 = (f32[32,4,8,128]{3,2,1,0:T(8,128)S(1)}, f32[32,4,8,128]{3,2,1,0:T(8,128)}, u32[]{:S(2)}) copy-start(f32[32,4,8,128]{3,2,1,0:T(8,128)} %copy-done.2) | copy-start | bytes 1572868

commit v2 on v0

--- a/solution.py
+++ b/solution.py
@@ -127,33 +127,31 @@
         out_ref[piece, 2 * slots] = facts
 
 
-def pick_kernel(slots, pieces_ref, out_ref, facts_ref, facts, spots, sem):
+def pick_kernel(slots, near, pieces_ref, *refs):
+    out_refs = refs[:near]
+    facts_ref, facts, spots, sem = refs[near:]
     count = facts_ref.shape[0]
     tiles = 2 * slots + 1
-    near = out_ref.shape[0] // (2 * APX * APY)
     for piece in range(count):
         tile = pieces_ref[piece * tiles + 2 * slots].astype(jnp.float32)
         facts_ref[piece:piece + 1] = tile.astype(jnp.int32)[0:1]
     copy = pltpu.make_async_copy(facts_ref, facts, sem)
     copy.start()
-    base = lax.axis_index("shot") // near * near
+    me = lax.axis_index("shot")
     copy.wait()
     for piece in range(count):
         for slot in range(slots):
             spots[facts[piece, slot]] = piece * tiles + 2 * slot
-
-    def one(shot, carry):
-        first = facts[base + shot, slots] * GRID_COLS + facts[base + shot, slots + 1]
+    for k, out_ref in enumerate(out_refs):
+        shot = me ^ k
+        first = facts[shot, slots] * GRID_COLS + facts[shot, slots + 1]
         for x in range(APX):
             found = []
             for y in range(APY):
                 spot = spots[first + x * GRID_COLS + y]
                 found += [pieces_ref[spot], pieces_ref[spot + 1]]
             for index, tile in enumerate(found):
-                out_ref[(shot * APX + x) * APY * 2 + index] = tile
-        return carry
-
-    lax.fori_loop(0, near, one, 0, unroll=2)
+                out_ref[x * APY * 2 + index] = tile
 
 
 def ends(shape):
@@ -254,31 +252,31 @@
     )(before, current)
 
 
-def wave_kernel(
-    model_ref, u_0, g_0, next_ref, out_ref,
-    kap, con, u_1, u_2, u_3, d_0, d_1, d_2, kb_3, kb_2, kb_1, g_1, g_2, d_3, b_2, b_1, image,
-):
+def wave_kernel(near, *refs):
+    model_refs = refs[:near]
+    u_0, g_0, next_ref = refs[near:near + 3]
+    out_refs = refs[near + 3:2 * near + 3]
+    kap, con, u_1, u_2, u_3, d_0, d_1, d_2, kb_3, kb_2, kb_1 = refs[2 * near + 3:2 * near + 14]
+    g_1, g_2, d_3, b_2, b_1, image, result = refs[2 * near + 14:]
     span_x, many = u_0.shape[:2]
     depth = u_0.shape[3]
-    block_y = model_ref.shape[2]
+    block_y = model_refs[0].shape[1]
     block_x = span_x // APX
+    place = lax.axis_index("shot") % near
     masks = ends((LANES, depth))
     each = range(many)
     for field in (u_1, u_2, u_3, d_0, d_1, d_2, kb_3, kb_2, kb_1):
         for v in each:
             field[span_x, v] = jnp.zeros((LANES, depth), jnp.float32)
 
-    def load(piece, carry):
+    for k, model_ref in enumerate(model_refs):
         for x in range(APX):
+            at = x * block_x + (place ^ k)
             for y in range(APY):
                 rows = pl.ds(y * block_y, block_y)
-                at = x * block_x + piece
                 tile = 2 * (x * APY + y)
-                kap[at, rows] = model_ref[piece, tile].astype(jnp.float32)
-                con[at, rows] = speed_factor * model_ref[piece, tile + 1].astype(jnp.float32)
-        return carry
-
-    lax.fori_loop(0, block_x, load, 0, unroll=4)
+                kap[at, rows] = model_ref[tile].astype(jnp.float32)
+                con[at, rows] = speed_factor * model_ref[tile + 1].astype(jnp.float32)
 
     def forward_0(x, carry):
         kaps, cons, grads = strided(kap, x), strided(con, x), registers(g_0, x)
@@ -324,8 +322,8 @@
                     back = back - b_after[x, v]
                 total = image[x, v] + grad[x, v] * back
                 if kb_next is None:
-                    total = (image_scale * total).astype(out_ref.dtype)
-                    out_ref[x % block_x, x // block_x * many + v] = total
+                    total = (image_scale * total).astype(result.dtype)
+                    result[x % block_x, x // block_x * many + v] = total
                 else:
                     image[x, v] = total
                     b_next[x, v] = back
@@ -336,26 +334,33 @@
     adjoint(kb_3, d_3, None, d_2, g_2, kb_2, b_2)
     adjoint(kb_2, b_2, d_3, d_1, g_1, kb_1, b_1)
     adjoint(kb_1, b_1, b_2, d_0, g_0, None, None)
-
-
-def wave(model, started):
+    for k, out_ref in enumerate(out_refs):
+        out_ref[...] = result[place ^ k]
+
+
+def wave(models, started):
     span_x, many, _, depth = started[0].shape
-    near, tiles, _, _ = model.shape
+    near = len(models)
     flat = pltpu.VMEM((span_x, many * LANES, depth), jnp.float32)
     field = pltpu.VMEM((span_x + 1, many, LANES, depth), jnp.float32)
     plain = pltpu.VMEM((span_x, many, LANES, depth), jnp.float32)
+    out = (APX * many, LANES, depth)
     return pl.pallas_call(
-        wave_kernel,
-        out_shape=jax.ShapeDtypeStruct((near, APX * many, LANES, depth), jnp.bfloat16),
-        in_specs=[vmem()] * 4,
-        out_specs=vmem(),
-        scratch_shapes=[flat] * 2 + [field] * 9 + [plain] * 6,
+        functools.partial(wave_kernel, near),
+        out_shape=(jax.ShapeDtypeStruct(out, jnp.bfloat16),) * near,
+        in_specs=[vmem()] * (near + 3),
+        out_specs=(vmem(),) * near,
+        scratch_shapes=[flat] * 2 + [field] * 9 + [plain] * 6
+        + [pltpu.VMEM((near,) + out, jnp.bfloat16)],
         compiler_params=limit(20),
         name="wave",
-    )(model, *started)
-
-
-def wave_split_depth(model, before, current):
+    )(*models, *started)
+
+
+def wave_split_depth(models, before, current):
+    near = len(models)
+    order = (lax.axis_index("shot") % near) ^ jnp.arange(near)
+    model = jnp.stack(models)[order]
     span_x, span_y, depth = before.shape
     block_x, tiles, block_y, _ = model.shape
     grids = model.reshape(block_x, APX, APY, 2, block_y, depth).transpose(3, 1, 0, 2, 4, 5)
@@ -369,17 +374,20 @@
     )
     many = span_y // LANES
     image = image.reshape(APX, block_x, LANES, many, depth).transpose(1, 0, 3, 2, 4)
-    return image.reshape(block_x, APX * many, LANES, depth).astype(jnp.bfloat16)
-
-
-def stack_kernel(slots, facts_ref, terms_ref, out_ref, facts, total, lined, sem):
-    shots, tiles = terms_ref.shape[:2]
+    image = image.reshape(near, APX * many, LANES, depth).astype(jnp.bfloat16)[order]
+    return [image[k] for k in range(near)]
+
+
+def stack_kernel(slots, near, facts_ref, *refs):
+    terms_refs = refs[:near]
+    out_ref, facts, total, lined, sem = refs[near:]
+    tiles = terms_refs[0].shape[0]
     wide = tiles // APX
     width = LANES // APY
     grid_rows = total.shape[0] // wide
     copy = pltpu.make_async_copy(facts_ref, facts, sem)
     copy.start()
-    base = lax.axis_index("shot") // shots * shots
+    me = lax.axis_index("shot")
 
     def clear(index, carry):
         total[index] = jnp.zeros(total.shape[1:], total.dtype)
@@ -388,18 +396,15 @@
     lax.fori_loop(0, total.shape[0], clear, 0, unroll=8)
     copy.wait()
 
-    def add(shot, carry):
-        first = facts[base + shot, slots] * wide
-        rows = pl.ds(facts[base + shot, slots + 1] * width, LANES)
+    for k, terms_ref in enumerate(terms_refs):
+        first = facts[me ^ k, slots] * wide
+        rows = pl.ds(facts[me ^ k, slots + 1] * width, LANES)
         sums = [
-            total[first + tile, rows] + terms_ref[shot, tile].astype(jnp.float32)
+            total[first + tile, rows] + terms_ref[tile].astype(jnp.float32)
             for tile in range(tiles)
         ]
         for tile in range(tiles):
             total[first + tile, rows] = sums[tile]
-        return carry
-
-    lax.fori_loop(0, shots, add, 0, unroll=2)
 
     for row in range(grid_rows):
         for part in range(wide):
@@ -451,7 +456,14 @@
         seafloor = seafloor - lax.axis_index("depth") * depth
 
     near = block_x
-    groups = [list(range(first, first + near)) for first in range(0, count, near)]
+    assert count % near == 0 and near & (near - 1) == 0
+
+    def swap(values):
+        return [
+            lax.ppermute(value, "shot", [(i, i ^ k) for i in range(count)]) if k else value
+            for k, value in enumerate(values)
+        ]
+
     sent = pl.pallas_call(
         prepare_kernel,
         out_shape=jax.ShapeDtypeStruct((count, 2 * slots + 1, block_y, depth), jnp.bfloat16),
@@ -473,14 +485,14 @@
     if not split:
         started = start(wave_prev[0], wave_now[0])
         pieces, started = lax.optimization_barrier((pieces, started))
-    picked, facts = pl.pallas_call(
-        functools.partial(pick_kernel, slots),
+    *picked, facts = pl.pallas_call(
+        functools.partial(pick_kernel, slots, near),
         out_shape=(
-            jax.ShapeDtypeStruct((near * patch * 2, block_y, depth), jnp.bfloat16),
+            *[jax.ShapeDtypeStruct((patch * 2, block_y, depth), jnp.bfloat16)] * near,
             jax.ShapeDtypeStruct((count, depth), jnp.int32),
         ),
         in_specs=[vmem()],
-        out_specs=(vmem(), vmem()),
+        out_specs=(vmem(),) * (near + 1),
         scratch_shapes=[
             pltpu.SMEM((count, depth), jnp.int32),
             pltpu.SMEM((count * slots,), jnp.int32),
@@ -489,23 +501,20 @@
         compiler_params=limit(3),
         name="pick",
     )(pieces.reshape(count * (2 * slots + 1), block_y, depth))
-    model = lax.all_to_all(
-        picked.reshape(near, patch * 2, block_y, depth), "shot", 0, 0,
-        axis_index_groups=groups, tiled=True,
-    )
+    models = swap(picked)
 
     if split:
-        terms = wave_split_depth(model, wave_prev[0], wave_now[0])
+        terms = wave_split_depth(models, wave_prev[0], wave_now[0])
     else:
-        terms = wave(model, started)
-    terms = lax.all_to_all(terms, "shot", 0, 0, axis_index_groups=groups, tiled=True)
+        terms = wave(models, started)
+    terms = swap(terms)
 
     grid_rows = count * slots // GRID_COLS
-    wide = terms.shape[1] // APX
+    wide = terms[0].shape[0] // APX
     sums = pl.pallas_call(
-        functools.partial(stack_kernel, slots),
+        functools.partial(stack_kernel, slots, near),
         out_shape=jax.ShapeDtypeStruct((count, slots, block_y, depth), jnp.bfloat16),
-        in_specs=[vmem(), vmem()],
+        in_specs=[vmem()] * (near + 1),
         out_specs=vmem(),
         scratch_shapes=[
             pltpu.SMEM(facts.shape, jnp.int32),
@@ -515,7 +524,7 @@
         ],
         compiler_params=limit(3),
         name="stack",
-    )(facts, terms)
+    )(facts, *terms)
     sums = lax.all_to_all(sums, "shot", 0, 0, tiled=True)
     return pl.pallas_call(
         finish_kernel,

time: 59.2 us -> 59.1 us (level)
  blocking collectives: 31.2 us -> 11 us
  starting transfers between devices: 7.5 us -> 19.7 us
  waiting for transfers between devices: 9.85 us -> 17.7 us
    all_to_all x2 -> x0, blocking collectives: 19.9 us -> none  [the longest x1 11.3 us: per_device(): lax.all_to_all(picked.reshape(near, patch * 2, block_y, depth), 'shot', 0...]
    ppermute x0 -> x14, starting transfers between devices: none -> 12.2 us  [swap(): lax.ppermute(value, 'shot', [(i, i ^ k) for i in range(count)])]
    ppermute x0 -> x14, waiting for transfers between devices: none -> 7.86 us  [swap(): lax.ppermute(value, 'shot', [(i, i ^ k) for i in range(count)])]
  transfers between devices with their start and end apart: 1 -> 15, of which waited for: 1 -> 8; matrix products, arithmetic and copies ran while one was open for 0% -> 0% of each run, Pallas kernels for 1% -> 1%
where the time goes in v2:
time: 59.1 us; the launch traced here: 58.8 us
  starting transfers between devices  19.7 us (33%)
  waiting for transfers between devices  17.7 us (30%)
  blocking collectives  11 us (19%)
  Pallas kernels  8.95 us (15%)
  between operations  1.4 us (2%)
    ppermute x14, starting transfers between devices, swap(): lax.ppermute(value, 'shot', [(i, i ^ k) for i in range(count)])  12.2 us
    all_to_all x1, blocking collectives, per_device(): sums = lax.all_to_all(sums, 'shot', 0, 0, tiled=True)  11 us
    all_to_all x1, waiting for transfers between devices, per_device(): pieces = lax.all_to_all(sent, 'shot', 0, 0, tiled=True)  9.85 us
    ppermute x14, waiting for transfers between devices, swap(): lax.ppermute(value, 'shot', [(i, i ^ k) for i in range(count)])  7.86 us
    all_to_all x1, starting transfers between devices, per_device(): pieces = lax.all_to_all(sent, 'shot', 0, 0, tiled=True)  7.5 us
    pallas_call x1, Pallas kernels, wave(): pl.pallas_call(functools.partial(wave_kernel, near), out_shape=(jax.Shape...  3.64 us
    pallas_call x1, Pallas kernels, per_device(): pl.pallas_call(prepare_kernel, out_shape=jax.ShapeDtypeStruct((count, 2 *...  1.83 us
    pallas_call x1, Pallas kernels, per_device(): pl.pallas_call(functools.partial(stack_kernel, slots, near), out_shape=ja...  1.2 us
  transfers between devices with their start and end apart: 15, of which 8 were waited for; matrix products, arithmetic and copies ran while one was open for 0% of the time, Pallas kernels for 1%

profile of v2, /device:TPU:0, one launch (start us, length us, event | category | flops | bytes accessed | tf_op | source)
XLA Modules:
  0.0 58.8 jit_solution(435546591345246437)
XLA Ops:
  1.3 1.8 %prepare.1 = bf16[16,9,8,128]{3,2,1,0:T(8,128)(2,1)} custom-call(s32[1]{0:T(128)S(6)} %copy.11.row_ref, s32[1]{0:T(128)S(6)} %copy.12.col_ref, s32[4]{0:T(128)} %ids_hbm.1, s32[4,8,8]{2,1,0:T(8,128)} %floor_hbm.1, bf16[4,8,8,128]{3,2,1,0:T(8,128)(2,1)} %p_hbm.1, bf16[4,8,8,128]{3,2,1,0:T(8,128)(2,1)} %s_hbm.1, bf16[4,8,8,128]{3,2,1,0:T(8,128)(2,1)} %rho_hbm.1, ...), custom_call_target="tpu_custom_call" | custom-call | tf_op jit(solution)/shard_map/prepare/pallas_call | solution.py:467
  3.1 0.0 copy-start
  3.2 0.0 copy-start.1
  3.2 7.5 %all-to-all-start = ((bf16[16,9,8,128]{3,2,1,0:T(8,128)(2,1)}), bf16[16,9,8,128]{3,2,1,0:T(8,128)(2,1)S(1)}, u32[]{:S(2)}, u32[]{:S(2)}) async-start(bf16[16,9,8,128]{3,2,1,0:T(8,128)(2,1)} %prepare.1), calls=%async_computation | async-start | bytes 589824 | tf_op jit(solution)/shard_map/all_to_all | solution.py:483
  10.7 0.0 copy-done
  10.7 0.0 copy-done.1
  10.7 0.7 %start.1 = (f32[32,4,8,128]{3,2,1,0:T(8,128)S(1)}, f32[32,4,8,128]{3,2,1,0:T(8,128)S(1)}, f32[32,4,8,128]{3,2,1,0:T(8,128)S(1)}) custom-call(bf16[32,32,128]{2,1,0:T(8,128)(2,1)S(1)} %bitcast.4, bf16[32,32,128]{2,1,0:T(8,128)(2,1)S(1)} %bitcast.5), custom_call_target="tpu_custom_call" | custom-call | flops 2621440 | bytes 2097152 | tf_op jit(solution)/shard_map/start/pallas_call | solution.py:241
  11.4 9.9 %all-to-all-done = bf16[16,9,8,128]{3,2,1,0:T(8,128)(2,1)S(1)} async-done(((bf16[16,9,8,128]{3,2,1,0:T(8,128)(2,1)}), bf16[16,9,8,128]{3,2,1,0:T(8,128)(2,1)S(1)}, u32[]{:S(2)}, u32[]{:S(2)}) %all-to-all-start) | async-done | bytes 294944 | tf_op jit(solution)/shard_map/all_to_all | solution.py:483
  21.2 0.9 %pick.1 = (bf16[32,8,128]{2,1,0:T(8,128)(2,1)S(1)}, bf16[32,8,128]{2,1,0:T(8,128)(2,1)S(1)}, bf16[32,8,128]{2,1,0:T(8,128)(2,1)S(1)}, bf16[32,8,128]{2,1,0:T(8,1...) custom-call(bf16[144,8,128]{2,1,0:T(8,128)(2,1)S(1)} %bitcast.3), custom_call_target="tpu_custom_call" | custom-call | tf_op jit(solution)/shard_map/pick/pallas_call | solution.py:488
  22.2 0.1 collective-permute-start
  22.2 0.7 %collective-permute-start.1 = (bf16[32,8,128]{2,1,0:T(8,128)(2,1)S(1)}, bf16[32,8,128]{2,1,0:T(8,128)(2,1)S(1)}, u32[]{:S(2)}, u32[]{:S(2)}) collective-permute-start(bf16[32,8,128]{2,1,0:T(8,128)(2,1)S(1)} %get-tuple-element.36), channel_id=1, source_target_pairs={{0,2},{1,3},{2,0},{3,1},{4,6},{5,7},{6,4},{7,5},{8,10},{9,11},{10,... | collective-permute-start | bytes 196616 | tf_op jit(solution)/shard_map/ppermute | solution.py:463
  22.9 1.2 %collective-permute-start.2 = (bf16[32,8,128]{2,1,0:T(8,128)(2,1)S(1)}, bf16[32,8,128]{2,1,0:T(8,128)(2,1)S(1)}, u32[]{:S(2)}, u32[]{:S(2)}) collective-permute-start(bf16[32,8,128]{2,1,0:T(8,128)(2,1)S(1)} %get-tuple-element.37), channel_id=1, source_target_pairs={{0,3},{1,2},{2,1},{3,0},{4,7},{5,6},{6,5},{7,4},{8,11},{9,10},{10,... | collective-permute-start | bytes 196616 | tf_op jit(solution)/shard_map/ppermute | solution.py:463
  24.1 0.4 collective-permute-start.3
  24.5 1.3 %collective-permute-start.4 = (bf16[32,8,128]{2,1,0:T(8,128)(2,1)S(1)}, bf16[32,8,128]{2,1,0:T(8,128)(2,1)S(1)}, u32[]{:S(2)}, u32[]{:S(2)}) collective-permute-start(bf16[32,8,128]{2,1,0:T(8,128)(2,1)S(1)} %get-tuple-element.39), channel_id=1, source_target_pairs={{0,5},{1,4},{2,7},{3,6},{4,1},{5,0},{6,3},{7,2},{8,13},{9,12},{10,... | collective-permute-start | bytes 196616 | tf_op jit(solution)/shard_map/ppermute | solution.py:463
  25.8 0.0 collective-permute-done.refs_1_
  25.8 1.0 %collective-permute-start.5 = (bf16[32,8,128]{2,1,0:T(8,128)(2,1)S(1)}, bf16[32,8,128]{2,1,0:T(8,128)(2,1)S(1)}, u32[]{:S(2)}, u32[]{:S(2)}) collective-permute-start(bf16[32,8,128]{2,1,0:T(8,128)(2,1)S(1)} %get-tuple-element.40), channel_id=1, source_target_pairs={{0,6},{1,7},{2,4},{3,5},{4,2},{5,3},{6,0},{7,1},{8,14},{9,15},{10,... | collective-permute-start | bytes 196616 | tf_op jit(solution)/shard_map/ppermute | solution.py:463
  26.8 0.4 collective-permute-done.1.refs_2_
  27.2 1.3 %collective-permute-start.6 = (bf16[32,8,128]{2,1,0:T(8,128)(2,1)S(1)}, bf16[32,8,128]{2,1,0:T(8,128)(2,1)S(1)}, u32[]{:S(2)}, u32[]{:S(2)}) collective-permute-start(bf16[32,8,128]{2,1,0:T(8,128)(2,1)S(1)} %get-tuple-element.41), channel_id=1, source_target_pairs={{0,7},{1,6},{2,5},{3,4},{4,3},{5,2},{6,1},{7,0},{8,15},{9,14},{10,... | collective-permute-start | bytes 196616 | tf_op jit(solution)/shard_map/ppermute | solution.py:463
  28.5 0.0 collective-permute-done.2.refs_3_
  28.5 0.5 collective-permute-done.3.refs_4_
  29.0 0.3 collective-permute-done.4.refs_5_
  29.3 2.2 %collective-permute-done.5.refs_6_ = bf16[32,8,128]{2,1,0:T(8,128)(2,1)S(1)} collective-permute-done((bf16[32,8,128]{2,1,0:T(8,128)(2,1)S(1)}, bf16[32,8,128]{2,1,0:T(8,128)(2,1)S(1)}, u32[]{:S(2)}, u32[]{:S(2)}) %collective-permute-start.5) | collective-permute-done | bytes 65568 | tf_op jit(solution)/shard_map/ppermute | solution.py:463
  31.5 1.0 %collective-permute-done.6.refs_7_ = bf16[32,8,128]{2,1,0:T(8,128)(2,1)S(1)} collective-permute-done((bf16[32,8,128]{2,1,0:T(8,128)(2,1)S(1)}, bf16[32,8,128]{2,1,0:T(8,128)(2,1)S(1)}, u32[]{:S(2)}, u32[]{:S(2)}) %collective-permute-start.6) | collective-permute-done | bytes 65568 | tf_op jit(solution)/shard_map/ppermute | solution.py:463
  32.5 3.6 %wave.1 = (bf16[16,8,128]{2,1,0:T(8,128)(2,1)S(1)}, bf16[16,8,128]{2,1,0:T(8,128)(2,1)S(1)}, bf16[16,8,128]{2,1,0:T(8,128)(2,1)S(1)}, bf16[16,8,128]{2,1,0:T(8,1...) custom-call(bf16[32,8,128]{2,1,0:T(8,128)(2,1)S(1)} %get-tuple-eleme, ...), custom_call_target="tpu_custom_call" | custom-call | tf_op jit(solution)/shard_map/wave/pallas_call | solution.py:348
  36.1 0.2 collective-permute-start.7
  36.3 1.4 %collective-permute-start.8 = (bf16[16,8,128]{2,1,0:T(8,128)(2,1)S(1)}, bf16[16,8,128]{2,1,0:T(8,128)(2,1)S(1)}, u32[]{:S(2)}, u32[]{:S(2)}) collective-permute-start(bf16[16,8,128]{2,1,0:T(8,128)(2,1)S(1)} %get-tuple-element.47), channel_id=1, source_target_pairs={{0,2},{1,3},{2,0},{3,1},{4,6},{5,7},{6,4},{7,5},{8,10},{9,11},{10,... | collective-permute-start | bytes 98312 | tf_op jit(solution)/shard_map/ppermute | solution.py:463
  37.7 0.4 collective-permute-start.9
  38.0 0.9 %collective-permute-start.10 = (bf16[16,8,128]{2,1,0:T(8,128)(2,1)S(1)}, bf16[16,8,128]{2,1,0:T(8,128)(2,1)S(1)}, u32[]{:S(2)}, u32[]{:S(2)}) collective-permute-start(bf16[16,8,128]{2,1,0:T(8,128)(2,1)S(1)} %get-tuple-element.49), channel_id=1, source_target_pairs={{0,4},{1,5},{2,6},{3,7},{4,0},{5,1},{6,2},{7,3},{8,12},{9,13},{10,... | collective-permute-start | bytes 98312 | tf_op jit(solution)/shard_map/ppermute | solution.py:463
  38.9 0.9 %collective-permute-start.11 = (bf16[16,8,128]{2,1,0:T(8,128)(2,1)S(1)}, bf16[16,8,128]{2,1,0:T(8,128)(2,1)S(1)}, u32[]{:S(2)}, u32[]{:S(2)}) collective-permute-start(bf16[16,8,128]{2,1,0:T(8,128)(2,1)S(1)} %get-tuple-element.50), channel_id=1, source_target_pairs={{0,5},{1,4},{2,7},{3,6},{4,1},{5,0},{6,3},{7,2},{8,13},{9,12},{10,... | collective-permute-start | bytes 98312 | tf_op jit(solution)/shard_map/ppermute | solution.py:463
  39.8 0.0 collective-permute-done.7.refs_1_
  39.8 1.7 %collective-permute-start.12 = (bf16[16,8,128]{2,1,0:T(8,128)(2,1)S(1)}, bf16[16,8,128]{2,1,0:T(8,128)(2,1)S(1)}, u32[]{:S(2)}, u32[]{:S(2)}) collective-permute-start(bf16[16,8,128]{2,1,0:T(8,128)(2,1)S(1)} %get-tuple-element.51), channel_id=1, source_target_pairs={{0,6},{1,7},{2,4},{3,5},{4,2},{5,3},{6,0},{7,1},{8,14},{9,15},{10,... | collective-permute-start | bytes 98312 | tf_op jit(solution)/shard_map/ppermute | solution.py:463
  41.6 0.0 collective-permute-done.8.refs_2_
  41.6 0.9 %collective-permute-start.13 = (bf16[16,8,128]{2,1,0:T(8,128)(2,1)S(1)}, bf16[16,8,128]{2,1,0:T(8,128)(2,1)S(1)}, u32[]{:S(2)}, u32[]{:S(2)}) collective-permute-start(bf16[16,8,128]{2,1,0:T(8,128)(2,1)S(1)} %get-tuple-element.52), channel_id=1, source_target_pairs={{0,7},{1,6},{2,5},{3,4},{4,3},{5,2},{6,1},{7,0},{8,15},{9,14},{10,... | collective-permute-start | bytes 98312 | tf_op jit(solution)/shard_map/ppermute | solution.py:463
  42.4 0.0 collective-permute-done.9.refs_3_
  42.4 0.0 collective-permute-done.10.refs_4_
  42.4 0.0 collective-permute-done.11.refs_5_
  42.4 2.2 %collective-permute-done.12.refs_6_ = bf16[16,8,128]{2,1,0:T(8,128)(2,1)S(1)} collective-permute-done((bf16[16,8,128]{2,1,0:T(8,128)(2,1)S(1)}, bf16[16,8,128]{2,1,0:T(8,128)(2,1)S(1)}, u32[]{:S(2)}, u32[]{:S(2)}) %collective-permute-start.12) | collective-permute-done | bytes 32800 | tf_op jit(solution)/shard_map/ppermute | solution.py:463
  44.6 1.3 %collective-permute-done.13.refs_7_ = bf16[16,8,128]{2,1,0:T(8,128)(2,1)S(1)} collective-permute-done((bf16[16,8,128]{2,1,0:T(8,128)(2,1)S(1)}, bf16[16,8,128]{2,1,0:T(8,128)(2,1)S(1)}, u32[]{:S(2)}, u32[]{:S(2)}) %collective-permute-start.13) | collective-permute-done | bytes 32800 | tf_op jit(solution)/shard_map/ppermute | solution.py:463
  45.9 1.2 %stack.1 = bf16[16,4,8,128]{3,2,1,0:T(8,128)(2,1)S(1)} custom-call(s32[16,128]{1,0:T(8,128)S(1)} %get-tuple-element.33.facts_ref, bf16[16,8,128]{2,1,0:T(8,128)(2,1)S(1)} %get-tuple-element.45.refs_0_, bf16[16,8,128]{2,1,0:T(8,128)(2,1)S(1)} %collective-permute-done.7.refs_1_, bf16[16,8,128]{2,1,0:T(8,128)(2,1)S(1)} %collective-permute-done.8.refs_2_, ...), custom_call_target="tpu_custom_call" | custom-call | tf_op jit(solution)/shard_map/stack/pallas_call | solution.py:514
  47.1 11.0 %all_to_all.10.sums_ref = bf16[16,4,8,128]{3,2,1,0:T(8,128)(2,1)S(1)} all-to-all(bf16[16,4,8,128]{3,2,1,0:T(8,128)(2,1)S(1)} %stack.1), channel_id=1, replica_groups=mesh['grp'=2,'shot'=16,'depth'=1] {'shot'}, dimensions={0} | all-to-all | bytes 262144 | tf_op jit(solution)/shard_map/all_to_all | solution.py:528
  58.2 0.7 %finish.1 = f32[4,8,8,128]{3,2,1,0:T(8,128)} custom-call(bf16[16,4,8,128]{3,2,1,0:T(8,128)(2,1)S(1)} %all_to_all.10.sums_ref), custom_call_target="tpu_custom_call" | custom-call | tf_op jit(solution)/shard_map/finish/pallas_call | solution.py:529
Async XLA Ops:
  3.1 7.5 %copy-start = (bf16[1,32,32,128]{3,2,1,0:T(8,128)(2,1)S(1)}, bf16[1,32,32,128]{3,2,1,0:T(8,128)(2,1)}, u32[]{:S(2)}) copy-start(bf16[1,32,32,128]{3,2,1,0:T(8,128)(2,1)} %param.18) | copy-start | bytes 786436
  3.2 7.5 %copy-start.1 = (bf16[1,32,32,128]{3,2,1,0:T(8,128)(2,1)S(1)}, bf16[1,32,32,128]{3,2,1,0:T(8,128)(2,1)}, u32[]{:S(2)}) copy-start(bf16[1,32,32,128]{3,2,1,0:T(8,128)(2,1)} %param.19) | copy-start | bytes 786436
  3.2 18.1 %all-to-all-start = ((bf16[16,9,8,128]{3,2,1,0:T(8,128)(2,1)}), bf16[16,9,8,128]{3,2,1,0:T(8,128)(2,1)S(1)}, u32[]{:S(2)}, u32[]{:S(2)}) async-start(bf16[16,9,8,128]{3,2,1,0:T(8,128)(2,1)} %prepare.1), calls=%async_computation | async-start | bytes 589824 | tf_op jit(solution)/shard_map/all_to_all | solution.py:483
  22.2 3.6 %collective-permute-start = (bf16[32,8,128]{2,1,0:T(8,128)(2,1)S(1)}, bf16[32,8,128]{2,1,0:T(8,128)(2,1)S(1)}, u32[]{:S(2)}, u32[]{:S(2)}) collective-permute-start(bf16[32,8,128]{2,1,0:T(8,128)(2,1)S(1)} %get-tuple-element.35), channel_id=1, source_target_pairs={{0,1},{1,0},{2,3},{3,2},{4,5},{5,4},{6,7},{7,6},{8,9},{9,8},{10,11... | collective-permute-start | bytes 196616 | tf_op jit(solution)/shard_map/ppermute | solution.py:463
  22.2 5.0 %collective-permute-start.1 = (bf16[32,8,128]{2,1,0:T(8,128)(2,1)S(1)}, bf16[32,8,128]{2,1,0:T(8,128)(2,1)S(1)}, u32[]{:S(2)}, u32[]{:S(2)}) collective-permute-start(bf16[32,8,128]{2,1,0:T(8,128)(2,1)S(1)} %get-tuple-element.36), channel_id=1, source_target_pairs={{0,2},{1,3},{2,0},{3,1},{4,6},{5,7},{6,4},{7,5},{8,10},{9,11},{10,... | collective-permute-start | bytes 196616 | tf_op jit(solution)/shard_map/ppermute | solution.py:463
  22.9 5.6 %collective-permute-start.2 = (bf16[32,8,128]{2,1,0:T(8,128)(2,1)S(1)}, bf16[32,8,128]{2,1,0:T(8,128)(2,1)S(1)}, u32[]{:S(2)}, u32[]{:S(2)}) collective-permute-start(bf16[32,8,128]{2,1,0:T(8,128)(2,1)S(1)} %get-tuple-element.37), channel_id=1, source_target_pairs={{0,3},{1,2},{2,1},{3,0},{4,7},{5,6},{6,5},{7,4},{8,11},{9,10},{10,... | collective-permute-start | bytes 196616 | tf_op jit(solution)/shard_map/ppermute | solution.py:463
  24.1 4.9 %collective-permute-start.3 = (bf16[32,8,128]{2,1,0:T(8,128)(2,1)S(1)}, bf16[32,8,128]{2,1,0:T(8,128)(2,1)S(1)}, u32[]{:S(2)}, u32[]{:S(2)}) collective-permute-start(bf16[32,8,128]{2,1,0:T(8,128)(2,1)S(1)} %get-tuple-element.38), channel_id=1, source_target_pairs={{0,4},{1,5},{2,6},{3,7},{4,0},{5,1},{6,2},{7,3},{8,12},{9,13},{10,... | collective-permute-start | bytes 196616 | tf_op jit(solution)/shard_map/ppermute | solution.py:463
  24.5 4.8 %collective-permute-start.4 = (bf16[32,8,128]{2,1,0:T(8,128)(2,1)S(1)}, bf16[32,8,128]{2,1,0:T(8,128)(2,1)S(1)}, u32[]{:S(2)}, u32[]{:S(2)}) collective-permute-start(bf16[32,8,128]{2,1,0:T(8,128)(2,1)S(1)} %get-tuple-element.39), channel_id=1, source_target_pairs={{0,5},{1,4},{2,7},{3,6},{4,1},{5,0},{6,3},{7,2},{8,13},{9,12},{10,... | collective-permute-start | bytes 196616 | tf_op jit(solution)/shard_map/ppermute | solution.py:463
  25.8 5.7 %collective-permute-start.5 = (bf16[32,8,128]{2,1,0:T(8,128)(2,1)S(1)}, bf16[32,8,128]{2,1,0:T(8,128)(2,1)S(1)}, u32[]{:S(2)}, u32[]{:S(2)}) collective-permute-start(bf16[32,8,128]{2,1,0:T(8,128)(2,1)S(1)} %get-tuple-element.40), channel_id=1, source_target_pairs={{0,6},{1,7},{2,4},{3,5},{4,2},{5,3},{6,0},{7,1},{8,14},{9,15},{10,... | collective-permute-start | bytes 196616 | tf_op jit(solution)/shard_map/ppermute | solution.py:463
  27.2 5.3 %collective-permute-start.6 = (bf16[32,8,128]{2,1,0:T(8,128)(2,1)S(1)}, bf16[32,8,128]{2,1,0:T(8,128)(2,1)S(1)}, u32[]{:S(2)}, u32[]{:S(2)}) collective-permute-start(bf16[32,8,128]{2,1,0:T(8,128)(2,1)S(1)} %get-tuple-element.41), channel_id=1, source_target_pairs={{0,7},{1,6},{2,5},{3,4},{4,3},{5,2},{6,1},{7,0},{8,15},{9,14},{10,... | collective-permute-start | bytes 196616 | tf_op jit(solution)/shard_map/ppermute | solution.py:463
  36.1 3.7 %collective-permute-start.7 = (bf16[16,8,128]{2,1,0:T(8,128)(2,1)S(1)}, bf16[16,8,128]{2,1,0:T(8,128)(2,1)S(1)}, u32[]{:S(2)}, u32[]{:S(2)}) collective-permute-start(bf16[16,8,128]{2,1,0:T(8,128)(2,1)S(1)} %get-tuple-element.46), channel_id=1, source_target_pairs={{0,1},{1,0},{2,3},{3,2},{4,5},{5,4},{6,7},{7,6},{8,9},{9,8},{10,11... | collective-permute-start | bytes 98312 | tf_op jit(solution)/shard_map/ppermute | solution.py:463
  36.3 5.3 %collective-permute-start.8 = (bf16[16,8,128]{2,1,0:T(8,128)(2,1)S(1)}, bf16[16,8,128]{2,1,0:T(8,128)(2,1)S(1)}, u32[]{:S(2)}, u32[]{:S(2)}) collective-permute-start(bf16[16,8,128]{2,1,0:T(8,128)(2,1)S(1)} %get-tuple-element.47), channel_id=1, source_target_pairs={{0,2},{1,3},{2,0},{3,1},{4,6},{5,7},{6,4},{7,5},{8,10},{9,11},{10,... | collective-permute-start | bytes 98312 | tf_op jit(solution)/shard_map/ppermute | solution.py:463
  37.7 4.8 %collective-permute-start.9 = (bf16[16,8,128]{2,1,0:T(8,128)(2,1)S(1)}, bf16[16,8,128]{2,1,0:T(8,128)(2,1)S(1)}, u32[]{:S(2)}, u32[]{:S(2)}) collective-permute-start(bf16[16,8,128]{2,1,0:T(8,128)(2,1)S(1)} %get-tuple-element.48), channel_id=1, source_target_pairs={{0,3},{1,2},{2,1},{3,0},{4,7},{5,6},{6,5},{7,4},{8,11},{9,10},{10,... | collective-permute-start | bytes 98312 | tf_op jit(solution)/shard_map/ppermute | solution.py:463
  38.0 4.4 %collective-permute-start.10 = (bf16[16,8,128]{2,1,0:T(8,128)(2,1)S(1)}, bf16[16,8,128]{2,1,0:T(8,128)(2,1)S(1)}, u32[]{:S(2)}, u32[]{:S(2)}) collective-permute-start(bf16[16,8,128]{2,1,0:T(8,128)(2,1)S(1)} %get-tuple-element.49), channel_id=1, source_target_pairs={{0,4},{1,5},{2,6},{3,7},{4,0},{5,1},{6,2},{7,3},{8,12},{9,13},{10,... | collective-permute-start | bytes 98312 | tf_op jit(solution)/shard_map/ppermute | solution.py:463
  38.9 3.5 %collective-permute-start.11 = (bf16[16,8,128]{2,1,0:T(8,128)(2,1)S(1)}, bf16[16,8,128]{2,1,0:T(8,128)(2,1)S(1)}, u32[]{:S(2)}, u32[]{:S(2)}) collective-permute-start(bf16[16,8,128]{2,1,0:T(8,128)(2,1)S(1)} %get-tuple-element.50), channel_id=1, source_target_pairs={{0,5},{1,4},{2,7},{3,6},{4,1},{5,0},{6,3},{7,2},{8,13},{9,12},{10,... | collective-permute-start | bytes 98312 | tf_op jit(solution)/shard_map/ppermute | solution.py:463
  39.8 4.8 %collective-permute-start.12 = (bf16[16,8,128]{2,1,0:T(8,128)(2,1)S(1)}, bf16[16,8,128]{2,1,0:T(8,128)(2,1)S(1)}, u32[]{:S(2)}, u32[]{:S(2)}) collective-permute-start(bf16[16,8,128]{2,1,0:T(8,128)(2,1)S(1)} %get-tuple-element.51), channel_id=1, source_target_pairs={{0,6},{1,7},{2,4},{3,5},{4,2},{5,3},{6,0},{7,1},{8,14},{9,15},{10,... | collective-permute-start | bytes 98312 | tf_op jit(solution)/shard_map/ppermute | solution.py:463
  41.6 4.3 %collective-permute-start.13 = (bf16[16,8,128]{2,1,0:T(8,128)(2,1)S(1)}, bf16[16,8,128]{2,1,0:T(8,128)(2,1)S(1)}, u32[]{:S(2)}, u32[]{:S(2)}) collective-permute-start(bf16[16,8,128]{2,1,0:T(8,128)(2,1)S(1)} %get-tuple-element.52), channel_id=1, source_target_pairs={{0,7},{1,6},{2,5},{3,4},{4,3},{5,2},{6,1},{7,0},{8,15},{9,14},{10,... | collective-permute-start | bytes 98312 | tf_op jit(solution)/shard_map/ppermute | solution.py:463

commit v3 on v2

--- a/solution.py
+++ b/solution.py
@@ -73,6 +73,10 @@
     return pltpu.CompilerParams(vmem_limit_bytes=mebibytes * 2**20)
 
 
+def chip_place(near):
+    return lax.axis_index("shot") // 2 % near
+
+
 def vmem():
     return pl.BlockSpec(memory_space=pltpu.VMEM)
 
@@ -81,12 +85,11 @@
     return pl.BlockSpec(memory_space=pltpu.SMEM)
 
 
-def prepare_kernel(
-    row_ref, col_ref, ids_hbm, floor_hbm, p_hbm, s_hbm, rho_hbm, pert_hbm, out_ref,
-    ids, floors, p, s, rho, pert, sems,
-):
+def prepare_kernel(near, row_ref, col_ref, *refs):
+    ids_hbm, floor_hbm, p_hbm, s_hbm, rho_hbm, pert_hbm = refs[:6]
+    out_refs = refs[6:6 + near]
+    ids, floors, p, s, rho, pert, coef, sems = refs[6 + near:]
     slots, block_x, block_y, depth = p.shape
-    near = block_x
     copies = [
         pltpu.make_async_copy(source, target, sems.at[index])
         for index, (source, target) in enumerate(
@@ -102,6 +105,7 @@
     same = lax.broadcasted_iota(jnp.int32, (block_y, block_y), 0) == (
         lax.broadcasted_iota(jnp.int32, (block_y, block_y), 1)
     )
+    place = chip_place(near)
     for copy in copies:
         copy.wait()
     for slot in range(slots):
@@ -113,45 +117,47 @@
             shear = s[slot, x].astype(jnp.float32)
             square = primary * primary
             stiffness = jnp.where(deep >= floor, square + shear * shear, square)
-            coef = speed_factor * stiffness / rho[slot, x].astype(jnp.float32)
-            coef = coef.astype(out_ref.dtype)
-            for piece in range(x, out_ref.shape[0], near):
-                out_ref[piece, 2 * slot] = coef
-                out_ref[piece, 2 * slot + 1] = pert[slot, x]
+            value = speed_factor * stiffness / rho[slot, x].astype(jnp.float32)
+            coef[slot, x] = value.astype(coef.dtype)
     facts = jnp.where(lane == slots, row_ref[0], 0)
     facts = jnp.where(lane == slots + 1, col_ref[0], facts)
     for slot in range(slots):
         facts = jnp.where(lane == slot, ids[slot], facts)
-    facts = facts.astype(jnp.float32).astype(out_ref.dtype)
-    for piece in range(out_ref.shape[0]):
-        out_ref[piece, 2 * slots] = facts
-
-
-def pick_kernel(slots, near, pieces_ref, *refs):
-    out_refs = refs[:near]
-    facts_ref, facts, spots, sem = refs[near:]
-    count = facts_ref.shape[0]
-    tiles = 2 * slots + 1
-    for piece in range(count):
-        tile = pieces_ref[piece * tiles + 2 * slots].astype(jnp.float32)
-        facts_ref[piece:piece + 1] = tile.astype(jnp.int32)[0:1]
+    facts = facts.astype(jnp.float32).astype(coef.dtype)
+    for j, out_ref in enumerate(out_refs):
+        for slot in range(slots):
+            for r in range(2):
+                x = 2 * (place ^ j) + r
+                out_ref[4 * slot + 2 * r] = coef[slot, x]
+                out_ref[4 * slot + 2 * r + 1] = pert[slot, x]
+        out_ref[4 * slots] = facts
+
+
+def pick_kernel(slots, near, count, *refs):
+    piece_refs = refs[:count]
+    out_refs = refs[count:count + near]
+    facts_ref, facts, spots, pieces, sem = refs[count + near:]
+    tiles = 4 * slots + 1
+    for t, piece_ref in enumerate(piece_refs):
+        tile = piece_ref[tiles - 1].astype(jnp.float32)
+        facts_ref[t:t + 1] = tile.astype(jnp.int32)[0:1]
     copy = pltpu.make_async_copy(facts_ref, facts, sem)
     copy.start()
-    me = lax.axis_index("shot")
+    for t, piece_ref in enumerate(piece_refs):
+        pieces[t * tiles:(t + 1) * tiles] = piece_ref[...]
     copy.wait()
-    for piece in range(count):
+    for t in range(count):
         for slot in range(slots):
-            spots[facts[piece, slot]] = piece * tiles + 2 * slot
+            spots[facts[t, slot]] = t * tiles + 4 * slot
     for k, out_ref in enumerate(out_refs):
-        shot = me ^ k
-        first = facts[shot, slots] * GRID_COLS + facts[shot, slots + 1]
+        first = facts[2 * k, slots] * GRID_COLS + facts[2 * k, slots + 1]
         for x in range(APX):
             found = []
             for y in range(APY):
                 spot = spots[first + x * GRID_COLS + y]
-                found += [pieces_ref[spot], pieces_ref[spot + 1]]
+                found += [pieces[spot + tile] for tile in range(4)]
             for index, tile in enumerate(found):
-                out_ref[x * APY * 2 + index] = tile
+                out_ref[x * APY * 4 + index] = tile
 
 
 def ends(shape):
@@ -262,7 +268,7 @@
     depth = u_0.shape[3]
     block_y = model_refs[0].shape[1]
     block_x = span_x // APX
-    place = lax.axis_index("shot") % near
+    place = chip_place(near)
     masks = ends((LANES, depth))
     each = range(many)
     for field in (u_1, u_2, u_3, d_0, d_1, d_2, kb_3, kb_2, kb_1):
@@ -271,12 +277,13 @@
 
     for k, model_ref in enumerate(model_refs):
         for x in range(APX):
-            at = x * block_x + (place ^ k)
             for y in range(APY):
                 rows = pl.ds(y * block_y, block_y)
-                tile = 2 * (x * APY + y)
-                kap[at, rows] = model_ref[tile].astype(jnp.float32)
-                con[at, rows] = speed_factor * model_ref[tile + 1].astype(jnp.float32)
+                for r in range(2):
+                    at = x * block_x + 2 * (place ^ k) + r
+                    tile = 4 * (x * APY + y) + 2 * r
+                    kap[at, rows] = model_ref[tile].astype(jnp.float32)
+                    con[at, rows] = speed_factor * model_ref[tile + 1].astype(jnp.float32)
 
     def forward_0(x, carry):
         kaps, cons, grads = strided(kap, x), strided(con, x), registers(g_0, x)
@@ -323,7 +330,7 @@
                 total = image[x, v] + grad[x, v] * back
                 if kb_next is None:
                     total = (image_scale * total).astype(result.dtype)
-                    result[x % block_x, x // block_x * many + v] = total
+                    result[x % block_x // 2, (x % 2 * APX + x // block_x) * many + v] = total
                 else:
                     image[x, v] = total
                     b_next[x, v] = back
@@ -344,7 +351,7 @@
     flat = pltpu.VMEM((span_x, many * LANES, depth), jnp.float32)
     field = pltpu.VMEM((span_x + 1, many, LANES, depth), jnp.float32)
     plain = pltpu.VMEM((span_x, many, LANES, depth), jnp.float32)
-    out = (APX * many, LANES, depth)
+    out = (2 * APX * many, LANES, depth)
     return pl.pallas_call(
         functools.partial(wave_kernel, near),
         out_shape=(jax.ShapeDtypeStruct(out, jnp.bfloat16),) * near,
@@ -359,11 +366,11 @@
 
 def wave_split_depth(models, before, current):
     near = len(models)
-    order = (lax.axis_index("shot") % near) ^ jnp.arange(near)
+    order = chip_place(near) ^ jnp.arange(near)
     model = jnp.stack(models)[order]
     span_x, span_y, depth = before.shape
-    block_x, tiles, block_y, _ = model.shape
-    grids = model.reshape(block_x, APX, APY, 2, block_y, depth).transpose(3, 1, 0, 2, 4, 5)
+    block_x, block_y = 2 * near, model.shape[2]
+    grids = model.reshape(near, APX, APY, 2, 2, block_y, depth).transpose(4, 1, 0, 3, 2, 5, 6)
     grids = grids.reshape(2, span_x, span_y, depth).astype(jnp.float32)
     image = image_scale * propagate(
         grids[0],
@@ -373,66 +380,83 @@
         laplace_many,
     )
     many = span_y // LANES
-    image = image.reshape(APX, block_x, LANES, many, depth).transpose(1, 0, 3, 2, 4)
-    image = image.reshape(near, APX * many, LANES, depth).astype(jnp.bfloat16)[order]
+    image = image.reshape(APX, near, 2, LANES, many, depth).transpose(1, 2, 0, 4, 3, 5)
+    image = image.reshape(near, 2 * APX * many, LANES, depth).astype(jnp.bfloat16)[order]
     return [image[k] for k in range(near)]
 
 
 def stack_kernel(slots, near, facts_ref, *refs):
     terms_refs = refs[:near]
-    out_ref, facts, total, lined, sem = refs[near:]
-    tiles = terms_refs[0].shape[0]
-    wide = tiles // APX
+    mine_ref, other_ref, facts, total, lined, sem = refs[near:]
+    count = facts_ref.shape[0]
+    half = terms_refs[0].shape[0] // 2
+    wide = half // APX
     width = LANES // APY
-    grid_rows = total.shape[0] // wide
+    grid_rows = total.shape[1] // wide
     copy = pltpu.make_async_copy(facts_ref, facts, sem)
     copy.start()
-    me = lax.axis_index("shot")
 
     def clear(index, carry):
-        total[index] = jnp.zeros(total.shape[1:], total.dtype)
+        for r in range(2):
+            total[r, index] = jnp.zeros(total.shape[2:], total.dtype)
         return carry
 
-    lax.fori_loop(0, total.shape[0], clear, 0, unroll=8)
+    lax.fori_loop(0, total.shape[1], clear, 0, unroll=8)
     copy.wait()
-
     for k, terms_ref in enumerate(terms_refs):
-        first = facts[me ^ k, slots] * wide
-        rows = pl.ds(facts[me ^ k, slots + 1] * width, LANES)
-        sums = [
-            total[first + tile, rows] + terms_ref[tile].astype(jnp.float32)
-            for tile in range(tiles)
-        ]
-        for tile in range(tiles):
-            total[first + tile, rows] = sums[tile]
-
-    for row in range(grid_rows):
-        for part in range(wide):
-            for tile in range(total.shape[1] // LANES):
-                at = pl.ds(tile * LANES * wide + part, LANES, stride=wide)
-                lined[row, at] = total[row * wide + part, tile * LANES:(tile + 1) * LANES]
-
-    def give(owner, carry):
-        found = []
+        first = facts[2 * k, slots] * wide
+        rows = pl.ds(facts[2 * k, slots + 1] * width, LANES)
+        for r in range(2):
+            sums = [
+                total[r, first + tile, rows] + terms_ref[r * half + tile].astype(jnp.float32)
+                for tile in range(half)
+            ]
+            for tile in range(half):
+                total[r, first + tile, rows] = sums[tile]
+
+    def line(row, carry):
+        for r in range(2):
+            for part in range(wide):
+                for tile in range(total.shape[2] // LANES):
+                    at = pl.ds(tile * LANES * wide + part, LANES, stride=wide)
+                    lined[r, row, at] = total[
+                        r, row * wide + part, tile * LANES:(tile + 1) * LANES
+                    ]
+        return carry
+
+    lax.fori_loop(0, grid_rows, line, 0, unroll=4)
+
+    def give(k, carry):
+        for own, out_ref in enumerate((mine_ref, other_ref)):
+            found = []
+            for slot in range(slots):
+                block = facts[2 * k + own, slot]
+                rows = pl.ds(pl.multiple_of(block % GRID_COLS * LANES, LANES), LANES)
+                found += [lined[r, block // GRID_COLS, rows] for r in range(2)]
+            for index, tile in enumerate(found):
+                out_ref[k, index] = tile.astype(out_ref.dtype)
+        return carry
+
+    lax.fori_loop(0, count // 2, give, 0, unroll=2)
+
+
+def join_kernel(mine_ref, other_ref, *out_refs):
+    for k, out_ref in enumerate(out_refs):
+        total = mine_ref[k] + other_ref[k].astype(jnp.float32)
+        out_ref[...] = total.astype(out_ref.dtype)
+
+
+def finish_kernel(near, *refs):
+    sums_refs, out_ref = refs[:-1], refs[-1]
+    slots = out_ref.shape[0]
+    place = chip_place(near)
+    for j in range(near):
         for slot in range(slots):
-            block = facts[owner, slot]
-            rows = pl.ds(pl.multiple_of(block % GRID_COLS * LANES, LANES), LANES)
-            found.append(lined[block // GRID_COLS, rows])
-        for slot in range(slots):
-            out_ref[owner, slot] = found[slot].astype(out_ref.dtype)
-        return carry
-
-    lax.fori_loop(0, out_ref.shape[0], give, 0, unroll=4)
-
-
-def finish_kernel(sums_ref, out_ref):
-    slots, block_x = out_ref.shape[:2]
-    for x in range(block_x):
-        for slot in range(slots):
-            result = sums_ref[x, slot].astype(jnp.float32)
-            for piece in range(x + block_x, sums_ref.shape[0], block_x):
-                result = result + sums_ref[piece, slot].astype(jnp.float32)
-            out_ref[slot, x] = result
+            for r in range(2):
+                result = sums_refs[j][2 * slot + r].astype(jnp.float32)
+                for k in range(j + near, len(sums_refs), near):
+                    result = result + sums_refs[k][2 * slot + r].astype(jnp.float32)
+                out_ref[slot, 2 * (place ^ j) + r] = result
 
 
 def per_device(
@@ -455,24 +479,29 @@
     if split:
         seafloor = seafloor - lax.axis_index("depth") * depth
 
-    near = block_x
-    assert count % near == 0 and near & (near - 1) == 0
+    chips = count // 2
+    near = block_x // 2
+    assert chips % near == 0 and chips & (chips - 1) == 0
 
     def swap(values):
-        return [
-            lax.ppermute(value, "shot", [(i, i ^ k) for i in range(count)]) if k else value
-            for k, value in enumerate(values)
-        ]
-
+        swapped = {0: values[0]}
+        for k in range(len(values) - 1, 0, -1):
+            swapped[k] = lax.ppermute(values[k], "shot", [(i, i ^ 2 * k) for i in range(count)])
+        return [swapped[k] for k in range(len(values))]
+
+    def across(value):
+        return lax.ppermute(value, "shot", [(i, i ^ 1) for i in range(count)])
+
+    out = jax.ShapeDtypeStruct((4 * slots + 1, block_y, depth), jnp.bfloat16)
     sent = pl.pallas_call(
-        prepare_kernel,
-        out_shape=jax.ShapeDtypeStruct((count, 2 * slots + 1, block_y, depth), jnp.bfloat16),
+        functools.partial(prepare_kernel, near),
+        out_shape=(out,) * near,
         in_specs=[smem()] * 2 + [pl.BlockSpec(memory_space=pltpu.HBM)] * 6,
-        out_specs=vmem(),
+        out_specs=(vmem(),) * near,
         scratch_shapes=[
             pltpu.SMEM(owner_ids.shape, jnp.int32),
             pltpu.VMEM(seafloor.shape, jnp.int32),
-            *[pltpu.VMEM(velocity_p.shape, jnp.bfloat16) for _ in range(4)],
+            *[pltpu.VMEM(velocity_p.shape, jnp.bfloat16) for _ in range(5)],
             pltpu.SemaphoreType.DMA((6,)),
         ],
         name="prepare",
@@ -480,29 +509,29 @@
         corner_x, corner_y, owner_ids, seafloor,
         velocity_p, velocity_s, density, perturbation,
     )
-    pieces = lax.all_to_all(sent, "shot", 0, 0, tiled=True)
-
+    pieces = swap([sent[k % near] for k in range(chips)])
+    pieces = [piece for own in pieces for piece in (own, across(own))]
     if not split:
         started = start(wave_prev[0], wave_now[0])
         pieces, started = lax.optimization_barrier((pieces, started))
     *picked, facts = pl.pallas_call(
-        functools.partial(pick_kernel, slots, near),
+        functools.partial(pick_kernel, slots, near, count),
         out_shape=(
-            *[jax.ShapeDtypeStruct((patch * 2, block_y, depth), jnp.bfloat16)] * near,
+            *[jax.ShapeDtypeStruct((patch * 4, block_y, depth), jnp.bfloat16)] * near,
             jax.ShapeDtypeStruct((count, depth), jnp.int32),
         ),
-        in_specs=[vmem()],
+        in_specs=[vmem()] * count,
         out_specs=(vmem(),) * (near + 1),
         scratch_shapes=[
             pltpu.SMEM((count, depth), jnp.int32),
             pltpu.SMEM((count * slots,), jnp.int32),
+            pltpu.VMEM((count * (4 * slots + 1), block_y, depth), jnp.bfloat16),
             pltpu.SemaphoreType.DMA,
         ],
         compiler_params=limit(3),
         name="pick",
-    )(pieces.reshape(count * (2 * slots + 1), block_y, depth))
+    )(*pieces)
     models = swap(picked)
-
     if split:
         terms = wave_split_depth(models, wave_prev[0], wave_now[0])
     else:
@@ -510,30 +539,40 @@
     terms = swap(terms)
 
     grid_rows = count * slots // GRID_COLS
-    wide = terms[0].shape[0] // APX
-    sums = pl.pallas_call(
+    wide = terms[0].shape[0] // 2 // APX
+    sums = (chips, 2 * slots, block_y, depth)
+    mine, other = pl.pallas_call(
         functools.partial(stack_kernel, slots, near),
-        out_shape=jax.ShapeDtypeStruct((count, slots, block_y, depth), jnp.bfloat16),
+        out_shape=(
+            jax.ShapeDtypeStruct(sums, jnp.float32), jax.ShapeDtypeStruct(sums, jnp.bfloat16)
+        ),
         in_specs=[vmem()] * (near + 1),
-        out_specs=vmem(),
+        out_specs=(vmem(), vmem()),
         scratch_shapes=[
             pltpu.SMEM(facts.shape, jnp.int32),
-            pltpu.VMEM((grid_rows * wide, GRID_COLS * LANES // APY, depth), jnp.float32),
-            pltpu.VMEM((grid_rows, GRID_COLS * block_y, depth), jnp.float32),
+            pltpu.VMEM((2, grid_rows * wide, GRID_COLS * LANES // APY, depth), jnp.float32),
+            pltpu.VMEM((2, grid_rows, GRID_COLS * block_y, depth), jnp.float32),
             pltpu.SemaphoreType.DMA,
         ],
-        compiler_params=limit(3),
+        compiler_params=limit(4),
         name="stack",
     )(facts, *terms)
-    sums = lax.all_to_all(sums, "shot", 0, 0, tiled=True)
+    joined = pl.pallas_call(
+        join_kernel,
+        out_shape=(jax.ShapeDtypeStruct(sums[1:], jnp.bfloat16),) * chips,
+        in_specs=[vmem()] * 2,
+        out_specs=(vmem(),) * chips,
+        compiler_params=limit(2),
+        name="join",
+    )(mine, across(other))
     return pl.pallas_call(
-        finish_kernel,
+        functools.partial(finish_kernel, near),
         out_shape=jax.ShapeDtypeStruct(velocity_p.shape, jnp.float32),
-        in_specs=[vmem()],
+        in_specs=[vmem()] * chips,
         out_specs=vmem(),
         compiler_params=limit(2),
         name="finish",
-    )(sums)
+    )(*swap(joined))
 
 
 def solution(mesh):

time: 59.1 us -> 62.9 us (1.064)
  starting transfers between devices: 19.7 us -> 33.1 us
  blocking collectives: 11 us -> 0 us
  local copies, waits for them, and re-layouts: 0.01 us -> 0.97 us
    ppermute x14 -> x29, starting transfers between devices: 12.2 us -> 33.1 us  [the longest x20 31.5 us: swap(): lax.ppermute(values[k], 'shot', [(i, i ^ 2 * k) for i in range(count)])]
    all_to_all x1 -> x0, blocking collectives: 11 us -> none  [per_device(): sums = lax.all_to_all(sums, 'shot', 0, 0, tiled=True)]
    ppermute x14 -> x29, waiting for transfers between devices: 7.86 us -> 18.2 us  [the longest x20 16.8 us: swap(): lax.ppermute(values[k], 'shot', [(i, i ^ 2 * k) for i in range(count)])]
    all_to_all x1 -> x0, waiting for transfers between devices: 9.85 us -> none  [per_device(): pieces = lax.all_to_all(sent, 'shot', 0, 0, tiled=True)]
    all_to_all x1 -> x0, starting transfers between devices: 7.5 us -> none  [per_device(): pieces = lax.all_to_all(sent, 'shot', 0, 0, tiled=True)]
    unnamed x4 -> x6, local copies, waits for them, and re-layouts: 0.01 us -> 0.97 us
    pallas_call x4 -> x5, Pallas kernels: 4.61 us -> 4.54 us  [the longest x1 1.77 us: per_device(): pl.pallas_call(functools.partial(prepare_kernel, near), out_shape=(out,)...]
  transfers between devices with their start and end apart: 15 -> 29, of which waited for: 8 -> 12; matrix products, arithmetic and copies ran while one was open for 0% -> 0% of each run, Pallas kernels for 1% -> 1%
where the time goes in v3:
time: 62.9 us; the launch traced here: 62.6 us
  starting transfers between devices  33.1 us (53%)
  waiting for transfers between devices  18.2 us (29%)
  Pallas kernels  8.84 us (14%)
  between operations  1.46 us (2%)
  local copies, waits for them, and re-layouts  0.97 us (2%)
    ppermute x20, starting transfers between devices, swap(): lax.ppermute(values[k], 'shot', [(i, i ^ 2 * k) for i in range(count)])  31.5 us
    ppermute x20, waiting for transfers between devices, swap(): lax.ppermute(values[k], 'shot', [(i, i ^ 2 * k) for i in range(count)])  16.8 us
    pallas_call x1, Pallas kernels, wave(): pl.pallas_call(functools.partial(wave_kernel, near), out_shape=(jax.Shape...  3.61 us
    pallas_call x1, Pallas kernels, per_device(): pl.pallas_call(functools.partial(prepare_kernel, near), out_shape=(out,)...  1.77 us
    ppermute x9, starting transfers between devices, across(): return lax.ppermute(value, 'shot', [(i, i ^ 1) for i in range(count)])  1.61 us
    ppermute x9, waiting for transfers between devices, across(): return lax.ppermute(value, 'shot', [(i, i ^ 1) for i in range(count)])  1.36 us
  transfers between devices with their start and end apart: 29, of which 12 were waited for; matrix products, arithmetic and copies ran while one was open for 0% of the time, Pallas kernels for 1%

profile of v3, /device:TPU:0, one launch (start us, length us, event | category | flops | bytes accessed | tf_op | source)
XLA Modules:
  0.0 62.6 jit_solution(14138720081409927566)
XLA Ops:
  1.3 1.8 %prepare.1 = (bf16[17,8,128]{2,1,0:T(8,128)(2,1)}, bf16[17,8,128]{2,1,0:T(8,128)(2,1)}, bf16[17,8,128]{2,1,0:T(8,128)(2,1)}, bf16[17,8,128]{2,1,0:T(8,128)(2,1)}) custom-call(s32[1]{0:T(128)S(6)} %copy.11.row_ref, s32[1]{0:T(128)S(6)} %copy.12.col_ref, s32[4]{0:T(128)} %refs_0_.1, s32[4,8,8]{2,1,0:T(8,128)} %refs_1_.1, bf16[4,8,8,128]{3,2,1,0:T(8,128)(2,1)} %refs_2_.1, ...), custom_call_target="tpu_custom_call" | custom-call | tf_op jit(solution)/shard_map/prepare/pallas_call | solution.py:496
  3.1 5.0 %collective-permute-start.9 = (bf16[17,8,128]{2,1,0:T(8,128)(2,1)}, bf16[17,8,128]{2,1,0:T(8,128)(2,1)S(1)}, u32[]{:S(2)}, u32[]{:S(2)}) collective-permute-start(bf16[17,8,128]{2,1,0:T(8,128)(2,1)} %get-tuple-element.51), channel_id=1, source_target_pairs={{0,10},{1,11},{2,8},{3,9},{4,14},{5,15},{6,12},{7,13},{8,2},{9,3},... | collective-permute-start | bytes 104456 | tf_op jit(solution)/shard_map/ppermute | solution.py:489
  8.1 0.5 collective-permute-start.1
  8.7 1.4 %collective-permute-start.11 = (bf16[17,8,128]{2,1,0:T(8,128)(2,1)}, bf16[17,8,128]{2,1,0:T(8,128)(2,1)S(1)}, u32[]{:S(2)}, u32[]{:S(2)}) collective-permute-start(bf16[17,8,128]{2,1,0:T(8,128)(2,1)} %get-tuple-element.52), channel_id=1, source_target_pairs={{0,12},{1,13},{2,14},{3,15},{4,8},{5,9},{6,10},{7,11},{8,4},{9,5},... | collective-permute-start | bytes 104456 | tf_op jit(solution)/shard_map/ppermute | solution.py:489
  10.0 0.2 collective-permute-start.3
  10.3 3.8 %collective-permute-start.13 = (bf16[17,8,128]{2,1,0:T(8,128)(2,1)}, bf16[17,8,128]{2,1,0:T(8,128)(2,1)S(1)}, u32[]{:S(2)}, u32[]{:S(2)}) collective-permute-start(bf16[17,8,128]{2,1,0:T(8,128)(2,1)} %get-tuple-element.53), channel_id=1, source_target_pairs={{0,14},{1,15},{2,12},{3,13},{4,10},{5,11},{6,8},{7,9},{8,6},{9,7},... | collective-permute-start | bytes 104456 | tf_op jit(solution)/shard_map/ppermute | solution.py:489
  14.1 0.0 collective-permute-done.9.refs_10_
  14.1 0.4 collective-permute-start.5
  14.5 0.0 collective-permute-done.1.refs_2_
  14.5 1.8 %collective-permute-start.7 = (bf16[17,8,128]{2,1,0:T(8,128)(2,1)}, bf16[17,8,128]{2,1,0:T(8,128)(2,1)S(1)}, u32[]{:S(2)}, u32[]{:S(2)}) collective-permute-start(bf16[17,8,128]{2,1,0:T(8,128)(2,1)} %get-tuple-element.57.refs_0_), channel_id=1, source_target_pairs={{0,8},{1,9},{2,10},{3,11},{4,12},{5,13},{6,14},{7,15},{8,0},{9,1},... | collective-permute-start | bytes 104456 | tf_op jit(solution)/shard_map/ppermute | solution.py:489
  16.4 0.0 collective-permute-done.11.refs_12_
  16.4 0.0 collective-permute-start
  16.4 0.0 collective-permute-done.3.refs_4_
  16.4 0.5 collective-permute-start.10
  16.9 0.2 collective-permute-done.13.refs_14_
  17.1 0.0 collective-permute-start.2
  17.1 2.0 %collective-permute-done.5.refs_6_ = bf16[17,8,128]{2,1,0:T(8,128)(2,1)S(1)} collective-permute-done((bf16[17,8,128]{2,1,0:T(8,128)(2,1)}, bf16[17,8,128]{2,1,0:T(8,128)(2,1)S(1)}, u32[]{:S(2)}, u32[]{:S(2)}) %collective-permute-start.5) | collective-permute-done | bytes 34848 | tf_op jit(solution)/shard_map/ppermute | solution.py:489
  19.2 0.0 collective-permute-start.12
  19.2 0.4 collective-permute-done.7.refs_8_
  19.6 0.1 collective-permute-start.4
  19.7 0.0 collective-permute-done.refs_1_
  19.7 0.4 collective-permute-start.14
  20.1 0.0 collective-permute-done.10.refs_11_
  20.1 0.1 collective-permute-start.6
  20.2 0.0 collective-permute-done.2.refs_3_
  20.2 0.4 collective-permute-start.8
  20.6 0.9 %copy-done.1 = bf16[1,32,32,128]{3,2,1,0:T(8,128)(2,1)S(1)} copy-done((bf16[1,32,32,128]{3,2,1,0:T(8,128)(2,1)S(1)}, bf16[1,32,32,128]{3,2,1,0:T(8,128)(2,1)}, u32[]{:S(2)}) %copy-start.1) | copy-done | bytes 262168
  21.6 0.7 %start.1 = (f32[32,4,8,128]{3,2,1,0:T(8,128)S(1)}, f32[32,4,8,128]{3,2,1,0:T(8,128)S(1)}, f32[32,4,8,128]{3,2,1,0:T(8,128)S(1)}) custom-call(bf16[32,32,128]{2,1,0:T(8,128)(2,1)S(1)} %bitcast.2, bf16[32,32,128]{2,1,0:T(8,128)(2,1)S(1)} %bitcast.3), custom_call_target="tpu_custom_call" | custom-call | flops 2621440 | bytes 2097152 | tf_op jit(solution)/shard_map/start/pallas_call | solution.py:247
  22.3 0.0 collective-permute-done.12.refs_13_
  22.3 0.0 collective-permute-done.4.refs_5_
  22.3 0.0 collective-permute-done.14.refs_15_
  22.3 0.0 collective-permute-done.6.refs_7_
  22.3 0.0 collective-permute-done.8.refs_9_
  22.3 0.0 copy-done.2
  22.3 0.8 %pick.1 = (bf16[64,8,128]{2,1,0:T(8,128)(2,1)S(1)}, bf16[64,8,128]{2,1,0:T(8,128)(2,1)S(1)}, bf16[64,8,128]{2,1,0:T(8,128)(2,1)S(1)}, bf16[64,8,128]{2,1,0:T(8,128)(2,1)S(1)}, s32[16,128]{1,0:T(8,128)S(1)}) custom-call(bf16[17,8,128]{2,1,0:T(8,128)(2,1)S(1)} %copy-done.2, bf16[17,8,128]{2,1,0:T(8,128)(2,1)S(1)} %collective-permute-done.refs_1_, ...), custom_call_target="tpu_custom_call" | custom-call | tf_op jit(solution)/shard_map/pick/pallas_call | solution.py:517
  23.2 1.6 %collective-permute-start.15 = (bf16[64,8,128]{2,1,0:T(8,128)(2,1)S(1)}, bf16[64,8,128]{2,1,0:T(8,128)(2,1)S(1)}, u32[]{:S(2)}, u32[]{:S(2)}) collective-permute-start(bf16[64,8,128]{2,1,0:T(8,128)(2,1)S(1)} %get-tuple-element.75), channel_id=1, source_target_pairs={{0,2},{1,3},{2,0},{3,1},{4,6},{5,7},{6,4},{7,5},{8,10},{9,11},{10,... | collective-permute-start | bytes 393224 | tf_op jit(solution)/shard_map/ppermute | solution.py:489
  24.7 1.6 %collective-permute-start.16 = (bf16[64,8,128]{2,1,0:T(8,128)(2,1)S(1)}, bf16[64,8,128]{2,1,0:T(8,128)(2,1)S(1)}, u32[]{:S(2)}, u32[]{:S(2)}) collective-permute-start(bf16[64,8,128]{2,1,0:T(8,128)(2,1)S(1)} %get-tuple-element.76), channel_id=1, source_target_pairs={{0,4},{1,5},{2,6},{3,7},{4,0},{5,1},{6,2},{7,3},{8,12},{9,13},{10,... | collective-permute-start | bytes 393224 | tf_op jit(solution)/shard_map/ppermute | solution.py:489
  26.3 0.4 collective-permute-start.17
  26.7 2.0 %collective-permute-done.15.refs_1_ = bf16[64,8,128]{2,1,0:T(8,128)(2,1)S(1)} collective-permute-done((bf16[64,8,128]{2,1,0:T(8,128)(2,1)S(1)}, bf16[64,8,128]{2,1,0:T(8,128)(2,1)S(1)}, u32[]{:S(2)}, u32[]{:S(2)}) %collective-permute-start.15) | collective-permute-done | bytes 131104 | tf_op jit(solution)/shard_map/ppermute | solution.py:489
  28.7 2.4 %collective-permute-done.16.refs_2_ = bf16[64,8,128]{2,1,0:T(8,128)(2,1)S(1)} collective-permute-done((bf16[64,8,128]{2,1,0:T(8,128)(2,1)S(1)}, bf16[64,8,128]{2,1,0:T(8,128)(2,1)S(1)}, u32[]{:S(2)}, u32[]{:S(2)}) %collective-permute-start.16) | collective-permute-done | bytes 131104 | tf_op jit(solution)/shard_map/ppermute | solution.py:489
  31.1 1.6 %collective-permute-done.17.refs_3_ = bf16[64,8,128]{2,1,0:T(8,128)(2,1)S(1)} collective-permute-done((bf16[64,8,128]{2,1,0:T(8,128)(2,1)S(1)}, bf16[64,8,128]{2,1,0:T(8,128)(2,1)S(1)}, u32[]{:S(2)}, u32[]{:S(2)}) %collective-permute-start.17) | collective-permute-done | bytes 131104 | tf_op jit(solution)/shard_map/ppermute | solution.py:489
  32.7 3.6 %wave.1 = (bf16[32,8,128]{2,1,0:T(8,128)(2,1)S(1)}, bf16[32,8,128]{2,1,0:T(8,128)(2,1)S(1)}, bf16[32,8,128]{2,1,0:T(8,128)(2,1)S(1)}, bf16[32,8,128]{2,1,0:T(8,128)(2,1)S(1)}) custom-call(bf16[64,8,128]{2,1,0:T(8,128)(2,1)S(1)} %get-tuple-element.74.refs_0_, bf16[64,8,128]{2,1,0:T(8,128)(2,1)S(1)} %collective-permute-done.15.refs_1_, ...), custom_call_target="tpu_custom_call" | custom-call | tf_op jit(solution)/shard_map/wave/pallas_call | solution.py:355
  36.4 1.5 %collective-permute-start.18 = (bf16[32,8,128]{2,1,0:T(8,128)(2,1)S(1)}, bf16[32,8,128]{2,1,0:T(8,128)(2,1)S(1)}, u32[]{:S(2)}, u32[]{:S(2)}) collective-permute-start(bf16[32,8,128]{2,1,0:T(8,128)(2,1)S(1)} %get-tuple-element.82), channel_id=1, source_target_pairs={{0,2},{1,3},{2,0},{3,1},{4,6},{5,7},{6,4},{7,5},{8,10},{9,11},{10,... | collective-permute-start | bytes 196616 | tf_op jit(solution)/shard_map/ppermute | solution.py:489
  37.9 1.6 %collective-permute-start.19 = (bf16[32,8,128]{2,1,0:T(8,128)(2,1)S(1)}, bf16[32,8,128]{2,1,0:T(8,128)(2,1)S(1)}, u32[]{:S(2)}, u32[]{:S(2)}) collective-permute-start(bf16[32,8,128]{2,1,0:T(8,128)(2,1)S(1)} %get-tuple-element.83), channel_id=1, source_target_pairs={{0,4},{1,5},{2,6},{3,7},{4,0},{5,1},{6,2},{7,3},{8,12},{9,13},{10,... | collective-permute-start | bytes 196616 | tf_op jit(solution)/shard_map/ppermute | solution.py:489
  39.5 0.4 collective-permute-start.20
  39.9 0.8 %collective-permute-done.18.refs_1_ = bf16[32,8,128]{2,1,0:T(8,128)(2,1)S(1)} collective-permute-done((bf16[32,8,128]{2,1,0:T(8,128)(2,1)S(1)}, bf16[32,8,128]{2,1,0:T(8,128)(2,1)S(1)}, u32[]{:S(2)}, u32[]{:S(2)}) %collective-permute-start.18) | collective-permute-done | bytes 65568 | tf_op jit(solution)/shard_map/ppermute | solution.py:489
  40.7 1.5 %collective-permute-done.19.refs_2_ = bf16[32,8,128]{2,1,0:T(8,128)(2,1)S(1)} collective-permute-done((bf16[32,8,128]{2,1,0:T(8,128)(2,1)S(1)}, bf16[32,8,128]{2,1,0:T(8,128)(2,1)S(1)}, u32[]{:S(2)}, u32[]{:S(2)}) %collective-permute-start.19) | collective-permute-done | bytes 65568 | tf_op jit(solution)/shard_map/ppermute | solution.py:489
  42.2 2.5 %collective-permute-done.20.refs_3_ = bf16[32,8,128]{2,1,0:T(8,128)(2,1)S(1)} collective-permute-done((bf16[32,8,128]{2,1,0:T(8,128)(2,1)S(1)}, bf16[32,8,128]{2,1,0:T(8,128)(2,1)S(1)}, u32[]{:S(2)}, u32[]{:S(2)}) %collective-permute-start.20) | collective-permute-done | bytes 65568 | tf_op jit(solution)/shard_map/ppermute | solution.py:489
  44.6 1.2 %stack.1 = (f32[8,8,8,128]{3,2,1,0:T(8,128)S(1)}, bf16[8,8,8,128]{3,2,1,0:T(8,128)(2,1)S(1)}) custom-call(s32[16,128]{1,0:T(8,128)S(1)} %get-tuple-element.73.facts_ref, bf16[32,8,128]{2,1,0:T(8,128)(2,1)S(1)} %get-tuple-element.81.refs_0_, bf16[32,8,128]{2,1,0:T(8,128)(2,1)S(1)} %collective-permute-done.18.refs_1_, ...), custom_call_target="tpu_custom_call" | custom-call | tf_op jit(solution)/shard_map/stack/pallas_call | solution.py:544
  45.9 0.1 collective-permute-start.21
  45.9 1.3 %collective-permute-done.21.other_ref = bf16[8,8,8,128]{3,2,1,0:T(8,128)(2,1)S(1)} collective-permute-done((bf16[8,8,8,128]{3,2,1,0:T(8,128)(2,1)S(1)}, bf16[8,8,8,128]{3,2,1,0:T(8,128)(2,1)S(1)}, u32[]{:S(2)}, u32[]{:S(2)}) %collective-permute-start.21) | collective-permute-done | bytes 131104 | tf_op jit(solution)/shard_map/ppermute | solution.py:493
  47.3 0.6 collective-permute-start.22
  47.9 0.7 %collective-permute-start.23 = (bf16[8,8,128]{2,1,0:T(8,128)(2,1)S(1)}, bf16[8,8,128]{2,1,0:T(8,128)(2,1)S(1)}, u32[]{:S(2)}, u32[]{:S(2)}) collective-permute-start(bf16[8,8,128]{2,1,0:T(8,128)(2,1)S(1)} %get-tuple-element.89), channel_id=1, source_target_pairs={{0,4},{1,5},{2,6},{3,7},{4,0},{5,1},{6,2},{7,3},{8,12},{9,13},{10,... | collective-permute-start | bytes 49160 | tf_op jit(solution)/shard_map/ppermute | solution.py:489
  48.6 2.2 %collective-permute-start.24 = (bf16[8,8,128]{2,1,0:T(8,128)(2,1)S(1)}, bf16[8,8,128]{2,1,0:T(8,128)(2,1)S(1)}, u32[]{:S(2)}, u32[]{:S(2)}) collective-permute-start(bf16[8,8,128]{2,1,0:T(8,128)(2,1)S(1)} %get-tuple-element.90), channel_id=1, source_target_pairs={{0,6},{1,7},{2,4},{3,5},{4,2},{5,3},{6,0},{7,1},{8,14},{9,15},{10,... | collective-permute-start | bytes 49160 | tf_op jit(solution)/shard_map/ppermute | solution.py:489
  50.9 0.3 collective-permute-start.25
  51.2 2.6 %collective-permute-start.26 = (bf16[8,8,128]{2,1,0:T(8,128)(2,1)S(1)}, bf16[8,8,128]{2,1,0:T(8,128)(2,1)S(1)}, u32[]{:S(2)}, u32[]{:S(2)}) collective-permute-start(bf16[8,8,128]{2,1,0:T(8,128)(2,1)S(1)} %get-tuple-element.92), channel_id=1, source_target_pairs={{0,10},{1,11},{2,8},{3,9},{4,14},{5,15},{6,12},{7,13},{8,2},{9,3},... | collective-permute-start | bytes 49160 | tf_op jit(solution)/shard_map/ppermute | solution.py:489
  53.8 0.0 collective-permute-done.22.refs_1_
  53.8 1.7 %collective-permute-start.27 = (bf16[8,8,128]{2,1,0:T(8,128)(2,1)S(1)}, bf16[8,8,128]{2,1,0:T(8,128)(2,1)S(1)}, u32[]{:S(2)}, u32[]{:S(2)}) collective-permute-start(bf16[8,8,128]{2,1,0:T(8,128)(2,1)S(1)} %get-tuple-element.93), channel_id=1, source_target_pairs={{0,12},{1,13},{2,14},{3,15},{4,8},{5,9},{6,10},{7,11},{8,4},{9,5},... | collective-permute-start | bytes 49160 | tf_op jit(solution)/shard_map/ppermute | solution.py:489
  55.5 0.0 collective-permute-done.23.refs_2_
  55.5 3.0 %collective-permute-start.28 = (bf16[8,8,128]{2,1,0:T(8,128)(2,1)S(1)}, bf16[8,8,128]{2,1,0:T(8,128)(2,1)S(1)}, u32[]{:S(2)}, u32[]{:S(2)}) collective-permute-start(bf16[8,8,128]{2,1,0:T(8,128)(2,1)S(1)} %get-tuple-element.94), channel_id=1, source_target_pairs={{0,14},{1,15},{2,12},{3,13},{4,10},{5,11},{6,8},{7,9},{8,6},{9,7},... | collective-permute-start | bytes 49160 | tf_op jit(solution)/shard_map/ppermute | solution.py:489
  58.5 0.0 collective-permute-done.24.refs_3_
  58.5 0.8 %collective-permute-done.27.refs_6_ = bf16[8,8,128]{2,1,0:T(8,128)(2,1)S(1)} collective-permute-done((bf16[8,8,128]{2,1,0:T(8,128)(2,1)S(1)}, bf16[8,8,128]{2,1,0:T(8,128)(2,1)S(1)}, u32[]{:S(2)}, u32[]{:S(2)}) %collective-permute-start.27) | collective-permute-done | bytes 16416 | tf_op jit(solution)/shard_map/ppermute | solution.py:489
  59.3 2.6 %collective-permute-done.28.refs_7_ = bf16[8,8,128]{2,1,0:T(8,128)(2,1)S(1)} collective-permute-done((bf16[8,8,128]{2,1,0:T(8,128)(2,1)S(1)}, bf16[8,8,128]{2,1,0:T(8,128)(2,1)S(1)}, u32[]{:S(2)}, u32[]{:S(2)}) %collective-permute-start.28) | collective-permute-done | bytes 16416 | tf_op jit(solution)/shard_map/ppermute | solution.py:489
  61.9 0.7 %finish.1 = f32[4,8,8,128]{3,2,1,0:T(8,128)} custom-call(bf16[8,8,128]{2,1,0:T(8,128)(2,1)S(1)} %get-tuple-element.87.refs_0_, bf16[8,8,128]{2,1,0:T(8,128)(2,1)S(1)} %collective-permute-done.22.refs_1_, bf16[8,8,128]{2,1,0:T(8,128)(2,1)S(1)} %collective-permute-done.23.refs_2_, bf16[8,8,128]{2,1,0:T(8,128)(2,1)S(1)} %collective-permute-done.24.refs_3_, ...), custom_call_target="tpu_custom_call" | custom-call | tf_op jit(solution)/shard_map/finish/pallas_call | solution.py:568
  (7 shorter events, 0.0 us)
Async XLA Ops:
  0.0 20.6 %copy-start = (bf16[1,32,32,128]{3,2,1,0:T(8,128)(2,1)S(1)}, bf16[1,32,32,128]{3,2,1,0:T(8,128)(2,1)}, u32[]{:S(2)}) copy-start(bf16[1,32,32,128]{3,2,1,0:T(8,128)(2,1)} %param.18) | copy-start | bytes 786436
  3.1 11.0 %collective-permute-start.9 = (bf16[17,8,128]{2,1,0:T(8,128)(2,1)}, bf16[17,8,128]{2,1,0:T(8,128)(2,1)S(1)}, u32[]{:S(2)}, u32[]{:S(2)}) collective-permute-start(bf16[17,8,128]{2,1,0:T(8,128)(2,1)} %get-tuple-element.51), channel_id=1, source_target_pairs={{0,10},{1,11},{2,8},{3,9},{4,14},{5,15},{6,12},{7,13},{8,2},{9,3},... | collective-permute-start | bytes 104456 | tf_op jit(solution)/shard_map/ppermute | solution.py:489
  8.1 6.4 %collective-permute-start.1 = (bf16[17,8,128]{2,1,0:T(8,128)(2,1)}, bf16[17,8,128]{2,1,0:T(8,128)(2,1)S(1)}, u32[]{:S(2)}, u32[]{:S(2)}) collective-permute-start(bf16[17,8,128]{2,1,0:T(8,128)(2,1)} %get-tuple-element.51), channel_id=1, source_target_pairs={{0,2},{1,3},{2,0},{3,1},{4,6},{5,7},{6,4},{7,5},{8,10},{9,11},{10,... | collective-permute-start | bytes 104456 | tf_op jit(solution)/shard_map/ppermute | solution.py:489
  8.7 7.7 %collective-permute-start.11 = (bf16[17,8,128]{2,1,0:T(8,128)(2,1)}, bf16[17,8,128]{2,1,0:T(8,128)(2,1)S(1)}, u32[]{:S(2)}, u32[]{:S(2)}) collective-permute-start(bf16[17,8,128]{2,1,0:T(8,128)(2,1)} %get-tuple-element.52), channel_id=1, source_target_pairs={{0,12},{1,13},{2,14},{3,15},{4,8},{5,9},{6,10},{7,11},{8,4},{9,5},... | collective-permute-start | bytes 104456 | tf_op jit(solution)/shard_map/ppermute | solution.py:489
  10.0 6.3 %collective-permute-start.3 = (bf16[17,8,128]{2,1,0:T(8,128)(2,1)}, bf16[17,8,128]{2,1,0:T(8,128)(2,1)S(1)}, u32[]{:S(2)}, u32[]{:S(2)}) collective-permute-start(bf16[17,8,128]{2,1,0:T(8,128)(2,1)} %get-tuple-element.52), channel_id=1, source_target_pairs={{0,4},{1,5},{2,6},{3,7},{4,0},{5,1},{6,2},{7,3},{8,12},{9,13},{10,... | collective-permute-start | bytes 104456 | tf_op jit(solution)/shard_map/ppermute | solution.py:489
  10.3 6.8 %collective-permute-start.13 = (bf16[17,8,128]{2,1,0:T(8,128)(2,1)}, bf16[17,8,128]{2,1,0:T(8,128)(2,1)S(1)}, u32[]{:S(2)}, u32[]{:S(2)}) collective-permute-start(bf16[17,8,128]{2,1,0:T(8,128)(2,1)} %get-tuple-element.53), channel_id=1, source_target_pairs={{0,14},{1,15},{2,12},{3,13},{4,10},{5,11},{6,8},{7,9},{8,6},{9,7},... | collective-permute-start | bytes 104456 | tf_op jit(solution)/shard_map/ppermute | solution.py:489
  14.1 5.0 %collective-permute-start.5 = (bf16[17,8,128]{2,1,0:T(8,128)(2,1)}, bf16[17,8,128]{2,1,0:T(8,128)(2,1)S(1)}, u32[]{:S(2)}, u32[]{:S(2)}) collective-permute-start(bf16[17,8,128]{2,1,0:T(8,128)(2,1)} %get-tuple-element.53), channel_id=1, source_target_pairs={{0,6},{1,7},{2,4},{3,5},{4,2},{5,3},{6,0},{7,1},{8,14},{9,15},{10,... | collective-permute-start | bytes 104456 | tf_op jit(solution)/shard_map/ppermute | solution.py:489
  14.5 5.0 %collective-permute-start.7 = (bf16[17,8,128]{2,1,0:T(8,128)(2,1)}, bf16[17,8,128]{2,1,0:T(8,128)(2,1)S(1)}, u32[]{:S(2)}, u32[]{:S(2)}) collective-permute-start(bf16[17,8,128]{2,1,0:T(8,128)(2,1)} %get-tuple-element.57.refs_0_), channel_id=1, source_target_pairs={{0,8},{1,9},{2,10},{3,11},{4,12},{5,13},{6,14},{7,15},{8,0},{9,1},... | collective-permute-start | bytes 104456 | tf_op jit(solution)/shard_map/ppermute | solution.py:489
  16.4 3.3 %collective-permute-start = (bf16[17,8,128]{2,1,0:T(8,128)(2,1)}, bf16[17,8,128]{2,1,0:T(8,128)(2,1)S(1)}, u32[]{:S(2)}, u32[]{:S(2)}) collective-permute-start(bf16[17,8,128]{2,1,0:T(8,128)(2,1)} %get-tuple-element.57.refs_0_), channel_id=1, source_target_pairs={{0,1},{1,0},{2,3},{3,2},{4,5},{5,4},{6,7},{7,6},{8,9},{9,8},{10,11... | collective-permute-start | bytes 104456 | tf_op jit(solution)/shard_map/ppermute | solution.py:493
  16.4 3.7 %collective-permute-start.10 = (bf16[17,8,128]{2,1,0:T(8,128)(2,1)S(1)}, bf16[17,8,128]{2,1,0:T(8,128)(2,1)S(1)}, u32[]{:S(2)}, u32[]{:S(2)}) collective-permute-start(bf16[17,8,128]{2,1,0:T(8,128)(2,1)S(1)} %collective-permute-done.9.refs_10_), channel_id=1, source_target_pairs={{0,1},{1,0},{2,3},{3,2},{4,5},{5,4},{6,7},{7,6},{8,9},{9,8},{10,11... | collective-permute-start | bytes 104456 | tf_op jit(solution)/shard_map/ppermute | solution.py:493
  17.1 3.1 %collective-permute-start.2 = (bf16[17,8,128]{2,1,0:T(8,128)(2,1)S(1)}, bf16[17,8,128]{2,1,0:T(8,128)(2,1)S(1)}, u32[]{:S(2)}, u32[]{:S(2)}) collective-permute-start(bf16[17,8,128]{2,1,0:T(8,128)(2,1)S(1)} %collective-permute-done.1.refs_2_), channel_id=1, source_target_pairs={{0,1},{1,0},{2,3},{3,2},{4,5},{5,4},{6,7},{7,6},{8,9},{9,8},{10,11... | collective-permute-start | bytes 104456 | tf_op jit(solution)/shard_map/ppermute | solution.py:493
  19.2 3.1 %collective-permute-start.12 = (bf16[17,8,128]{2,1,0:T(8,128)(2,1)S(1)}, bf16[17,8,128]{2,1,0:T(8,128)(2,1)S(1)}, u32[]{:S(2)}, u32[]{:S(2)}) collective-permute-start(bf16[17,8,128]{2,1,0:T(8,128)(2,1)S(1)} %collective-permute-done.11.refs_12_), channel_id=1, source_target_pairs={{0,1},{1,0},{2,3},{3,2},{4,5},{5,4},{6,7},{7,6},{8,9},{9,8},{10,11... | collective-permute-start | bytes 104456 | tf_op jit(solution)/shard_map/ppermute | solution.py:493
  19.6 2.7 %collective-permute-start.4 = (bf16[17,8,128]{2,1,0:T(8,128)(2,1)S(1)}, bf16[17,8,128]{2,1,0:T(8,128)(2,1)S(1)}, u32[]{:S(2)}, u32[]{:S(2)}) collective-permute-start(bf16[17,8,128]{2,1,0:T(8,128)(2,1)S(1)} %collective-permute-done.3.refs_4_), channel_id=1, source_target_pairs={{0,1},{1,0},{2,3},{3,2},{4,5},{5,4},{6,7},{7,6},{8,9},{9,8},{10,11... | collective-permute-start | bytes 104456 | tf_op jit(solution)/shard_map/ppermute | solution.py:493
  19.7 2.6 %collective-permute-start.14 = (bf16[17,8,128]{2,1,0:T(8,128)(2,1)S(1)}, bf16[17,8,128]{2,1,0:T(8,128)(2,1)S(1)}, u32[]{:S(2)}, u32[]{:S(2)}) collective-permute-start(bf16[17,8,128]{2,1,0:T(8,128)(2,1)S(1)} %collective-permute-done.13.refs_14_), channel_id=1, source_target_pairs={{0,1},{1,0},{2,3},{3,2},{4,5},{5,4},{6,7},{7,6},{8,9},{9,8},{10,11... | collective-permute-start | bytes 104456 | tf_op jit(solution)/shard_map/ppermute | solution.py:493
  20.1 2.2 %collective-permute-start.6 = (bf16[17,8,128]{2,1,0:T(8,128)(2,1)S(1)}, bf16[17,8,128]{2,1,0:T(8,128)(2,1)S(1)}, u32[]{:S(2)}, u32[]{:S(2)}) collective-permute-start(bf16[17,8,128]{2,1,0:T(8,128)(2,1)S(1)} %collective-permute-done.5.refs_6_), channel_id=1, source_target_pairs={{0,1},{1,0},{2,3},{3,2},{4,5},{5,4},{6,7},{7,6},{8,9},{9,8},{10,11... | collective-permute-start | bytes 104456 | tf_op jit(solution)/shard_map/ppermute | solution.py:493
  20.2 2.1 %collective-permute-start.8 = (bf16[17,8,128]{2,1,0:T(8,128)(2,1)S(1)}, bf16[17,8,128]{2,1,0:T(8,128)(2,1)S(1)}, u32[]{:S(2)}, u32[]{:S(2)}) collective-permute-start(bf16[17,8,128]{2,1,0:T(8,128)(2,1)S(1)} %collective-permute-done.7.refs_8_), channel_id=1, source_target_pairs={{0,1},{1,0},{2,3},{3,2},{4,5},{5,4},{6,7},{7,6},{8,9},{9,8},{10,11... | collective-permute-start | bytes 104456 | tf_op jit(solution)/shard_map/ppermute | solution.py:493
  20.6 1.0 %copy-start.1 = (bf16[1,32,32,128]{3,2,1,0:T(8,128)(2,1)S(1)}, bf16[1,32,32,128]{3,2,1,0:T(8,128)(2,1)}, u32[]{:S(2)}) copy-start(bf16[1,32,32,128]{3,2,1,0:T(8,128)(2,1)} %param.19) | copy-start | bytes 786436
  21.6 0.8 %copy-start.2 = (bf16[17,8,128]{2,1,0:T(8,128)(2,1)S(1)}, bf16[17,8,128]{2,1,0:T(8,128)(2,1)}, u32[]{:S(2)}) copy-start(bf16[17,8,128]{2,1,0:T(8,128)(2,1)} %get-tuple-element.57.refs_0_) | copy-start | bytes 104452
  23.2 5.6 %collective-permute-start.15 = (bf16[64,8,128]{2,1,0:T(8,128)(2,1)S(1)}, bf16[64,8,128]{2,1,0:T(8,128)(2,1)S(1)}, u32[]{:S(2)}, u32[]{:S(2)}) collective-permute-start(bf16[64,8,128]{2,1,0:T(8,128)(2,1)S(1)} %get-tuple-element.75), channel_id=1, source_target_pairs={{0,2},{1,3},{2,0},{3,1},{4,6},{5,7},{6,4},{7,5},{8,10},{9,11},{10,... | collective-permute-start | bytes 393224 | tf_op jit(solution)/shard_map/ppermute | solution.py:489
  24.7 6.4 %collective-permute-start.16 = (bf16[64,8,128]{2,1,0:T(8,128)(2,1)S(1)}, bf16[64,8,128]{2,1,0:T(8,128)(2,1)S(1)}, u32[]{:S(2)}, u32[]{:S(2)}) collective-permute-start(bf16[64,8,128]{2,1,0:T(8,128)(2,1)S(1)} %get-tuple-element.76), channel_id=1, source_target_pairs={{0,4},{1,5},{2,6},{3,7},{4,0},{5,1},{6,2},{7,3},{8,12},{9,13},{10,... | collective-permute-start | bytes 393224 | tf_op jit(solution)/shard_map/ppermute | solution.py:489
  26.3 6.4 %collective-permute-start.17 = (bf16[64,8,128]{2,1,0:T(8,128)(2,1)S(1)}, bf16[64,8,128]{2,1,0:T(8,128)(2,1)S(1)}, u32[]{:S(2)}, u32[]{:S(2)}) collective-permute-start(bf16[64,8,128]{2,1,0:T(8,128)(2,1)S(1)} %get-tuple-element.77), channel_id=1, source_target_pairs={{0,6},{1,7},{2,4},{3,5},{4,2},{5,3},{6,0},{7,1},{8,14},{9,15},{10,... | collective-permute-start | bytes 393224 | tf_op jit(solution)/shard_map/ppermute | solution.py:489
  36.4 4.3 %collective-permute-start.18 = (bf16[32,8,128]{2,1,0:T(8,128)(2,1)S(1)}, bf16[32,8,128]{2,1,0:T(8,128)(2,1)S(1)}, u32[]{:S(2)}, u32[]{:S(2)}) collective-permute-start(bf16[32,8,128]{2,1,0:T(8,128)(2,1)S(1)} %get-tuple-element.82), channel_id=1, source_target_pairs={{0,2},{1,3},{2,0},{3,1},{4,6},{5,7},{6,4},{7,5},{8,10},{9,11},{10,... | collective-permute-start | bytes 196616 | tf_op jit(solution)/shard_map/ppermute | solution.py:489
  37.9 4.3 %collective-permute-start.19 = (bf16[32,8,128]{2,1,0:T(8,128)(2,1)S(1)}, bf16[32,8,128]{2,1,0:T(8,128)(2,1)S(1)}, u32[]{:S(2)}, u32[]{:S(2)}) collective-permute-start(bf16[32,8,128]{2,1,0:T(8,128)(2,1)S(1)} %get-tuple-element.83), channel_id=1, source_target_pairs={{0,4},{1,5},{2,6},{3,7},{4,0},{5,1},{6,2},{7,3},{8,12},{9,13},{10,... | collective-permute-start | bytes 196616 | tf_op jit(solution)/shard_map/ppermute | solution.py:489
  39.5 5.2 %collective-permute-start.20 = (bf16[32,8,128]{2,1,0:T(8,128)(2,1)S(1)}, bf16[32,8,128]{2,1,0:T(8,128)(2,1)S(1)}, u32[]{:S(2)}, u32[]{:S(2)}) collective-permute-start(bf16[32,8,128]{2,1,0:T(8,128)(2,1)S(1)} %get-tuple-element.84), channel_id=1, source_target_pairs={{0,6},{1,7},{2,4},{3,5},{4,2},{5,3},{6,0},{7,1},{8,14},{9,15},{10,... | collective-permute-start | bytes 196616 | tf_op jit(solution)/shard_map/ppermute | solution.py:489
  45.9 1.4 %collective-permute-start.21 = (bf16[8,8,8,128]{3,2,1,0:T(8,128)(2,1)S(1)}, bf16[8,8,8,128]{3,2,1,0:T(8,128)(2,1)S(1)}, u32[]{:S(2)}, u32[]{:S(2)}) collective-permute-start(bf16[8,8,8,128]{3,2,1,0:T(8,128)(2,1)S(1)} %get-tuple-element.86), channel_id=1, source_target_pairs={{0,1},{1,0},{2,3},{3,2},{4,5},{5,4},{6,7},{7,6},{8,9},{9,8},{10,11... | collective-permute-start | bytes 393224 | tf_op jit(solution)/shard_map/ppermute | solution.py:493
  47.3 6.5 %collective-permute-start.22 = (bf16[8,8,128]{2,1,0:T(8,128)(2,1)S(1)}, bf16[8,8,128]{2,1,0:T(8,128)(2,1)S(1)}, u32[]{:S(2)}, u32[]{:S(2)}) collective-permute-start(bf16[8,8,128]{2,1,0:T(8,128)(2,1)S(1)} %get-tuple-element.88), channel_id=1, source_target_pairs={{0,2},{1,3},{2,0},{3,1},{4,6},{5,7},{6,4},{7,5},{8,10},{9,11},{10,... | collective-permute-start | bytes 49160 | tf_op jit(solution)/shard_map/ppermute | solution.py:489
  47.9 7.6 %collective-permute-start.23 = (bf16[8,8,128]{2,1,0:T(8,128)(2,1)S(1)}, bf16[8,8,128]{2,1,0:T(8,128)(2,1)S(1)}, u32[]{:S(2)}, u32[]{:S(2)}) collective-permute-start(bf16[8,8,128]{2,1,0:T(8,128)(2,1)S(1)} %get-tuple-element.89), channel_id=1, source_target_pairs={{0,4},{1,5},{2,6},{3,7},{4,0},{5,1},{6,2},{7,3},{8,12},{9,13},{10,... | collective-permute-start | bytes 49160 | tf_op jit(solution)/shard_map/ppermute | solution.py:489
  48.6 9.9 %collective-permute-start.24 = (bf16[8,8,128]{2,1,0:T(8,128)(2,1)S(1)}, bf16[8,8,128]{2,1,0:T(8,128)(2,1)S(1)}, u32[]{:S(2)}, u32[]{:S(2)}) collective-permute-start(bf16[8,8,128]{2,1,0:T(8,128)(2,1)S(1)} %get-tuple-element.90), channel_id=1, source_target_pairs={{0,6},{1,7},{2,4},{3,5},{4,2},{5,3},{6,0},{7,1},{8,14},{9,15},{10,... | collective-permute-start | bytes 49160 | tf_op jit(solution)/shard_map/ppermute | solution.py:489
  50.9 7.7 %collective-permute-start.25 = (bf16[8,8,128]{2,1,0:T(8,128)(2,1)S(1)}, bf16[8,8,128]{2,1,0:T(8,128)(2,1)S(1)}, u32[]{:S(2)}, u32[]{:S(2)}) collective-permute-start(bf16[8,8,128]{2,1,0:T(8,128)(2,1)S(1)} %get-tuple-element.91), channel_id=1, source_target_pairs={{0,8},{1,9},{2,10},{3,11},{4,12},{5,13},{6,14},{7,15},{8,0},{9,1},... | collective-permute-start | bytes 49160 | tf_op jit(solution)/shard_map/ppermute | solution.py:489
  51.2 7.3 %collective-permute-start.26 = (bf16[8,8,128]{2,1,0:T(8,128)(2,1)S(1)}, bf16[8,8,128]{2,1,0:T(8,128)(2,1)S(1)}, u32[]{:S(2)}, u32[]{:S(2)}) collective-permute-start(bf16[8,8,128]{2,1,0:T(8,128)(2,1)S(1)} %get-tuple-element.92), channel_id=1, source_target_pairs={{0,10},{1,11},{2,8},{3,9},{4,14},{5,15},{6,12},{7,13},{8,2},{9,3},... | collective-permute-start | bytes 49160 | tf_op jit(solution)/shard_map/ppermute | solution.py:489
  53.8 5.5 %collective-permute-start.27 = (bf16[8,8,128]{2,1,0:T(8,128)(2,1)S(1)}, bf16[8,8,128]{2,1,0:T(8,128)(2,1)S(1)}, u32[]{:S(2)}, u32[]{:S(2)}) collective-permute-start(bf16[8,8,128]{2,1,0:T(8,128)(2,1)S(1)} %get-tuple-element.93), channel_id=1, source_target_pairs={{0,12},{1,13},{2,14},{3,15},{4,8},{5,9},{6,10},{7,11},{8,4},{9,5},... | collective-permute-start | bytes 49160 | tf_op jit(solution)/shard_map/ppermute | solution.py:489
  55.5 6.4 %collective-permute-start.28 = (bf16[8,8,128]{2,1,0:T(8,128)(2,1)S(1)}, bf16[8,8,128]{2,1,0:T(8,128)(2,1)S(1)}, u32[]{:S(2)}, u32[]{:S(2)}) collective-permute-start(bf16[8,8,128]{2,1,0:T(8,128)(2,1)S(1)} %get-tuple-element.94), channel_id=1, source_target_pairs={{0,14},{1,15},{2,12},{3,13},{4,10},{5,11},{6,8},{7,9},{8,6},{9,7},... | collective-permute-start | bytes 49160 | tf_op jit(solution)/shard_map/ppermute | solution.py:489

commit v4 on v2

--- a/solution.py
+++ b/solution.py
@@ -128,7 +128,7 @@
 
 
 def pick_kernel(slots, near, pieces_ref, *refs):
-    out_refs = refs[:near]
+    out_refs = refs[:near][::-1]
     facts_ref, facts, spots, sem = refs[near:]
     count = facts_ref.shape[0]
     tiles = 2 * slots + 1
@@ -255,7 +255,7 @@
 def wave_kernel(near, *refs):
     model_refs = refs[:near]
     u_0, g_0, next_ref = refs[near:near + 3]
-    out_refs = refs[near + 3:2 * near + 3]
+    out_refs = refs[near + 3:2 * near + 3][::-1]
     kap, con, u_1, u_2, u_3, d_0, d_1, d_2, kb_3, kb_2, kb_1 = refs[2 * near + 3:2 * near + 14]
     g_1, g_2, d_3, b_2, b_1, image, result = refs[2 * near + 14:]
     span_x, many = u_0.shape[:2]
@@ -345,7 +345,7 @@
     field = pltpu.VMEM((span_x + 1, many, LANES, depth), jnp.float32)
     plain = pltpu.VMEM((span_x, many, LANES, depth), jnp.float32)
     out = (APX * many, LANES, depth)
-    return pl.pallas_call(
+    terms = pl.pallas_call(
         functools.partial(wave_kernel, near),
         out_shape=(jax.ShapeDtypeStruct(out, jnp.bfloat16),) * near,
         in_specs=[vmem()] * (near + 3),
@@ -355,6 +355,7 @@
         compiler_params=limit(20),
         name="wave",
     )(*models, *started)
+    return terms[::-1]
 
 
 def wave_split_depth(models, before, current):
@@ -459,10 +460,10 @@
     assert count % near == 0 and near & (near - 1) == 0
 
     def swap(values):
-        return [
-            lax.ppermute(value, "shot", [(i, i ^ k) for i in range(count)]) if k else value
-            for k, value in enumerate(values)
-        ]
+        swapped = {0: values[0]}
+        for k in range(near - 1, 0, -1):
+            swapped[k] = lax.ppermute(values[k], "shot", [(i, i ^ k) for i in range(count)])
+        return [swapped[k] for k in range(near)]
 
     sent = pl.pallas_call(
         prepare_kernel,
@@ -501,7 +502,7 @@
         compiler_params=limit(3),
         name="pick",
     )(pieces.reshape(count * (2 * slots + 1), block_y, depth))
-    models = swap(picked)
+    models = swap(picked[::-1])
 
     if split:
         terms = wave_split_depth(models, wave_prev[0], wave_now[0])

time: 59.1 us -> 59.1 us (level)
  no operation moved by 1% of the time
where the time goes in v4:
time: 59.1 us; the launch traced here: 58.8 us
  starting transfers between devices  19.7 us (33%)
  waiting for transfers between devices  17.7 us (30%)
  blocking collectives  11 us (19%)
  Pallas kernels  8.95 us (15%)
  between operations  1.4 us (2%)
    ppermute x14, starting transfers between devices, swap(): lax.ppermute(values[k], 'shot', [(i, i ^ k) for i in range(count)])  12.2 us
    all_to_all x1, blocking collectives, per_device(): sums = lax.all_to_all(sums, 'shot', 0, 0, tiled=True)  11 us
    all_to_all x1, waiting for transfers between devices, per_device(): pieces = lax.all_to_all(sent, 'shot', 0, 0, tiled=True)  9.85 us
    ppermute x14, waiting for transfers between devices, swap(): lax.ppermute(values[k], 'shot', [(i, i ^ k) for i in range(count)])  7.86 us
    all_to_all x1, starting transfers between devices, per_device(): pieces = lax.all_to_all(sent, 'shot', 0, 0, tiled=True)  7.5 us
    pallas_call x1, Pallas kernels, wave(): pl.pallas_call(functools.partial(wave_kernel, near), out_shape=(jax.Shape...  3.64 us
    pallas_call x1, Pallas kernels, per_device(): pl.pallas_call(prepare_kernel, out_shape=jax.ShapeDtypeStruct((count, 2 *...  1.83 us
    pallas_call x1, Pallas kernels, per_device(): pl.pallas_call(functools.partial(stack_kernel, slots, near), out_shape=ja...  1.2 us
  transfers between devices with their start and end apart: 15, of which 8 were waited for; matrix products, arithmetic and copies ran while one was open for 0% of the time, Pallas kernels for 1%

profile of v4, /device:TPU:0, one launch (start us, length us, event | category | flops | bytes accessed | tf_op | source)
XLA Modules:
  0.0 58.8 jit_solution(16436211737008277698)
XLA Ops:
  1.3 1.8 %prepare.1 = bf16[16,9,8,128]{3,2,1,0:T(8,128)(2,1)} custom-call(s32[1]{0:T(128)S(6)} %copy.11.row_ref, s32[1]{0:T(128)S(6)} %copy.12.col_ref, s32[4]{0:T(128)} %ids_hbm.1, s32[4,8,8]{2,1,0:T(8,128)} %floor_hbm.1, bf16[4,8,8,128]{3,2,1,0:T(8,128)(2,1)} %p_hbm.1, bf16[4,8,8,128]{3,2,1,0:T(8,128)(2,1)} %s_hbm.1, bf16[4,8,8,128]{3,2,1,0:T(8,128)(2,1)} %rho_hbm.1, ...), custom_call_target="tpu_custom_call" | custom-call | tf_op jit(solution)/shard_map/prepare/pallas_call | solution.py:468
  3.1 0.0 copy-start
  3.2 0.0 copy-start.1
  3.2 7.5 %all-to-all-start = ((bf16[16,9,8,128]{3,2,1,0:T(8,128)(2,1)}), bf16[16,9,8,128]{3,2,1,0:T(8,128)(2,1)S(1)}, u32[]{:S(2)}, u32[]{:S(2)}) async-start(bf16[16,9,8,128]{3,2,1,0:T(8,128)(2,1)} %prepare.1), calls=%async_computation | async-start | bytes 589824 | tf_op jit(solution)/shard_map/all_to_all | solution.py:484
  10.7 0.0 copy-done
  10.7 0.0 copy-done.1
  10.7 0.7 %start.1 = (f32[32,4,8,128]{3,2,1,0:T(8,128)S(1)}, f32[32,4,8,128]{3,2,1,0:T(8,128)S(1)}, f32[32,4,8,128]{3,2,1,0:T(8,128)S(1)}) custom-call(bf16[32,32,128]{2,1,0:T(8,128)(2,1)S(1)} %bitcast.4, bf16[32,32,128]{2,1,0:T(8,128)(2,1)S(1)} %bitcast.5), custom_call_target="tpu_custom_call" | custom-call | flops 2621440 | bytes 2097152 | tf_op jit(solution)/shard_map/start/pallas_call | solution.py:241
  11.4 9.9 %all-to-all-done = bf16[16,9,8,128]{3,2,1,0:T(8,128)(2,1)S(1)} async-done(((bf16[16,9,8,128]{3,2,1,0:T(8,128)(2,1)}), bf16[16,9,8,128]{3,2,1,0:T(8,128)(2,1)S(1)}, u32[]{:S(2)}, u32[]{:S(2)}) %all-to-all-start) | async-done | bytes 294944 | tf_op jit(solution)/shard_map/all_to_all | solution.py:484
  21.2 0.9 %pick.1 = (bf16[32,8,128]{2,1,0:T(8,128)(2,1)S(1)}, bf16[32,8,128]{2,1,0:T(8,128)(2,1)S(1)}, bf16[32,8,128]{2,1,0:T(8,128)(2,1)S(1)}, bf16[32,8,128]{2,1,0:T(8,1...) custom-call(bf16[144,8,128]{2,1,0:T(8,128)(2,1)S(1)} %bitcast.3), custom_call_target="tpu_custom_call" | custom-call | tf_op jit(solution)/shard_map/pick/pallas_call | solution.py:489
  22.2 0.1 collective-permute-start
  22.2 0.7 %collective-permute-start.1 = (bf16[32,8,128]{2,1,0:T(8,128)(2,1)S(1)}, bf16[32,8,128]{2,1,0:T(8,128)(2,1)S(1)}, u32[]{:S(2)}, u32[]{:S(2)}) collective-permute-start(bf16[32,8,128]{2,1,0:T(8,128)(2,1)S(1)} %get-tuple-element.36), channel_id=1, source_target_pairs={{0,2},{1,3},{2,0},{3,1},{4,6},{5,7},{6,4},{7,5},{8,10},{9,11},{10,... | collective-permute-start | bytes 196616 | tf_op jit(solution)/shard_map/ppermute | solution.py:465
  22.9 1.2 %collective-permute-start.2 = (bf16[32,8,128]{2,1,0:T(8,128)(2,1)S(1)}, bf16[32,8,128]{2,1,0:T(8,128)(2,1)S(1)}, u32[]{:S(2)}, u32[]{:S(2)}) collective-permute-start(bf16[32,8,128]{2,1,0:T(8,128)(2,1)S(1)} %get-tuple-element.37), channel_id=1, source_target_pairs={{0,3},{1,2},{2,1},{3,0},{4,7},{5,6},{6,5},{7,4},{8,11},{9,10},{10,... | collective-permute-start | bytes 196616 | tf_op jit(solution)/shard_map/ppermute | solution.py:465
  24.1 0.4 collective-permute-start.3
  24.5 1.3 %collective-permute-start.4 = (bf16[32,8,128]{2,1,0:T(8,128)(2,1)S(1)}, bf16[32,8,128]{2,1,0:T(8,128)(2,1)S(1)}, u32[]{:S(2)}, u32[]{:S(2)}) collective-permute-start(bf16[32,8,128]{2,1,0:T(8,128)(2,1)S(1)} %get-tuple-element.39), channel_id=1, source_target_pairs={{0,5},{1,4},{2,7},{3,6},{4,1},{5,0},{6,3},{7,2},{8,13},{9,12},{10,... | collective-permute-start | bytes 196616 | tf_op jit(solution)/shard_map/ppermute | solution.py:465
  25.8 0.0 collective-permute-done.refs_1_
  25.8 1.0 %collective-permute-start.5 = (bf16[32,8,128]{2,1,0:T(8,128)(2,1)S(1)}, bf16[32,8,128]{2,1,0:T(8,128)(2,1)S(1)}, u32[]{:S(2)}, u32[]{:S(2)}) collective-permute-start(bf16[32,8,128]{2,1,0:T(8,128)(2,1)S(1)} %get-tuple-element.40), channel_id=1, source_target_pairs={{0,6},{1,7},{2,4},{3,5},{4,2},{5,3},{6,0},{7,1},{8,14},{9,15},{10,... | collective-permute-start | bytes 196616 | tf_op jit(solution)/shard_map/ppermute | solution.py:465
  26.8 0.4 collective-permute-done.1.refs_2_
  27.2 1.3 %collective-permute-start.6 = (bf16[32,8,128]{2,1,0:T(8,128)(2,1)S(1)}, bf16[32,8,128]{2,1,0:T(8,128)(2,1)S(1)}, u32[]{:S(2)}, u32[]{:S(2)}) collective-permute-start(bf16[32,8,128]{2,1,0:T(8,128)(2,1)S(1)} %get-tuple-element.41), channel_id=1, source_target_pairs={{0,7},{1,6},{2,5},{3,4},{4,3},{5,2},{6,1},{7,0},{8,15},{9,14},{10,... | collective-permute-start | bytes 196616 | tf_op jit(solution)/shard_map/ppermute | solution.py:465
  28.5 0.0 collective-permute-done.2.refs_3_
  28.5 0.5 collective-permute-done.3.refs_4_
  29.0 0.3 collective-permute-done.4.refs_5_
  29.3 2.2 %collective-permute-done.5.refs_6_ = bf16[32,8,128]{2,1,0:T(8,128)(2,1)S(1)} collective-permute-done((bf16[32,8,128]{2,1,0:T(8,128)(2,1)S(1)}, bf16[32,8,128]{2,1,0:T(8,128)(2,1)S(1)}, u32[]{:S(2)}, u32[]{:S(2)}) %collective-permute-start.5) | collective-permute-done | bytes 65568 | tf_op jit(solution)/shard_map/ppermute | solution.py:465
  31.5 1.0 %collective-permute-done.6.refs_7_ = bf16[32,8,128]{2,1,0:T(8,128)(2,1)S(1)} collective-permute-done((bf16[32,8,128]{2,1,0:T(8,128)(2,1)S(1)}, bf16[32,8,128]{2,1,0:T(8,128)(2,1)S(1)}, u32[]{:S(2)}, u32[]{:S(2)}) %collective-permute-start.6) | collective-permute-done | bytes 65568 | tf_op jit(solution)/shard_map/ppermute | solution.py:465
  32.5 3.6 %wave.1 = (bf16[16,8,128]{2,1,0:T(8,128)(2,1)S(1)}, bf16[16,8,128]{2,1,0:T(8,128)(2,1)S(1)}, bf16[16,8,128]{2,1,0:T(8,128)(2,1)S(1)}, bf16[16,8,128]{2,1,0:T(8,1...) custom-call(bf16[32,8,128]{2,1,0:T(8,128)(2,1)S(1)} %get-tuple-eleme, ...), custom_call_target="tpu_custom_call" | custom-call | tf_op jit(solution)/shard_map/wave/pallas_call | solution.py:348
  36.1 0.2 collective-permute-start.7
  36.3 1.4 %collective-permute-start.8 = (bf16[16,8,128]{2,1,0:T(8,128)(2,1)S(1)}, bf16[16,8,128]{2,1,0:T(8,128)(2,1)S(1)}, u32[]{:S(2)}, u32[]{:S(2)}) collective-permute-start(bf16[16,8,128]{2,1,0:T(8,128)(2,1)S(1)} %get-tuple-element.47), channel_id=1, source_target_pairs={{0,2},{1,3},{2,0},{3,1},{4,6},{5,7},{6,4},{7,5},{8,10},{9,11},{10,... | collective-permute-start | bytes 98312 | tf_op jit(solution)/shard_map/ppermute | solution.py:465
  37.7 0.4 collective-permute-start.9
  38.0 0.9 %collective-permute-start.10 = (bf16[16,8,128]{2,1,0:T(8,128)(2,1)S(1)}, bf16[16,8,128]{2,1,0:T(8,128)(2,1)S(1)}, u32[]{:S(2)}, u32[]{:S(2)}) collective-permute-start(bf16[16,8,128]{2,1,0:T(8,128)(2,1)S(1)} %get-tuple-element.49), channel_id=1, source_target_pairs={{0,4},{1,5},{2,6},{3,7},{4,0},{5,1},{6,2},{7,3},{8,12},{9,13},{10,... | collective-permute-start | bytes 98312 | tf_op jit(solution)/shard_map/ppermute | solution.py:465
  38.9 0.9 %collective-permute-start.11 = (bf16[16,8,128]{2,1,0:T(8,128)(2,1)S(1)}, bf16[16,8,128]{2,1,0:T(8,128)(2,1)S(1)}, u32[]{:S(2)}, u32[]{:S(2)}) collective-permute-start(bf16[16,8,128]{2,1,0:T(8,128)(2,1)S(1)} %get-tuple-element.50), channel_id=1, source_target_pairs={{0,5},{1,4},{2,7},{3,6},{4,1},{5,0},{6,3},{7,2},{8,13},{9,12},{10,... | collective-permute-start | bytes 98312 | tf_op jit(solution)/shard_map/ppermute | solution.py:465
  39.8 0.0 collective-permute-done.7.refs_1_
  39.8 1.7 %collective-permute-start.12 = (bf16[16,8,128]{2,1,0:T(8,128)(2,1)S(1)}, bf16[16,8,128]{2,1,0:T(8,128)(2,1)S(1)}, u32[]{:S(2)}, u32[]{:S(2)}) collective-permute-start(bf16[16,8,128]{2,1,0:T(8,128)(2,1)S(1)} %get-tuple-element.51), channel_id=1, source_target_pairs={{0,6},{1,7},{2,4},{3,5},{4,2},{5,3},{6,0},{7,1},{8,14},{9,15},{10,... | collective-permute-start | bytes 98312 | tf_op jit(solution)/shard_map/ppermute | solution.py:465
  41.6 0.0 collective-permute-done.8.refs_2_
  41.6 0.9 %collective-permute-start.13 = (bf16[16,8,128]{2,1,0:T(8,128)(2,1)S(1)}, bf16[16,8,128]{2,1,0:T(8,128)(2,1)S(1)}, u32[]{:S(2)}, u32[]{:S(2)}) collective-permute-start(bf16[16,8,128]{2,1,0:T(8,128)(2,1)S(1)} %get-tuple-element.52), channel_id=1, source_target_pairs={{0,7},{1,6},{2,5},{3,4},{4,3},{5,2},{6,1},{7,0},{8,15},{9,14},{10,... | collective-permute-start | bytes 98312 | tf_op jit(solution)/shard_map/ppermute | solution.py:465
  42.4 0.0 collective-permute-done.9.refs_3_
  42.4 0.0 collective-permute-done.10.refs_4_
  42.4 0.0 collective-permute-done.11.refs_5_
  42.4 2.2 %collective-permute-done.12.refs_6_ = bf16[16,8,128]{2,1,0:T(8,128)(2,1)S(1)} collective-permute-done((bf16[16,8,128]{2,1,0:T(8,128)(2,1)S(1)}, bf16[16,8,128]{2,1,0:T(8,128)(2,1)S(1)}, u32[]{:S(2)}, u32[]{:S(2)}) %collective-permute-start.12) | collective-permute-done | bytes 32800 | tf_op jit(solution)/shard_map/ppermute | solution.py:465
  44.6 1.3 %collective-permute-done.13.refs_7_ = bf16[16,8,128]{2,1,0:T(8,128)(2,1)S(1)} collective-permute-done((bf16[16,8,128]{2,1,0:T(8,128)(2,1)S(1)}, bf16[16,8,128]{2,1,0:T(8,128)(2,1)S(1)}, u32[]{:S(2)}, u32[]{:S(2)}) %collective-permute-start.13) | collective-permute-done | bytes 32800 | tf_op jit(solution)/shard_map/ppermute | solution.py:465
  45.9 1.2 %stack.1 = bf16[16,4,8,128]{3,2,1,0:T(8,128)(2,1)S(1)} custom-call(s32[16,128]{1,0:T(8,128)S(1)} %get-tuple-element.33.facts_ref, bf16[16,8,128]{2,1,0:T(8,128)(2,1)S(1)} %get-tuple-element.45.refs_0_, bf16[16,8,128]{2,1,0:T(8,128)(2,1)S(1)} %collective-permute-done.7.refs_1_, bf16[16,8,128]{2,1,0:T(8,128)(2,1)S(1)} %collective-permute-done.8.refs_2_, ...), custom_call_target="tpu_custom_call" | custom-call | tf_op jit(solution)/shard_map/stack/pallas_call | solution.py:515
  47.1 11.0 %all_to_all.10.sums_ref = bf16[16,4,8,128]{3,2,1,0:T(8,128)(2,1)S(1)} all-to-all(bf16[16,4,8,128]{3,2,1,0:T(8,128)(2,1)S(1)} %stack.1), channel_id=1, replica_groups=mesh['grp'=2,'shot'=16,'depth'=1] {'shot'}, dimensions={0} | all-to-all | bytes 262144 | tf_op jit(solution)/shard_map/all_to_all | solution.py:529
  58.2 0.7 %finish.1 = f32[4,8,8,128]{3,2,1,0:T(8,128)} custom-call(bf16[16,4,8,128]{3,2,1,0:T(8,128)(2,1)S(1)} %all_to_all.10.sums_ref), custom_call_target="tpu_custom_call" | custom-call | tf_op jit(solution)/shard_map/finish/pallas_call | solution.py:530
Async XLA Ops:
  3.1 7.5 %copy-start = (bf16[1,32,32,128]{3,2,1,0:T(8,128)(2,1)S(1)}, bf16[1,32,32,128]{3,2,1,0:T(8,128)(2,1)}, u32[]{:S(2)}) copy-start(bf16[1,32,32,128]{3,2,1,0:T(8,128)(2,1)} %param.18) | copy-start | bytes 786436
  3.2 7.5 %copy-start.1 = (bf16[1,32,32,128]{3,2,1,0:T(8,128)(2,1)S(1)}, bf16[1,32,32,128]{3,2,1,0:T(8,128)(2,1)}, u32[]{:S(2)}) copy-start(bf16[1,32,32,128]{3,2,1,0:T(8,128)(2,1)} %param.19) | copy-start | bytes 786436
  3.2 18.1 %all-to-all-start = ((bf16[16,9,8,128]{3,2,1,0:T(8,128)(2,1)}), bf16[16,9,8,128]{3,2,1,0:T(8,128)(2,1)S(1)}, u32[]{:S(2)}, u32[]{:S(2)}) async-start(bf16[16,9,8,128]{3,2,1,0:T(8,128)(2,1)} %prepare.1), calls=%async_computation | async-start | bytes 589824 | tf_op jit(solution)/shard_map/all_to_all | solution.py:484
  22.2 3.6 %collective-permute-start = (bf16[32,8,128]{2,1,0:T(8,128)(2,1)S(1)}, bf16[32,8,128]{2,1,0:T(8,128)(2,1)S(1)}, u32[]{:S(2)}, u32[]{:S(2)}) collective-permute-start(bf16[32,8,128]{2,1,0:T(8,128)(2,1)S(1)} %get-tuple-element.35), channel_id=1, source_target_pairs={{0,1},{1,0},{2,3},{3,2},{4,5},{5,4},{6,7},{7,6},{8,9},{9,8},{10,11... | collective-permute-start | bytes 196616 | tf_op jit(solution)/shard_map/ppermute | solution.py:465
  22.2 5.0 %collective-permute-start.1 = (bf16[32,8,128]{2,1,0:T(8,128)(2,1)S(1)}, bf16[32,8,128]{2,1,0:T(8,128)(2,1)S(1)}, u32[]{:S(2)}, u32[]{:S(2)}) collective-permute-start(bf16[32,8,128]{2,1,0:T(8,128)(2,1)S(1)} %get-tuple-element.36), channel_id=1, source_target_pairs={{0,2},{1,3},{2,0},{3,1},{4,6},{5,7},{6,4},{7,5},{8,10},{9,11},{10,... | collective-permute-start | bytes 196616 | tf_op jit(solution)/shard_map/ppermute | solution.py:465
  22.9 5.6 %collective-permute-start.2 = (bf16[32,8,128]{2,1,0:T(8,128)(2,1)S(1)}, bf16[32,8,128]{2,1,0:T(8,128)(2,1)S(1)}, u32[]{:S(2)}, u32[]{:S(2)}) collective-permute-start(bf16[32,8,128]{2,1,0:T(8,128)(2,1)S(1)} %get-tuple-element.37), channel_id=1, source_target_pairs={{0,3},{1,2},{2,1},{3,0},{4,7},{5,6},{6,5},{7,4},{8,11},{9,10},{10,... | collective-permute-start | bytes 196616 | tf_op jit(solution)/shard_map/ppermute | solution.py:465
  24.1 4.9 %collective-permute-start.3 = (bf16[32,8,128]{2,1,0:T(8,128)(2,1)S(1)}, bf16[32,8,128]{2,1,0:T(8,128)(2,1)S(1)}, u32[]{:S(2)}, u32[]{:S(2)}) collective-permute-start(bf16[32,8,128]{2,1,0:T(8,128)(2,1)S(1)} %get-tuple-element.38), channel_id=1, source_target_pairs={{0,4},{1,5},{2,6},{3,7},{4,0},{5,1},{6,2},{7,3},{8,12},{9,13},{10,... | collective-permute-start | bytes 196616 | tf_op jit(solution)/shard_map/ppermute | solution.py:465
  24.5 4.8 %collective-permute-start.4 = (bf16[32,8,128]{2,1,0:T(8,128)(2,1)S(1)}, bf16[32,8,128]{2,1,0:T(8,128)(2,1)S(1)}, u32[]{:S(2)}, u32[]{:S(2)}) collective-permute-start(bf16[32,8,128]{2,1,0:T(8,128)(2,1)S(1)} %get-tuple-element.39), channel_id=1, source_target_pairs={{0,5},{1,4},{2,7},{3,6},{4,1},{5,0},{6,3},{7,2},{8,13},{9,12},{10,... | collective-permute-start | bytes 196616 | tf_op jit(solution)/shard_map/ppermute | solution.py:465
  25.8 5.7 %collective-permute-start.5 = (bf16[32,8,128]{2,1,0:T(8,128)(2,1)S(1)}, bf16[32,8,128]{2,1,0:T(8,128)(2,1)S(1)}, u32[]{:S(2)}, u32[]{:S(2)}) collective-permute-start(bf16[32,8,128]{2,1,0:T(8,128)(2,1)S(1)} %get-tuple-element.40), channel_id=1, source_target_pairs={{0,6},{1,7},{2,4},{3,5},{4,2},{5,3},{6,0},{7,1},{8,14},{9,15},{10,... | collective-permute-start | bytes 196616 | tf_op jit(solution)/shard_map/ppermute | solution.py:465
  27.2 5.3 %collective-permute-start.6 = (bf16[32,8,128]{2,1,0:T(8,128)(2,1)S(1)}, bf16[32,8,128]{2,1,0:T(8,128)(2,1)S(1)}, u32[]{:S(2)}, u32[]{:S(2)}) collective-permute-start(bf16[32,8,128]{2,1,0:T(8,128)(2,1)S(1)} %get-tuple-element.41), channel_id=1, source_target_pairs={{0,7},{1,6},{2,5},{3,4},{4,3},{5,2},{6,1},{7,0},{8,15},{9,14},{10,... | collective-permute-start | bytes 196616 | tf_op jit(solution)/shard_map/ppermute | solution.py:465
  36.1 3.7 %collective-permute-start.7 = (bf16[16,8,128]{2,1,0:T(8,128)(2,1)S(1)}, bf16[16,8,128]{2,1,0:T(8,128)(2,1)S(1)}, u32[]{:S(2)}, u32[]{:S(2)}) collective-permute-start(bf16[16,8,128]{2,1,0:T(8,128)(2,1)S(1)} %get-tuple-element.46), channel_id=1, source_target_pairs={{0,1},{1,0},{2,3},{3,2},{4,5},{5,4},{6,7},{7,6},{8,9},{9,8},{10,11... | collective-permute-start | bytes 98312 | tf_op jit(solution)/shard_map/ppermute | solution.py:465
  36.3 5.3 %collective-permute-start.8 = (bf16[16,8,128]{2,1,0:T(8,128)(2,1)S(1)}, bf16[16,8,128]{2,1,0:T(8,128)(2,1)S(1)}, u32[]{:S(2)}, u32[]{:S(2)}) collective-permute-start(bf16[16,8,128]{2,1,0:T(8,128)(2,1)S(1)} %get-tuple-element.47), channel_id=1, source_target_pairs={{0,2},{1,3},{2,0},{3,1},{4,6},{5,7},{6,4},{7,5},{8,10},{9,11},{10,... | collective-permute-start | bytes 98312 | tf_op jit(solution)/shard_map/ppermute | solution.py:465
  37.7 4.8 %collective-permute-start.9 = (bf16[16,8,128]{2,1,0:T(8,128)(2,1)S(1)}, bf16[16,8,128]{2,1,0:T(8,128)(2,1)S(1)}, u32[]{:S(2)}, u32[]{:S(2)}) collective-permute-start(bf16[16,8,128]{2,1,0:T(8,128)(2,1)S(1)} %get-tuple-element.48), channel_id=1, source_target_pairs={{0,3},{1,2},{2,1},{3,0},{4,7},{5,6},{6,5},{7,4},{8,11},{9,10},{10,... | collective-permute-start | bytes 98312 | tf_op jit(solution)/shard_map/ppermute | solution.py:465
  38.0 4.4 %collective-permute-start.10 = (bf16[16,8,128]{2,1,0:T(8,128)(2,1)S(1)}, bf16[16,8,128]{2,1,0:T(8,128)(2,1)S(1)}, u32[]{:S(2)}, u32[]{:S(2)}) collective-permute-start(bf16[16,8,128]{2,1,0:T(8,128)(2,1)S(1)} %get-tuple-element.49), channel_id=1, source_target_pairs={{0,4},{1,5},{2,6},{3,7},{4,0},{5,1},{6,2},{7,3},{8,12},{9,13},{10,... | collective-permute-start | bytes 98312 | tf_op jit(solution)/shard_map/ppermute | solution.py:465
  38.9 3.5 %collective-permute-start.11 = (bf16[16,8,128]{2,1,0:T(8,128)(2,1)S(1)}, bf16[16,8,128]{2,1,0:T(8,128)(2,1)S(1)}, u32[]{:S(2)}, u32[]{:S(2)}) collective-permute-start(bf16[16,8,128]{2,1,0:T(8,128)(2,1)S(1)} %get-tuple-element.50), channel_id=1, source_target_pairs={{0,5},{1,4},{2,7},{3,6},{4,1},{5,0},{6,3},{7,2},{8,13},{9,12},{10,... | collective-permute-start | bytes 98312 | tf_op jit(solution)/shard_map/ppermute | solution.py:465
  39.8 4.8 %collective-permute-start.12 = (bf16[16,8,128]{2,1,0:T(8,128)(2,1)S(1)}, bf16[16,8,128]{2,1,0:T(8,128)(2,1)S(1)}, u32[]{:S(2)}, u32[]{:S(2)}) collective-permute-start(bf16[16,8,128]{2,1,0:T(8,128)(2,1)S(1)} %get-tuple-element.51), channel_id=1, source_target_pairs={{0,6},{1,7},{2,4},{3,5},{4,2},{5,3},{6,0},{7,1},{8,14},{9,15},{10,... | collective-permute-start | bytes 98312 | tf_op jit(solution)/shard_map/ppermute | solution.py:465
  41.6 4.3 %collective-permute-start.13 = (bf16[16,8,128]{2,1,0:T(8,128)(2,1)S(1)}, bf16[16,8,128]{2,1,0:T(8,128)(2,1)S(1)}, u32[]{:S(2)}, u32[]{:S(2)}) collective-permute-start(bf16[16,8,128]{2,1,0:T(8,128)(2,1)S(1)} %get-tuple-element.52), channel_id=1, source_target_pairs={{0,7},{1,6},{2,5},{3,4},{4,3},{5,2},{6,1},{7,0},{8,15},{9,14},{10,... | collective-permute-start | bytes 98312 | tf_op jit(solution)/shard_map/ppermute | solution.py:465

commit v5 on v4

--- a/solution.py
+++ b/solution.py
@@ -253,7 +253,7 @@
 
 
 def wave_kernel(near, *refs):
-    model_refs = refs[:near]
+    model_refs = refs[:near][::-1]
     u_0, g_0, next_ref = refs[near:near + 3]
     out_refs = refs[near + 3:2 * near + 3][::-1]
     kap, con, u_1, u_2, u_3, d_0, d_1, d_2, kb_3, kb_2, kb_1 = refs[2 * near + 3:2 * near + 14]
@@ -354,7 +354,7 @@
         + [pltpu.VMEM((near,) + out, jnp.bfloat16)],
         compiler_params=limit(20),
         name="wave",
-    )(*models, *started)
+    )(*models[::-1], *started)
     return terms[::-1]
 
 
@@ -380,7 +380,7 @@
 
 
 def stack_kernel(slots, near, facts_ref, *refs):
-    terms_refs = refs[:near]
+    terms_refs = refs[:near][::-1]
     out_ref, facts, total, lined, sem = refs[near:]
     tiles = terms_refs[0].shape[0]
     wide = tiles // APX
@@ -525,7 +525,7 @@
         ],
         compiler_params=limit(3),
         name="stack",
-    )(facts, *terms)
+    )(facts, *terms[::-1])
     sums = lax.all_to_all(sums, "shot", 0, 0, tiled=True)
     return pl.pallas_call(
         finish_kernel,

time: 59.1 us -> 57.9 us (0.980)
  transfers between devices with their start and end apart: 15 -> 15, of which waited for: 8 -> 9; matrix products, arithmetic and copies ran while one was open for 0% -> 0% of each run, Pallas kernels for 1% -> 1%
where the time goes in v5:
time: 57.9 us; the launch traced here: 57.6 us
  starting transfers between devices  19.2 us (33%)
  waiting for transfers between devices  17.2 us (30%)
  blocking collectives  10.8 us (19%)
  Pallas kernels  8.95 us (15%)
  between operations  1.39 us (2%)
    ppermute x14, starting transfers between devices, swap(): lax.ppermute(values[k], 'shot', [(i, i ^ k) for i in range(count)])  11.7 us
    all_to_all x1, blocking collectives, per_device(): sums = lax.all_to_all(sums, 'shot', 0, 0, tiled=True)  10.8 us
    all_to_all x1, waiting for transfers between devices, per_device(): pieces = lax.all_to_all(sent, 'shot', 0, 0, tiled=True)  9.85 us
    all_to_all x1, starting transfers between devices, per_device(): pieces = lax.all_to_all(sent, 'shot', 0, 0, tiled=True)  7.5 us
    ppermute x14, waiting for transfers between devices, swap(): lax.ppermute(values[k], 'shot', [(i, i ^ k) for i in range(count)])  7.38 us
    pallas_call x1, Pallas kernels, wave(): pl.pallas_call(functools.partial(wave_kernel, near), out_shape=(jax.Shape...  3.64 us
    pallas_call x1, Pallas kernels, per_device(): pl.pallas_call(prepare_kernel, out_shape=jax.ShapeDtypeStruct((count, 2 *...  1.83 us
    pallas_call x1, Pallas kernels, per_device(): pl.pallas_call(functools.partial(stack_kernel, slots, near), out_shape=ja...  1.2 us
  transfers between devices with their start and end apart: 15, of which 9 were waited for; matrix products, arithmetic and copies ran while one was open for 0% of the time, Pallas kernels for 1%

profile of v5, /device:TPU:0, one launch (start us, length us, event | category | flops | bytes accessed | tf_op | source)
XLA Modules:
  0.0 57.6 jit_solution(10447588081702829242)
XLA Ops:
  1.3 1.8 %prepare.1 = bf16[16,9,8,128]{3,2,1,0:T(8,128)(2,1)} custom-call(s32[1]{0:T(128)S(6)} %copy.11.row_ref, s32[1]{0:T(128)S(6)} %copy.12.col_ref, s32[4]{0:T(128)} %ids_hbm.1, s32[4,8,8]{2,1,0:T(8,128)} %floor_hbm.1, bf16[4,8,8,128]{3,2,1,0:T(8,128)(2,1)} %p_hbm.1, bf16[4,8,8,128]{3,2,1,0:T(8,128)(2,1)} %s_hbm.1, bf16[4,8,8,128]{3,2,1,0:T(8,128)(2,1)} %rho_hbm.1, ...), custom_call_target="tpu_custom_call" | custom-call | tf_op jit(solution)/shard_map/prepare/pallas_call | solution.py:468
  3.1 0.0 copy-start
  3.2 0.0 copy-start.1
  3.2 7.5 %all-to-all-start = ((bf16[16,9,8,128]{3,2,1,0:T(8,128)(2,1)}), bf16[16,9,8,128]{3,2,1,0:T(8,128)(2,1)S(1)}, u32[]{:S(2)}, u32[]{:S(2)}) async-start(bf16[16,9,8,128]{3,2,1,0:T(8,128)(2,1)} %prepare.1), calls=%async_computation | async-start | bytes 589824 | tf_op jit(solution)/shard_map/all_to_all | solution.py:484
  10.7 0.0 copy-done
  10.7 0.0 copy-done.1
  10.7 0.7 %start.1 = (f32[32,4,8,128]{3,2,1,0:T(8,128)S(1)}, f32[32,4,8,128]{3,2,1,0:T(8,128)S(1)}, f32[32,4,8,128]{3,2,1,0:T(8,128)S(1)}) custom-call(bf16[32,32,128]{2,1,0:T(8,128)(2,1)S(1)} %bitcast.4, bf16[32,32,128]{2,1,0:T(8,128)(2,1)S(1)} %bitcast.5), custom_call_target="tpu_custom_call" | custom-call | flops 2621440 | bytes 2097152 | tf_op jit(solution)/shard_map/start/pallas_call | solution.py:241
  11.4 9.9 %all-to-all-done = bf16[16,9,8,128]{3,2,1,0:T(8,128)(2,1)S(1)} async-done(((bf16[16,9,8,128]{3,2,1,0:T(8,128)(2,1)}), bf16[16,9,8,128]{3,2,1,0:T(8,128)(2,1)S(1)}, u32[]{:S(2)}, u32[]{:S(2)}) %all-to-all-start) | async-done | bytes 294944 | tf_op jit(solution)/shard_map/all_to_all | solution.py:484
  21.2 0.9 %pick.1 = (bf16[32,8,128]{2,1,0:T(8,128)(2,1)S(1)}, bf16[32,8,128]{2,1,0:T(8,128)(2,1)S(1)}, bf16[32,8,128]{2,1,0:T(8,128)(2,1)S(1)}, bf16[32,8,128]{2,1,0:T(8,1...) custom-call(bf16[144,8,128]{2,1,0:T(8,128)(2,1)S(1)} %bitcast.3), custom_call_target="tpu_custom_call" | custom-call | tf_op jit(solution)/shard_map/pick/pallas_call | solution.py:489
  22.2 0.7 %collective-permute-start = (bf16[32,8,128]{2,1,0:T(8,128)(2,1)S(1)}, bf16[32,8,128]{2,1,0:T(8,128)(2,1)S(1)}, u32[]{:S(2)}, u32[]{:S(2)}) collective-permute-start(bf16[32,8,128]{2,1,0:T(8,128)(2,1)S(1)} %get-tuple-element.34), channel_id=1, source_target_pairs={{0,7},{1,6},{2,5},{3,4},{4,3},{5,2},{6,1},{7,0},{8,15},{9,14},{10,... | collective-permute-start | bytes 196616 | tf_op jit(solution)/shard_map/ppermute | solution.py:465
  22.9 1.7 %collective-permute-start.1 = (bf16[32,8,128]{2,1,0:T(8,128)(2,1)S(1)}, bf16[32,8,128]{2,1,0:T(8,128)(2,1)S(1)}, u32[]{:S(2)}, u32[]{:S(2)}) collective-permute-start(bf16[32,8,128]{2,1,0:T(8,128)(2,1)S(1)} %get-tuple-element.35), channel_id=1, source_target_pairs={{0,6},{1,7},{2,4},{3,5},{4,2},{5,3},{6,0},{7,1},{8,14},{9,15},{10,... | collective-permute-start | bytes 196616 | tf_op jit(solution)/shard_map/ppermute | solution.py:465
  24.6 0.1 collective-permute-start.2
  24.8 1.9 %collective-permute-start.3 = (bf16[32,8,128]{2,1,0:T(8,128)(2,1)S(1)}, bf16[32,8,128]{2,1,0:T(8,128)(2,1)S(1)}, u32[]{:S(2)}, u32[]{:S(2)}) collective-permute-start(bf16[32,8,128]{2,1,0:T(8,128)(2,1)S(1)} %get-tuple-element.37), channel_id=1, source_target_pairs={{0,4},{1,5},{2,6},{3,7},{4,0},{5,1},{6,2},{7,3},{8,12},{9,13},{10,... | collective-permute-start | bytes 196616 | tf_op jit(solution)/shard_map/ppermute | solution.py:465
  26.6 0.3 collective-permute-start.4
  26.9 0.6 collective-permute-done.refs_0_
  27.5 0.7 %collective-permute-start.5 = (bf16[32,8,128]{2,1,0:T(8,128)(2,1)S(1)}, bf16[32,8,128]{2,1,0:T(8,128)(2,1)S(1)}, u32[]{:S(2)}, u32[]{:S(2)}) collective-permute-start(bf16[32,8,128]{2,1,0:T(8,128)(2,1)S(1)} %get-tuple-element.39), channel_id=1, source_target_pairs={{0,2},{1,3},{2,0},{3,1},{4,6},{5,7},{6,4},{7,5},{8,10},{9,11},{10,... | collective-permute-start | bytes 196616 | tf_op jit(solution)/shard_map/ppermute | solution.py:465
  28.1 0.8 %collective-permute-done.1.refs_1_ = bf16[32,8,128]{2,1,0:T(8,128)(2,1)S(1)} collective-permute-done((bf16[32,8,128]{2,1,0:T(8,128)(2,1)S(1)}, bf16[32,8,128]{2,1,0:T(8,128)(2,1)S(1)}, u32[]{:S(2)}, u32[]{:S(2)}) %collective-permute-start.1) | collective-permute-done | bytes 65568 | tf_op jit(solution)/shard_map/ppermute | solution.py:465
  29.0 0.0 collective-permute-start.6
  29.0 0.0 collective-permute-done.2.refs_2_
  29.0 1.7 %collective-permute-done.3.refs_3_ = bf16[32,8,128]{2,1,0:T(8,128)(2,1)S(1)} collective-permute-done((bf16[32,8,128]{2,1,0:T(8,128)(2,1)S(1)}, bf16[32,8,128]{2,1,0:T(8,128)(2,1)S(1)}, u32[]{:S(2)}, u32[]{:S(2)}) %collective-permute-start.3) | collective-permute-done | bytes 65568 | tf_op jit(solution)/shard_map/ppermute | solution.py:465
  30.7 0.3 collective-permute-done.4.refs_4_
  30.9 1.5 %collective-permute-done.5.refs_5_ = bf16[32,8,128]{2,1,0:T(8,128)(2,1)S(1)} collective-permute-done((bf16[32,8,128]{2,1,0:T(8,128)(2,1)S(1)}, bf16[32,8,128]{2,1,0:T(8,128)(2,1)S(1)}, u32[]{:S(2)}, u32[]{:S(2)}) %collective-permute-start.5) | collective-permute-done | bytes 65568 | tf_op jit(solution)/shard_map/ppermute | solution.py:465
  32.4 0.0 collective-permute-done.6.refs_6_
  32.4 3.6 %wave.1 = (bf16[16,8,128]{2,1,0:T(8,128)(2,1)S(1)}, bf16[16,8,128]{2,1,0:T(8,128)(2,1)S(1)}, bf16[16,8,128]{2,1,0:T(8,128)(2,1)S(1)}, bf16[16,8,128]{2,1,0:T(8,1...) custom-call(bf16[32,8,128]{2,1,0:T(8,128)(2,1)S(1)} %collective-perm, ...), custom_call_target="tpu_custom_call" | custom-call | tf_op jit(solution)/shard_map/wave/pallas_call | solution.py:348
  36.1 0.3 collective-permute-start.7
  36.3 2.4 %collective-permute-start.8 = (bf16[16,8,128]{2,1,0:T(8,128)(2,1)S(1)}, bf16[16,8,128]{2,1,0:T(8,128)(2,1)S(1)}, u32[]{:S(2)}, u32[]{:S(2)}) collective-permute-start(bf16[16,8,128]{2,1,0:T(8,128)(2,1)S(1)} %get-tuple-element.46), channel_id=1, source_target_pairs={{0,6},{1,7},{2,4},{3,5},{4,2},{5,3},{6,0},{7,1},{8,14},{9,15},{10,... | collective-permute-start | bytes 98312 | tf_op jit(solution)/shard_map/ppermute | solution.py:465
  38.7 0.1 collective-permute-start.9
  38.8 1.7 %collective-permute-start.10 = (bf16[16,8,128]{2,1,0:T(8,128)(2,1)S(1)}, bf16[16,8,128]{2,1,0:T(8,128)(2,1)S(1)}, u32[]{:S(2)}, u32[]{:S(2)}) collective-permute-start(bf16[16,8,128]{2,1,0:T(8,128)(2,1)S(1)} %get-tuple-element.48), channel_id=1, source_target_pairs={{0,4},{1,5},{2,6},{3,7},{4,0},{5,1},{6,2},{7,3},{8,12},{9,13},{10,... | collective-permute-start | bytes 98312 | tf_op jit(solution)/shard_map/ppermute | solution.py:465
  40.5 0.0 collective-permute-start.11
  40.5 0.0 collective-permute-done.7.refs_0_
  40.5 1.7 %collective-permute-start.12 = (bf16[16,8,128]{2,1,0:T(8,128)(2,1)S(1)}, bf16[16,8,128]{2,1,0:T(8,128)(2,1)S(1)}, u32[]{:S(2)}, u32[]{:S(2)}) collective-permute-start(bf16[16,8,128]{2,1,0:T(8,128)(2,1)S(1)} %get-tuple-element.50), channel_id=1, source_target_pairs={{0,2},{1,3},{2,0},{3,1},{4,6},{5,7},{6,4},{7,5},{8,10},{9,11},{10,... | collective-permute-start | bytes 98312 | tf_op jit(solution)/shard_map/ppermute | solution.py:465
  42.2 0.0 collective-permute-done.8.refs_1_
  42.2 0.2 collective-permute-start.13
  42.4 0.0 collective-permute-done.9.refs_2_
  42.4 0.7 %collective-permute-done.10.refs_3_ = bf16[16,8,128]{2,1,0:T(8,128)(2,1)S(1)} collective-permute-done((bf16[16,8,128]{2,1,0:T(8,128)(2,1)S(1)}, bf16[16,8,128]{2,1,0:T(8,128)(2,1)S(1)}, u32[]{:S(2)}, u32[]{:S(2)}) %collective-permute-start.10) | collective-permute-done | bytes 32800 | tf_op jit(solution)/shard_map/ppermute | solution.py:465
  43.1 0.9 %collective-permute-done.11.refs_4_ = bf16[16,8,128]{2,1,0:T(8,128)(2,1)S(1)} collective-permute-done((bf16[16,8,128]{2,1,0:T(8,128)(2,1)S(1)}, bf16[16,8,128]{2,1,0:T(8,128)(2,1)S(1)}, u32[]{:S(2)}, u32[]{:S(2)}) %collective-permute-start.11) | collective-permute-done | bytes 32800 | tf_op jit(solution)/shard_map/ppermute | solution.py:465
  44.0 0.9 %collective-permute-done.12.refs_5_ = bf16[16,8,128]{2,1,0:T(8,128)(2,1)S(1)} collective-permute-done((bf16[16,8,128]{2,1,0:T(8,128)(2,1)S(1)}, bf16[16,8,128]{2,1,0:T(8,128)(2,1)S(1)}, u32[]{:S(2)}, u32[]{:S(2)}) %collective-permute-start.12) | collective-permute-done | bytes 32800 | tf_op jit(solution)/shard_map/ppermute | solution.py:465
  44.9 0.0 collective-permute-done.13.refs_6_
  44.9 1.2 %stack.1 = bf16[16,4,8,128]{3,2,1,0:T(8,128)(2,1)S(1)} custom-call(s32[16,128]{1,0:T(8,128)S(1)} %get-tuple-element.33.facts_ref, bf16[16,8,128]{2,1,0:T(8,128)(2,1)S(1)} %collective-permute-done.7.refs_0_, bf16[16,8,128]{2,1,0:T(8,128)(2,1)S(1)} %collective-permute-done.8.refs_1_, bf16[16,8,128]{2,1,0:T(8,128)(2,1)S(1)} %collective-permute-done.9.refs_2_, ...), custom_call_target="tpu_custom_call" | custom-call | tf_op jit(solution)/shard_map/stack/pallas_call | solution.py:515
  46.1 10.8 %all_to_all.10.sums_ref = bf16[16,4,8,128]{3,2,1,0:T(8,128)(2,1)S(1)} all-to-all(bf16[16,4,8,128]{3,2,1,0:T(8,128)(2,1)S(1)} %stack.1), channel_id=1, replica_groups=mesh['grp'=2,'shot'=16,'depth'=1] {'shot'}, dimensions={0} | all-to-all | bytes 262144 | tf_op jit(solution)/shard_map/all_to_all | solution.py:529
  57.0 0.7 %finish.1 = f32[4,8,8,128]{3,2,1,0:T(8,128)} custom-call(bf16[16,4,8,128]{3,2,1,0:T(8,128)(2,1)S(1)} %all_to_all.10.sums_ref), custom_call_target="tpu_custom_call" | custom-call | tf_op jit(solution)/shard_map/finish/pallas_call | solution.py:530
Async XLA Ops:
  3.1 7.5 %copy-start = (bf16[1,32,32,128]{3,2,1,0:T(8,128)(2,1)S(1)}, bf16[1,32,32,128]{3,2,1,0:T(8,128)(2,1)}, u32[]{:S(2)}) copy-start(bf16[1,32,32,128]{3,2,1,0:T(8,128)(2,1)} %param.18) | copy-start | bytes 786436
  3.2 7.5 %copy-start.1 = (bf16[1,32,32,128]{3,2,1,0:T(8,128)(2,1)S(1)}, bf16[1,32,32,128]{3,2,1,0:T(8,128)(2,1)}, u32[]{:S(2)}) copy-start(bf16[1,32,32,128]{3,2,1,0:T(8,128)(2,1)} %param.19) | copy-start | bytes 786436
  3.2 18.1 %all-to-all-start = ((bf16[16,9,8,128]{3,2,1,0:T(8,128)(2,1)}), bf16[16,9,8,128]{3,2,1,0:T(8,128)(2,1)S(1)}, u32[]{:S(2)}, u32[]{:S(2)}) async-start(bf16[16,9,8,128]{3,2,1,0:T(8,128)(2,1)} %prepare.1), calls=%async_computation | async-start | bytes 589824 | tf_op jit(solution)/shard_map/all_to_all | solution.py:484
  22.2 5.3 %collective-permute-start = (bf16[32,8,128]{2,1,0:T(8,128)(2,1)S(1)}, bf16[32,8,128]{2,1,0:T(8,128)(2,1)S(1)}, u32[]{:S(2)}, u32[]{:S(2)}) collective-permute-start(bf16[32,8,128]{2,1,0:T(8,128)(2,1)S(1)} %get-tuple-element.34), channel_id=1, source_target_pairs={{0,7},{1,6},{2,5},{3,4},{4,3},{5,2},{6,1},{7,0},{8,15},{9,14},{10,... | collective-permute-start | bytes 196616 | tf_op jit(solution)/shard_map/ppermute | solution.py:465
  22.9 6.1 %collective-permute-start.1 = (bf16[32,8,128]{2,1,0:T(8,128)(2,1)S(1)}, bf16[32,8,128]{2,1,0:T(8,128)(2,1)S(1)}, u32[]{:S(2)}, u32[]{:S(2)}) collective-permute-start(bf16[32,8,128]{2,1,0:T(8,128)(2,1)S(1)} %get-tuple-element.35), channel_id=1, source_target_pairs={{0,6},{1,7},{2,4},{3,5},{4,2},{5,3},{6,0},{7,1},{8,14},{9,15},{10,... | collective-permute-start | bytes 196616 | tf_op jit(solution)/shard_map/ppermute | solution.py:465
  24.6 4.3 %collective-permute-start.2 = (bf16[32,8,128]{2,1,0:T(8,128)(2,1)S(1)}, bf16[32,8,128]{2,1,0:T(8,128)(2,1)S(1)}, u32[]{:S(2)}, u32[]{:S(2)}) collective-permute-start(bf16[32,8,128]{2,1,0:T(8,128)(2,1)S(1)} %get-tuple-element.36), channel_id=1, source_target_pairs={{0,5},{1,4},{2,7},{3,6},{4,1},{5,0},{6,3},{7,2},{8,13},{9,12},{10,... | collective-permute-start | bytes 196616 | tf_op jit(solution)/shard_map/ppermute | solution.py:465
  24.8 5.9 %collective-permute-start.3 = (bf16[32,8,128]{2,1,0:T(8,128)(2,1)S(1)}, bf16[32,8,128]{2,1,0:T(8,128)(2,1)S(1)}, u32[]{:S(2)}, u32[]{:S(2)}) collective-permute-start(bf16[32,8,128]{2,1,0:T(8,128)(2,1)S(1)} %get-tuple-element.37), channel_id=1, source_target_pairs={{0,4},{1,5},{2,6},{3,7},{4,0},{5,1},{6,2},{7,3},{8,12},{9,13},{10,... | collective-permute-start | bytes 196616 | tf_op jit(solution)/shard_map/ppermute | solution.py:465
  26.6 4.3 %collective-permute-start.4 = (bf16[32,8,128]{2,1,0:T(8,128)(2,1)S(1)}, bf16[32,8,128]{2,1,0:T(8,128)(2,1)S(1)}, u32[]{:S(2)}, u32[]{:S(2)}) collective-permute-start(bf16[32,8,128]{2,1,0:T(8,128)(2,1)S(1)} %get-tuple-element.38), channel_id=1, source_target_pairs={{0,3},{1,2},{2,1},{3,0},{4,7},{5,6},{6,5},{7,4},{8,11},{9,10},{10,... | collective-permute-start | bytes 196616 | tf_op jit(solution)/shard_map/ppermute | solution.py:465
  27.5 5.0 %collective-permute-start.5 = (bf16[32,8,128]{2,1,0:T(8,128)(2,1)S(1)}, bf16[32,8,128]{2,1,0:T(8,128)(2,1)S(1)}, u32[]{:S(2)}, u32[]{:S(2)}) collective-permute-start(bf16[32,8,128]{2,1,0:T(8,128)(2,1)S(1)} %get-tuple-element.39), channel_id=1, source_target_pairs={{0,2},{1,3},{2,0},{3,1},{4,6},{5,7},{6,4},{7,5},{8,10},{9,11},{10,... | collective-permute-start | bytes 196616 | tf_op jit(solution)/shard_map/ppermute | solution.py:465
  29.0 3.4 %collective-permute-start.6 = (bf16[32,8,128]{2,1,0:T(8,128)(2,1)S(1)}, bf16[32,8,128]{2,1,0:T(8,128)(2,1)S(1)}, u32[]{:S(2)}, u32[]{:S(2)}) collective-permute-start(bf16[32,8,128]{2,1,0:T(8,128)(2,1)S(1)} %get-tuple-element.40), channel_id=1, source_target_pairs={{0,1},{1,0},{2,3},{3,2},{4,5},{5,4},{6,7},{7,6},{8,9},{9,8},{10,11... | collective-permute-start | bytes 196616 | tf_op jit(solution)/shard_map/ppermute | solution.py:465
  36.1 4.5 %collective-permute-start.7 = (bf16[16,8,128]{2,1,0:T(8,128)(2,1)S(1)}, bf16[16,8,128]{2,1,0:T(8,128)(2,1)S(1)}, u32[]{:S(2)}, u32[]{:S(2)}) collective-permute-start(bf16[16,8,128]{2,1,0:T(8,128)(2,1)S(1)} %get-tuple-element.45), channel_id=1, source_target_pairs={{0,7},{1,6},{2,5},{3,4},{4,3},{5,2},{6,1},{7,0},{8,15},{9,14},{10,... | collective-permute-start | bytes 98312 | tf_op jit(solution)/shard_map/ppermute | solution.py:465
  36.3 5.9 %collective-permute-start.8 = (bf16[16,8,128]{2,1,0:T(8,128)(2,1)S(1)}, bf16[16,8,128]{2,1,0:T(8,128)(2,1)S(1)}, u32[]{:S(2)}, u32[]{:S(2)}) collective-permute-start(bf16[16,8,128]{2,1,0:T(8,128)(2,1)S(1)} %get-tuple-element.46), channel_id=1, source_target_pairs={{0,6},{1,7},{2,4},{3,5},{4,2},{5,3},{6,0},{7,1},{8,14},{9,15},{10,... | collective-permute-start | bytes 98312 | tf_op jit(solution)/shard_map/ppermute | solution.py:465
  38.7 3.7 %collective-permute-start.9 = (bf16[16,8,128]{2,1,0:T(8,128)(2,1)S(1)}, bf16[16,8,128]{2,1,0:T(8,128)(2,1)S(1)}, u32[]{:S(2)}, u32[]{:S(2)}) collective-permute-start(bf16[16,8,128]{2,1,0:T(8,128)(2,1)S(1)} %get-tuple-element.47), channel_id=1, source_target_pairs={{0,5},{1,4},{2,7},{3,6},{4,1},{5,0},{6,3},{7,2},{8,13},{9,12},{10,... | collective-permute-start | bytes 98312 | tf_op jit(solution)/shard_map/ppermute | solution.py:465
  38.8 4.3 %collective-permute-start.10 = (bf16[16,8,128]{2,1,0:T(8,128)(2,1)S(1)}, bf16[16,8,128]{2,1,0:T(8,128)(2,1)S(1)}, u32[]{:S(2)}, u32[]{:S(2)}) collective-permute-start(bf16[16,8,128]{2,1,0:T(8,128)(2,1)S(1)} %get-tuple-element.48), channel_id=1, source_target_pairs={{0,4},{1,5},{2,6},{3,7},{4,0},{5,1},{6,2},{7,3},{8,12},{9,13},{10,... | collective-permute-start | bytes 98312 | tf_op jit(solution)/shard_map/ppermute | solution.py:465
  40.5 3.5 %collective-permute-start.11 = (bf16[16,8,128]{2,1,0:T(8,128)(2,1)S(1)}, bf16[16,8,128]{2,1,0:T(8,128)(2,1)S(1)}, u32[]{:S(2)}, u32[]{:S(2)}) collective-permute-start(bf16[16,8,128]{2,1,0:T(8,128)(2,1)S(1)} %get-tuple-element.49), channel_id=1, source_target_pairs={{0,3},{1,2},{2,1},{3,0},{4,7},{5,6},{6,5},{7,4},{8,11},{9,10},{10,... | collective-permute-start | bytes 98312 | tf_op jit(solution)/shard_map/ppermute | solution.py:465
  40.5 4.4 %collective-permute-start.12 = (bf16[16,8,128]{2,1,0:T(8,128)(2,1)S(1)}, bf16[16,8,128]{2,1,0:T(8,128)(2,1)S(1)}, u32[]{:S(2)}, u32[]{:S(2)}) collective-permute-start(bf16[16,8,128]{2,1,0:T(8,128)(2,1)S(1)} %get-tuple-element.50), channel_id=1, source_target_pairs={{0,2},{1,3},{2,0},{3,1},{4,6},{5,7},{6,4},{7,5},{8,10},{9,11},{10,... | collective-permute-start | bytes 98312 | tf_op jit(solution)/shard_map/ppermute | solution.py:465
  42.2 2.7 %collective-permute-start.13 = (bf16[16,8,128]{2,1,0:T(8,128)(2,1)S(1)}, bf16[16,8,128]{2,1,0:T(8,128)(2,1)S(1)}, u32[]{:S(2)}, u32[]{:S(2)}) collective-permute-start(bf16[16,8,128]{2,1,0:T(8,128)(2,1)S(1)} %get-tuple-element.51), channel_id=1, source_target_pairs={{0,1},{1,0},{2,3},{3,2},{4,5},{5,4},{6,7},{7,6},{8,9},{9,8},{10,11... | collective-permute-start | bytes 98312 | tf_op jit(solution)/shard_map/ppermute | solution.py:465

commit v6 on v4

--- a/solution.py
+++ b/solution.py
@@ -71,6 +71,17 @@
 
 def limit(mebibytes):
     return pltpu.CompilerParams(vmem_limit_bytes=mebibytes * 2**20)
+
+
+def parts(refs):
+    chips = len(refs) // 2
+    own, other = refs[:chips][::-1], refs[chips:][::-1]
+    length = refs[0].shape[0] // 2
+    return [
+        ref.at[pl.ds(side * length, length)]
+        for pair in zip(own, other)
+        for side, ref in enumerate(pair)
+    ]
 
 
 def vmem():
@@ -128,8 +139,9 @@
 
 
 def pick_kernel(slots, near, pieces_ref, *refs):
-    out_refs = refs[:near][::-1]
-    facts_ref, facts, spots, sem = refs[near:]
+    chips = near // 2
+    out_refs = refs[:chips][::-1]
+    facts_ref, facts, spots, sem = refs[chips:]
     count = facts_ref.shape[0]
     tiles = 2 * slots + 1
     for piece in range(count):
@@ -142,8 +154,9 @@
     for piece in range(count):
         for slot in range(slots):
             spots[facts[piece, slot]] = piece * tiles + 2 * slot
-    for k, out_ref in enumerate(out_refs):
-        shot = me ^ k
+    for t in range(near):
+        shot = me ^ t
+        out_ref, start_tile = out_refs[t // 2], t % 2 * APX * APY * 2
         first = facts[shot, slots] * GRID_COLS + facts[shot, slots + 1]
         for x in range(APX):
             found = []
@@ -151,7 +164,7 @@
                 spot = spots[first + x * GRID_COLS + y]
                 found += [pieces_ref[spot], pieces_ref[spot + 1]]
             for index, tile in enumerate(found):
-                out_ref[x * APY * 2 + index] = tile
+                out_ref[start_tile + x * APY * 2 + index] = tile
 
 
 def ends(shape):
@@ -253,11 +266,13 @@
 
 
 def wave_kernel(near, *refs):
-    model_refs = refs[:near]
+    chips = near // 2
+    model_refs = parts(refs[:near])
     u_0, g_0, next_ref = refs[near:near + 3]
-    out_refs = refs[near + 3:2 * near + 3][::-1]
-    kap, con, u_1, u_2, u_3, d_0, d_1, d_2, kb_3, kb_2, kb_1 = refs[2 * near + 3:2 * near + 14]
-    g_1, g_2, d_3, b_2, b_1, image, result = refs[2 * near + 14:]
+    refs = refs[near + 3:]
+    out_refs = refs[:chips][::-1]
+    kap, con, u_1, u_2, u_3, d_0, d_1, d_2, kb_3, kb_2, kb_1 = refs[chips:chips + 11]
+    g_1, g_2, d_3, b_2, b_1, image, result = refs[chips + 11:]
     span_x, many = u_0.shape[:2]
     depth = u_0.shape[3]
     block_y = model_refs[0].shape[1]
@@ -334,8 +349,9 @@
     adjoint(kb_3, d_3, None, d_2, g_2, kb_2, b_2)
     adjoint(kb_2, b_2, d_3, d_1, g_1, kb_1, b_1)
     adjoint(kb_1, b_1, b_2, d_0, g_0, None, None)
-    for k, out_ref in enumerate(out_refs):
-        out_ref[...] = result[place ^ k]
+    length = result.shape[1]
+    for t in range(near):
+        out_refs[t // 2][pl.ds(t % 2 * length, length)] = result[place ^ t]
 
 
 def wave(models, started):
@@ -344,14 +360,15 @@
     flat = pltpu.VMEM((span_x, many * LANES, depth), jnp.float32)
     field = pltpu.VMEM((span_x + 1, many, LANES, depth), jnp.float32)
     plain = pltpu.VMEM((span_x, many, LANES, depth), jnp.float32)
-    out = (APX * many, LANES, depth)
+    tiles = APX * many
+    out = jax.ShapeDtypeStruct((2 * tiles, LANES, depth), jnp.bfloat16)
     terms = pl.pallas_call(
         functools.partial(wave_kernel, near),
-        out_shape=(jax.ShapeDtypeStruct(out, jnp.bfloat16),) * near,
+        out_shape=(out,) * (near // 2),
         in_specs=[vmem()] * (near + 3),
-        out_specs=(vmem(),) * near,
+        out_specs=(vmem(),) * (near // 2),
         scratch_shapes=[flat] * 2 + [field] * 9 + [plain] * 6
-        + [pltpu.VMEM((near,) + out, jnp.bfloat16)],
+        + [pltpu.VMEM((near, tiles, LANES, depth), jnp.bfloat16)],
         compiler_params=limit(20),
         name="wave",
     )(*models, *started)
@@ -361,7 +378,11 @@
 def wave_split_depth(models, before, current):
     near = len(models)
     order = (lax.axis_index("shot") % near) ^ jnp.arange(near)
-    model = jnp.stack(models)[order]
+    chips = near // 2
+    length = models[0].shape[0] // 2
+    pairs = zip(models[:chips][::-1], models[chips:][::-1])
+    model = jnp.stack([part for own, other in pairs for part in (own[:length], other[length:])])
+    model = model[order]
     span_x, span_y, depth = before.shape
     block_x, tiles, block_y, _ = model.shape
     grids = model.reshape(block_x, APX, APY, 2, block_y, depth).transpose(3, 1, 0, 2, 4, 5)
@@ -376,11 +397,11 @@
     many = span_y // LANES
     image = image.reshape(APX, block_x, LANES, many, depth).transpose(1, 0, 3, 2, 4)
     image = image.reshape(near, APX * many, LANES, depth).astype(jnp.bfloat16)[order]
-    return [image[k] for k in range(near)]
+    return [jnp.concatenate([image[2 * k], image[2 * k + 1]]) for k in range(chips)]
 
 
 def stack_kernel(slots, near, facts_ref, *refs):
-    terms_refs = refs[:near]
+    terms_refs = parts(refs[:near])
     out_ref, facts, total, lined, sem = refs[near:]
     tiles = terms_refs[0].shape[0]
     wide = tiles // APX
@@ -460,10 +481,12 @@
     assert count % near == 0 and near & (near - 1) == 0
 
     def swap(values):
-        swapped = {0: values[0]}
-        for k in range(near - 1, 0, -1):
-            swapped[k] = lax.ppermute(values[k], "shot", [(i, i ^ k) for i in range(count)])
-        return [swapped[k] for k in range(near)]
+        own = [
+            lax.ppermute(values[k], "shot", [(i, i ^ 2 * k) for i in range(count)])
+            if k else values[0]
+            for k in range(len(values) - 1, -1, -1)
+        ]
+        return own + [lax.ppermute(v, "shot", [(i, i ^ 1) for i in range(count)]) for v in own]
 
     sent = pl.pallas_call(
         prepare_kernel,
@@ -489,11 +512,11 @@
     *picked, facts = pl.pallas_call(
         functools.partial(pick_kernel, slots, near),
         out_shape=(
-            *[jax.ShapeDtypeStruct((patch * 2, block_y, depth), jnp.bfloat16)] * near,
+            *[jax.ShapeDtypeStruct((patch * 4, block_y, depth), jnp.bfloat16)] * (near // 2),
             jax.ShapeDtypeStruct((count, depth), jnp.int32),
         ),
         in_specs=[vmem()],
-        out_specs=(vmem(),) * (near + 1),
+        out_specs=(vmem(),) * (near // 2 + 1),
         scratch_shapes=[
             pltpu.SMEM((count, depth), jnp.int32),
             pltpu.SMEM((count * slots,), jnp.int32),
@@ -511,7 +534,7 @@
     terms = swap(terms)
 
     grid_rows = count * slots // GRID_COLS
-    wide = terms[0].shape[0] // APX
+    wide = terms[0].shape[0] // 2 // APX
     sums = pl.pallas_call(
         functools.partial(stack_kernel, slots, near),
         out_shape=jax.ShapeDtypeStruct((count, slots, block_y, depth), jnp.bfloat16),

time: 59.1 us -> 57.6 us (0.975)
  starting transfers between devices: 19.7 us -> 15.3 us
  waiting for transfers between devices: 17.7 us -> 20.4 us
    ppermute x14, starting transfers between devices: 12.2 us -> 7.77 us  [the longest x6 7.11 us: swap(): lax.ppermute(values[k], 'shot', [(i, i ^ 2 * k) for i in range(count)])]
    ppermute x14, waiting for transfers between devices: 7.86 us -> 10.6 us  [the longest x6 8 us: swap(): lax.ppermute(values[k], 'shot', [(i, i ^ 2 * k) for i in range(count)])]
  transfers between devices with their start and end apart: 15 -> 15, of which waited for: 8 -> 12; matrix products, arithmetic and copies ran while one was open for 0% -> 0% of each run, Pallas kernels for 1% -> 1%
where the time goes in v6:
time: 57.6 us; the launch traced here: 57.3 us
  waiting for transfers between devices  20.4 us (35%)
  starting transfers between devices  15.3 us (27%)
  blocking collectives  11.3 us (20%)
  Pallas kernels  8.94 us (16%)
  between operations  1.39 us (2%)
    all_to_all x1, blocking collectives, per_device(): sums = lax.all_to_all(sums, 'shot', 0, 0, tiled=True)  11.3 us
    all_to_all x1, waiting for transfers between devices, per_device(): pieces = lax.all_to_all(sent, 'shot', 0, 0, tiled=True)  9.85 us
    ppermute x6, waiting for transfers between devices, swap(): lax.ppermute(values[k], 'shot', [(i, i ^ 2 * k) for i in range(count)])  8 us
    all_to_all x1, starting transfers between devices, per_device(): pieces = lax.all_to_all(sent, 'shot', 0, 0, tiled=True)  7.5 us
    ppermute x6, starting transfers between devices, swap(): lax.ppermute(values[k], 'shot', [(i, i ^ 2 * k) for i in range(count)])  7.11 us
    pallas_call x1, Pallas kernels, wave(): pl.pallas_call(functools.partial(wave_kernel, near), out_shape=(out,) * (...  3.64 us
    ppermute x8, waiting for transfers between devices, swap(): lax.ppermute(v, 'shot', [(i, i ^ 1) for i in range(count)])  2.56 us
    pallas_call x1, Pallas kernels, per_device(): pl.pallas_call(prepare_kernel, out_shape=jax.ShapeDtypeStruct((count, 2 *...  1.83 us
  transfers between devices with their start and end apart: 15, of which 12 were waited for; matrix products, arithmetic and copies ran while one was open for 0% of the time, Pallas kernels for 1%

profile of v6, /device:TPU:0, one launch (start us, length us, event | category | flops | bytes accessed | tf_op | source)
XLA Modules:
  0.0 57.3 jit_solution(4953245991456752130)
XLA Ops:
  1.3 1.8 %prepare.1 = bf16[16,9,8,128]{3,2,1,0:T(8,128)(2,1)} custom-call(s32[1]{0:T(128)S(6)} %copy.11.row_ref, s32[1]{0:T(128)S(6)} %copy.12.col_ref, s32[4]{0:T(128)} %ids_hbm.1, s32[4,8,8]{2,1,0:T(8,128)} %floor_hbm.1, bf16[4,8,8,128]{3,2,1,0:T(8,128)(2,1)} %p_hbm.1, bf16[4,8,8,128]{3,2,1,0:T(8,128)(2,1)} %s_hbm.1, bf16[4,8,8,128]{3,2,1,0:T(8,128)(2,1)} %rho_hbm.1, ...), custom_call_target="tpu_custom_call" | custom-call | tf_op jit(solution)/shard_map/prepare/pallas_call | solution.py:491
  3.1 0.0 copy-start
  3.2 0.0 copy-start.1
  3.2 7.5 %all-to-all-start = ((bf16[16,9,8,128]{3,2,1,0:T(8,128)(2,1)}), bf16[16,9,8,128]{3,2,1,0:T(8,128)(2,1)S(1)}, u32[]{:S(2)}, u32[]{:S(2)}) async-start(bf16[16,9,8,128]{3,2,1,0:T(8,128)(2,1)} %prepare.1), calls=%async_computation | async-start | bytes 589824 | tf_op jit(solution)/shard_map/all_to_all | solution.py:507
  10.7 0.0 copy-done
  10.7 0.0 copy-done.1
  10.7 0.7 %start.1 = (f32[32,4,8,128]{3,2,1,0:T(8,128)S(1)}, f32[32,4,8,128]{3,2,1,0:T(8,128)S(1)}, f32[32,4,8,128]{3,2,1,0:T(8,128)S(1)}) custom-call(bf16[32,32,128]{2,1,0:T(8,128)(2,1)S(1)} %bitcast.4, bf16[32,32,128]{2,1,0:T(8,128)(2,1)S(1)} %bitcast.5), custom_call_target="tpu_custom_call" | custom-call | flops 2621440 | bytes 2097152 | tf_op jit(solution)/shard_map/start/pallas_call | solution.py:254
  11.4 9.9 %all-to-all-done = bf16[16,9,8,128]{3,2,1,0:T(8,128)(2,1)S(1)} async-done(((bf16[16,9,8,128]{3,2,1,0:T(8,128)(2,1)}), bf16[16,9,8,128]{3,2,1,0:T(8,128)(2,1)S(1)}, u32[]{:S(2)}, u32[]{:S(2)}) %all-to-all-start) | async-done | bytes 294944 | tf_op jit(solution)/shard_map/all_to_all | solution.py:507
  21.2 0.9 %pick.1 = (bf16[64,8,128]{2,1,0:T(8,128)(2,1)S(1)}, bf16[64,8,128]{2,1,0:T(8,128)(2,1)S(1)}, bf16[64,8,128]{2,1,0:T(8,128)(2,1)S(1)}, bf16[64,8,128]{2,1,0:T(8,128)(2,1)S(1)}, s32[16,128]{1,0:T(8,128)S(1)}) custom-call(bf16[144,8,128]{2,1,0:T(8,128)(2,1)S(1)} %bitcast.3), custom_call_target="tpu_custom_call" | custom-call | tf_op jit(solution)/shard_map/pick/pallas_call | solution.py:512
  22.2 0.8 %collective-permute-start = (bf16[64,8,128]{2,1,0:T(8,128)(2,1)S(1)}, bf16[64,8,128]{2,1,0:T(8,128)(2,1)S(1)}, u32[]{:S(2)}, u32[]{:S(2)}) collective-permute-start(bf16[64,8,128]{2,1,0:T(8,128)(2,1)S(1)} %get-tuple-element.26), channel_id=1, source_target_pairs={{0,6},{1,7},{2,4},{3,5},{4,2},{5,3},{6,0},{7,1},{8,14},{9,15},{10,... | collective-permute-start | bytes 393224 | tf_op jit(solution)/shard_map/ppermute | solution.py:485
  23.0 0.3 collective-permute-start.1
  23.3 2.4 %collective-permute-start.2 = (bf16[64,8,128]{2,1,0:T(8,128)(2,1)S(1)}, bf16[64,8,128]{2,1,0:T(8,128)(2,1)S(1)}, u32[]{:S(2)}, u32[]{:S(2)}) collective-permute-start(bf16[64,8,128]{2,1,0:T(8,128)(2,1)S(1)} %get-tuple-element.28), channel_id=1, source_target_pairs={{0,2},{1,3},{2,0},{3,1},{4,6},{5,7},{6,4},{7,5},{8,10},{9,11},{10,... | collective-permute-start | bytes 393224 | tf_op jit(solution)/shard_map/ppermute | solution.py:485
  25.7 0.0 collective-permute-start.6
  25.7 3.8 %collective-permute-done.refs_0_ = bf16[64,8,128]{2,1,0:T(8,128)(2,1)S(1)} collective-permute-done((bf16[64,8,128]{2,1,0:T(8,128)(2,1)S(1)}, bf16[64,8,128]{2,1,0:T(8,128)(2,1)S(1)}, u32[]{:S(2)}, u32[]{:S(2)}) %collective-permute-start) | collective-permute-done | bytes 131104 | tf_op jit(solution)/shard_map/ppermute | solution.py:485
  29.5 0.0 collective-permute-start.3
  29.5 0.9 %collective-permute-done.1.refs_1_ = bf16[64,8,128]{2,1,0:T(8,128)(2,1)S(1)} collective-permute-done((bf16[64,8,128]{2,1,0:T(8,128)(2,1)S(1)}, bf16[64,8,128]{2,1,0:T(8,128)(2,1)S(1)}, u32[]{:S(2)}, u32[]{:S(2)}) %collective-permute-start.1) | collective-permute-done | bytes 131104 | tf_op jit(solution)/shard_map/ppermute | solution.py:485
  30.4 0.2 collective-permute-start.4
  30.6 0.6 %collective-permute-done.2.refs_2_ = bf16[64,8,128]{2,1,0:T(8,128)(2,1)S(1)} collective-permute-done((bf16[64,8,128]{2,1,0:T(8,128)(2,1)S(1)}, bf16[64,8,128]{2,1,0:T(8,128)(2,1)S(1)}, u32[]{:S(2)}, u32[]{:S(2)}) %collective-permute-start.2) | collective-permute-done | bytes 131104 | tf_op jit(solution)/shard_map/ppermute | solution.py:485
  31.2 0.0 collective-permute-start.5
  31.2 0.0 collective-permute-done.6.refs_7_
  31.2 0.0 collective-permute-done.3.refs_4_
  31.3 0.5 collective-permute-done.4.refs_5_
  31.8 0.8 %collective-permute-done.5.refs_6_ = bf16[64,8,128]{2,1,0:T(8,128)(2,1)S(1)} collective-permute-done((bf16[64,8,128]{2,1,0:T(8,128)(2,1)S(1)}, bf16[64,8,128]{2,1,0:T(8,128)(2,1)S(1)}, u32[]{:S(2)}, u32[]{:S(2)}) %collective-permute-start.5) | collective-permute-done | bytes 131104 | tf_op jit(solution)/shard_map/ppermute | solution.py:489
  32.6 3.6 %wave.1 = (bf16[32,8,128]{2,1,0:T(8,128)(2,1)S(1)}, bf16[32,8,128]{2,1,0:T(8,128)(2,1)S(1)}, bf16[32,8,128]{2,1,0:T(8,128)(2,1)S(1)}, bf16[32,8,128]{2,1,0:T(8,128)(2,1)S(1)}) custom-call(bf16[64,8,128]{2,1,0:T(8,128)(2,1)S(1)} %collective-permute-done.refs_0_, bf16[64,8,128]{2,1,0:T(8,128)(2,1)S(1)} %collective-permute-done.1.refs_1_, ...), custom_call_target="tpu_custom_call" | custom-call | tf_op jit(solution)/shard_map/wave/pallas_call | solution.py:365
  36.2 1.3 %collective-permute-start.7 = (bf16[32,8,128]{2,1,0:T(8,128)(2,1)S(1)}, bf16[32,8,128]{2,1,0:T(8,128)(2,1)S(1)}, u32[]{:S(2)}, u32[]{:S(2)}) collective-permute-start(bf16[32,8,128]{2,1,0:T(8,128)(2,1)S(1)} %get-tuple-element.33), channel_id=1, source_target_pairs={{0,6},{1,7},{2,4},{3,5},{4,2},{5,3},{6,0},{7,1},{8,14},{9,15},{10,... | collective-permute-start | bytes 196616 | tf_op jit(solution)/shard_map/ppermute | solution.py:485
  37.5 1.0 %collective-permute-start.8 = (bf16[32,8,128]{2,1,0:T(8,128)(2,1)S(1)}, bf16[32,8,128]{2,1,0:T(8,128)(2,1)S(1)}, u32[]{:S(2)}, u32[]{:S(2)}) collective-permute-start(bf16[32,8,128]{2,1,0:T(8,128)(2,1)S(1)} %get-tuple-element.34), channel_id=1, source_target_pairs={{0,4},{1,5},{2,6},{3,7},{4,0},{5,1},{6,2},{7,3},{8,12},{9,13},{10,... | collective-permute-start | bytes 196616 | tf_op jit(solution)/shard_map/ppermute | solution.py:485
  38.5 1.3 %collective-permute-start.9 = (bf16[32,8,128]{2,1,0:T(8,128)(2,1)S(1)}, bf16[32,8,128]{2,1,0:T(8,128)(2,1)S(1)}, u32[]{:S(2)}, u32[]{:S(2)}) collective-permute-start(bf16[32,8,128]{2,1,0:T(8,128)(2,1)S(1)} %get-tuple-element.35), channel_id=1, source_target_pairs={{0,2},{1,3},{2,0},{3,1},{4,6},{5,7},{6,4},{7,5},{8,10},{9,11},{10,... | collective-permute-start | bytes 196616 | tf_op jit(solution)/shard_map/ppermute | solution.py:485
  39.8 0.0 collective-permute-start.13
  39.8 2.4 %collective-permute-done.7.refs_0_ = bf16[32,8,128]{2,1,0:T(8,128)(2,1)S(1)} collective-permute-done((bf16[32,8,128]{2,1,0:T(8,128)(2,1)S(1)}, bf16[32,8,128]{2,1,0:T(8,128)(2,1)S(1)}, u32[]{:S(2)}, u32[]{:S(2)}) %collective-permute-start.7) | collective-permute-done | bytes 65568 | tf_op jit(solution)/shard_map/ppermute | solution.py:485
  42.1 0.0 collective-permute-start.10
  42.1 0.1 collective-permute-done.8.refs_1_
  42.2 0.5 collective-permute-start.11
  42.6 0.3 collective-permute-done.9.refs_2_
  42.9 0.0 collective-permute-start.12
  42.9 0.0 collective-permute-done.13.refs_7_
  42.9 0.5 collective-permute-done.10.refs_4_
  43.4 0.2 collective-permute-done.11.refs_5_
  43.5 0.6 %collective-permute-done.12.refs_6_ = bf16[32,8,128]{2,1,0:T(8,128)(2,1)S(1)} collective-permute-done((bf16[32,8,128]{2,1,0:T(8,128)(2,1)S(1)}, bf16[32,8,128]{2,1,0:T(8,128)(2,1)S(1)}, u32[]{:S(2)}, u32[]{:S(2)}) %collective-permute-start.12) | collective-permute-done | bytes 65568 | tf_op jit(solution)/shard_map/ppermute | solution.py:489
  44.2 1.2 %stack.1 = bf16[16,4,8,128]{3,2,1,0:T(8,128)(2,1)S(1)} custom-call(s32[16,128]{1,0:T(8,128)S(1)} %get-tuple-element.25.facts_ref, bf16[32,8,128]{2,1,0:T(8,128)(2,1)S(1)} %collective-permute-done.7.refs_0_, bf16[32,8,128]{2,1,0:T(8,128)(2,1)S(1)} %collective-permute-done.8.refs_1_, bf16[32,8,128]{2,1,0:T(8,128)(2,1)S(1)} %collective-permute-done.9.refs_2_, ...), custom_call_target="tpu_custom_call" | custom-call | tf_op jit(solution)/shard_map/stack/pallas_call | solution.py:538
  45.4 11.3 %all_to_all.10.sums_ref = bf16[16,4,8,128]{3,2,1,0:T(8,128)(2,1)S(1)} all-to-all(bf16[16,4,8,128]{3,2,1,0:T(8,128)(2,1)S(1)} %stack.1), channel_id=1, replica_groups=mesh['grp'=2,'shot'=16,'depth'=1] {'shot'}, dimensions={0} | all-to-all | bytes 262144 | tf_op jit(solution)/shard_map/all_to_all | solution.py:552
  56.6 0.7 %finish.1 = f32[4,8,8,128]{3,2,1,0:T(8,128)} custom-call(bf16[16,4,8,128]{3,2,1,0:T(8,128)(2,1)S(1)} %all_to_all.10.sums_ref), custom_call_target="tpu_custom_call" | custom-call | tf_op jit(solution)/shard_map/finish/pallas_call | solution.py:553
Async XLA Ops:
  3.1 7.5 %copy-start = (bf16[1,32,32,128]{3,2,1,0:T(8,128)(2,1)S(1)}, bf16[1,32,32,128]{3,2,1,0:T(8,128)(2,1)}, u32[]{:S(2)}) copy-start(bf16[1,32,32,128]{3,2,1,0:T(8,128)(2,1)} %param.18) | copy-start | bytes 786436
  3.2 7.5 %copy-start.1 = (bf16[1,32,32,128]{3,2,1,0:T(8,128)(2,1)S(1)}, bf16[1,32,32,128]{3,2,1,0:T(8,128)(2,1)}, u32[]{:S(2)}) copy-start(bf16[1,32,32,128]{3,2,1,0:T(8,128)(2,1)} %param.19) | copy-start | bytes 786436
  3.2 18.1 %all-to-all-start = ((bf16[16,9,8,128]{3,2,1,0:T(8,128)(2,1)}), bf16[16,9,8,128]{3,2,1,0:T(8,128)(2,1)S(1)}, u32[]{:S(2)}, u32[]{:S(2)}) async-start(bf16[16,9,8,128]{3,2,1,0:T(8,128)(2,1)} %prepare.1), calls=%async_computation | async-start | bytes 589824 | tf_op jit(solution)/shard_map/all_to_all | solution.py:507
  22.2 7.3 %collective-permute-start = (bf16[64,8,128]{2,1,0:T(8,128)(2,1)S(1)}, bf16[64,8,128]{2,1,0:T(8,128)(2,1)S(1)}, u32[]{:S(2)}, u32[]{:S(2)}) collective-permute-start(bf16[64,8,128]{2,1,0:T(8,128)(2,1)S(1)} %get-tuple-element.26), channel_id=1, source_target_pairs={{0,6},{1,7},{2,4},{3,5},{4,2},{5,3},{6,0},{7,1},{8,14},{9,15},{10,... | collective-permute-start | bytes 393224 | tf_op jit(solution)/shard_map/ppermute | solution.py:485
  23.0 7.5 %collective-permute-start.1 = (bf16[64,8,128]{2,1,0:T(8,128)(2,1)S(1)}, bf16[64,8,128]{2,1,0:T(8,128)(2,1)S(1)}, u32[]{:S(2)}, u32[]{:S(2)}) collective-permute-start(bf16[64,8,128]{2,1,0:T(8,128)(2,1)S(1)} %get-tuple-element.27), channel_id=1, source_target_pairs={{0,4},{1,5},{2,6},{3,7},{4,0},{5,1},{6,2},{7,3},{8,12},{9,13},{10,... | collective-permute-start | bytes 393224 | tf_op jit(solution)/shard_map/ppermute | solution.py:485
  23.3 7.9 %collective-permute-start.2 = (bf16[64,8,128]{2,1,0:T(8,128)(2,1)S(1)}, bf16[64,8,128]{2,1,0:T(8,128)(2,1)S(1)}, u32[]{:S(2)}, u32[]{:S(2)}) collective-permute-start(bf16[64,8,128]{2,1,0:T(8,128)(2,1)S(1)} %get-tuple-element.28), channel_id=1, source_target_pairs={{0,2},{1,3},{2,0},{3,1},{4,6},{5,7},{6,4},{7,5},{8,10},{9,11},{10,... | collective-permute-start | bytes 393224 | tf_op jit(solution)/shard_map/ppermute | solution.py:485
  25.7 5.5 %collective-permute-start.6 = (bf16[64,8,128]{2,1,0:T(8,128)(2,1)S(1)}, bf16[64,8,128]{2,1,0:T(8,128)(2,1)S(1)}, u32[]{:S(2)}, u32[]{:S(2)}) collective-permute-start(bf16[64,8,128]{2,1,0:T(8,128)(2,1)S(1)} %get-tuple-element.29.refs_3_), channel_id=1, source_target_pairs={{0,1},{1,0},{2,3},{3,2},{4,5},{5,4},{6,7},{7,6},{8,9},{9,8},{10,11... | collective-permute-start | bytes 393224 | tf_op jit(solution)/shard_map/ppermute | solution.py:489
  29.5 1.8 %collective-permute-start.3 = (bf16[64,8,128]{2,1,0:T(8,128)(2,1)S(1)}, bf16[64,8,128]{2,1,0:T(8,128)(2,1)S(1)}, u32[]{:S(2)}, u32[]{:S(2)}) collective-permute-start(bf16[64,8,128]{2,1,0:T(8,128)(2,1)S(1)} %collective-permute-done.refs_0_), channel_id=1, source_target_pairs={{0,1},{1,0},{2,3},{3,2},{4,5},{5,4},{6,7},{7,6},{8,9},{9,8},{10,11... | collective-permute-start | bytes 393224 | tf_op jit(solution)/shard_map/ppermute | solution.py:489
  30.4 1.3 %collective-permute-start.4 = (bf16[64,8,128]{2,1,0:T(8,128)(2,1)S(1)}, bf16[64,8,128]{2,1,0:T(8,128)(2,1)S(1)}, u32[]{:S(2)}, u32[]{:S(2)}) collective-permute-start(bf16[64,8,128]{2,1,0:T(8,128)(2,1)S(1)} %collective-permute-done.1.refs_1_), channel_id=1, source_target_pairs={{0,1},{1,0},{2,3},{3,2},{4,5},{5,4},{6,7},{7,6},{8,9},{9,8},{10,11... | collective-permute-start | bytes 393224 | tf_op jit(solution)/shard_map/ppermute | solution.py:489
  31.2 1.3 %collective-permute-start.5 = (bf16[64,8,128]{2,1,0:T(8,128)(2,1)S(1)}, bf16[64,8,128]{2,1,0:T(8,128)(2,1)S(1)}, u32[]{:S(2)}, u32[]{:S(2)}) collective-permute-start(bf16[64,8,128]{2,1,0:T(8,128)(2,1)S(1)} %collective-permute-done.2.refs_2_), channel_id=1, source_target_pairs={{0,1},{1,0},{2,3},{3,2},{4,5},{5,4},{6,7},{7,6},{8,9},{9,8},{10,11... | collective-permute-start | bytes 393224 | tf_op jit(solution)/shard_map/ppermute | solution.py:489
  36.2 5.9 %collective-permute-start.7 = (bf16[32,8,128]{2,1,0:T(8,128)(2,1)S(1)}, bf16[32,8,128]{2,1,0:T(8,128)(2,1)S(1)}, u32[]{:S(2)}, u32[]{:S(2)}) collective-permute-start(bf16[32,8,128]{2,1,0:T(8,128)(2,1)S(1)} %get-tuple-element.33), channel_id=1, source_target_pairs={{0,6},{1,7},{2,4},{3,5},{4,2},{5,3},{6,0},{7,1},{8,14},{9,15},{10,... | collective-permute-start | bytes 196616 | tf_op jit(solution)/shard_map/ppermute | solution.py:485
  37.5 4.7 %collective-permute-start.8 = (bf16[32,8,128]{2,1,0:T(8,128)(2,1)S(1)}, bf16[32,8,128]{2,1,0:T(8,128)(2,1)S(1)}, u32[]{:S(2)}, u32[]{:S(2)}) collective-permute-start(bf16[32,8,128]{2,1,0:T(8,128)(2,1)S(1)} %get-tuple-element.34), channel_id=1, source_target_pairs={{0,4},{1,5},{2,6},{3,7},{4,0},{5,1},{6,2},{7,3},{8,12},{9,13},{10,... | collective-permute-start | bytes 196616 | tf_op jit(solution)/shard_map/ppermute | solution.py:485
  38.5 4.4 %collective-permute-start.9 = (bf16[32,8,128]{2,1,0:T(8,128)(2,1)S(1)}, bf16[32,8,128]{2,1,0:T(8,128)(2,1)S(1)}, u32[]{:S(2)}, u32[]{:S(2)}) collective-permute-start(bf16[32,8,128]{2,1,0:T(8,128)(2,1)S(1)} %get-tuple-element.35), channel_id=1, source_target_pairs={{0,2},{1,3},{2,0},{3,1},{4,6},{5,7},{6,4},{7,5},{8,10},{9,11},{10,... | collective-permute-start | bytes 196616 | tf_op jit(solution)/shard_map/ppermute | solution.py:485
  39.8 3.1 %collective-permute-start.13 = (bf16[32,8,128]{2,1,0:T(8,128)(2,1)S(1)}, bf16[32,8,128]{2,1,0:T(8,128)(2,1)S(1)}, u32[]{:S(2)}, u32[]{:S(2)}) collective-permute-start(bf16[32,8,128]{2,1,0:T(8,128)(2,1)S(1)} %get-tuple-element.36.refs_3_), channel_id=1, source_target_pairs={{0,1},{1,0},{2,3},{3,2},{4,5},{5,4},{6,7},{7,6},{8,9},{9,8},{10,11... | collective-permute-start | bytes 196616 | tf_op jit(solution)/shard_map/ppermute | solution.py:489
  42.1 1.3 %collective-permute-start.10 = (bf16[32,8,128]{2,1,0:T(8,128)(2,1)S(1)}, bf16[32,8,128]{2,1,0:T(8,128)(2,1)S(1)}, u32[]{:S(2)}, u32[]{:S(2)}) collective-permute-start(bf16[32,8,128]{2,1,0:T(8,128)(2,1)S(1)} %collective-permute-done.7.refs_0_), channel_id=1, source_target_pairs={{0,1},{1,0},{2,3},{3,2},{4,5},{5,4},{6,7},{7,6},{8,9},{9,8},{10,11... | collective-permute-start | bytes 196616 | tf_op jit(solution)/shard_map/ppermute | solution.py:489
  42.2 1.4 %collective-permute-start.11 = (bf16[32,8,128]{2,1,0:T(8,128)(2,1)S(1)}, bf16[32,8,128]{2,1,0:T(8,128)(2,1)S(1)}, u32[]{:S(2)}, u32[]{:S(2)}) collective-permute-start(bf16[32,8,128]{2,1,0:T(8,128)(2,1)S(1)} %collective-permute-done.8.refs_1_), channel_id=1, source_target_pairs={{0,1},{1,0},{2,3},{3,2},{4,5},{5,4},{6,7},{7,6},{8,9},{9,8},{10,11... | collective-permute-start | bytes 196616 | tf_op jit(solution)/shard_map/ppermute | solution.py:489
  42.9 1.3 %collective-permute-start.12 = (bf16[32,8,128]{2,1,0:T(8,128)(2,1)S(1)}, bf16[32,8,128]{2,1,0:T(8,128)(2,1)S(1)}, u32[]{:S(2)}, u32[]{:S(2)}) collective-permute-start(bf16[32,8,128]{2,1,0:T(8,128)(2,1)S(1)} %collective-permute-done.9.refs_2_), channel_id=1, source_target_pairs={{0,1},{1,0},{2,3},{3,2},{4,5},{5,4},{6,7},{7,6},{8,9},{9,8},{10,11... | collective-permute-start | bytes 196616 | tf_op jit(solution)/shard_map/ppermute | solution.py:489

commit v7 on v6

--- a/solution.py
+++ b/solution.py
@@ -73,6 +73,10 @@
     return pltpu.CompilerParams(vmem_limit_bytes=mebibytes * 2**20)
 
 
+def chip_place(near):
+    return lax.axis_index("shot") // 2 % near
+
+
 def parts(refs):
     chips = len(refs) // 2
     own, other = refs[:chips][::-1], refs[chips:][::-1]
@@ -92,12 +96,11 @@
     return pl.BlockSpec(memory_space=pltpu.SMEM)
 
 
-def prepare_kernel(
-    row_ref, col_ref, ids_hbm, floor_hbm, p_hbm, s_hbm, rho_hbm, pert_hbm, out_ref,
-    ids, floors, p, s, rho, pert, sems,
-):
+def prepare_kernel(near, row_ref, col_ref, *refs):
+    ids_hbm, floor_hbm, p_hbm, s_hbm, rho_hbm, pert_hbm = refs[:6]
+    out_refs = refs[6:6 + near]
+    ids, floors, p, s, rho, pert, coef, sems = refs[6 + near:]
     slots, block_x, block_y, depth = p.shape
-    near = block_x
     copies = [
         pltpu.make_async_copy(source, target, sems.at[index])
         for index, (source, target) in enumerate(
@@ -113,6 +116,7 @@
     same = lax.broadcasted_iota(jnp.int32, (block_y, block_y), 0) == (
         lax.broadcasted_iota(jnp.int32, (block_y, block_y), 1)
     )
+    place = chip_place(near)
     for copy in copies:
         copy.wait()
     for slot in range(slots):
@@ -124,47 +128,48 @@
             shear = s[slot, x].astype(jnp.float32)
             square = primary * primary
             stiffness = jnp.where(deep >= floor, square + shear * shear, square)
-            coef = speed_factor * stiffness / rho[slot, x].astype(jnp.float32)
-            coef = coef.astype(out_ref.dtype)
-            for piece in range(x, out_ref.shape[0], near):
-                out_ref[piece, 2 * slot] = coef
-                out_ref[piece, 2 * slot + 1] = pert[slot, x]
+            value = speed_factor * stiffness / rho[slot, x].astype(jnp.float32)
+            coef[slot, x] = value.astype(coef.dtype)
     facts = jnp.where(lane == slots, row_ref[0], 0)
     facts = jnp.where(lane == slots + 1, col_ref[0], facts)
     for slot in range(slots):
         facts = jnp.where(lane == slot, ids[slot], facts)
-    facts = facts.astype(jnp.float32).astype(out_ref.dtype)
-    for piece in range(out_ref.shape[0]):
-        out_ref[piece, 2 * slots] = facts
-
-
-def pick_kernel(slots, near, pieces_ref, *refs):
-    chips = near // 2
-    out_refs = refs[:chips][::-1]
-    facts_ref, facts, spots, sem = refs[chips:]
-    count = facts_ref.shape[0]
-    tiles = 2 * slots + 1
-    for piece in range(count):
-        tile = pieces_ref[piece * tiles + 2 * slots].astype(jnp.float32)
-        facts_ref[piece:piece + 1] = tile.astype(jnp.int32)[0:1]
+    facts = facts.astype(jnp.float32).astype(coef.dtype)
+    for j, out_ref in enumerate(out_refs):
+        for slot in range(slots):
+            for r in range(2):
+                x = 2 * (place ^ j) + r
+                out_ref[4 * slot + 2 * r] = coef[slot, x]
+                out_ref[4 * slot + 2 * r + 1] = pert[slot, x]
+        out_ref[4 * slots] = facts
+
+
+def pick_kernel(slots, near, count, *refs):
+    own, other = refs[:count // 2][::-1], refs[count // 2:count][::-1]
+    piece_refs = [ref for pair in zip(own, other) for ref in pair]
+    out_refs = refs[count:count + near][::-1]
+    facts_ref, facts, spots, pieces, sem = refs[count + near:]
+    tiles = 4 * slots + 1
+    for t, piece_ref in enumerate(piece_refs):
+        tile = piece_ref[tiles - 1].astype(jnp.float32)
+        facts_ref[t:t + 1] = tile.astype(jnp.int32)[0:1]
     copy = pltpu.make_async_copy(facts_ref, facts, sem)
     copy.start()
-    me = lax.axis_index("shot")
+    for t, piece_ref in enumerate(piece_refs):
+        pieces[t * tiles:(t + 1) * tiles] = piece_ref[...]
     copy.wait()
-    for piece in range(count):
+    for t in range(count):
         for slot in range(slots):
-            spots[facts[piece, slot]] = piece * tiles + 2 * slot
-    for t in range(near):
-        shot = me ^ t
-        out_ref, start_tile = out_refs[t // 2], t % 2 * APX * APY * 2
-        first = facts[shot, slots] * GRID_COLS + facts[shot, slots + 1]
+            spots[facts[t, slot]] = t * tiles + 4 * slot
+    for k, out_ref in enumerate(out_refs):
+        first = facts[2 * k, slots] * GRID_COLS + facts[2 * k, slots + 1]
         for x in range(APX):
             found = []
             for y in range(APY):
                 spot = spots[first + x * GRID_COLS + y]
-                found += [pieces_ref[spot], pieces_ref[spot + 1]]
+                found += [pieces[spot + tile] for tile in range(4)]
             for index, tile in enumerate(found):
-                out_ref[start_tile + x * APY * 2 + index] = tile
+                out_ref[x * APY * 4 + index] = tile
 
 
 def ends(shape):
@@ -267,9 +272,9 @@
 
 def wave_kernel(near, *refs):
     chips = near // 2
-    model_refs = parts(refs[:near])
-    u_0, g_0, next_ref = refs[near:near + 3]
-    refs = refs[near + 3:]
+    model_refs = refs[:chips][::-1]
+    u_0, g_0, next_ref = refs[chips:chips + 3]
+    refs = refs[chips + 3:]
     out_refs = refs[:chips][::-1]
     kap, con, u_1, u_2, u_3, d_0, d_1, d_2, kb_3, kb_2, kb_1 = refs[chips:chips + 11]
     g_1, g_2, d_3, b_2, b_1, image, result = refs[chips + 11:]
@@ -286,12 +291,13 @@
 
     for k, model_ref in enumerate(model_refs):
         for x in range(APX):
-            at = x * block_x + (place ^ k)
             for y in range(APY):
                 rows = pl.ds(y * block_y, block_y)
-                tile = 2 * (x * APY + y)
-                kap[at, rows] = model_ref[tile].astype(jnp.float32)
-                con[at, rows] = speed_factor * model_ref[tile + 1].astype(jnp.float32)
+                for r in range(2):
+                    at = x * block_x + 2 * (place // 2 ^ k) + r
+                    tile = 4 * (x * APY + y) + 2 * r
+                    kap[at, rows] = model_ref[tile].astype(jnp.float32)
+                    con[at, rows] = speed_factor * model_ref[tile + 1].astype(jnp.float32)
 
     def forward_0(x, carry):
         kaps, cons, grads = strided(kap, x), strided(con, x), registers(g_0, x)
@@ -356,7 +362,7 @@
 
 def wave(models, started):
     span_x, many, _, depth = started[0].shape
-    near = len(models)
+    near = 2 * len(models)
     flat = pltpu.VMEM((span_x, many * LANES, depth), jnp.float32)
     field = pltpu.VMEM((span_x + 1, many, LANES, depth), jnp.float32)
     plain = pltpu.VMEM((span_x, many, LANES, depth), jnp.float32)
@@ -365,7 +371,7 @@
     terms = pl.pallas_call(
         functools.partial(wave_kernel, near),
         out_shape=(out,) * (near // 2),
-        in_specs=[vmem()] * (near + 3),
+        in_specs=[vmem()] * (near // 2 + 3),
         out_specs=(vmem(),) * (near // 2),
         scratch_shapes=[flat] * 2 + [field] * 9 + [plain] * 6
         + [pltpu.VMEM((near, tiles, LANES, depth), jnp.bfloat16)],
@@ -376,16 +382,13 @@
 
 
 def wave_split_depth(models, before, current):
-    near = len(models)
+    chips = len(models)
+    near = 2 * chips
     order = (lax.axis_index("shot") % near) ^ jnp.arange(near)
-    chips = near // 2
-    length = models[0].shape[0] // 2
-    pairs = zip(models[:chips][::-1], models[chips:][::-1])
-    model = jnp.stack([part for own, other in pairs for part in (own[:length], other[length:])])
-    model = model[order]
+    model = jnp.stack(models[::-1])[chip_place(chips) ^ jnp.arange(chips)]
     span_x, span_y, depth = before.shape
-    block_x, tiles, block_y, _ = model.shape
-    grids = model.reshape(block_x, APX, APY, 2, block_y, depth).transpose(3, 1, 0, 2, 4, 5)
+    block_x, block_y = 2 * chips, model.shape[2]
+    grids = model.reshape(chips, APX, APY, 2, 2, block_y, depth).transpose(4, 1, 0, 3, 2, 5, 6)
     grids = grids.reshape(2, span_x, span_y, depth).astype(jnp.float32)
     image = image_scale * propagate(
         grids[0],
@@ -419,8 +422,8 @@
     copy.wait()
 
     for k, terms_ref in enumerate(terms_refs):
-        first = facts[me ^ k, slots] * wide
-        rows = pl.ds(facts[me ^ k, slots + 1] * width, LANES)
+        first = facts[k, slots] * wide
+        rows = pl.ds(facts[k, slots + 1] * width, LANES)
         sums = [
             total[first + tile, rows] + terms_ref[tile].astype(jnp.float32)
             for tile in range(tiles)
@@ -437,7 +440,7 @@
     def give(owner, carry):
         found = []
         for slot in range(slots):
-            block = facts[owner, slot]
+            block = facts[me ^ owner, slot]
             rows = pl.ds(pl.multiple_of(block % GRID_COLS * LANES, LANES), LANES)
             found.append(lined[block // GRID_COLS, rows])
         for slot in range(slots):
@@ -477,26 +480,32 @@
     if split:
         seafloor = seafloor - lax.axis_index("depth") * depth
 
-    near = block_x
-    assert count % near == 0 and near & (near - 1) == 0
+    chips = count // 2
+    near = block_x // 2
+    assert chips % near == 0 and chips & (chips - 1) == 0
 
     def swap(values):
-        own = [
+        return [
             lax.ppermute(values[k], "shot", [(i, i ^ 2 * k) for i in range(count)])
             if k else values[0]
             for k in range(len(values) - 1, -1, -1)
         ]
-        return own + [lax.ppermute(v, "shot", [(i, i ^ 1) for i in range(count)]) for v in own]
-
+
+    def shared(values):
+        return values + [
+            lax.ppermute(value, "shot", [(i, i ^ 1) for i in range(count)]) for value in values
+        ]
+
+    out = jax.ShapeDtypeStruct((4 * slots + 1, block_y, depth), jnp.bfloat16)
     sent = pl.pallas_call(
-        prepare_kernel,
-        out_shape=jax.ShapeDtypeStruct((count, 2 * slots + 1, block_y, depth), jnp.bfloat16),
+        functools.partial(prepare_kernel, near),
+        out_shape=(out,) * near,
         in_specs=[smem()] * 2 + [pl.BlockSpec(memory_space=pltpu.HBM)] * 6,
-        out_specs=vmem(),
+        out_specs=(vmem(),) * near,
         scratch_shapes=[
             pltpu.SMEM(owner_ids.shape, jnp.int32),
             pltpu.VMEM(seafloor.shape, jnp.int32),
-            *[pltpu.VMEM(velocity_p.shape, jnp.bfloat16) for _ in range(4)],
+            *[pltpu.VMEM(velocity_p.shape, jnp.bfloat16) for _ in range(5)],
             pltpu.SemaphoreType.DMA((6,)),
         ],
         name="prepare",
@@ -504,41 +513,38 @@
         corner_x, corner_y, owner_ids, seafloor,
         velocity_p, velocity_s, density, perturbation,
     )
-    pieces = lax.all_to_all(sent, "shot", 0, 0, tiled=True)
-
-    if not split:
-        started = start(wave_prev[0], wave_now[0])
-        pieces, started = lax.optimization_barrier((pieces, started))
+    pieces = shared(swap([sent[k % near] for k in range(chips)]))
     *picked, facts = pl.pallas_call(
-        functools.partial(pick_kernel, slots, near),
+        functools.partial(pick_kernel, slots, near, count),
         out_shape=(
-            *[jax.ShapeDtypeStruct((patch * 4, block_y, depth), jnp.bfloat16)] * (near // 2),
+            *[jax.ShapeDtypeStruct((patch * 4, block_y, depth), jnp.bfloat16)] * near,
             jax.ShapeDtypeStruct((count, depth), jnp.int32),
         ),
-        in_specs=[vmem()],
-        out_specs=(vmem(),) * (near // 2 + 1),
+        in_specs=[vmem()] * count,
+        out_specs=(vmem(),) * (near + 1),
         scratch_shapes=[
             pltpu.SMEM((count, depth), jnp.int32),
             pltpu.SMEM((count * slots,), jnp.int32),
+            pltpu.VMEM((count * (4 * slots + 1), block_y, depth), jnp.bfloat16),
             pltpu.SemaphoreType.DMA,
         ],
         compiler_params=limit(3),
         name="pick",
-    )(pieces.reshape(count * (2 * slots + 1), block_y, depth))
+    )(*pieces)
     models = swap(picked[::-1])
 
     if split:
         terms = wave_split_depth(models, wave_prev[0], wave_now[0])
     else:
-        terms = wave(models, started)
-    terms = swap(terms)
+        terms = wave(models, start(wave_prev[0], wave_now[0]))
+    terms = shared(swap(terms))
 
     grid_rows = count * slots // GRID_COLS
     wide = terms[0].shape[0] // 2 // APX
     sums = pl.pallas_call(
-        functools.partial(stack_kernel, slots, near),
+        functools.partial(stack_kernel, slots, 2 * near),
         out_shape=jax.ShapeDtypeStruct((count, slots, block_y, depth), jnp.bfloat16),
-        in_specs=[vmem()] * (near + 1),
+        in_specs=[vmem()] * (2 * near + 1),
         out_specs=vmem(),
         scratch_shapes=[
             pltpu.SMEM(facts.shape, jnp.int32),

time: 57.6 us -> 59.4 us (1.031)
  waiting for transfers between devices: 20.4 us -> 14 us
  starting transfers between devices: 15.3 us -> 21.4 us
  blocking collectives: 11.3 us -> 12.8 us
  local copies, waits for them, and re-layouts: 0.01 us -> 0.77 us
    ppermute x6 -> x13, starting transfers between devices: 7.11 us -> 19.7 us  [swap(): lax.ppermute(values[k], 'shot', [(i, i ^ 2 * k) for i in range(count)])]
    all_to_all x1 -> x0, waiting for transfers between devices: 9.85 us -> none  [per_device(): pieces = lax.all_to_all(sent, 'shot', 0, 0, tiled=True)]
    all_to_all x1 -> x0, starting transfers between devices: 7.5 us -> none  [per_device(): pieces = lax.all_to_all(sent, 'shot', 0, 0, tiled=True)]
    ppermute x6 -> x13, waiting for transfers between devices: 8 us -> 11.7 us  [swap(): lax.ppermute(values[k], 'shot', [(i, i ^ 2 * k) for i in range(count)])]
    all_to_all x1, blocking collectives: 11.3 us -> 12.8 us  [per_device(): sums = lax.all_to_all(sums, 'shot', 0, 0, tiled=True)]
    ppermute x8 -> x12, starting transfers between devices: 0.66 us -> 1.68 us  [shared(): lax.ppermute(value, 'shot', [(i, i ^ 1) for i in range(count)])]
    unnamed x4 -> x6, local copies, waits for them, and re-layouts: 0.01 us -> 0.77 us
    ppermute x8 -> x12, waiting for transfers between devices: 2.56 us -> 2.33 us  [shared(): lax.ppermute(value, 'shot', [(i, i ^ 1) for i in range(count)])]
  transfers between devices with their start and end apart: 15 -> 25, of which waited for: 12 -> 13; matrix products, arithmetic and copies ran while one was open for 0% -> 0% of each run, Pallas kernels for 1% -> 1%
where the time goes in v7:
time: 59.4 us; the launch traced here: 59.2 us
  starting transfers between devices  21.4 us (36%)
  waiting for transfers between devices  14 us (24%)
  blocking collectives  12.8 us (22%)
  Pallas kernels  8.75 us (15%)
  between operations  1.38 us (2%)
  local copies, waits for them, and re-layouts  0.77 us (1%)
    ppermute x13, starting transfers between devices, swap(): lax.ppermute(values[k], 'shot', [(i, i ^ 2 * k) for i in range(count)])  19.7 us
    all_to_all x1, blocking collectives, per_device(): sums = lax.all_to_all(sums, 'shot', 0, 0, tiled=True)  12.8 us
    ppermute x13, waiting for transfers between devices, swap(): lax.ppermute(values[k], 'shot', [(i, i ^ 2 * k) for i in range(count)])  11.7 us
    pallas_call x1, Pallas kernels, wave(): pl.pallas_call(functools.partial(wave_kernel, near), out_shape=(out,) * (...  3.57 us
    ppermute x12, waiting for transfers between devices, shared(): lax.ppermute(value, 'shot', [(i, i ^ 1) for i in range(count)])  2.33 us
    pallas_call x1, Pallas kernels, per_device(): pl.pallas_call(functools.partial(prepare_kernel, near), out_shape=(out,)...  1.77 us
    ppermute x12, starting transfers between devices, shared(): lax.ppermute(value, 'shot', [(i, i ^ 1) for i in range(count)])  1.68 us
    pallas_call x1, Pallas kernels, per_device(): pl.pallas_call(functools.partial(stack_kernel, slots, 2 * near), out_shap...  1.21 us
  transfers between devices with their start and end apart: 25, of which 13 were waited for; matrix products, arithmetic and copies ran while one was open for 0% of the time, Pallas kernels for 1%

profile of v7, /device:TPU:0, one launch (start us, length us, event | category | flops | bytes accessed | tf_op | source)
XLA Modules:
  0.0 59.2 jit_solution(13555513556416917902)
XLA Ops:
  1.3 1.8 %prepare.1 = (bf16[17,8,128]{2,1,0:T(8,128)(2,1)}, bf16[17,8,128]{2,1,0:T(8,128)(2,1)}, bf16[17,8,128]{2,1,0:T(8,128)(2,1)}, bf16[17,8,128]{2,1,0:T(8,128)(2,1)}) custom-call(s32[1]{0:T(128)S(6)} %copy.11.row_ref, s32[1]{0:T(128)S(6)} %copy.12.col_ref, s32[4]{0:T(128)} %refs_0_.1, s32[4,8,8]{2,1,0:T(8,128)} %refs_1_.1, bf16[4,8,8,128]{3,2,1,0:T(8,128)(2,1)} %refs_2_.1, ...), custom_call_target="tpu_custom_call" | custom-call | tf_op jit(solution)/shard_map/prepare/pallas_call | solution.py:500
  3.1 4.0 %collective-permute-start.4 = (bf16[17,8,128]{2,1,0:T(8,128)(2,1)}, bf16[17,8,128]{2,1,0:T(8,128)(2,1)S(1)}, u32[]{:S(2)}, u32[]{:S(2)}) collective-permute-start(bf16[17,8,128]{2,1,0:T(8,128)(2,1)} %get-tuple-element.21), channel_id=1, source_target_pairs={{0,6},{1,7},{2,4},{3,5},{4,2},{5,3},{6,0},{7,1},{8,14},{9,15},{10,... | collective-permute-start | bytes 104456 | tf_op jit(solution)/shard_map/ppermute | solution.py:489
  7.1 2.4 %collective-permute-start = (bf16[17,8,128]{2,1,0:T(8,128)(2,1)}, bf16[17,8,128]{2,1,0:T(8,128)(2,1)S(1)}, u32[]{:S(2)}, u32[]{:S(2)}) collective-permute-start(bf16[17,8,128]{2,1,0:T(8,128)(2,1)} %get-tuple-element.21), channel_id=1, source_target_pairs={{0,14},{1,15},{2,12},{3,13},{4,10},{5,11},{6,8},{7,9},{8,6},{9,7},... | collective-permute-start | bytes 104456 | tf_op jit(solution)/shard_map/ppermute | solution.py:489
  9.5 0.7 %collective-permute-start.5 = (bf16[17,8,128]{2,1,0:T(8,128)(2,1)}, bf16[17,8,128]{2,1,0:T(8,128)(2,1)S(1)}, u32[]{:S(2)}, u32[]{:S(2)}) collective-permute-start(bf16[17,8,128]{2,1,0:T(8,128)(2,1)} %get-tuple-element.22), channel_id=1, source_target_pairs={{0,4},{1,5},{2,6},{3,7},{4,0},{5,1},{6,2},{7,3},{8,12},{9,13},{10,... | collective-permute-start | bytes 104456 | tf_op jit(solution)/shard_map/ppermute | solution.py:489
  10.2 0.9 %collective-permute-start.1 = (bf16[17,8,128]{2,1,0:T(8,128)(2,1)}, bf16[17,8,128]{2,1,0:T(8,128)(2,1)S(1)}, u32[]{:S(2)}, u32[]{:S(2)}) collective-permute-start(bf16[17,8,128]{2,1,0:T(8,128)(2,1)} %get-tuple-element.22), channel_id=1, source_target_pairs={{0,12},{1,13},{2,14},{3,15},{4,8},{5,9},{6,10},{7,11},{8,4},{9,5},... | collective-permute-start | bytes 104456 | tf_op jit(solution)/shard_map/ppermute | solution.py:489
  11.2 1.2 %collective-permute-start.6 = (bf16[17,8,128]{2,1,0:T(8,128)(2,1)}, bf16[17,8,128]{2,1,0:T(8,128)(2,1)S(1)}, u32[]{:S(2)}, u32[]{:S(2)}) collective-permute-start(bf16[17,8,128]{2,1,0:T(8,128)(2,1)} %get-tuple-element.23), channel_id=1, source_target_pairs={{0,2},{1,3},{2,0},{3,1},{4,6},{5,7},{6,4},{7,5},{8,10},{9,11},{10,... | collective-permute-start | bytes 104456 | tf_op jit(solution)/shard_map/ppermute | solution.py:489
  12.4 0.0 collective-permute-done.4.refs_4_
  12.4 2.1 %collective-permute-start.2 = (bf16[17,8,128]{2,1,0:T(8,128)(2,1)}, bf16[17,8,128]{2,1,0:T(8,128)(2,1)S(1)}, u32[]{:S(2)}, u32[]{:S(2)}) collective-permute-start(bf16[17,8,128]{2,1,0:T(8,128)(2,1)} %get-tuple-element.23), channel_id=1, source_target_pairs={{0,10},{1,11},{2,8},{3,9},{4,14},{5,15},{6,12},{7,13},{8,2},{9,3},... | collective-permute-start | bytes 104456 | tf_op jit(solution)/shard_map/ppermute | solution.py:489
  14.5 0.0 collective-permute-done.refs_0_
  14.5 0.0 copy-start
  14.5 0.0 copy-start.1
  14.5 0.0 collective-permute-start.14
  14.5 0.0 collective-permute-done.5.refs_5_
  14.5 1.2 %collective-permute-start.3 = (bf16[17,8,128]{2,1,0:T(8,128)(2,1)}, bf16[17,8,128]{2,1,0:T(8,128)(2,1)S(1)}, u32[]{:S(2)}, u32[]{:S(2)}) collective-permute-start(bf16[17,8,128]{2,1,0:T(8,128)(2,1)} %get-tuple-element.24.refs_7_), channel_id=1, source_target_pairs={{0,8},{1,9},{2,10},{3,11},{4,12},{5,13},{6,14},{7,15},{8,0},{9,1},... | collective-permute-start | bytes 104456 | tf_op jit(solution)/shard_map/ppermute | solution.py:489
  15.8 0.4 collective-permute-done.1.refs_1_
  16.2 0.0 collective-permute-start.11
  16.2 0.0 collective-permute-done.6.refs_6_
  16.2 0.5 collective-permute-start.7
  16.7 1.6 %collective-permute-done.2.refs_2_ = bf16[17,8,128]{2,1,0:T(8,128)(2,1)S(1)} collective-permute-done((bf16[17,8,128]{2,1,0:T(8,128)(2,1)}, bf16[17,8,128]{2,1,0:T(8,128)(2,1)S(1)}, u32[]{:S(2)}, u32[]{:S(2)}) %collective-permute-start.2) | collective-permute-done | bytes 34848 | tf_op jit(solution)/shard_map/ppermute | solution.py:489
  18.3 0.0 collective-permute-start.12
  18.3 0.0 collective-permute-done.14.refs_15_
  18.3 0.5 collective-permute-start.8
  18.9 0.8 %collective-permute-done.3.refs_3_ = bf16[17,8,128]{2,1,0:T(8,128)(2,1)S(1)} collective-permute-done((bf16[17,8,128]{2,1,0:T(8,128)(2,1)}, bf16[17,8,128]{2,1,0:T(8,128)(2,1)S(1)}, u32[]{:S(2)}, u32[]{:S(2)}) %collective-permute-start.3) | collective-permute-done | bytes 34848 | tf_op jit(solution)/shard_map/ppermute | solution.py:489
  19.6 0.0 collective-permute-start.13
  19.6 0.0 collective-permute-done.11.refs_12_
  19.6 0.5 collective-permute-start.9
  20.2 0.0 collective-permute-done.7.refs_8_
  20.2 0.1 collective-permute-start.10
  20.2 0.0 collective-permute-done.12.refs_13_
  20.2 0.0 collective-permute-done.8.refs_9_
  20.2 0.6 %collective-permute-done.13.refs_14_ = bf16[17,8,128]{2,1,0:T(8,128)(2,1)S(1)} collective-permute-done((bf16[17,8,128]{2,1,0:T(8,128)(2,1)S(1)}, bf16[17,8,128]{2,1,0:T(8,128)(2,1)S(1)}, u32[]{:S(2)}, u32[]{:S(2)}) %collective-permute-start.13) | collective-permute-done | bytes 34848 | tf_op jit(solution)/shard_map/ppermute | solution.py:496
  20.8 0.2 collective-permute-done.9.refs_10_
  21.0 0.4 collective-permute-done.10.refs_11_
  21.4 0.0 copy-start.2
  21.4 0.8 %copy-done.2 = bf16[17,8,128]{2,1,0:T(8,128)(2,1)S(1)} copy-done((bf16[17,8,128]{2,1,0:T(8,128)(2,1)S(1)}, bf16[17,8,128]{2,1,0:T(8,128)(2,1)}, u32[]{:S(2)}) %copy-start.2) | copy-done | bytes 34840
  22.1 0.8 %pick.1 = (bf16[64,8,128]{2,1,0:T(8,128)(2,1)S(1)}, bf16[64,8,128]{2,1,0:T(8,128)(2,1)S(1)}, bf16[64,8,128]{2,1,0:T(8,128)(2,1)S(1)}, bf16[64,8,128]{2,1,0:T(8,128)(2,1)S(1)}, s32[16,128]{1,0:T(8,128)S(1)}) custom-call(bf16[17,8,128]{2,1,0:T(8,128)(2,1)S(1)} %collective-permute-done.refs_0_, bf16[17,8,128]{2,1,0:T(8,128)(2,1)S(1)} %collective-permute-done.1.refs_1_, ...), custom_call_target="tpu_custom_call" | custom-call | tf_op jit(solution)/shard_map/pick/pallas_call | solution.py:517
  23.0 2.6 %collective-permute-start.15 = (bf16[64,8,128]{2,1,0:T(8,128)(2,1)S(1)}, bf16[64,8,128]{2,1,0:T(8,128)(2,1)S(1)}, u32[]{:S(2)}, u32[]{:S(2)}) collective-permute-start(bf16[64,8,128]{2,1,0:T(8,128)(2,1)S(1)} %get-tuple-element.26), channel_id=1, source_target_pairs={{0,6},{1,7},{2,4},{3,5},{4,2},{5,3},{6,0},{7,1},{8,14},{9,15},{10,... | collective-permute-start | bytes 393224 | tf_op jit(solution)/shard_map/ppermute | solution.py:489
  25.5 0.4 collective-permute-start.16
  26.0 0.5 collective-permute-start.17
  26.5 0.0 copy-done
  26.5 0.0 copy-done.1
  26.5 0.7 %start.1 = (f32[32,4,8,128]{3,2,1,0:T(8,128)S(1)}, f32[32,4,8,128]{3,2,1,0:T(8,128)S(1)}, f32[32,4,8,128]{3,2,1,0:T(8,128)S(1)}) custom-call(bf16[32,32,128]{2,1,0:T(8,128)(2,1)S(1)} %bitcast.2, bf16[32,32,128]{2,1,0:T(8,128)(2,1)S(1)} %bitcast.3), custom_call_target="tpu_custom_call" | custom-call | flops 2621440 | bytes 2097152 | tf_op jit(solution)/shard_map/start/pallas_call | solution.py:259
  27.2 3.1 %collective-permute-done.15.refs_0_ = bf16[64,8,128]{2,1,0:T(8,128)(2,1)S(1)} collective-permute-done((bf16[64,8,128]{2,1,0:T(8,128)(2,1)S(1)}, bf16[64,8,128]{2,1,0:T(8,128)(2,1)S(1)}, u32[]{:S(2)}, u32[]{:S(2)}) %collective-permute-start.15) | collective-permute-done | bytes 131104 | tf_op jit(solution)/shard_map/ppermute | solution.py:489
  30.3 2.1 %collective-permute-done.16.refs_1_ = bf16[64,8,128]{2,1,0:T(8,128)(2,1)S(1)} collective-permute-done((bf16[64,8,128]{2,1,0:T(8,128)(2,1)S(1)}, bf16[64,8,128]{2,1,0:T(8,128)(2,1)S(1)}, u32[]{:S(2)}, u32[]{:S(2)}) %collective-permute-start.16) | collective-permute-done | bytes 131104 | tf_op jit(solution)/shard_map/ppermute | solution.py:489
  32.3 0.0 collective-permute-done.17.refs_2_
  32.3 3.6 %wave.1 = (bf16[32,8,128]{2,1,0:T(8,128)(2,1)S(1)}, bf16[32,8,128]{2,1,0:T(8,128)(2,1)S(1)}, bf16[32,8,128]{2,1,0:T(8,128)(2,1)S(1)}, bf16[32,8,128]{2,1,0:T(8,128)(2,1)S(1)}) custom-call(bf16[64,8,128]{2,1,0:T(8,128)(2,1)S(1)} %collective-permute-done.15.refs_0_, bf16[64,8,128]{2,1,0:T(8,128)(2,1)S(1)} %collective-permute-done.16.refs_1_, ...), custom_call_target="tpu_custom_call" | custom-call | tf_op jit(solution)/shard_map/wave/pallas_call | solution.py:371
  35.9 2.5 %collective-permute-start.18 = (bf16[32,8,128]{2,1,0:T(8,128)(2,1)S(1)}, bf16[32,8,128]{2,1,0:T(8,128)(2,1)S(1)}, u32[]{:S(2)}, u32[]{:S(2)}) collective-permute-start(bf16[32,8,128]{2,1,0:T(8,128)(2,1)S(1)} %get-tuple-element.33), channel_id=1, source_target_pairs={{0,6},{1,7},{2,4},{3,5},{4,2},{5,3},{6,0},{7,1},{8,14},{9,15},{10,... | collective-permute-start | bytes 196616 | tf_op jit(solution)/shard_map/ppermute | solution.py:489
  38.5 0.4 collective-permute-start.19
  38.9 0.6 collective-permute-start.20
  39.5 0.0 collective-permute-start.24
  39.5 2.4 %collective-permute-done.18.refs_0_ = bf16[32,8,128]{2,1,0:T(8,128)(2,1)S(1)} collective-permute-done((bf16[32,8,128]{2,1,0:T(8,128)(2,1)S(1)}, bf16[32,8,128]{2,1,0:T(8,128)(2,1)S(1)}, u32[]{:S(2)}, u32[]{:S(2)}) %collective-permute-start.18) | collective-permute-done | bytes 65568 | tf_op jit(solution)/shard_map/ppermute | solution.py:489
  41.9 0.0 collective-permute-start.21
  41.9 0.8 %collective-permute-done.19.refs_1_ = bf16[32,8,128]{2,1,0:T(8,128)(2,1)S(1)} collective-permute-done((bf16[32,8,128]{2,1,0:T(8,128)(2,1)S(1)}, bf16[32,8,128]{2,1,0:T(8,128)(2,1)S(1)}, u32[]{:S(2)}, u32[]{:S(2)}) %collective-permute-start.19) | collective-permute-done | bytes 65568 | tf_op jit(solution)/shard_map/ppermute | solution.py:489
  42.7 0.0 collective-permute-start.22
  42.7 0.4 collective-permute-done.20.refs_2_
  43.2 0.1 collective-permute-start.23
  43.2 0.0 collective-permute-done.24.refs_7_
  43.2 0.0 collective-permute-done.21.refs_4_
  43.3 0.7 %collective-permute-done.22.refs_5_ = bf16[32,8,128]{2,1,0:T(8,128)(2,1)S(1)} collective-permute-done((bf16[32,8,128]{2,1,0:T(8,128)(2,1)S(1)}, bf16[32,8,128]{2,1,0:T(8,128)(2,1)S(1)}, u32[]{:S(2)}, u32[]{:S(2)}) %collective-permute-start.22) | collective-permute-done | bytes 65568 | tf_op jit(solution)/shard_map/ppermute | solution.py:496
  44.0 0.4 collective-permute-done.23.refs_6_
  44.4 1.2 %stack.1 = bf16[16,4,8,128]{3,2,1,0:T(8,128)(2,1)S(1)} custom-call(s32[16,128]{1,0:T(8,128)S(1)} %get-tuple-element.25.facts_ref, bf16[32,8,128]{2,1,0:T(8,128)(2,1)S(1)} %collective-permute-done.18.refs_0_, bf16[32,8,128]{2,1,0:T(8,128)(2,1)S(1)} %collective-permute-done.19.refs_1_, bf16[32,8,128]{2,1,0:T(8,128)(2,1)S(1)} %collective-permute-done.20.refs_2_, ...), custom_call_target="tpu_custom_call" | custom-call | tf_op jit(solution)/shard_map/stack/pallas_call | solution.py:544
  45.6 12.8 %all_to_all.5.sums_ref = bf16[16,4,8,128]{3,2,1,0:T(8,128)(2,1)S(1)} all-to-all(bf16[16,4,8,128]{3,2,1,0:T(8,128)(2,1)S(1)} %stack.1), channel_id=1, replica_groups=mesh['grp'=2,'shot'=16,'depth'=1] {'shot'}, dimensions={0} | all-to-all | bytes 262144 | tf_op jit(solution)/shard_map/all_to_all | solution.py:558
  58.5 0.7 %finish.1 = f32[4,8,8,128]{3,2,1,0:T(8,128)} custom-call(bf16[16,4,8,128]{3,2,1,0:T(8,128)(2,1)S(1)} %all_to_all.5.sums_ref), custom_call_target="tpu_custom_call" | custom-call | tf_op jit(solution)/shard_map/finish/pallas_call | solution.py:559
Async XLA Ops:
  3.1 9.3 %collective-permute-start.4 = (bf16[17,8,128]{2,1,0:T(8,128)(2,1)}, bf16[17,8,128]{2,1,0:T(8,128)(2,1)S(1)}, u32[]{:S(2)}, u32[]{:S(2)}) collective-permute-start(bf16[17,8,128]{2,1,0:T(8,128)(2,1)} %get-tuple-element.21), channel_id=1, source_target_pairs={{0,6},{1,7},{2,4},{3,5},{4,2},{5,3},{6,0},{7,1},{8,14},{9,15},{10,... | collective-permute-start | bytes 104456 | tf_op jit(solution)/shard_map/ppermute | solution.py:489
  7.1 7.4 %collective-permute-start = (bf16[17,8,128]{2,1,0:T(8,128)(2,1)}, bf16[17,8,128]{2,1,0:T(8,128)(2,1)S(1)}, u32[]{:S(2)}, u32[]{:S(2)}) collective-permute-start(bf16[17,8,128]{2,1,0:T(8,128)(2,1)} %get-tuple-element.21), channel_id=1, source_target_pairs={{0,14},{1,15},{2,12},{3,13},{4,10},{5,11},{6,8},{7,9},{8,6},{9,7},... | collective-permute-start | bytes 104456 | tf_op jit(solution)/shard_map/ppermute | solution.py:489
  9.5 5.0 %collective-permute-start.5 = (bf16[17,8,128]{2,1,0:T(8,128)(2,1)}, bf16[17,8,128]{2,1,0:T(8,128)(2,1)S(1)}, u32[]{:S(2)}, u32[]{:S(2)}) collective-permute-start(bf16[17,8,128]{2,1,0:T(8,128)(2,1)} %get-tuple-element.22), channel_id=1, source_target_pairs={{0,4},{1,5},{2,6},{3,7},{4,0},{5,1},{6,2},{7,3},{8,12},{9,13},{10,... | collective-permute-start | bytes 104456 | tf_op jit(solution)/shard_map/ppermute | solution.py:489
  10.2 5.9 %collective-permute-start.1 = (bf16[17,8,128]{2,1,0:T(8,128)(2,1)}, bf16[17,8,128]{2,1,0:T(8,128)(2,1)S(1)}, u32[]{:S(2)}, u32[]{:S(2)}) collective-permute-start(bf16[17,8,128]{2,1,0:T(8,128)(2,1)} %get-tuple-element.22), channel_id=1, source_target_pairs={{0,12},{1,13},{2,14},{3,15},{4,8},{5,9},{6,10},{7,11},{8,4},{9,5},... | collective-permute-start | bytes 104456 | tf_op jit(solution)/shard_map/ppermute | solution.py:489
  11.2 5.0 %collective-permute-start.6 = (bf16[17,8,128]{2,1,0:T(8,128)(2,1)}, bf16[17,8,128]{2,1,0:T(8,128)(2,1)S(1)}, u32[]{:S(2)}, u32[]{:S(2)}) collective-permute-start(bf16[17,8,128]{2,1,0:T(8,128)(2,1)} %get-tuple-element.23), channel_id=1, source_target_pairs={{0,2},{1,3},{2,0},{3,1},{4,6},{5,7},{6,4},{7,5},{8,10},{9,11},{10,... | collective-permute-start | bytes 104456 | tf_op jit(solution)/shard_map/ppermute | solution.py:489
  12.4 5.9 %collective-permute-start.2 = (bf16[17,8,128]{2,1,0:T(8,128)(2,1)}, bf16[17,8,128]{2,1,0:T(8,128)(2,1)S(1)}, u32[]{:S(2)}, u32[]{:S(2)}) collective-permute-start(bf16[17,8,128]{2,1,0:T(8,128)(2,1)} %get-tuple-element.23), channel_id=1, source_target_pairs={{0,10},{1,11},{2,8},{3,9},{4,14},{5,15},{6,12},{7,13},{8,2},{9,3},... | collective-permute-start | bytes 104456 | tf_op jit(solution)/shard_map/ppermute | solution.py:489
  14.5 12.0 %copy-start = (bf16[1,32,32,128]{3,2,1,0:T(8,128)(2,1)S(1)}, bf16[1,32,32,128]{3,2,1,0:T(8,128)(2,1)}, u32[]{:S(2)}) copy-start(bf16[1,32,32,128]{3,2,1,0:T(8,128)(2,1)} %param.18) | copy-start | bytes 786436
  14.5 12.0 %copy-start.1 = (bf16[1,32,32,128]{3,2,1,0:T(8,128)(2,1)S(1)}, bf16[1,32,32,128]{3,2,1,0:T(8,128)(2,1)}, u32[]{:S(2)}) copy-start(bf16[1,32,32,128]{3,2,1,0:T(8,128)(2,1)} %param.19) | copy-start | bytes 786436
  14.5 3.8 %collective-permute-start.14 = (bf16[17,8,128]{2,1,0:T(8,128)(2,1)}, bf16[17,8,128]{2,1,0:T(8,128)(2,1)S(1)}, u32[]{:S(2)}, u32[]{:S(2)}) collective-permute-start(bf16[17,8,128]{2,1,0:T(8,128)(2,1)} %get-tuple-element.24.refs_7_), channel_id=1, source_target_pairs={{0,1},{1,0},{2,3},{3,2},{4,5},{5,4},{6,7},{7,6},{8,9},{9,8},{10,11... | collective-permute-start | bytes 104456 | tf_op jit(solution)/shard_map/ppermute | solution.py:496
  14.5 5.1 %collective-permute-start.3 = (bf16[17,8,128]{2,1,0:T(8,128)(2,1)}, bf16[17,8,128]{2,1,0:T(8,128)(2,1)S(1)}, u32[]{:S(2)}, u32[]{:S(2)}) collective-permute-start(bf16[17,8,128]{2,1,0:T(8,128)(2,1)} %get-tuple-element.24.refs_7_), channel_id=1, source_target_pairs={{0,8},{1,9},{2,10},{3,11},{4,12},{5,13},{6,14},{7,15},{8,0},{9,1},... | collective-permute-start | bytes 104456 | tf_op jit(solution)/shard_map/ppermute | solution.py:489
  16.2 3.5 %collective-permute-start.11 = (bf16[17,8,128]{2,1,0:T(8,128)(2,1)S(1)}, bf16[17,8,128]{2,1,0:T(8,128)(2,1)S(1)}, u32[]{:S(2)}, u32[]{:S(2)}) collective-permute-start(bf16[17,8,128]{2,1,0:T(8,128)(2,1)S(1)} %collective-permute-done.4.refs_4_), channel_id=1, source_target_pairs={{0,1},{1,0},{2,3},{3,2},{4,5},{5,4},{6,7},{7,6},{8,9},{9,8},{10,11... | collective-permute-start | bytes 104456 | tf_op jit(solution)/shard_map/ppermute | solution.py:496
  16.2 4.0 %collective-permute-start.7 = (bf16[17,8,128]{2,1,0:T(8,128)(2,1)S(1)}, bf16[17,8,128]{2,1,0:T(8,128)(2,1)S(1)}, u32[]{:S(2)}, u32[]{:S(2)}) collective-permute-start(bf16[17,8,128]{2,1,0:T(8,128)(2,1)S(1)} %collective-permute-done.refs_0_), channel_id=1, source_target_pairs={{0,1},{1,0},{2,3},{3,2},{4,5},{5,4},{6,7},{7,6},{8,9},{9,8},{10,11... | collective-permute-start | bytes 104456 | tf_op jit(solution)/shard_map/ppermute | solution.py:496
  18.3 1.9 %collective-permute-start.12 = (bf16[17,8,128]{2,1,0:T(8,128)(2,1)S(1)}, bf16[17,8,128]{2,1,0:T(8,128)(2,1)S(1)}, u32[]{:S(2)}, u32[]{:S(2)}) collective-permute-start(bf16[17,8,128]{2,1,0:T(8,128)(2,1)S(1)} %collective-permute-done.5.refs_5_), channel_id=1, source_target_pairs={{0,1},{1,0},{2,3},{3,2},{4,5},{5,4},{6,7},{7,6},{8,9},{9,8},{10,11... | collective-permute-start | bytes 104456 | tf_op jit(solution)/shard_map/ppermute | solution.py:496
  18.3 1.9 %collective-permute-start.8 = (bf16[17,8,128]{2,1,0:T(8,128)(2,1)S(1)}, bf16[17,8,128]{2,1,0:T(8,128)(2,1)S(1)}, u32[]{:S(2)}, u32[]{:S(2)}) collective-permute-start(bf16[17,8,128]{2,1,0:T(8,128)(2,1)S(1)} %collective-permute-done.1.refs_1_), channel_id=1, source_target_pairs={{0,1},{1,0},{2,3},{3,2},{4,5},{5,4},{6,7},{7,6},{8,9},{9,8},{10,11... | collective-permute-start | bytes 104456 | tf_op jit(solution)/shard_map/ppermute | solution.py:496
  19.6 1.2 %collective-permute-start.13 = (bf16[17,8,128]{2,1,0:T(8,128)(2,1)S(1)}, bf16[17,8,128]{2,1,0:T(8,128)(2,1)S(1)}, u32[]{:S(2)}, u32[]{:S(2)}) collective-permute-start(bf16[17,8,128]{2,1,0:T(8,128)(2,1)S(1)} %collective-permute-done.6.refs_6_), channel_id=1, source_target_pairs={{0,1},{1,0},{2,3},{3,2},{4,5},{5,4},{6,7},{7,6},{8,9},{9,8},{10,11... | collective-permute-start | bytes 104456 | tf_op jit(solution)/shard_map/ppermute | solution.py:496
  19.6 1.4 %collective-permute-start.9 = (bf16[17,8,128]{2,1,0:T(8,128)(2,1)S(1)}, bf16[17,8,128]{2,1,0:T(8,128)(2,1)S(1)}, u32[]{:S(2)}, u32[]{:S(2)}) collective-permute-start(bf16[17,8,128]{2,1,0:T(8,128)(2,1)S(1)} %collective-permute-done.2.refs_2_), channel_id=1, source_target_pairs={{0,1},{1,0},{2,3},{3,2},{4,5},{5,4},{6,7},{7,6},{8,9},{9,8},{10,11... | collective-permute-start | bytes 104456 | tf_op jit(solution)/shard_map/ppermute | solution.py:496
  20.2 1.2 %collective-permute-start.10 = (bf16[17,8,128]{2,1,0:T(8,128)(2,1)S(1)}, bf16[17,8,128]{2,1,0:T(8,128)(2,1)S(1)}, u32[]{:S(2)}, u32[]{:S(2)}) collective-permute-start(bf16[17,8,128]{2,1,0:T(8,128)(2,1)S(1)} %collective-permute-done.3.refs_3_), channel_id=1, source_target_pairs={{0,1},{1,0},{2,3},{3,2},{4,5},{5,4},{6,7},{7,6},{8,9},{9,8},{10,11... | collective-permute-start | bytes 104456 | tf_op jit(solution)/shard_map/ppermute | solution.py:496
  21.4 0.8 %copy-start.2 = (bf16[17,8,128]{2,1,0:T(8,128)(2,1)S(1)}, bf16[17,8,128]{2,1,0:T(8,128)(2,1)}, u32[]{:S(2)}) copy-start(bf16[17,8,128]{2,1,0:T(8,128)(2,1)} %get-tuple-element.24.refs_7_) | copy-start | bytes 104452
  23.0 7.3 %collective-permute-start.15 = (bf16[64,8,128]{2,1,0:T(8,128)(2,1)S(1)}, bf16[64,8,128]{2,1,0:T(8,128)(2,1)S(1)}, u32[]{:S(2)}, u32[]{:S(2)}) collective-permute-start(bf16[64,8,128]{2,1,0:T(8,128)(2,1)S(1)} %get-tuple-element.26), channel_id=1, source_target_pairs={{0,6},{1,7},{2,4},{3,5},{4,2},{5,3},{6,0},{7,1},{8,14},{9,15},{10,... | collective-permute-start | bytes 393224 | tf_op jit(solution)/shard_map/ppermute | solution.py:489
  25.5 6.8 %collective-permute-start.16 = (bf16[64,8,128]{2,1,0:T(8,128)(2,1)S(1)}, bf16[64,8,128]{2,1,0:T(8,128)(2,1)S(1)}, u32[]{:S(2)}, u32[]{:S(2)}) collective-permute-start(bf16[64,8,128]{2,1,0:T(8,128)(2,1)S(1)} %get-tuple-element.27), channel_id=1, source_target_pairs={{0,4},{1,5},{2,6},{3,7},{4,0},{5,1},{6,2},{7,3},{8,12},{9,13},{10,... | collective-permute-start | bytes 393224 | tf_op jit(solution)/shard_map/ppermute | solution.py:489
  26.0 6.3 %collective-permute-start.17 = (bf16[64,8,128]{2,1,0:T(8,128)(2,1)S(1)}, bf16[64,8,128]{2,1,0:T(8,128)(2,1)S(1)}, u32[]{:S(2)}, u32[]{:S(2)}) collective-permute-start(bf16[64,8,128]{2,1,0:T(8,128)(2,1)S(1)} %get-tuple-element.28), channel_id=1, source_target_pairs={{0,2},{1,3},{2,0},{3,1},{4,6},{5,7},{6,4},{7,5},{8,10},{9,11},{10,... | collective-permute-start | bytes 393224 | tf_op jit(solution)/shard_map/ppermute | solution.py:489
  35.9 6.0 %collective-permute-start.18 = (bf16[32,8,128]{2,1,0:T(8,128)(2,1)S(1)}, bf16[32,8,128]{2,1,0:T(8,128)(2,1)S(1)}, u32[]{:S(2)}, u32[]{:S(2)}) collective-permute-start(bf16[32,8,128]{2,1,0:T(8,128)(2,1)S(1)} %get-tuple-element.33), channel_id=1, source_target_pairs={{0,6},{1,7},{2,4},{3,5},{4,2},{5,3},{6,0},{7,1},{8,14},{9,15},{10,... | collective-permute-start | bytes 196616 | tf_op jit(solution)/shard_map/ppermute | solution.py:489
  38.5 4.3 %collective-permute-start.19 = (bf16[32,8,128]{2,1,0:T(8,128)(2,1)S(1)}, bf16[32,8,128]{2,1,0:T(8,128)(2,1)S(1)}, u32[]{:S(2)}, u32[]{:S(2)}) collective-permute-start(bf16[32,8,128]{2,1,0:T(8,128)(2,1)S(1)} %get-tuple-element.34), channel_id=1, source_target_pairs={{0,4},{1,5},{2,6},{3,7},{4,0},{5,1},{6,2},{7,3},{8,12},{9,13},{10,... | collective-permute-start | bytes 196616 | tf_op jit(solution)/shard_map/ppermute | solution.py:489
  38.9 4.3 %collective-permute-start.20 = (bf16[32,8,128]{2,1,0:T(8,128)(2,1)S(1)}, bf16[32,8,128]{2,1,0:T(8,128)(2,1)S(1)}, u32[]{:S(2)}, u32[]{:S(2)}) collective-permute-start(bf16[32,8,128]{2,1,0:T(8,128)(2,1)S(1)} %get-tuple-element.35), channel_id=1, source_target_pairs={{0,2},{1,3},{2,0},{3,1},{4,6},{5,7},{6,4},{7,5},{8,10},{9,11},{10,... | collective-permute-start | bytes 196616 | tf_op jit(solution)/shard_map/ppermute | solution.py:489
  39.5 3.8 %collective-permute-start.24 = (bf16[32,8,128]{2,1,0:T(8,128)(2,1)S(1)}, bf16[32,8,128]{2,1,0:T(8,128)(2,1)S(1)}, u32[]{:S(2)}, u32[]{:S(2)}) collective-permute-start(bf16[32,8,128]{2,1,0:T(8,128)(2,1)S(1)} %get-tuple-element.36.refs_3_), channel_id=1, source_target_pairs={{0,1},{1,0},{2,3},{3,2},{4,5},{5,4},{6,7},{7,6},{8,9},{9,8},{10,11... | collective-permute-start | bytes 196616 | tf_op jit(solution)/shard_map/ppermute | solution.py:496
  41.9 1.3 %collective-permute-start.21 = (bf16[32,8,128]{2,1,0:T(8,128)(2,1)S(1)}, bf16[32,8,128]{2,1,0:T(8,128)(2,1)S(1)}, u32[]{:S(2)}, u32[]{:S(2)}) collective-permute-start(bf16[32,8,128]{2,1,0:T(8,128)(2,1)S(1)} %collective-permute-done.18.refs_0_), channel_id=1, source_target_pairs={{0,1},{1,0},{2,3},{3,2},{4,5},{5,4},{6,7},{7,6},{8,9},{9,8},{10,11... | collective-permute-start | bytes 196616 | tf_op jit(solution)/shard_map/ppermute | solution.py:496
  42.7 1.3 %collective-permute-start.22 = (bf16[32,8,128]{2,1,0:T(8,128)(2,1)S(1)}, bf16[32,8,128]{2,1,0:T(8,128)(2,1)S(1)}, u32[]{:S(2)}, u32[]{:S(2)}) collective-permute-start(bf16[32,8,128]{2,1,0:T(8,128)(2,1)S(1)} %collective-permute-done.19.refs_1_), channel_id=1, source_target_pairs={{0,1},{1,0},{2,3},{3,2},{4,5},{5,4},{6,7},{7,6},{8,9},{9,8},{10,11... | collective-permute-start | bytes 196616 | tf_op jit(solution)/shard_map/ppermute | solution.py:496
  43.2 1.3 %collective-permute-start.23 = (bf16[32,8,128]{2,1,0:T(8,128)(2,1)S(1)}, bf16[32,8,128]{2,1,0:T(8,128)(2,1)S(1)}, u32[]{:S(2)}, u32[]{:S(2)}) collective-permute-start(bf16[32,8,128]{2,1,0:T(8,128)(2,1)S(1)} %collective-permute-done.20.refs_2_), channel_id=1, source_target_pairs={{0,1},{1,0},{2,3},{3,2},{4,5},{5,4},{6,7},{7,6},{8,9},{9,8},{10,11... | collective-permute-start | bytes 196616 | tf_op jit(solution)/shard_map/ppermute | solution.py:496

commit v8 on v6

--- a/solution.py
+++ b/solution.py
@@ -71,6 +71,10 @@
 
 def limit(mebibytes):
     return pltpu.CompilerParams(vmem_limit_bytes=mebibytes * 2**20)
+
+
+def chip_place(near):
+    return lax.axis_index("shot") // 2 % near
 
 
 def parts(refs):
@@ -243,7 +247,7 @@
         for v in range(many):
             grad_ref[x, v] = grads[v]
 
-    sweep(span_x, [field], body, 16)
+    sweep(span_x, [field], body, 32)
 
 
 def start(before, current):
@@ -301,7 +305,7 @@
             u_1[x, v] = older[v] + kaps[v] * grads[v]
         return carry
 
-    lax.fori_loop(0, span_x, forward_0, 0, unroll=16)
+    lax.fori_loop(0, span_x, forward_0, 0, unroll=32)
 
     def forward(u_now, u_prev, d_now, d_prev, u_next, d_next, g_now):
         def body(x, rows):
@@ -321,7 +325,7 @@
                     g_now[x, v] = grads[v]
                     u_next[x, v] = 2.0 * waves[1][v] - u_prev[x, v] + kaps[v] * grads[v]
 
-        sweep(span_x, [u_now, d_now], body, 16)
+        sweep(span_x, [u_now, d_now], body, 32)
 
     forward(u_1, u_0, d_0, None, u_2, d_1, g_1)
     forward(u_2, u_1, d_1, d_0, u_3, d_2, g_2)
@@ -338,20 +342,19 @@
                 total = image[x, v] + grad[x, v] * back
                 if kb_next is None:
                     total = (image_scale * total).astype(result.dtype)
-                    result[x % block_x, x // block_x * many + v] = total
+                    result[x % block_x // 2, (x % 2 * APX + x // block_x) * many + v] = total
                 else:
                     image[x, v] = total
                     b_next[x, v] = back
                     kb_next[x, v] = kaps[v] * back
 
-        sweep(span_x, [kb], body, 16)
+        sweep(span_x, [kb], body, 32)
 
     adjoint(kb_3, d_3, None, d_2, g_2, kb_2, b_2)
     adjoint(kb_2, b_2, d_3, d_1, g_1, kb_1, b_1)
     adjoint(kb_1, b_1, b_2, d_0, g_0, None, None)
-    length = result.shape[1]
-    for t in range(near):
-        out_refs[t // 2][pl.ds(t % 2 * length, length)] = result[place ^ t]
+    for k, out_ref in enumerate(out_refs):
+        out_ref[...] = result[place // 2 ^ k]
 
 
 def wave(models, started):
@@ -368,7 +371,7 @@
         in_specs=[vmem()] * (near + 3),
         out_specs=(vmem(),) * (near // 2),
         scratch_shapes=[flat] * 2 + [field] * 9 + [plain] * 6
-        + [pltpu.VMEM((near, tiles, LANES, depth), jnp.bfloat16)],
+        + [pltpu.VMEM((near // 2, 2 * tiles, LANES, depth), jnp.bfloat16)],
         compiler_params=limit(20),
         name="wave",
     )(*models, *started)
@@ -395,66 +398,82 @@
         laplace_many,
     )
     many = span_y // LANES
-    image = image.reshape(APX, block_x, LANES, many, depth).transpose(1, 0, 3, 2, 4)
-    image = image.reshape(near, APX * many, LANES, depth).astype(jnp.bfloat16)[order]
-    return [jnp.concatenate([image[2 * k], image[2 * k + 1]]) for k in range(chips)]
+    image = image.reshape(APX, chips, 2, LANES, many, depth).transpose(1, 2, 0, 4, 3, 5)
+    image = image.reshape(chips, 2 * APX * many, LANES, depth).astype(jnp.bfloat16)
+    image = image[chip_place(chips) ^ jnp.arange(chips)]
+    return [image[k] for k in range(chips)]
 
 
 def stack_kernel(slots, near, facts_ref, *refs):
-    terms_refs = parts(refs[:near])
-    out_ref, facts, total, lined, sem = refs[near:]
-    tiles = terms_refs[0].shape[0]
-    wide = tiles // APX
+    terms_refs = refs[:near][::-1]
+    mine_ref, other_ref, facts, total, lined, sem = refs[near:]
+    count = facts_ref.shape[0]
+    half = terms_refs[0].shape[0] // 2
+    wide = half // APX
     width = LANES // APY
-    grid_rows = total.shape[0] // wide
+    grid_rows = total.shape[1] // wide
     copy = pltpu.make_async_copy(facts_ref, facts, sem)
     copy.start()
     me = lax.axis_index("shot")
 
     def clear(index, carry):
-        total[index] = jnp.zeros(total.shape[1:], total.dtype)
+        for r in range(2):
+            total[r, index] = jnp.zeros(total.shape[2:], total.dtype)
         return carry
 
-    lax.fori_loop(0, total.shape[0], clear, 0, unroll=8)
+    lax.fori_loop(0, total.shape[1], clear, 0, unroll=8)
     copy.wait()
-
     for k, terms_ref in enumerate(terms_refs):
-        first = facts[me ^ k, slots] * wide
-        rows = pl.ds(facts[me ^ k, slots + 1] * width, LANES)
-        sums = [
-            total[first + tile, rows] + terms_ref[tile].astype(jnp.float32)
-            for tile in range(tiles)
-        ]
-        for tile in range(tiles):
-            total[first + tile, rows] = sums[tile]
-
-    for row in range(grid_rows):
-        for part in range(wide):
-            for tile in range(total.shape[1] // LANES):
-                at = pl.ds(tile * LANES * wide + part, LANES, stride=wide)
-                lined[row, at] = total[row * wide + part, tile * LANES:(tile + 1) * LANES]
-
-    def give(owner, carry):
-        found = []
-        for slot in range(slots):
-            block = facts[owner, slot]
-            rows = pl.ds(pl.multiple_of(block % GRID_COLS * LANES, LANES), LANES)
-            found.append(lined[block // GRID_COLS, rows])
-        for slot in range(slots):
-            out_ref[owner, slot] = found[slot].astype(out_ref.dtype)
+        first = facts[me ^ 2 * k, slots] * wide
+        rows = pl.ds(facts[me ^ 2 * k, slots + 1] * width, LANES)
+        for r in range(2):
+            sums = [
+                total[r, first + tile, rows] + terms_ref[r * half + tile].astype(jnp.float32)
+                for tile in range(half)
+            ]
+            for tile in range(half):
+                total[r, first + tile, rows] = sums[tile]
+
+    def line(row, carry):
+        for r in range(2):
+            for part in range(wide):
+                for tile in range(total.shape[2] // LANES):
+                    at = pl.ds(tile * LANES * wide + part, LANES, stride=wide)
+                    lined[r, row, at] = total[
+                        r, row * wide + part, tile * LANES:(tile + 1) * LANES
+                    ]
         return carry
 
-    lax.fori_loop(0, out_ref.shape[0], give, 0, unroll=4)
-
-
-def finish_kernel(sums_ref, out_ref):
-    slots, block_x = out_ref.shape[:2]
-    for x in range(block_x):
-        for slot in range(slots):
-            result = sums_ref[x, slot].astype(jnp.float32)
-            for piece in range(x + block_x, sums_ref.shape[0], block_x):
-                result = result + sums_ref[piece, slot].astype(jnp.float32)
-            out_ref[slot, x] = result
+    lax.fori_loop(0, grid_rows, line, 0, unroll=4)
+
+    def give(chip, carry):
+        for own, out_ref in enumerate((mine_ref, other_ref)):
+            found = []
+            for slot in range(slots):
+                block = facts[2 * chip + (me + own) % 2, slot]
+                rows = pl.ds(pl.multiple_of(block % GRID_COLS * LANES, LANES), LANES)
+                found += [lined[r, block // GRID_COLS, rows] for r in range(2)]
+            for index, tile in enumerate(found):
+                out_ref[chip, index] = tile.astype(out_ref.dtype)
+        return carry
+
+    lax.fori_loop(0, count // 2, give, 0, unroll=2)
+
+
+def join_kernel(mine_ref, other_ref, out_ref):
+    for chip in range(out_ref.shape[0]):
+        total = mine_ref[chip] + other_ref[chip].astype(jnp.float32)
+        out_ref[chip] = total.astype(out_ref.dtype)
+
+
+def finish_kernel(near, sums_ref, out_ref):
+    for place in range(near):
+        for slot in range(out_ref.shape[0]):
+            for r in range(2):
+                result = sums_ref[place, 2 * slot + r].astype(jnp.float32)
+                for chip in range(place + near, sums_ref.shape[0], near):
+                    result = result + sums_ref[chip, 2 * slot + r].astype(jnp.float32)
+                out_ref[slot, 2 * place + r] = result
 
 
 def per_device(
@@ -481,12 +500,14 @@
     assert count % near == 0 and near & (near - 1) == 0
 
     def swap(values):
-        own = [
+        return [
             lax.ppermute(values[k], "shot", [(i, i ^ 2 * k) for i in range(count)])
             if k else values[0]
             for k in range(len(values) - 1, -1, -1)
         ]
-        return own + [lax.ppermute(v, "shot", [(i, i ^ 1) for i in range(count)]) for v in own]
+
+    def across(value):
+        return lax.ppermute(value, "shot", [(i, i ^ 1) for i in range(count)])
 
     sent = pl.pallas_call(
         prepare_kernel,
@@ -526,6 +547,7 @@
         name="pick",
     )(pieces.reshape(count * (2 * slots + 1), block_y, depth))
     models = swap(picked[::-1])
+    models = models + [across(value) for value in models]
 
     if split:
         terms = wave_split_depth(models, wave_prev[0], wave_now[0])
@@ -533,25 +555,40 @@
         terms = wave(models, started)
     terms = swap(terms)
 
+    chips = count // 2
     grid_rows = count * slots // GRID_COLS
     wide = terms[0].shape[0] // 2 // APX
-    sums = pl.pallas_call(
-        functools.partial(stack_kernel, slots, near),
-        out_shape=jax.ShapeDtypeStruct((count, slots, block_y, depth), jnp.bfloat16),
-        in_specs=[vmem()] * (near + 1),
-        out_specs=vmem(),
+    shape = (chips, 2 * slots, block_y, depth)
+    mine, other = pl.pallas_call(
+        functools.partial(stack_kernel, slots, near // 2),
+        out_shape=(
+            jax.ShapeDtypeStruct(shape, jnp.float32), jax.ShapeDtypeStruct(shape, jnp.bfloat16)
+        ),
+        in_specs=[vmem()] * (near // 2 + 1),
+        out_specs=(vmem(), vmem()),
         scratch_shapes=[
             pltpu.SMEM(facts.shape, jnp.int32),
-            pltpu.VMEM((grid_rows * wide, GRID_COLS * LANES // APY, depth), jnp.float32),
-            pltpu.VMEM((grid_rows, GRID_COLS * block_y, depth), jnp.float32),
+            pltpu.VMEM((2, grid_rows * wide, GRID_COLS * LANES // APY, depth), jnp.float32),
+            pltpu.VMEM((2, grid_rows, GRID_COLS * block_y, depth), jnp.float32),
             pltpu.SemaphoreType.DMA,
         ],
-        compiler_params=limit(3),
+        compiler_params=limit(4),
         name="stack",
     )(facts, *terms)
-    sums = lax.all_to_all(sums, "shot", 0, 0, tiled=True)
+    joined = pl.pallas_call(
+        join_kernel,
+        out_shape=jax.ShapeDtypeStruct(shape, jnp.bfloat16),
+        in_specs=[vmem()] * 2,
+        out_specs=vmem(),
+        compiler_params=limit(2),
+        name="join",
+    )(mine, across(other))
+    sums = lax.all_to_all(
+        joined, "shot", 0, 0, tiled=True,
+        axis_index_groups=[list(range(core, count, 2)) for core in range(2)],
+    )
     return pl.pallas_call(
-        finish_kernel,
+        functools.partial(finish_kernel, near // 2),
         out_shape=jax.ShapeDtypeStruct(velocity_p.shape, jnp.float32),
         in_specs=[vmem()],
         out_specs=vmem(),

time: 57.6 us -> 56.5 us (0.981)
  blocking collectives: 11.3 us -> 10.6 us
  Pallas kernels: 8.94 us -> 8.25 us
  waiting for transfers between devices: 20.4 us -> 21 us
    pallas_call x1, Pallas kernels: 3.64 us -> 2.93 us  [wave(): pl.pallas_call(functools.partial(wave_kernel, near), out_shape=(out,) * (...]
    all_to_all x1, blocking collectives: 11.3 us -> 10.6 us  [per_device(): lax.all_to_all(joined, 'shot', 0, 0, tiled=True, axis_index_groups=[list(...]
    pallas_call x2 -> x3, Pallas kernels: 1.87 us -> 1.96 us  [the longest x1 1.25 us: per_device(): pl.pallas_call(functools.partial(stack_kernel, slots, near // 2), out_sha...]
    ppermute x8 -> x5, waiting for transfers between devices: 2.56 us -> 2.65 us  [across(): return lax.ppermute(value, 'shot', [(i, i ^ 1) for i in range(count)])]
  transfers between devices with their start and end apart: 15 -> 12, of which waited for: 12 -> 10; matrix products, arithmetic and copies ran while one was open for 0% -> 0% of each run, Pallas kernels for 1% -> 1%
where the time goes in v8:
time: 56.5 us; the launch traced here: 56.2 us
  waiting for transfers between devices  21 us (37%)
  starting transfers between devices  14.9 us (26%)
  blocking collectives  10.6 us (19%)
  Pallas kernels  8.25 us (15%)
  between operations  1.39 us (2%)
    all_to_all x1, blocking collectives, per_device(): lax.all_to_all(joined, 'shot', 0, 0, tiled=True, axis_index_groups=[list(...  10.6 us
    all_to_all x1, waiting for transfers between devices, per_device(): pieces = lax.all_to_all(sent, 'shot', 0, 0, tiled=True)  9.92 us
    ppermute x6, waiting for transfers between devices, swap(): lax.ppermute(values[k], 'shot', [(i, i ^ 2 * k) for i in range(count)])  8.46 us
    all_to_all x1, starting transfers between devices, per_device(): pieces = lax.all_to_all(sent, 'shot', 0, 0, tiled=True)  7.5 us
    ppermute x6, starting transfers between devices, swap(): lax.ppermute(values[k], 'shot', [(i, i ^ 2 * k) for i in range(count)])  7.11 us
    pallas_call x1, Pallas kernels, wave(): pl.pallas_call(functools.partial(wave_kernel, near), out_shape=(out,) * (...  2.93 us
    ppermute x5, waiting for transfers between devices, across(): return lax.ppermute(value, 'shot', [(i, i ^ 1) for i in range(count)])  2.65 us
    pallas_call x1, Pallas kernels, per_device(): pl.pallas_call(prepare_kernel, out_shape=jax.ShapeDtypeStruct((count, 2 *...  1.84 us
  transfers between devices with their start and end apart: 12, of which 10 were waited for; matrix products, arithmetic and copies ran while one was open for 0% of the time, Pallas kernels for 1%

profile of v8, /device:TPU:0, one launch (start us, length us, event | category | flops | bytes accessed | tf_op | source)
XLA Modules:
  0.0 56.2 jit_solution(9998407122232705601)
XLA Ops:
  1.3 1.8 %prepare.1 = bf16[16,9,8,128]{3,2,1,0:T(8,128)(2,1)} custom-call(s32[1]{0:T(128)S(6)} %copy.11.row_ref, s32[1]{0:T(128)S(6)} %copy.12.col_ref, s32[4]{0:T(128)} %ids_hbm.1, s32[4,8,8]{2,1,0:T(8,128)} %floor_hbm.1, bf16[4,8,8,128]{3,2,1,0:T(8,128)(2,1)} %p_hbm.1, bf16[4,8,8,128]{3,2,1,0:T(8,128)(2,1)} %s_hbm.1, bf16[4,8,8,128]{3,2,1,0:T(8,128)(2,1)} %rho_hbm.1, ...), custom_call_target="tpu_custom_call" | custom-call | tf_op jit(solution)/shard_map/prepare/pallas_call | solution.py:512
  3.1 0.0 copy-start
  3.2 0.0 copy-start.1
  3.2 7.5 %all-to-all-start = ((bf16[16,9,8,128]{3,2,1,0:T(8,128)(2,1)}), bf16[16,9,8,128]{3,2,1,0:T(8,128)(2,1)S(1)}, u32[]{:S(2)}, u32[]{:S(2)}) async-start(bf16[16,9,8,128]{3,2,1,0:T(8,128)(2,1)} %prepare.1), calls=%async_computation | async-start | bytes 589824 | tf_op jit(solution)/shard_map/all_to_all | solution.py:528
  10.7 0.0 copy-done
  10.7 0.0 copy-done.1
  10.7 0.6 %start.1 = (f32[32,4,8,128]{3,2,1,0:T(8,128)S(1)}, f32[32,4,8,128]{3,2,1,0:T(8,128)S(1)}, f32[32,4,8,128]{3,2,1,0:T(8,128)S(1)}) custom-call(bf16[32,32,128]{2,1,0:T(8,128)(2,1)S(1)} %bitcast.4, bf16[32,32,128]{2,1,0:T(8,128)(2,1)S(1)} %bitcast.5), custom_call_target="tpu_custom_call" | custom-call | flops 2621440 | bytes 2097152 | tf_op jit(solution)/shard_map/start/pallas_call | solution.py:258
  11.3 9.9 %all-to-all-done = bf16[16,9,8,128]{3,2,1,0:T(8,128)(2,1)S(1)} async-done(((bf16[16,9,8,128]{3,2,1,0:T(8,128)(2,1)}), bf16[16,9,8,128]{3,2,1,0:T(8,128)(2,1)S(1)}, u32[]{:S(2)}, u32[]{:S(2)}) %all-to-all-start) | async-done | bytes 294944 | tf_op jit(solution)/shard_map/all_to_all | solution.py:528
  21.2 0.9 %pick.1 = (bf16[64,8,128]{2,1,0:T(8,128)(2,1)S(1)}, bf16[64,8,128]{2,1,0:T(8,128)(2,1)S(1)}, bf16[64,8,128]{2,1,0:T(8,128)(2,1)S(1)}, bf16[64,8,128]{2,1,0:T(8,128)(2,1)S(1)}, s32[16,128]{1,0:T(8,128)S(1)}) custom-call(bf16[144,8,128]{2,1,0:T(8,128)(2,1)S(1)} %bitcast.3), custom_call_target="tpu_custom_call" | custom-call | tf_op jit(solution)/shard_map/pick/pallas_call | solution.py:533
  22.2 0.8 %collective-permute-start = (bf16[64,8,128]{2,1,0:T(8,128)(2,1)S(1)}, bf16[64,8,128]{2,1,0:T(8,128)(2,1)S(1)}, u32[]{:S(2)}, u32[]{:S(2)}) collective-permute-start(bf16[64,8,128]{2,1,0:T(8,128)(2,1)S(1)} %get-tuple-element.28), channel_id=1, source_target_pairs={{0,6},{1,7},{2,4},{3,5},{4,2},{5,3},{6,0},{7,1},{8,14},{9,15},{10,... | collective-permute-start | bytes 393224 | tf_op jit(solution)/shard_map/ppermute | solution.py:504
  23.0 0.3 collective-permute-start.1
  23.3 2.4 %collective-permute-start.2 = (bf16[64,8,128]{2,1,0:T(8,128)(2,1)S(1)}, bf16[64,8,128]{2,1,0:T(8,128)(2,1)S(1)}, u32[]{:S(2)}, u32[]{:S(2)}) collective-permute-start(bf16[64,8,128]{2,1,0:T(8,128)(2,1)S(1)} %get-tuple-element.30), channel_id=1, source_target_pairs={{0,2},{1,3},{2,0},{3,1},{4,6},{5,7},{6,4},{7,5},{8,10},{9,11},{10,... | collective-permute-start | bytes 393224 | tf_op jit(solution)/shard_map/ppermute | solution.py:504
  25.7 0.0 collective-permute-start.6
  25.7 3.8 %collective-permute-done.refs_0_ = bf16[64,8,128]{2,1,0:T(8,128)(2,1)S(1)} collective-permute-done((bf16[64,8,128]{2,1,0:T(8,128)(2,1)S(1)}, bf16[64,8,128]{2,1,0:T(8,128)(2,1)S(1)}, u32[]{:S(2)}, u32[]{:S(2)}) %collective-permute-start) | collective-permute-done | bytes 131104 | tf_op jit(solution)/shard_map/ppermute | solution.py:504
  29.5 0.0 collective-permute-start.3
  29.5 0.9 %collective-permute-done.1.refs_1_ = bf16[64,8,128]{2,1,0:T(8,128)(2,1)S(1)} collective-permute-done((bf16[64,8,128]{2,1,0:T(8,128)(2,1)S(1)}, bf16[64,8,128]{2,1,0:T(8,128)(2,1)S(1)}, u32[]{:S(2)}, u32[]{:S(2)}) %collective-permute-start.1) | collective-permute-done | bytes 131104 | tf_op jit(solution)/shard_map/ppermute | solution.py:504
  30.4 0.2 collective-permute-start.4
  30.6 0.6 %collective-permute-done.2.refs_2_ = bf16[64,8,128]{2,1,0:T(8,128)(2,1)S(1)} collective-permute-done((bf16[64,8,128]{2,1,0:T(8,128)(2,1)S(1)}, bf16[64,8,128]{2,1,0:T(8,128)(2,1)S(1)}, u32[]{:S(2)}, u32[]{:S(2)}) %collective-permute-start.2) | collective-permute-done | bytes 131104 | tf_op jit(solution)/shard_map/ppermute | solution.py:504
  31.2 0.0 collective-permute-start.5
  31.2 0.0 collective-permute-done.6.refs_7_
  31.3 0.0 collective-permute-done.3.refs_4_
  31.3 0.5 collective-permute-done.4.refs_5_
  31.8 0.8 %collective-permute-done.5.refs_6_ = bf16[64,8,128]{2,1,0:T(8,128)(2,1)S(1)} collective-permute-done((bf16[64,8,128]{2,1,0:T(8,128)(2,1)S(1)}, bf16[64,8,128]{2,1,0:T(8,128)(2,1)S(1)}, u32[]{:S(2)}, u32[]{:S(2)}) %collective-permute-start.5) | collective-permute-done | bytes 131104 | tf_op jit(solution)/shard_map/ppermute | solution.py:510
  32.6 2.9 %wave.1 = (bf16[32,8,128]{2,1,0:T(8,128)(2,1)S(1)}, bf16[32,8,128]{2,1,0:T(8,128)(2,1)S(1)}, bf16[32,8,128]{2,1,0:T(8,128)(2,1)S(1)}, bf16[32,8,128]{2,1,0:T(8,128)(2,1)S(1)}) custom-call(bf16[64,8,128]{2,1,0:T(8,128)(2,1)S(1)} %collective-permute-done.refs_0_, bf16[64,8,128]{2,1,0:T(8,128)(2,1)S(1)} %collective-permute-done.1.refs_1_, ...), custom_call_target="tpu_custom_call" | custom-call | tf_op jit(solution)/shard_map/wave/pallas_call | solution.py:368
  35.5 1.3 %collective-permute-start.7 = (bf16[32,8,128]{2,1,0:T(8,128)(2,1)S(1)}, bf16[32,8,128]{2,1,0:T(8,128)(2,1)S(1)}, u32[]{:S(2)}, u32[]{:S(2)}) collective-permute-start(bf16[32,8,128]{2,1,0:T(8,128)(2,1)S(1)} %get-tuple-element.35), channel_id=1, source_target_pairs={{0,6},{1,7},{2,4},{3,5},{4,2},{5,3},{6,0},{7,1},{8,14},{9,15},{10,... | collective-permute-start | bytes 196616 | tf_op jit(solution)/shard_map/ppermute | solution.py:504
  36.8 1.0 %collective-permute-start.8 = (bf16[32,8,128]{2,1,0:T(8,128)(2,1)S(1)}, bf16[32,8,128]{2,1,0:T(8,128)(2,1)S(1)}, u32[]{:S(2)}, u32[]{:S(2)}) collective-permute-start(bf16[32,8,128]{2,1,0:T(8,128)(2,1)S(1)} %get-tuple-element.36), channel_id=1, source_target_pairs={{0,4},{1,5},{2,6},{3,7},{4,0},{5,1},{6,2},{7,3},{8,12},{9,13},{10,... | collective-permute-start | bytes 196616 | tf_op jit(solution)/shard_map/ppermute | solution.py:504
  37.8 1.3 %collective-permute-start.9 = (bf16[32,8,128]{2,1,0:T(8,128)(2,1)S(1)}, bf16[32,8,128]{2,1,0:T(8,128)(2,1)S(1)}, u32[]{:S(2)}, u32[]{:S(2)}) collective-permute-start(bf16[32,8,128]{2,1,0:T(8,128)(2,1)S(1)} %get-tuple-element.37), channel_id=1, source_target_pairs={{0,2},{1,3},{2,0},{3,1},{4,6},{5,7},{6,4},{7,5},{8,10},{9,11},{10,... | collective-permute-start | bytes 196616 | tf_op jit(solution)/shard_map/ppermute | solution.py:504
  39.1 2.4 %collective-permute-done.7.refs_0_ = bf16[32,8,128]{2,1,0:T(8,128)(2,1)S(1)} collective-permute-done((bf16[32,8,128]{2,1,0:T(8,128)(2,1)S(1)}, bf16[32,8,128]{2,1,0:T(8,128)(2,1)S(1)}, u32[]{:S(2)}, u32[]{:S(2)}) %collective-permute-start.7) | collective-permute-done | bytes 65568 | tf_op jit(solution)/shard_map/ppermute | solution.py:504
  41.4 0.1 collective-permute-done.8.refs_1_
  41.5 0.7 %collective-permute-done.9.refs_2_ = bf16[32,8,128]{2,1,0:T(8,128)(2,1)S(1)} collective-permute-done((bf16[32,8,128]{2,1,0:T(8,128)(2,1)S(1)}, bf16[32,8,128]{2,1,0:T(8,128)(2,1)S(1)}, u32[]{:S(2)}, u32[]{:S(2)}) %collective-permute-start.9) | collective-permute-done | bytes 65568 | tf_op jit(solution)/shard_map/ppermute | solution.py:504
  42.2 1.2 %stack.1 = (f32[8,8,8,128]{3,2,1,0:T(8,128)S(1)}, bf16[8,8,8,128]{3,2,1,0:T(8,128)(2,1)S(1)}) custom-call(s32[16,128]{1,0:T(8,128)S(1)} %get-tuple-element.27.facts_ref, bf16[32,8,128]{2,1,0:T(8,128)(2,1)S(1)} %collective-permute-done.7.refs_0_, bf16[32,8,128]{2,1,0:T(8,128)(2,1)S(1)} %collective-permute-done.8.refs_1_, ...), custom_call_target="tpu_custom_call" | custom-call | tf_op jit(solution)/shard_map/stack/pallas_call | solution.py:562
  43.4 0.1 collective-permute-start.10
  43.5 1.3 %collective-permute-done.10.other_ref = bf16[8,8,8,128]{3,2,1,0:T(8,128)(2,1)S(1)} collective-permute-done((bf16[8,8,8,128]{3,2,1,0:T(8,128)(2,1)S(1)}, bf16[8,8,8,128]{3,2,1,0:T(8,128)(2,1)S(1)}, u32[]{:S(2)}, u32[]{:S(2)}) %collective-permute-start.10) | collective-permute-done | bytes 131104 | tf_op jit(solution)/shard_map/ppermute | solution.py:510
  44.9 10.6 %all_to_all.10.sums_ref = bf16[8,8,8,128]{3,2,1,0:T(8,128)(2,1)S(1)} all-to-all(bf16[8,8,8,128]{3,2,1,0:T(8,128)(2,1)S(1)} %join.1), channel_id=1, replica_groups={{0,2,4,6,8,10,12,14},{1,3,5,7,9,11,13,15},{16,18,20,22,24,26,28,30},{17..., dimensions={0} | all-to-all | bytes 262144 | tf_op jit(solution)/shard_map/all_to_all | solution.py:586
  55.5 0.7 %finish.1 = f32[4,8,8,128]{3,2,1,0:T(8,128)} custom-call(bf16[8,8,8,128]{3,2,1,0:T(8,128)(2,1)S(1)} %all_to_all.10.sums_ref), custom_call_target="tpu_custom_call" | custom-call | tf_op jit(solution)/shard_map/finish/pallas_call | solution.py:590
  (1 shorter events, 0.0 us)
Async XLA Ops:
  3.1 7.5 %copy-start = (bf16[1,32,32,128]{3,2,1,0:T(8,128)(2,1)S(1)}, bf16[1,32,32,128]{3,2,1,0:T(8,128)(2,1)}, u32[]{:S(2)}) copy-start(bf16[1,32,32,128]{3,2,1,0:T(8,128)(2,1)} %param.18) | copy-start | bytes 786436
  3.2 7.5 %copy-start.1 = (bf16[1,32,32,128]{3,2,1,0:T(8,128)(2,1)S(1)}, bf16[1,32,32,128]{3,2,1,0:T(8,128)(2,1)}, u32[]{:S(2)}) copy-start(bf16[1,32,32,128]{3,2,1,0:T(8,128)(2,1)} %param.19) | copy-start | bytes 786436
  3.2 18.1 %all-to-all-start = ((bf16[16,9,8,128]{3,2,1,0:T(8,128)(2,1)}), bf16[16,9,8,128]{3,2,1,0:T(8,128)(2,1)S(1)}, u32[]{:S(2)}, u32[]{:S(2)}) async-start(bf16[16,9,8,128]{3,2,1,0:T(8,128)(2,1)} %prepare.1), calls=%async_computation | async-start | bytes 589824 | tf_op jit(solution)/shard_map/all_to_all | solution.py:528
  22.2 7.3 %collective-permute-start = (bf16[64,8,128]{2,1,0:T(8,128)(2,1)S(1)}, bf16[64,8,128]{2,1,0:T(8,128)(2,1)S(1)}, u32[]{:S(2)}, u32[]{:S(2)}) collective-permute-start(bf16[64,8,128]{2,1,0:T(8,128)(2,1)S(1)} %get-tuple-element.28), channel_id=1, source_target_pairs={{0,6},{1,7},{2,4},{3,5},{4,2},{5,3},{6,0},{7,1},{8,14},{9,15},{10,... | collective-permute-start | bytes 393224 | tf_op jit(solution)/shard_map/ppermute | solution.py:504
  23.0 7.5 %collective-permute-start.1 = (bf16[64,8,128]{2,1,0:T(8,128)(2,1)S(1)}, bf16[64,8,128]{2,1,0:T(8,128)(2,1)S(1)}, u32[]{:S(2)}, u32[]{:S(2)}) collective-permute-start(bf16[64,8,128]{2,1,0:T(8,128)(2,1)S(1)} %get-tuple-element.29), channel_id=1, source_target_pairs={{0,4},{1,5},{2,6},{3,7},{4,0},{5,1},{6,2},{7,3},{8,12},{9,13},{10,... | collective-permute-start | bytes 393224 | tf_op jit(solution)/shard_map/ppermute | solution.py:504
  23.3 7.9 %collective-permute-start.2 = (bf16[64,8,128]{2,1,0:T(8,128)(2,1)S(1)}, bf16[64,8,128]{2,1,0:T(8,128)(2,1)S(1)}, u32[]{:S(2)}, u32[]{:S(2)}) collective-permute-start(bf16[64,8,128]{2,1,0:T(8,128)(2,1)S(1)} %get-tuple-element.30), channel_id=1, source_target_pairs={{0,2},{1,3},{2,0},{3,1},{4,6},{5,7},{6,4},{7,5},{8,10},{9,11},{10,... | collective-permute-start | bytes 393224 | tf_op jit(solution)/shard_map/ppermute | solution.py:504
  25.7 5.5 %collective-permute-start.6 = (bf16[64,8,128]{2,1,0:T(8,128)(2,1)S(1)}, bf16[64,8,128]{2,1,0:T(8,128)(2,1)S(1)}, u32[]{:S(2)}, u32[]{:S(2)}) collective-permute-start(bf16[64,8,128]{2,1,0:T(8,128)(2,1)S(1)} %get-tuple-element.31.refs_3_), channel_id=1, source_target_pairs={{0,1},{1,0},{2,3},{3,2},{4,5},{5,4},{6,7},{7,6},{8,9},{9,8},{10,11... | collective-permute-start | bytes 393224 | tf_op jit(solution)/shard_map/ppermute | solution.py:510
  29.5 1.8 %collective-permute-start.3 = (bf16[64,8,128]{2,1,0:T(8,128)(2,1)S(1)}, bf16[64,8,128]{2,1,0:T(8,128)(2,1)S(1)}, u32[]{:S(2)}, u32[]{:S(2)}) collective-permute-start(bf16[64,8,128]{2,1,0:T(8,128)(2,1)S(1)} %collective-permute-done.refs_0_), channel_id=1, source_target_pairs={{0,1},{1,0},{2,3},{3,2},{4,5},{5,4},{6,7},{7,6},{8,9},{9,8},{10,11... | collective-permute-start | bytes 393224 | tf_op jit(solution)/shard_map/ppermute | solution.py:510
  30.4 1.3 %collective-permute-start.4 = (bf16[64,8,128]{2,1,0:T(8,128)(2,1)S(1)}, bf16[64,8,128]{2,1,0:T(8,128)(2,1)S(1)}, u32[]{:S(2)}, u32[]{:S(2)}) collective-permute-start(bf16[64,8,128]{2,1,0:T(8,128)(2,1)S(1)} %collective-permute-done.1.refs_1_), channel_id=1, source_target_pairs={{0,1},{1,0},{2,3},{3,2},{4,5},{5,4},{6,7},{7,6},{8,9},{9,8},{10,11... | collective-permute-start | bytes 393224 | tf_op jit(solution)/shard_map/ppermute | solution.py:510
  31.2 1.3 %collective-permute-start.5 = (bf16[64,8,128]{2,1,0:T(8,128)(2,1)S(1)}, bf16[64,8,128]{2,1,0:T(8,128)(2,1)S(1)}, u32[]{:S(2)}, u32[]{:S(2)}) collective-permute-start(bf16[64,8,128]{2,1,0:T(8,128)(2,1)S(1)} %collective-permute-done.2.refs_2_), channel_id=1, source_target_pairs={{0,1},{1,0},{2,3},{3,2},{4,5},{5,4},{6,7},{7,6},{8,9},{9,8},{10,11... | collective-permute-start | bytes 393224 | tf_op jit(solution)/shard_map/ppermute | solution.py:510
  35.5 5.9 %collective-permute-start.7 = (bf16[32,8,128]{2,1,0:T(8,128)(2,1)S(1)}, bf16[32,8,128]{2,1,0:T(8,128)(2,1)S(1)}, u32[]{:S(2)}, u32[]{:S(2)}) collective-permute-start(bf16[32,8,128]{2,1,0:T(8,128)(2,1)S(1)} %get-tuple-element.35), channel_id=1, source_target_pairs={{0,6},{1,7},{2,4},{3,5},{4,2},{5,3},{6,0},{7,1},{8,14},{9,15},{10,... | collective-permute-start | bytes 196616 | tf_op jit(solution)/shard_map/ppermute | solution.py:504
  36.8 4.7 %collective-permute-start.8 = (bf16[32,8,128]{2,1,0:T(8,128)(2,1)S(1)}, bf16[32,8,128]{2,1,0:T(8,128)(2,1)S(1)}, u32[]{:S(2)}, u32[]{:S(2)}) collective-permute-start(bf16[32,8,128]{2,1,0:T(8,128)(2,1)S(1)} %get-tuple-element.36), channel_id=1, source_target_pairs={{0,4},{1,5},{2,6},{3,7},{4,0},{5,1},{6,2},{7,3},{8,12},{9,13},{10,... | collective-permute-start | bytes 196616 | tf_op jit(solution)/shard_map/ppermute | solution.py:504
  37.8 4.4 %collective-permute-start.9 = (bf16[32,8,128]{2,1,0:T(8,128)(2,1)S(1)}, bf16[32,8,128]{2,1,0:T(8,128)(2,1)S(1)}, u32[]{:S(2)}, u32[]{:S(2)}) collective-permute-start(bf16[32,8,128]{2,1,0:T(8,128)(2,1)S(1)} %get-tuple-element.37), channel_id=1, source_target_pairs={{0,2},{1,3},{2,0},{3,1},{4,6},{5,7},{6,4},{7,5},{8,10},{9,11},{10,... | collective-permute-start | bytes 196616 | tf_op jit(solution)/shard_map/ppermute | solution.py:504
  43.4 1.4 %collective-permute-start.10 = (bf16[8,8,8,128]{3,2,1,0:T(8,128)(2,1)S(1)}, bf16[8,8,8,128]{3,2,1,0:T(8,128)(2,1)S(1)}, u32[]{:S(2)}, u32[]{:S(2)}) collective-permute-start(bf16[8,8,8,128]{3,2,1,0:T(8,128)(2,1)S(1)} %get-tuple-element.40), channel_id=1, source_target_pairs={{0,1},{1,0},{2,3},{3,2},{4,5},{5,4},{6,7},{7,6},{8,9},{9,8},{10,11... | collective-permute-start | bytes 393224 | tf_op jit(solution)/shard_map/ppermute | solution.py:510

commit v9 on v8

--- a/solution.py
+++ b/solution.py
@@ -77,14 +77,11 @@
     return lax.axis_index("shot") // 2 % near
 
 
-def parts(refs):
+def parts(refs, length):
     chips = len(refs) // 2
     own, other = refs[:chips][::-1], refs[chips:][::-1]
-    length = refs[0].shape[0] // 2
     return [
-        ref.at[pl.ds(side * length, length)]
-        for pair in zip(own, other)
-        for side, ref in enumerate(pair)
+        part for first, second in zip(own, other) for part in (first.at[pl.ds(0, length)], second)
     ]
 
 
@@ -145,7 +142,7 @@
 def pick_kernel(slots, near, pieces_ref, *refs):
     chips = near // 2
     out_refs = refs[:chips][::-1]
-    facts_ref, facts, spots, sem = refs[chips:]
+    beside_ref, facts_ref, facts, spots, sem = refs[chips:]
     count = facts_ref.shape[0]
     tiles = 2 * slots + 1
     for piece in range(count):
@@ -161,6 +158,8 @@
     for t in range(near):
         shot = me ^ t
         out_ref, start_tile = out_refs[t // 2], t % 2 * APX * APY * 2
+        if t == 1:
+            out_ref, start_tile = beside_ref, 0
         first = facts[shot, slots] * GRID_COLS + facts[shot, slots + 1]
         for x in range(APX):
             found = []
@@ -271,7 +270,7 @@
 
 def wave_kernel(near, *refs):
     chips = near // 2
-    model_refs = parts(refs[:near])
+    model_refs = parts(refs[:near], 2 * APX * APY)
     u_0, g_0, next_ref = refs[near:near + 3]
     refs = refs[near + 3:]
     out_refs = refs[:chips][::-1]
@@ -382,9 +381,9 @@
     near = len(models)
     order = (lax.axis_index("shot") % near) ^ jnp.arange(near)
     chips = near // 2
-    length = models[0].shape[0] // 2
+    length = models[-1].shape[0]
     pairs = zip(models[:chips][::-1], models[chips:][::-1])
-    model = jnp.stack([part for own, other in pairs for part in (own[:length], other[length:])])
+    model = jnp.stack([part for own, other in pairs for part in (own[:length], other)])
     model = model[order]
     span_x, span_y, depth = before.shape
     block_x, tiles, block_y, _ = model.shape
@@ -444,7 +443,7 @@
                     ]
         return carry
 
-    lax.fori_loop(0, grid_rows, line, 0, unroll=4)
+    lax.fori_loop(0, grid_rows, line, 0, unroll=8)
 
     def give(chip, carry):
         for own, out_ref in enumerate((mine_ref, other_ref)):
@@ -457,7 +456,7 @@
                 out_ref[chip, index] = tile.astype(out_ref.dtype)
         return carry
 
-    lax.fori_loop(0, count // 2, give, 0, unroll=2)
+    lax.fori_loop(0, count // 2, give, 0, unroll=8)
 
 
 def join_kernel(mine_ref, other_ref, out_ref):
@@ -533,11 +532,14 @@
     *picked, facts = pl.pallas_call(
         functools.partial(pick_kernel, slots, near),
         out_shape=(
-            *[jax.ShapeDtypeStruct((patch * 4, block_y, depth), jnp.bfloat16)] * (near // 2),
+            *[
+                jax.ShapeDtypeStruct((patch * tiles, block_y, depth), jnp.bfloat16)
+                for tiles in [4] * (near // 2 - 1) + [2, 2]
+            ],
             jax.ShapeDtypeStruct((count, depth), jnp.int32),
         ),
         in_specs=[vmem()],
-        out_specs=(vmem(),) * (near // 2 + 1),
+        out_specs=(vmem(),) * (near // 2 + 2),
         scratch_shapes=[
             pltpu.SMEM((count, depth), jnp.int32),
             pltpu.SMEM((count * slots,), jnp.int32),
@@ -546,8 +548,10 @@
         compiler_params=limit(3),
         name="pick",
     )(pieces.reshape(count * (2 * slots + 1), block_y, depth))
+    *picked, beside = picked
     models = swap(picked[::-1])
-    models = models + [across(value) for value in models]
+    handed = [value[patch * 2:] for value in models[:-1]] + [beside]
+    models = models + [across(value) for value in handed]
 
     if split:
         terms = wave_split_depth(models, wave_prev[0], wave_now[0])

time: 56.5 us -> 56.3 us (level)
  no operation moved by 1% of the time
where the time goes in v9:
time: 56.3 us; the launch traced here: 56 us
  waiting for transfers between devices  21 us (37%)
  starting transfers between devices  14.9 us (26%)
  blocking collectives  10.5 us (19%)
  Pallas kernels  8.21 us (15%)
  between operations  1.4 us (2%)
    all_to_all x1, blocking collectives, per_device(): lax.all_to_all(joined, 'shot', 0, 0, tiled=True, axis_index_groups=[list(...  10.5 us
    all_to_all x1, waiting for transfers between devices, per_device(): pieces = lax.all_to_all(sent, 'shot', 0, 0, tiled=True)  9.92 us
    ppermute x6, waiting for transfers between devices, swap(): lax.ppermute(values[k], 'shot', [(i, i ^ 2 * k) for i in range(count)])  8.48 us
    all_to_all x1, starting transfers between devices, per_device(): pieces = lax.all_to_all(sent, 'shot', 0, 0, tiled=True)  7.5 us
    ppermute x6, starting transfers between devices, swap(): lax.ppermute(values[k], 'shot', [(i, i ^ 2 * k) for i in range(count)])  7.11 us
    pallas_call x1, Pallas kernels, wave(): pl.pallas_call(functools.partial(wave_kernel, near), out_shape=(out,) * (...  3 us
    ppermute x5, waiting for transfers between devices, across(): return lax.ppermute(value, 'shot', [(i, i ^ 1) for i in range(count)])  2.55 us
    pallas_call x1, Pallas kernels, per_device(): pl.pallas_call(prepare_kernel, out_shape=jax.ShapeDtypeStruct((count, 2 *...  1.84 us
  transfers between devices with their start and end apart: 12, of which 10 were waited for; matrix products, arithmetic and copies ran while one was open for 0% of the time, Pallas kernels for 1%

profile of v9, /device:TPU:0, one launch (start us, length us, event | category | flops | bytes accessed | tf_op | source)
XLA Modules:
  0.0 56.0 jit_solution(10047937315217468492)
XLA Ops:
  1.3 1.8 %prepare.1 = bf16[16,9,8,128]{3,2,1,0:T(8,128)(2,1)} custom-call(s32[1]{0:T(128)S(6)} %copy.11.row_ref, s32[1]{0:T(128)S(6)} %copy.12.col_ref, s32[4]{0:T(128)} %ids_hbm.1, s32[4,8,8]{2,1,0:T(8,128)} %floor_hbm.1, bf16[4,8,8,128]{3,2,1,0:T(8,128)(2,1)} %p_hbm.1, bf16[4,8,8,128]{3,2,1,0:T(8,128)(2,1)} %s_hbm.1, bf16[4,8,8,128]{3,2,1,0:T(8,128)(2,1)} %rho_hbm.1, ...), custom_call_target="tpu_custom_call" | custom-call | tf_op jit(solution)/shard_map/prepare/pallas_call | solution.py:511
  3.1 0.0 copy-start
  3.2 0.0 copy-start.1
  3.2 7.5 %all-to-all-start = ((bf16[16,9,8,128]{3,2,1,0:T(8,128)(2,1)}), bf16[16,9,8,128]{3,2,1,0:T(8,128)(2,1)S(1)}, u32[]{:S(2)}, u32[]{:S(2)}) async-start(bf16[16,9,8,128]{3,2,1,0:T(8,128)(2,1)} %prepare.1), calls=%async_computation | async-start | bytes 589824 | tf_op jit(solution)/shard_map/all_to_all | solution.py:527
  10.7 0.0 copy-done
  10.7 0.0 copy-done.1
  10.7 0.6 %start.1 = (f32[32,4,8,128]{3,2,1,0:T(8,128)S(1)}, f32[32,4,8,128]{3,2,1,0:T(8,128)S(1)}, f32[32,4,8,128]{3,2,1,0:T(8,128)S(1)}) custom-call(bf16[32,32,128]{2,1,0:T(8,128)(2,1)S(1)} %bitcast.4, bf16[32,32,128]{2,1,0:T(8,128)(2,1)S(1)} %bitcast.5), custom_call_target="tpu_custom_call" | custom-call | flops 2621440 | bytes 2097152 | tf_op jit(solution)/shard_map/start/pallas_call | solution.py:257
  11.3 9.9 %all-to-all-done = bf16[16,9,8,128]{3,2,1,0:T(8,128)(2,1)S(1)} async-done(((bf16[16,9,8,128]{3,2,1,0:T(8,128)(2,1)}), bf16[16,9,8,128]{3,2,1,0:T(8,128)(2,1)S(1)}, u32[]{:S(2)}, u32[]{:S(2)}) %all-to-all-start) | async-done | bytes 294944 | tf_op jit(solution)/shard_map/all_to_all | solution.py:527
  21.2 0.9 %pick.1 = (bf16[64,8,128]{2,1,0:T(8,128)(2,1)S(1)}, bf16[64,8,128]{2,1,0:T(8,128)(2,1)S(1)}, bf16[64,8,128]{2,1,0:T(8,128)(2,1)S(1)}, bf16[32,8,128]{2,1,0:T(8,1...) custom-call(bf16[144,8,128]{2,1,0:T(8,128)(2,1)S(1)} %bitcast.3), custom_call_target="tpu_custom_call" | custom-call | tf_op jit(solution)/shard_map/pick/pallas_call | solution.py:532
  22.2 0.8 %collective-permute-start = (bf16[64,8,128]{2,1,0:T(8,128)(2,1)S(1)}, bf16[64,8,128]{2,1,0:T(8,128)(2,1)S(1)}, u32[]{:S(2)}, u32[]{:S(2)}) collective-permute-start(bf16[64,8,128]{2,1,0:T(8,128)(2,1)S(1)} %get-tuple-element.29), channel_id=1, source_target_pairs={{0,6},{1,7},{2,4},{3,5},{4,2},{5,3},{6,0},{7,1},{8,14},{9,15},{10,... | collective-permute-start | bytes 393224 | tf_op jit(solution)/shard_map/ppermute | solution.py:503
  23.0 0.3 collective-permute-start.1
  23.3 2.4 %collective-permute-start.2 = (bf16[64,8,128]{2,1,0:T(8,128)(2,1)S(1)}, bf16[64,8,128]{2,1,0:T(8,128)(2,1)S(1)}, u32[]{:S(2)}, u32[]{:S(2)}) collective-permute-start(bf16[64,8,128]{2,1,0:T(8,128)(2,1)S(1)} %get-tuple-element.31), channel_id=1, source_target_pairs={{0,2},{1,3},{2,0},{3,1},{4,6},{5,7},{6,4},{7,5},{8,10},{9,11},{10,... | collective-permute-start | bytes 393224 | tf_op jit(solution)/shard_map/ppermute | solution.py:503
  25.7 0.0 collective-permute-start.6
  25.7 3.8 %collective-permute-done.refs_0_ = bf16[64,8,128]{2,1,0:T(8,128)(2,1)S(1)} collective-permute-done((bf16[64,8,128]{2,1,0:T(8,128)(2,1)S(1)}, bf16[64,8,128]{2,1,0:T(8,128)(2,1)S(1)}, u32[]{:S(2)}, u32[]{:S(2)}) %collective-permute-start) | collective-permute-done | bytes 131104 | tf_op jit(solution)/shard_map/ppermute | solution.py:503
  29.5 0.0 collective-permute-start.3
  29.5 0.9 %collective-permute-done.1.refs_1_ = bf16[64,8,128]{2,1,0:T(8,128)(2,1)S(1)} collective-permute-done((bf16[64,8,128]{2,1,0:T(8,128)(2,1)S(1)}, bf16[64,8,128]{2,1,0:T(8,128)(2,1)S(1)}, u32[]{:S(2)}, u32[]{:S(2)}) %collective-permute-start.1) | collective-permute-done | bytes 131104 | tf_op jit(solution)/shard_map/ppermute | solution.py:503
  30.4 0.2 collective-permute-start.4
  30.6 0.6 %collective-permute-done.2.refs_2_ = bf16[64,8,128]{2,1,0:T(8,128)(2,1)S(1)} collective-permute-done((bf16[64,8,128]{2,1,0:T(8,128)(2,1)S(1)}, bf16[64,8,128]{2,1,0:T(8,128)(2,1)S(1)}, u32[]{:S(2)}, u32[]{:S(2)}) %collective-permute-start.2) | collective-permute-done | bytes 131104 | tf_op jit(solution)/shard_map/ppermute | solution.py:503
  31.2 0.0 collective-permute-start.5
  31.3 0.0 collective-permute-done.6.refs_7_
  31.3 0.0 collective-permute-done.3.refs_4_
  31.3 0.4 collective-permute-done.4.refs_5_
  31.7 0.8 %collective-permute-done.5.refs_6_ = bf16[32,8,128]{2,1,0:T(8,128)(2,1)S(1)} collective-permute-done((bf16[32,8,128]{2,1,0:T(8,128)(2,1)S(1)}, bf16[32,8,128]{2,1,0:T(8,128)(2,1)S(1)}, u32[]{:S(2)}, u32[]{:S(2)}) %collective-permute-start.5) | collective-permute-done | bytes 65568 | tf_op jit(solution)/shard_map/ppermute | solution.py:509
  32.5 3.0 %wave.1 = (bf16[32,8,128]{2,1,0:T(8,128)(2,1)S(1)}, bf16[32,8,128]{2,1,0:T(8,128)(2,1)S(1)}, bf16[32,8,128]{2,1,0:T(8,128)(2,1)S(1)}, bf16[32,8,128]{2,1,0:T(8,128)(2,1)S(1)}) custom-call(bf16[64,8,128]{2,1,0:T(8,128)(2,1)S(1)} %collective-permute-done.refs_0_, bf16[64,8,128]{2,1,0:T(8,128)(2,1)S(1)} %collective-permute-done.1.refs_1_, ...), custom_call_target="tpu_custom_call" | custom-call | tf_op jit(solution)/shard_map/wave/pallas_call | solution.py:367
  35.5 1.3 %collective-permute-start.7 = (bf16[32,8,128]{2,1,0:T(8,128)(2,1)S(1)}, bf16[32,8,128]{2,1,0:T(8,128)(2,1)S(1)}, u32[]{:S(2)}, u32[]{:S(2)}) collective-permute-start(bf16[32,8,128]{2,1,0:T(8,128)(2,1)S(1)} %get-tuple-element.37), channel_id=1, source_target_pairs={{0,6},{1,7},{2,4},{3,5},{4,2},{5,3},{6,0},{7,1},{8,14},{9,15},{10,... | collective-permute-start | bytes 196616 | tf_op jit(solution)/shard_map/ppermute | solution.py:503
  36.8 1.0 %collective-permute-start.8 = (bf16[32,8,128]{2,1,0:T(8,128)(2,1)S(1)}, bf16[32,8,128]{2,1,0:T(8,128)(2,1)S(1)}, u32[]{:S(2)}, u32[]{:S(2)}) collective-permute-start(bf16[32,8,128]{2,1,0:T(8,128)(2,1)S(1)} %get-tuple-element.38), channel_id=1, source_target_pairs={{0,4},{1,5},{2,6},{3,7},{4,0},{5,1},{6,2},{7,3},{8,12},{9,13},{10,... | collective-permute-start | bytes 196616 | tf_op jit(solution)/shard_map/ppermute | solution.py:503
  37.8 1.2 %collective-permute-start.9 = (bf16[32,8,128]{2,1,0:T(8,128)(2,1)S(1)}, bf16[32,8,128]{2,1,0:T(8,128)(2,1)S(1)}, u32[]{:S(2)}, u32[]{:S(2)}) collective-permute-start(bf16[32,8,128]{2,1,0:T(8,128)(2,1)S(1)} %get-tuple-element.39), channel_id=1, source_target_pairs={{0,2},{1,3},{2,0},{3,1},{4,6},{5,7},{6,4},{7,5},{8,10},{9,11},{10,... | collective-permute-start | bytes 196616 | tf_op jit(solution)/shard_map/ppermute | solution.py:503
  39.0 2.4 %collective-permute-done.7.refs_0_ = bf16[32,8,128]{2,1,0:T(8,128)(2,1)S(1)} collective-permute-done((bf16[32,8,128]{2,1,0:T(8,128)(2,1)S(1)}, bf16[32,8,128]{2,1,0:T(8,128)(2,1)S(1)}, u32[]{:S(2)}, u32[]{:S(2)}) %collective-permute-start.7) | collective-permute-done | bytes 65568 | tf_op jit(solution)/shard_map/ppermute | solution.py:503
  41.4 0.1 collective-permute-done.8.refs_1_
  41.5 0.7 %collective-permute-done.9.refs_2_ = bf16[32,8,128]{2,1,0:T(8,128)(2,1)S(1)} collective-permute-done((bf16[32,8,128]{2,1,0:T(8,128)(2,1)S(1)}, bf16[32,8,128]{2,1,0:T(8,128)(2,1)S(1)}, u32[]{:S(2)}, u32[]{:S(2)}) %collective-permute-start.9) | collective-permute-done | bytes 65568 | tf_op jit(solution)/shard_map/ppermute | solution.py:503
  42.2 1.1 %stack.1 = (f32[8,8,8,128]{3,2,1,0:T(8,128)S(1)}, bf16[8,8,8,128]{3,2,1,0:T(8,128)(2,1)S(1)}) custom-call(s32[16,128]{1,0:T(8,128)S(1)} %get-tuple-element.28.facts_ref, bf16[32,8,128]{2,1,0:T(8,128)(2,1)S(1)} %collective-permute-done.7.refs_0_, bf16[32,8,128]{2,1,0:T(8,128)(2,1)S(1)} %collective-permute-done.8.refs_1_, ...), custom_call_target="tpu_custom_call" | custom-call | tf_op jit(solution)/shard_map/stack/pallas_call | solution.py:566
  43.4 0.1 collective-permute-start.10
  43.4 1.3 %collective-permute-done.10.other_ref = bf16[8,8,8,128]{3,2,1,0:T(8,128)(2,1)S(1)} collective-permute-done((bf16[8,8,8,128]{3,2,1,0:T(8,128)(2,1)S(1)}, bf16[8,8,8,128]{3,2,1,0:T(8,128)(2,1)S(1)}, u32[]{:S(2)}, u32[]{:S(2)}) %collective-permute-start.10) | collective-permute-done | bytes 131104 | tf_op jit(solution)/shard_map/ppermute | solution.py:509
  44.8 10.5 %all_to_all.10.sums_ref = bf16[8,8,8,128]{3,2,1,0:T(8,128)(2,1)S(1)} all-to-all(bf16[8,8,8,128]{3,2,1,0:T(8,128)(2,1)S(1)} %join.1), channel_id=1, replica_groups={{0,2,4,6,8,10,12,14},{1,3,5,7,9,11,13,15},{16,18,20,22,24,26,28,30},{17..., dimensions={0} | all-to-all | bytes 262144 | tf_op jit(solution)/shard_map/all_to_all | solution.py:590
  55.4 0.7 %finish.1 = f32[4,8,8,128]{3,2,1,0:T(8,128)} custom-call(bf16[8,8,8,128]{3,2,1,0:T(8,128)(2,1)S(1)} %all_to_all.10.sums_ref), custom_call_target="tpu_custom_call" | custom-call | tf_op jit(solution)/shard_map/finish/pallas_call | solution.py:594
  (4 shorter events, 0.0 us)
Async XLA Ops:
  3.1 7.5 %copy-start = (bf16[1,32,32,128]{3,2,1,0:T(8,128)(2,1)S(1)}, bf16[1,32,32,128]{3,2,1,0:T(8,128)(2,1)}, u32[]{:S(2)}) copy-start(bf16[1,32,32,128]{3,2,1,0:T(8,128)(2,1)} %param.18) | copy-start | bytes 786436
  3.2 7.5 %copy-start.1 = (bf16[1,32,32,128]{3,2,1,0:T(8,128)(2,1)S(1)}, bf16[1,32,32,128]{3,2,1,0:T(8,128)(2,1)}, u32[]{:S(2)}) copy-start(bf16[1,32,32,128]{3,2,1,0:T(8,128)(2,1)} %param.19) | copy-start | bytes 786436
  3.2 18.1 %all-to-all-start = ((bf16[16,9,8,128]{3,2,1,0:T(8,128)(2,1)}), bf16[16,9,8,128]{3,2,1,0:T(8,128)(2,1)S(1)}, u32[]{:S(2)}, u32[]{:S(2)}) async-start(bf16[16,9,8,128]{3,2,1,0:T(8,128)(2,1)} %prepare.1), calls=%async_computation | async-start | bytes 589824 | tf_op jit(solution)/shard_map/all_to_all | solution.py:527
  22.2 7.3 %collective-permute-start = (bf16[64,8,128]{2,1,0:T(8,128)(2,1)S(1)}, bf16[64,8,128]{2,1,0:T(8,128)(2,1)S(1)}, u32[]{:S(2)}, u32[]{:S(2)}) collective-permute-start(bf16[64,8,128]{2,1,0:T(8,128)(2,1)S(1)} %get-tuple-element.29), channel_id=1, source_target_pairs={{0,6},{1,7},{2,4},{3,5},{4,2},{5,3},{6,0},{7,1},{8,14},{9,15},{10,... | collective-permute-start | bytes 393224 | tf_op jit(solution)/shard_map/ppermute | solution.py:503
  23.0 7.5 %collective-permute-start.1 = (bf16[64,8,128]{2,1,0:T(8,128)(2,1)S(1)}, bf16[64,8,128]{2,1,0:T(8,128)(2,1)S(1)}, u32[]{:S(2)}, u32[]{:S(2)}) collective-permute-start(bf16[64,8,128]{2,1,0:T(8,128)(2,1)S(1)} %get-tuple-element.30), channel_id=1, source_target_pairs={{0,4},{1,5},{2,6},{3,7},{4,0},{5,1},{6,2},{7,3},{8,12},{9,13},{10,... | collective-permute-start | bytes 393224 | tf_op jit(solution)/shard_map/ppermute | solution.py:503
  23.3 7.9 %collective-permute-start.2 = (bf16[64,8,128]{2,1,0:T(8,128)(2,1)S(1)}, bf16[64,8,128]{2,1,0:T(8,128)(2,1)S(1)}, u32[]{:S(2)}, u32[]{:S(2)}) collective-permute-start(bf16[64,8,128]{2,1,0:T(8,128)(2,1)S(1)} %get-tuple-element.31), channel_id=1, source_target_pairs={{0,2},{1,3},{2,0},{3,1},{4,6},{5,7},{6,4},{7,5},{8,10},{9,11},{10,... | collective-permute-start | bytes 393224 | tf_op jit(solution)/shard_map/ppermute | solution.py:503
  25.7 5.5 %collective-permute-start.6 = (bf16[32,8,128]{2,1,0:T(8,128)(2,1)S(1)}, bf16[32,8,128]{2,1,0:T(8,128)(2,1)S(1)}, u32[]{:S(2)}, u32[]{:S(2)}) collective-permute-start(bf16[32,8,128]{2,1,0:T(8,128)(2,1)S(1)} %get-tuple-element.33), channel_id=1, source_target_pairs={{0,1},{1,0},{2,3},{3,2},{4,5},{5,4},{6,7},{7,6},{8,9},{9,8},{10,11... | collective-permute-start | bytes 196616 | tf_op jit(solution)/shard_map/ppermute | solution.py:509
  29.5 1.8 %collective-permute-start.3 = (bf16[32,8,128]{2,1,0:T(8,128)(2,1)S(1)}, bf16[32,8,128]{2,1,0:T(8,128)(2,1)S(1)}, u32[]{:S(2)}, u32[]{:S(2)}) collective-permute-start(bf16[32,8,128]{2,1,0:T(8,128)(2,1)S(1)} %slice.12), channel_id=1, source_target_pairs={{0,1},{1,0},{2,3},{3,2},{4,5},{5,4},{6,7},{7,6},{8,9},{9,8},{10,11... | collective-permute-start | bytes 196616 | tf_op jit(solution)/shard_map/ppermute | solution.py:509
  30.4 1.3 %collective-permute-start.4 = (bf16[32,8,128]{2,1,0:T(8,128)(2,1)S(1)}, bf16[32,8,128]{2,1,0:T(8,128)(2,1)S(1)}, u32[]{:S(2)}, u32[]{:S(2)}) collective-permute-start(bf16[32,8,128]{2,1,0:T(8,128)(2,1)S(1)} %slice.13), channel_id=1, source_target_pairs={{0,1},{1,0},{2,3},{3,2},{4,5},{5,4},{6,7},{7,6},{8,9},{9,8},{10,11... | collective-permute-start | bytes 196616 | tf_op jit(solution)/shard_map/ppermute | solution.py:509
  31.2 1.3 %collective-permute-start.5 = (bf16[32,8,128]{2,1,0:T(8,128)(2,1)S(1)}, bf16[32,8,128]{2,1,0:T(8,128)(2,1)S(1)}, u32[]{:S(2)}, u32[]{:S(2)}) collective-permute-start(bf16[32,8,128]{2,1,0:T(8,128)(2,1)S(1)} %slice.14), channel_id=1, source_target_pairs={{0,1},{1,0},{2,3},{3,2},{4,5},{5,4},{6,7},{7,6},{8,9},{9,8},{10,11... | collective-permute-start | bytes 196616 | tf_op jit(solution)/shard_map/ppermute | solution.py:509
  35.5 5.9 %collective-permute-start.7 = (bf16[32,8,128]{2,1,0:T(8,128)(2,1)S(1)}, bf16[32,8,128]{2,1,0:T(8,128)(2,1)S(1)}, u32[]{:S(2)}, u32[]{:S(2)}) collective-permute-start(bf16[32,8,128]{2,1,0:T(8,128)(2,1)S(1)} %get-tuple-element.37), channel_id=1, source_target_pairs={{0,6},{1,7},{2,4},{3,5},{4,2},{5,3},{6,0},{7,1},{8,14},{9,15},{10,... | collective-permute-start | bytes 196616 | tf_op jit(solution)/shard_map/ppermute | solution.py:503
  36.8 4.7 %collective-permute-start.8 = (bf16[32,8,128]{2,1,0:T(8,128)(2,1)S(1)}, bf16[32,8,128]{2,1,0:T(8,128)(2,1)S(1)}, u32[]{:S(2)}, u32[]{:S(2)}) collective-permute-start(bf16[32,8,128]{2,1,0:T(8,128)(2,1)S(1)} %get-tuple-element.38), channel_id=1, source_target_pairs={{0,4},{1,5},{2,6},{3,7},{4,0},{5,1},{6,2},{7,3},{8,12},{9,13},{10,... | collective-permute-start | bytes 196616 | tf_op jit(solution)/shard_map/ppermute | solution.py:503
  37.8 4.4 %collective-permute-start.9 = (bf16[32,8,128]{2,1,0:T(8,128)(2,1)S(1)}, bf16[32,8,128]{2,1,0:T(8,128)(2,1)S(1)}, u32[]{:S(2)}, u32[]{:S(2)}) collective-permute-start(bf16[32,8,128]{2,1,0:T(8,128)(2,1)S(1)} %get-tuple-element.39), channel_id=1, source_target_pairs={{0,2},{1,3},{2,0},{3,1},{4,6},{5,7},{6,4},{7,5},{8,10},{9,11},{10,... | collective-permute-start | bytes 196616 | tf_op jit(solution)/shard_map/ppermute | solution.py:503
  43.4 1.4 %collective-permute-start.10 = (bf16[8,8,8,128]{3,2,1,0:T(8,128)(2,1)S(1)}, bf16[8,8,8,128]{3,2,1,0:T(8,128)(2,1)S(1)}, u32[]{:S(2)}, u32[]{:S(2)}) collective-permute-start(bf16[8,8,8,128]{3,2,1,0:T(8,128)(2,1)S(1)} %get-tuple-element.42), channel_id=1, source_target_pairs={{0,1},{1,0},{2,3},{3,2},{4,5},{5,4},{6,7},{7,6},{8,9},{9,8},{10,11... | collective-permute-start | bytes 393224 | tf_op jit(solution)/shard_map/ppermute | solution.py:509

commit v10 on v9

--- a/solution.py
+++ b/solution.py
@@ -403,44 +403,39 @@
     return [image[k] for k in range(chips)]
 
 
-def stack_kernel(slots, near, facts_ref, *refs):
+def stack_kernel(slots, near, r, facts_ref, *refs):
     terms_refs = refs[:near][::-1]
     mine_ref, other_ref, facts, total, lined, sem = refs[near:]
     count = facts_ref.shape[0]
     half = terms_refs[0].shape[0] // 2
     wide = half // APX
     width = LANES // APY
-    grid_rows = total.shape[1] // wide
+    grid_rows = total.shape[0] // wide
     copy = pltpu.make_async_copy(facts_ref, facts, sem)
     copy.start()
     me = lax.axis_index("shot")
 
     def clear(index, carry):
-        for r in range(2):
-            total[r, index] = jnp.zeros(total.shape[2:], total.dtype)
+        total[index] = jnp.zeros(total.shape[1:], total.dtype)
         return carry
 
-    lax.fori_loop(0, total.shape[1], clear, 0, unroll=8)
+    lax.fori_loop(0, total.shape[0], clear, 0, unroll=16)
     copy.wait()
     for k, terms_ref in enumerate(terms_refs):
         first = facts[me ^ 2 * k, slots] * wide
         rows = pl.ds(facts[me ^ 2 * k, slots + 1] * width, LANES)
-        for r in range(2):
-            sums = [
-                total[r, first + tile, rows] + terms_ref[r * half + tile].astype(jnp.float32)
-                for tile in range(half)
-            ]
-            for tile in range(half):
-                total[r, first + tile, rows] = sums[tile]
+        sums = [
+            total[first + tile, rows] + terms_ref[r * half + tile].astype(jnp.float32)
+            for tile in range(half)
+        ]
+        for tile in range(half):
+            total[first + tile, rows] = sums[tile]
 
     def line(row, carry):
-        for r in range(2):
-            for part in range(wide):
-                for tile in range(total.shape[2] // LANES):
-                    at = pl.ds(tile * LANES * wide + part, LANES, stride=wide)
-                    lined[r, row, at] = total[
-                        r, row * wide + part, tile * LANES:(tile + 1) * LANES
-                    ]
+        for part in range(wide):
+            for tile in range(total.shape[1] // LANES):
+                at = pl.ds(tile * LANES * wide + part, LANES, stride=wide)
+                lined[row, at] = total[row * wide + part, tile * LANES:(tile + 1) * LANES]
         return carry
 
     lax.fori_loop(0, grid_rows, line, 0, unroll=8)
@@ -451,7 +446,7 @@
             for slot in range(slots):
                 block = facts[2 * chip + (me + own) % 2, slot]
                 rows = pl.ds(pl.multiple_of(block % GRID_COLS * LANES, LANES), LANES)
-                found += [lined[r, block // GRID_COLS, rows] for r in range(2)]
+                found.append(lined[block // GRID_COLS, rows])
             for index, tile in enumerate(found):
                 out_ref[chip, index] = tile.astype(out_ref.dtype)
         return carry
@@ -459,19 +454,21 @@
     lax.fori_loop(0, count // 2, give, 0, unroll=8)
 
 
-def join_kernel(mine_ref, other_ref, out_ref):
+def join_kernel(*refs):
+    mine_refs, other_refs, out_ref = refs[:2], refs[2:4], refs[4]
     for chip in range(out_ref.shape[0]):
-        total = mine_ref[chip] + other_ref[chip].astype(jnp.float32)
-        out_ref[chip] = total.astype(out_ref.dtype)
+        for r in range(2):
+            total = mine_refs[r][chip] + other_refs[r][chip].astype(jnp.float32)
+            out_ref[chip, r] = total.astype(out_ref.dtype)
 
 
 def finish_kernel(near, sums_ref, out_ref):
     for place in range(near):
         for slot in range(out_ref.shape[0]):
             for r in range(2):
-                result = sums_ref[place, 2 * slot + r].astype(jnp.float32)
+                result = sums_ref[place, r, slot].astype(jnp.float32)
                 for chip in range(place + near, sums_ref.shape[0], near):
-                    result = result + sums_ref[chip, 2 * slot + r].astype(jnp.float32)
+                    result = result + sums_ref[chip, r, slot].astype(jnp.float32)
                 out_ref[slot, 2 * place + r] = result
 
 
@@ -562,31 +559,38 @@
     chips = count // 2
     grid_rows = count * slots // GRID_COLS
     wide = terms[0].shape[0] // 2 // APX
-    shape = (chips, 2 * slots, block_y, depth)
-    mine, other = pl.pallas_call(
-        functools.partial(stack_kernel, slots, near // 2),
-        out_shape=(
-            jax.ShapeDtypeStruct(shape, jnp.float32), jax.ShapeDtypeStruct(shape, jnp.bfloat16)
-        ),
-        in_specs=[vmem()] * (near // 2 + 1),
-        out_specs=(vmem(), vmem()),
-        scratch_shapes=[
-            pltpu.SMEM(facts.shape, jnp.int32),
-            pltpu.VMEM((2, grid_rows * wide, GRID_COLS * LANES // APY, depth), jnp.float32),
-            pltpu.VMEM((2, grid_rows, GRID_COLS * block_y, depth), jnp.float32),
-            pltpu.SemaphoreType.DMA,
-        ],
-        compiler_params=limit(4),
-        name="stack",
-    )(facts, *terms)
+    shape = (chips, slots, block_y, depth)
+    mine, other = [], []
+    for r in range(2):
+        own, theirs = pl.pallas_call(
+            functools.partial(stack_kernel, slots, near // 2, r),
+            out_shape=(
+                jax.ShapeDtypeStruct(shape, jnp.float32), jax.ShapeDtypeStruct(shape, jnp.bfloat16)
+            ),
+            in_specs=[vmem()] * (near // 2 + 1),
+            out_specs=(vmem(), vmem()),
+            scratch_shapes=[
+                pltpu.SMEM(facts.shape, jnp.int32),
+                pltpu.VMEM((grid_rows * wide, GRID_COLS * LANES // APY, depth), jnp.float32),
+                pltpu.VMEM((grid_rows, GRID_COLS * block_y, depth), jnp.float32),
+                pltpu.SemaphoreType.DMA,
+            ],
+            compiler_params=limit(4),
+            cost_estimate=pl.CostEstimate(
+                flops=8 * terms[0].size, bytes_accessed=8 * terms[0].size, transcendentals=0
+            ),
+            name="stack",
+        )(facts, *terms)
+        mine.append(own)
+        other.append(across(theirs))
     joined = pl.pallas_call(
         join_kernel,
-        out_shape=jax.ShapeDtypeStruct(shape, jnp.bfloat16),
-        in_specs=[vmem()] * 2,
+        out_shape=jax.ShapeDtypeStruct((chips, 2) + shape[1:], jnp.bfloat16),
+        in_specs=[vmem()] * 4,
         out_specs=vmem(),
         compiler_params=limit(2),
         name="join",
-    )(mine, across(other))
+    )(*mine, *other)
     sums = lax.all_to_all(
         joined, "shot", 0, 0, tiled=True,
         axis_index_groups=[list(range(core, count, 2)) for core in range(2)],

time: 56.3 us -> 57.7 us (1.025)
  Pallas kernels: 8.21 us -> 9.33 us
    pallas_call x2 -> x3, Pallas kernels: 1.17 us -> 2.29 us  [the longest x2 2.27 us: per_device(): pl.pallas_call(functools.partial(stack_kernel, slots, near // 2, r), out_...]
    ppermute x5 -> x6, waiting for transfers between devices: 2.55 us -> 2.12 us  [across(): return lax.ppermute(value, 'shot', [(i, i ^ 1) for i in range(count)])]
  transfers between devices with their start and end apart: 12 -> 13, of which waited for: 10 -> 10; matrix products, arithmetic and copies ran while one was open for 0% -> 0% of each run, Pallas kernels for 1% -> 3%
where the time goes in v10:
time: 57.7 us; the launch traced here: 57.4 us
  waiting for transfers between devices  20.5 us (36%)
  starting transfers between devices  15.4 us (27%)
  blocking collectives  10.7 us (19%)
  Pallas kernels  9.33 us (16%)
  between operations  1.41 us (2%)
    all_to_all x1, blocking collectives, per_device(): lax.all_to_all(joined, 'shot', 0, 0, tiled=True, axis_index_groups=[list(...  10.7 us
    all_to_all x1, waiting for transfers between devices, per_device(): pieces = lax.all_to_all(sent, 'shot', 0, 0, tiled=True)  9.92 us
    ppermute x6, waiting for transfers between devices, swap(): lax.ppermute(values[k], 'shot', [(i, i ^ 2 * k) for i in range(count)])  8.48 us
    all_to_all x1, starting transfers between devices, per_device(): pieces = lax.all_to_all(sent, 'shot', 0, 0, tiled=True)  7.5 us
    ppermute x6, starting transfers between devices, swap(): lax.ppermute(values[k], 'shot', [(i, i ^ 2 * k) for i in range(count)])  7.11 us
    pallas_call x1, Pallas kernels, wave(): pl.pallas_call(functools.partial(wave_kernel, near), out_shape=(out,) * (...  3 us
    pallas_call x2, Pallas kernels, per_device(): pl.pallas_call(functools.partial(stack_kernel, slots, near // 2, r), out_...  2.27 us
    ppermute x6, waiting for transfers between devices, across(): return lax.ppermute(value, 'shot', [(i, i ^ 1) for i in range(count)])  2.12 us
  transfers between devices with their start and end apart: 13, of which 10 were waited for; matrix products, arithmetic and copies ran while one was open for 0% of the time, Pallas kernels for 3%

profile of v10, /device:TPU:0, one launch (start us, length us, event | category | flops | bytes accessed | tf_op | source)
XLA Modules:
  0.0 57.4 jit_solution(7707569536942844952)
XLA Ops:
  1.3 1.8 %prepare.1 = bf16[16,9,8,128]{3,2,1,0:T(8,128)(2,1)} custom-call(s32[1]{0:T(128)S(6)} %copy.11.row_ref, s32[1]{0:T(128)S(6)} %copy.12.col_ref, s32[4]{0:T(128)} %ids_hbm.1, s32[4,8,8]{2,1,0:T(8,128)} %floor_hbm.1, bf16[4,8,8,128]{3,2,1,0:T(8,128)(2,1)} %p_hbm.1, bf16[4,8,8,128]{3,2,1,0:T(8,128)(2,1)} %s_hbm.1, bf16[4,8,8,128]{3,2,1,0:T(8,128)(2,1)} %rho_hbm.1, ...), custom_call_target="tpu_custom_call" | custom-call | tf_op jit(solution)/shard_map/prepare/pallas_call | solution.py:508
  3.1 0.0 copy-start
  3.2 0.0 copy-start.1
  3.2 7.5 %all-to-all-start = ((bf16[16,9,8,128]{3,2,1,0:T(8,128)(2,1)}), bf16[16,9,8,128]{3,2,1,0:T(8,128)(2,1)S(1)}, u32[]{:S(2)}, u32[]{:S(2)}) async-start(bf16[16,9,8,128]{3,2,1,0:T(8,128)(2,1)} %prepare.1), calls=%async_computation | async-start | bytes 589824 | tf_op jit(solution)/shard_map/all_to_all | solution.py:524
  10.7 0.0 copy-done
  10.7 0.0 copy-done.1
  10.7 0.6 %start.1 = (f32[32,4,8,128]{3,2,1,0:T(8,128)S(1)}, f32[32,4,8,128]{3,2,1,0:T(8,128)S(1)}, f32[32,4,8,128]{3,2,1,0:T(8,128)S(1)}) custom-call(bf16[32,32,128]{2,1,0:T(8,128)(2,1)S(1)} %bitcast.4, bf16[32,32,128]{2,1,0:T(8,128)(2,1)S(1)} %bitcast.5), custom_call_target="tpu_custom_call" | custom-call | flops 2621440 | bytes 2097152 | tf_op jit(solution)/shard_map/start/pallas_call | solution.py:257
  11.3 9.9 %all-to-all-done = bf16[16,9,8,128]{3,2,1,0:T(8,128)(2,1)S(1)} async-done(((bf16[16,9,8,128]{3,2,1,0:T(8,128)(2,1)}), bf16[16,9,8,128]{3,2,1,0:T(8,128)(2,1)S(1)}, u32[]{:S(2)}, u32[]{:S(2)}) %all-to-all-start) | async-done | bytes 294944 | tf_op jit(solution)/shard_map/all_to_all | solution.py:524
  21.2 0.9 %pick.1 = (bf16[64,8,128]{2,1,0:T(8,128)(2,1)S(1)}, bf16[64,8,128]{2,1,0:T(8,128)(2,1)S(1)}, bf16[64,8,128]{2,1,0:T(8,128)(2,1)S(1)}, bf16[32,8,128]{2,1,0:T(8,1...) custom-call(bf16[144,8,128]{2,1,0:T(8,128)(2,1)S(1)} %bitcast.3), custom_call_target="tpu_custom_call" | custom-call | tf_op jit(solution)/shard_map/pick/pallas_call | solution.py:529
  22.2 0.8 %collective-permute-start = (bf16[64,8,128]{2,1,0:T(8,128)(2,1)S(1)}, bf16[64,8,128]{2,1,0:T(8,128)(2,1)S(1)}, u32[]{:S(2)}, u32[]{:S(2)}) collective-permute-start(bf16[64,8,128]{2,1,0:T(8,128)(2,1)S(1)} %get-tuple-element.31), channel_id=1, source_target_pairs={{0,6},{1,7},{2,4},{3,5},{4,2},{5,3},{6,0},{7,1},{8,14},{9,15},{10,... | collective-permute-start | bytes 393224 | tf_op jit(solution)/shard_map/ppermute | solution.py:500
  23.0 0.3 collective-permute-start.1
  23.3 2.4 %collective-permute-start.2 = (bf16[64,8,128]{2,1,0:T(8,128)(2,1)S(1)}, bf16[64,8,128]{2,1,0:T(8,128)(2,1)S(1)}, u32[]{:S(2)}, u32[]{:S(2)}) collective-permute-start(bf16[64,8,128]{2,1,0:T(8,128)(2,1)S(1)} %get-tuple-element.33), channel_id=1, source_target_pairs={{0,2},{1,3},{2,0},{3,1},{4,6},{5,7},{6,4},{7,5},{8,10},{9,11},{10,... | collective-permute-start | bytes 393224 | tf_op jit(solution)/shard_map/ppermute | solution.py:500
  25.7 0.0 collective-permute-start.6
  25.7 3.8 %collective-permute-done.refs_0_ = bf16[64,8,128]{2,1,0:T(8,128)(2,1)S(1)} collective-permute-done((bf16[64,8,128]{2,1,0:T(8,128)(2,1)S(1)}, bf16[64,8,128]{2,1,0:T(8,128)(2,1)S(1)}, u32[]{:S(2)}, u32[]{:S(2)}) %collective-permute-start) | collective-permute-done | bytes 131104 | tf_op jit(solution)/shard_map/ppermute | solution.py:500
  29.5 0.0 collective-permute-start.3
  29.5 0.9 %collective-permute-done.1.refs_1_ = bf16[64,8,128]{2,1,0:T(8,128)(2,1)S(1)} collective-permute-done((bf16[64,8,128]{2,1,0:T(8,128)(2,1)S(1)}, bf16[64,8,128]{2,1,0:T(8,128)(2,1)S(1)}, u32[]{:S(2)}, u32[]{:S(2)}) %collective-permute-start.1) | collective-permute-done | bytes 131104 | tf_op jit(solution)/shard_map/ppermute | solution.py:500
  30.4 0.2 collective-permute-start.4
  30.6 0.6 %collective-permute-done.2.refs_2_ = bf16[64,8,128]{2,1,0:T(8,128)(2,1)S(1)} collective-permute-done((bf16[64,8,128]{2,1,0:T(8,128)(2,1)S(1)}, bf16[64,8,128]{2,1,0:T(8,128)(2,1)S(1)}, u32[]{:S(2)}, u32[]{:S(2)}) %collective-permute-start.2) | collective-permute-done | bytes 131104 | tf_op jit(solution)/shard_map/ppermute | solution.py:500
  31.2 0.0 collective-permute-start.5
  31.3 0.0 collective-permute-done.6.refs_7_
  31.3 0.0 collective-permute-done.3.refs_4_
  31.3 0.4 collective-permute-done.4.refs_5_
  31.7 0.8 %collective-permute-done.5.refs_6_ = bf16[32,8,128]{2,1,0:T(8,128)(2,1)S(1)} collective-permute-done((bf16[32,8,128]{2,1,0:T(8,128)(2,1)S(1)}, bf16[32,8,128]{2,1,0:T(8,128)(2,1)S(1)}, u32[]{:S(2)}, u32[]{:S(2)}) %collective-permute-start.5) | collective-permute-done | bytes 65568 | tf_op jit(solution)/shard_map/ppermute | solution.py:506
  32.5 3.0 %wave.1 = (bf16[32,8,128]{2,1,0:T(8,128)(2,1)S(1)}, bf16[32,8,128]{2,1,0:T(8,128)(2,1)S(1)}, bf16[32,8,128]{2,1,0:T(8,128)(2,1)S(1)}, bf16[32,8,128]{2,1,0:T(8,128)(2,1)S(1)}) custom-call(bf16[64,8,128]{2,1,0:T(8,128)(2,1)S(1)} %collective-permute-done.refs_0_, bf16[64,8,128]{2,1,0:T(8,128)(2,1)S(1)} %collective-permute-done.1.refs_1_, ...), custom_call_target="tpu_custom_call" | custom-call | tf_op jit(solution)/shard_map/wave/pallas_call | solution.py:367
  35.5 1.3 %collective-permute-start.7 = (bf16[32,8,128]{2,1,0:T(8,128)(2,1)S(1)}, bf16[32,8,128]{2,1,0:T(8,128)(2,1)S(1)}, u32[]{:S(2)}, u32[]{:S(2)}) collective-permute-start(bf16[32,8,128]{2,1,0:T(8,128)(2,1)S(1)} %get-tuple-element.39), channel_id=1, source_target_pairs={{0,6},{1,7},{2,4},{3,5},{4,2},{5,3},{6,0},{7,1},{8,14},{9,15},{10,... | collective-permute-start | bytes 196616 | tf_op jit(solution)/shard_map/ppermute | solution.py:500
  36.8 1.0 %collective-permute-start.8 = (bf16[32,8,128]{2,1,0:T(8,128)(2,1)S(1)}, bf16[32,8,128]{2,1,0:T(8,128)(2,1)S(1)}, u32[]{:S(2)}, u32[]{:S(2)}) collective-permute-start(bf16[32,8,128]{2,1,0:T(8,128)(2,1)S(1)} %get-tuple-element.40), channel_id=1, source_target_pairs={{0,4},{1,5},{2,6},{3,7},{4,0},{5,1},{6,2},{7,3},{8,12},{9,13},{10,... | collective-permute-start | bytes 196616 | tf_op jit(solution)/shard_map/ppermute | solution.py:500
  37.8 1.2 %collective-permute-start.9 = (bf16[32,8,128]{2,1,0:T(8,128)(2,1)S(1)}, bf16[32,8,128]{2,1,0:T(8,128)(2,1)S(1)}, u32[]{:S(2)}, u32[]{:S(2)}) collective-permute-start(bf16[32,8,128]{2,1,0:T(8,128)(2,1)S(1)} %get-tuple-element.41), channel_id=1, source_target_pairs={{0,2},{1,3},{2,0},{3,1},{4,6},{5,7},{6,4},{7,5},{8,10},{9,11},{10,... | collective-permute-start | bytes 196616 | tf_op jit(solution)/shard_map/ppermute | solution.py:500
  39.0 2.4 %collective-permute-done.7.refs_0_ = bf16[32,8,128]{2,1,0:T(8,128)(2,1)S(1)} collective-permute-done((bf16[32,8,128]{2,1,0:T(8,128)(2,1)S(1)}, bf16[32,8,128]{2,1,0:T(8,128)(2,1)S(1)}, u32[]{:S(2)}, u32[]{:S(2)}) %collective-permute-start.7) | collective-permute-done | bytes 65568 | tf_op jit(solution)/shard_map/ppermute | solution.py:500
  41.4 0.1 collective-permute-done.8.refs_1_
  41.5 0.7 %collective-permute-done.9.refs_2_ = bf16[32,8,128]{2,1,0:T(8,128)(2,1)S(1)} collective-permute-done((bf16[32,8,128]{2,1,0:T(8,128)(2,1)S(1)}, bf16[32,8,128]{2,1,0:T(8,128)(2,1)S(1)}, u32[]{:S(2)}, u32[]{:S(2)}) %collective-permute-start.9) | collective-permute-done | bytes 65568 | tf_op jit(solution)/shard_map/ppermute | solution.py:500
  42.2 1.1 %stack.3 = (f32[8,4,8,128]{3,2,1,0:T(8,128)S(1)}, bf16[8,4,8,128]{3,2,1,0:T(8,128)(2,1)S(1)}) custom-call(s32[16,128]{1,0:T(8,128)S(1)} %get-tuple-element.30.facts_ref, bf16[32,8,128]{2,1,0:T(8,128)(2,1)S(1)} %collective-permute-done.7.refs_0_, bf16[32,8,128]{2,1,0:T(8,128)(2,1)S(1)} %collective-permute-done.8.refs_1_, ...), custom_call_target="tpu_custom_call" | custom-call | flops 262144 | bytes 262144 | tf_op jit(solution)/shard_map/stack/pallas_call | solution.py:565
  43.3 0.1 collective-permute-start.11
  43.4 1.1 %stack.2 = (f32[8,4,8,128]{3,2,1,0:T(8,128)S(1)}, bf16[8,4,8,128]{3,2,1,0:T(8,128)(2,1)S(1)}) custom-call(s32[16,128]{1,0:T(8,128)S(1)} %get-tuple-element.30.facts_ref, bf16[32,8,128]{2,1,0:T(8,128)(2,1)S(1)} %collective-permute-done.7.refs_0_, bf16[32,8,128]{2,1,0:T(8,128)(2,1)S(1)} %collective-permute-done.8.refs_1_, ...), custom_call_target="tpu_custom_call" | custom-call | flops 262144 | bytes 262144 | tf_op jit(solution)/shard_map/stack/pallas_call | solution.py:565
  44.6 0.6 collective-permute-start.10
  45.1 0.0 collective-permute-done.11.refs_3_
  45.1 0.9 %collective-permute-done.10.refs_2_ = bf16[8,4,8,128]{3,2,1,0:T(8,128)(2,1)S(1)} collective-permute-done((bf16[8,4,8,128]{3,2,1,0:T(8,128)(2,1)S(1)}, bf16[8,4,8,128]{3,2,1,0:T(8,128)(2,1)S(1)}, u32[]{:S(2)}, u32[]{:S(2)}) %collective-permute-start.10) | collective-permute-done | bytes 65568 | tf_op jit(solution)/shard_map/ppermute | solution.py:506
  46.1 10.7 %all_to_all.10.sums_ref = bf16[8,2,4,8,128]{4,3,2,1,0:T(8,128)(2,1)S(1)} all-to-all(bf16[8,2,4,8,128]{4,3,2,1,0:T(8,128)(2,1)S(1)} %join.1), channel_id=1, replica_groups={{0,2,4,6,8,10,12,14},{1,3,5,7,9,11,13,15},{16,18,20,22,24,26,28,30},{17..., dimensions={0} | all-to-all | bytes 262144 | tf_op jit(solution)/shard_map/all_to_all | solution.py:594
  56.8 0.7 %finish.1 = f32[4,8,8,128]{3,2,1,0:T(8,128)} custom-call(bf16[8,2,4,8,128]{4,3,2,1,0:T(8,128)(2,1)S(1)} %all_to_all.10.sums_ref), custom_call_target="tpu_custom_call" | custom-call | tf_op jit(solution)/shard_map/finish/pallas_call | solution.py:598
  (4 shorter events, 0.0 us)
Async XLA Ops:
  3.1 7.5 %copy-start = (bf16[1,32,32,128]{3,2,1,0:T(8,128)(2,1)S(1)}, bf16[1,32,32,128]{3,2,1,0:T(8,128)(2,1)}, u32[]{:S(2)}) copy-start(bf16[1,32,32,128]{3,2,1,0:T(8,128)(2,1)} %param.18) | copy-start | bytes 786436
  3.2 7.5 %copy-start.1 = (bf16[1,32,32,128]{3,2,1,0:T(8,128)(2,1)S(1)}, bf16[1,32,32,128]{3,2,1,0:T(8,128)(2,1)}, u32[]{:S(2)}) copy-start(bf16[1,32,32,128]{3,2,1,0:T(8,128)(2,1)} %param.19) | copy-start | bytes 786436
  3.2 18.1 %all-to-all-start = ((bf16[16,9,8,128]{3,2,1,0:T(8,128)(2,1)}), bf16[16,9,8,128]{3,2,1,0:T(8,128)(2,1)S(1)}, u32[]{:S(2)}, u32[]{:S(2)}) async-start(bf16[16,9,8,128]{3,2,1,0:T(8,128)(2,1)} %prepare.1), calls=%async_computation | async-start | bytes 589824 | tf_op jit(solution)/shard_map/all_to_all | solution.py:524
  22.2 7.3 %collective-permute-start = (bf16[64,8,128]{2,1,0:T(8,128)(2,1)S(1)}, bf16[64,8,128]{2,1,0:T(8,128)(2,1)S(1)}, u32[]{:S(2)}, u32[]{:S(2)}) collective-permute-start(bf16[64,8,128]{2,1,0:T(8,128)(2,1)S(1)} %get-tuple-element.31), channel_id=1, source_target_pairs={{0,6},{1,7},{2,4},{3,5},{4,2},{5,3},{6,0},{7,1},{8,14},{9,15},{10,... | collective-permute-start | bytes 393224 | tf_op jit(solution)/shard_map/ppermute | solution.py:500
  23.0 7.5 %collective-permute-start.1 = (bf16[64,8,128]{2,1,0:T(8,128)(2,1)S(1)}, bf16[64,8,128]{2,1,0:T(8,128)(2,1)S(1)}, u32[]{:S(2)}, u32[]{:S(2)}) collective-permute-start(bf16[64,8,128]{2,1,0:T(8,128)(2,1)S(1)} %get-tuple-element.32), channel_id=1, source_target_pairs={{0,4},{1,5},{2,6},{3,7},{4,0},{5,1},{6,2},{7,3},{8,12},{9,13},{10,... | collective-permute-start | bytes 393224 | tf_op jit(solution)/shard_map/ppermute | solution.py:500
  23.3 7.9 %collective-permute-start.2 = (bf16[64,8,128]{2,1,0:T(8,128)(2,1)S(1)}, bf16[64,8,128]{2,1,0:T(8,128)(2,1)S(1)}, u32[]{:S(2)}, u32[]{:S(2)}) collective-permute-start(bf16[64,8,128]{2,1,0:T(8,128)(2,1)S(1)} %get-tuple-element.33), channel_id=1, source_target_pairs={{0,2},{1,3},{2,0},{3,1},{4,6},{5,7},{6,4},{7,5},{8,10},{9,11},{10,... | collective-permute-start | bytes 393224 | tf_op jit(solution)/shard_map/ppermute | solution.py:500
  25.7 5.5 %collective-permute-start.6 = (bf16[32,8,128]{2,1,0:T(8,128)(2,1)S(1)}, bf16[32,8,128]{2,1,0:T(8,128)(2,1)S(1)}, u32[]{:S(2)}, u32[]{:S(2)}) collective-permute-start(bf16[32,8,128]{2,1,0:T(8,128)(2,1)S(1)} %get-tuple-element.35), channel_id=1, source_target_pairs={{0,1},{1,0},{2,3},{3,2},{4,5},{5,4},{6,7},{7,6},{8,9},{9,8},{10,11... | collective-permute-start | bytes 196616 | tf_op jit(solution)/shard_map/ppermute | solution.py:506
  29.5 1.8 %collective-permute-start.3 = (bf16[32,8,128]{2,1,0:T(8,128)(2,1)S(1)}, bf16[32,8,128]{2,1,0:T(8,128)(2,1)S(1)}, u32[]{:S(2)}, u32[]{:S(2)}) collective-permute-start(bf16[32,8,128]{2,1,0:T(8,128)(2,1)S(1)} %slice.12), channel_id=1, source_target_pairs={{0,1},{1,0},{2,3},{3,2},{4,5},{5,4},{6,7},{7,6},{8,9},{9,8},{10,11... | collective-permute-start | bytes 196616 | tf_op jit(solution)/shard_map/ppermute | solution.py:506
  30.4 1.3 %collective-permute-start.4 = (bf16[32,8,128]{2,1,0:T(8,128)(2,1)S(1)}, bf16[32,8,128]{2,1,0:T(8,128)(2,1)S(1)}, u32[]{:S(2)}, u32[]{:S(2)}) collective-permute-start(bf16[32,8,128]{2,1,0:T(8,128)(2,1)S(1)} %slice.13), channel_id=1, source_target_pairs={{0,1},{1,0},{2,3},{3,2},{4,5},{5,4},{6,7},{7,6},{8,9},{9,8},{10,11... | collective-permute-start | bytes 196616 | tf_op jit(solution)/shard_map/ppermute | solution.py:506
  31.2 1.3 %collective-permute-start.5 = (bf16[32,8,128]{2,1,0:T(8,128)(2,1)S(1)}, bf16[32,8,128]{2,1,0:T(8,128)(2,1)S(1)}, u32[]{:S(2)}, u32[]{:S(2)}) collective-permute-start(bf16[32,8,128]{2,1,0:T(8,128)(2,1)S(1)} %slice.14), channel_id=1, source_target_pairs={{0,1},{1,0},{2,3},{3,2},{4,5},{5,4},{6,7},{7,6},{8,9},{9,8},{10,11... | collective-permute-start | bytes 196616 | tf_op jit(solution)/shard_map/ppermute | solution.py:506
  35.5 5.9 %collective-permute-start.7 = (bf16[32,8,128]{2,1,0:T(8,128)(2,1)S(1)}, bf16[32,8,128]{2,1,0:T(8,128)(2,1)S(1)}, u32[]{:S(2)}, u32[]{:S(2)}) collective-permute-start(bf16[32,8,128]{2,1,0:T(8,128)(2,1)S(1)} %get-tuple-element.39), channel_id=1, source_target_pairs={{0,6},{1,7},{2,4},{3,5},{4,2},{5,3},{6,0},{7,1},{8,14},{9,15},{10,... | collective-permute-start | bytes 196616 | tf_op jit(solution)/shard_map/ppermute | solution.py:500
  36.8 4.7 %collective-permute-start.8 = (bf16[32,8,128]{2,1,0:T(8,128)(2,1)S(1)}, bf16[32,8,128]{2,1,0:T(8,128)(2,1)S(1)}, u32[]{:S(2)}, u32[]{:S(2)}) collective-permute-start(bf16[32,8,128]{2,1,0:T(8,128)(2,1)S(1)} %get-tuple-element.40), channel_id=1, source_target_pairs={{0,4},{1,5},{2,6},{3,7},{4,0},{5,1},{6,2},{7,3},{8,12},{9,13},{10,... | collective-permute-start | bytes 196616 | tf_op jit(solution)/shard_map/ppermute | solution.py:500
  37.8 4.4 %collective-permute-start.9 = (bf16[32,8,128]{2,1,0:T(8,128)(2,1)S(1)}, bf16[32,8,128]{2,1,0:T(8,128)(2,1)S(1)}, u32[]{:S(2)}, u32[]{:S(2)}) collective-permute-start(bf16[32,8,128]{2,1,0:T(8,128)(2,1)S(1)} %get-tuple-element.41), channel_id=1, source_target_pairs={{0,2},{1,3},{2,0},{3,1},{4,6},{5,7},{6,4},{7,5},{8,10},{9,11},{10,... | collective-permute-start | bytes 196616 | tf_op jit(solution)/shard_map/ppermute | solution.py:500
  43.3 1.8 %collective-permute-start.11 = (bf16[8,4,8,128]{3,2,1,0:T(8,128)(2,1)S(1)}, bf16[8,4,8,128]{3,2,1,0:T(8,128)(2,1)S(1)}, u32[]{:S(2)}, u32[]{:S(2)}) collective-permute-start(bf16[8,4,8,128]{3,2,1,0:T(8,128)(2,1)S(1)} %get-tuple-element.46), channel_id=1, source_target_pairs={{0,1},{1,0},{2,3},{3,2},{4,5},{5,4},{6,7},{7,6},{8,9},{9,8},{10,11... | collective-permute-start | bytes 196616 | tf_op jit(solution)/shard_map/ppermute | solution.py:506
  44.6 1.5 %collective-permute-start.10 = (bf16[8,4,8,128]{3,2,1,0:T(8,128)(2,1)S(1)}, bf16[8,4,8,128]{3,2,1,0:T(8,128)(2,1)S(1)}, u32[]{:S(2)}, u32[]{:S(2)}) collective-permute-start(bf16[8,4,8,128]{3,2,1,0:T(8,128)(2,1)S(1)} %get-tuple-element.45), channel_id=1, source_target_pairs={{0,1},{1,0},{2,3},{3,2},{4,5},{5,4},{6,7},{7,6},{8,9},{9,8},{10,11... | collective-permute-start | bytes 196616 | tf_op jit(solution)/shard_map/ppermute | solution.py:506

commit v11 on v9

--- a/solution.py
+++ b/solution.py
@@ -11,6 +11,7 @@
 APY = 4
 STEPS = 4
 GRID_COLS = 8
+FACTS = 8
 LANES = 8
 
 speed_factor = 0.28
@@ -130,6 +131,7 @@
             for piece in range(x, out_ref.shape[0], near):
                 out_ref[piece, 2 * slot] = coef
                 out_ref[piece, 2 * slot + 1] = pert[slot, x]
+    lane = lane - FACTS * lax.axis_index("shot")
     facts = jnp.where(lane == slots, row_ref[0], 0)
     facts = jnp.where(lane == slots + 1, col_ref[0], facts)
     for slot in range(slots):
@@ -143,24 +145,25 @@
     chips = near // 2
     out_refs = refs[:chips][::-1]
     beside_ref, facts_ref, facts, spots, sem = refs[chips:]
-    count = facts_ref.shape[0]
+    count = spots.shape[0] // slots
     tiles = 2 * slots + 1
-    for piece in range(count):
-        tile = pieces_ref[piece * tiles + 2 * slots].astype(jnp.float32)
-        facts_ref[piece:piece + 1] = tile.astype(jnp.int32)[0:1]
+    line = pieces_ref[2 * slots].astype(jnp.float32)
+    for piece in range(1, count):
+        line = line + pieces_ref[piece * tiles + 2 * slots].astype(jnp.float32)
+    facts_ref[...] = line.astype(jnp.int32)[0:1]
     copy = pltpu.make_async_copy(facts_ref, facts, sem)
     copy.start()
     me = lax.axis_index("shot")
     copy.wait()
     for piece in range(count):
         for slot in range(slots):
-            spots[facts[piece, slot]] = piece * tiles + 2 * slot
+            spots[facts[0, FACTS * piece + slot]] = piece * tiles + 2 * slot
     for t in range(near):
         shot = me ^ t
         out_ref, start_tile = out_refs[t // 2], t % 2 * APX * APY * 2
         if t == 1:
             out_ref, start_tile = beside_ref, 0
-        first = facts[shot, slots] * GRID_COLS + facts[shot, slots + 1]
+        first = facts[0, FACTS * shot + slots] * GRID_COLS + facts[0, FACTS * shot + slots + 1]
         for x in range(APX):
             found = []
             for y in range(APY):
@@ -406,7 +409,7 @@
 def stack_kernel(slots, near, facts_ref, *refs):
     terms_refs = refs[:near][::-1]
     mine_ref, other_ref, facts, total, lined, sem = refs[near:]
-    count = facts_ref.shape[0]
+    count = 2 * mine_ref.shape[0]
     half = terms_refs[0].shape[0] // 2
     wide = half // APX
     width = LANES // APY
@@ -423,8 +426,9 @@
     lax.fori_loop(0, total.shape[1], clear, 0, unroll=8)
     copy.wait()
     for k, terms_ref in enumerate(terms_refs):
-        first = facts[me ^ 2 * k, slots] * wide
-        rows = pl.ds(facts[me ^ 2 * k, slots + 1] * width, LANES)
+        shot = FACTS * (me ^ 2 * k)
+        first = facts[0, shot + slots] * wide
+        rows = pl.ds(facts[0, shot + slots + 1] * width, LANES)
         for r in range(2):
             sums = [
                 total[r, first + tile, rows] + terms_ref[r * half + tile].astype(jnp.float32)
@@ -449,7 +453,7 @@
         for own, out_ref in enumerate((mine_ref, other_ref)):
             found = []
             for slot in range(slots):
-                block = facts[2 * chip + (me + own) % 2, slot]
+                block = facts[0, FACTS * (2 * chip + (me + own) % 2) + slot]
                 rows = pl.ds(pl.multiple_of(block % GRID_COLS * LANES, LANES), LANES)
                 found += [lined[r, block // GRID_COLS, rows] for r in range(2)]
             for index, tile in enumerate(found):
@@ -490,6 +494,7 @@
     slots, block_x, block_y, depth = velocity_p.shape
     count = lax.axis_size("shot")
     assert count == 2 * block_x and block_y == LANES
+    assert slots + 2 <= FACTS and FACTS * count <= depth
     patch = APX * APY
     split = lax.axis_size("depth") > 1
     if split:
@@ -536,12 +541,12 @@
                 jax.ShapeDtypeStruct((patch * tiles, block_y, depth), jnp.bfloat16)
                 for tiles in [4] * (near // 2 - 1) + [2, 2]
             ],
-            jax.ShapeDtypeStruct((count, depth), jnp.int32),
+            jax.ShapeDtypeStruct((1, depth), jnp.int32),
         ),
         in_specs=[vmem()],
         out_specs=(vmem(),) * (near // 2 + 2),
         scratch_shapes=[
-            pltpu.SMEM((count, depth), jnp.int32),
+            pltpu.SMEM((1, depth), jnp.int32),
             pltpu.SMEM((count * slots,), jnp.int32),
             pltpu.SemaphoreType.DMA,
         ],

time: 56.3 us -> 56.1 us (level)
  no operation moved by 1% of the time
where the time goes in v11:
time: 56.1 us; the launch traced here: 55.8 us
  waiting for transfers between devices  21 us (37%)
  starting transfers between devices  14.9 us (27%)
  blocking collectives  10.5 us (19%)
  Pallas kernels  7.97 us (14%)
  between operations  1.4 us (2%)
    all_to_all x1, blocking collectives, per_device(): lax.all_to_all(joined, 'shot', 0, 0, tiled=True, axis_index_groups=[list(...  10.5 us
    all_to_all x1, waiting for transfers between devices, per_device(): pieces = lax.all_to_all(sent, 'shot', 0, 0, tiled=True)  9.92 us
    ppermute x6, waiting for transfers between devices, swap(): lax.ppermute(values[k], 'shot', [(i, i ^ 2 * k) for i in range(count)])  8.48 us
    all_to_all x1, starting transfers between devices, per_device(): pieces = lax.all_to_all(sent, 'shot', 0, 0, tiled=True)  7.5 us
    ppermute x6, starting transfers between devices, swap(): lax.ppermute(values[k], 'shot', [(i, i ^ 2 * k) for i in range(count)])  7.11 us
    pallas_call x1, Pallas kernels, wave(): pl.pallas_call(functools.partial(wave_kernel, near), out_shape=(out,) * (...  3.01 us
    ppermute x5, waiting for transfers between devices, across(): return lax.ppermute(value, 'shot', [(i, i ^ 1) for i in range(count)])  2.55 us
    pallas_call x1, Pallas kernels, per_device(): pl.pallas_call(prepare_kernel, out_shape=jax.ShapeDtypeStruct((count, 2 *...  1.84 us
  transfers between devices with their start and end apart: 12, of which 10 were waited for; matrix products, arithmetic and copies ran while one was open for 0% of the time, Pallas kernels for 1%

profile of v11, /device:TPU:0, one launch (start us, length us, event | category | flops | bytes accessed | tf_op | source)
XLA Modules:
  0.0 55.8 jit_solution(10330411379552557043)
XLA Ops:
  1.3 1.8 %prepare.1 = bf16[16,9,8,128]{3,2,1,0:T(8,128)(2,1)} custom-call(s32[1]{0:T(128)S(6)} %copy.11.row_ref, s32[1]{0:T(128)S(6)} %copy.12.col_ref, s32[4]{0:T(128)} %ids_hbm.1, s32[4,8,8]{2,1,0:T(8,128)} %floor_hbm.1, bf16[4,8,8,128]{3,2,1,0:T(8,128)(2,1)} %p_hbm.1, bf16[4,8,8,128]{3,2,1,0:T(8,128)(2,1)} %s_hbm.1, bf16[4,8,8,128]{3,2,1,0:T(8,128)(2,1)} %rho_hbm.1, ...), custom_call_target="tpu_custom_call" | custom-call | tf_op jit(solution)/shard_map/prepare/pallas_call | solution.py:516
  3.1 0.0 copy-start
  3.2 0.0 copy-start.1
  3.2 7.5 %all-to-all-start = ((bf16[16,9,8,128]{3,2,1,0:T(8,128)(2,1)}), bf16[16,9,8,128]{3,2,1,0:T(8,128)(2,1)S(1)}, u32[]{:S(2)}, u32[]{:S(2)}) async-start(bf16[16,9,8,128]{3,2,1,0:T(8,128)(2,1)} %prepare.1), calls=%async_computation | async-start | bytes 589824 | tf_op jit(solution)/shard_map/all_to_all | solution.py:532
  10.7 0.0 copy-done
  10.7 0.0 copy-done.1
  10.7 0.6 %start.1 = (f32[32,4,8,128]{3,2,1,0:T(8,128)S(1)}, f32[32,4,8,128]{3,2,1,0:T(8,128)S(1)}, f32[32,4,8,128]{3,2,1,0:T(8,128)S(1)}) custom-call(bf16[32,32,128]{2,1,0:T(8,128)(2,1)S(1)} %bitcast.4, bf16[32,32,128]{2,1,0:T(8,128)(2,1)S(1)} %bitcast.5), custom_call_target="tpu_custom_call" | custom-call | flops 2621440 | bytes 2097152 | tf_op jit(solution)/shard_map/start/pallas_call | solution.py:260
  11.3 9.9 %all-to-all-done = bf16[16,9,8,128]{3,2,1,0:T(8,128)(2,1)S(1)} async-done(((bf16[16,9,8,128]{3,2,1,0:T(8,128)(2,1)}), bf16[16,9,8,128]{3,2,1,0:T(8,128)(2,1)S(1)}, u32[]{:S(2)}, u32[]{:S(2)}) %all-to-all-start) | async-done | bytes 294944 | tf_op jit(solution)/shard_map/all_to_all | solution.py:532
  21.2 0.8 %pick.1 = (bf16[64,8,128]{2,1,0:T(8,128)(2,1)S(1)}, bf16[64,8,128]{2,1,0:T(8,128)(2,1)S(1)}, bf16[64,8,128]{2,1,0:T(8,128)(2,1)S(1)}, bf16[32,8,128]{2,1,0:T(8,1...) custom-call(bf16[144,8,128]{2,1,0:T(8,128)(2,1)S(1)} %bitcast.3), custom_call_target="tpu_custom_call" | custom-call | tf_op jit(solution)/shard_map/pick/pallas_call | solution.py:537
  22.0 0.8 %collective-permute-start = (bf16[64,8,128]{2,1,0:T(8,128)(2,1)S(1)}, bf16[64,8,128]{2,1,0:T(8,128)(2,1)S(1)}, u32[]{:S(2)}, u32[]{:S(2)}) collective-permute-start(bf16[64,8,128]{2,1,0:T(8,128)(2,1)S(1)} %get-tuple-element.29), channel_id=1, source_target_pairs={{0,6},{1,7},{2,4},{3,5},{4,2},{5,3},{6,0},{7,1},{8,14},{9,15},{10,... | collective-permute-start | bytes 393224 | tf_op jit(solution)/shard_map/ppermute | solution.py:508
  22.9 0.3 collective-permute-start.1
  23.2 2.4 %collective-permute-start.2 = (bf16[64,8,128]{2,1,0:T(8,128)(2,1)S(1)}, bf16[64,8,128]{2,1,0:T(8,128)(2,1)S(1)}, u32[]{:S(2)}, u32[]{:S(2)}) collective-permute-start(bf16[64,8,128]{2,1,0:T(8,128)(2,1)S(1)} %get-tuple-element.31), channel_id=1, source_target_pairs={{0,2},{1,3},{2,0},{3,1},{4,6},{5,7},{6,4},{7,5},{8,10},{9,11},{10,... | collective-permute-start | bytes 393224 | tf_op jit(solution)/shard_map/ppermute | solution.py:508
  25.6 0.0 collective-permute-start.6
  25.6 3.8 %collective-permute-done.refs_0_ = bf16[64,8,128]{2,1,0:T(8,128)(2,1)S(1)} collective-permute-done((bf16[64,8,128]{2,1,0:T(8,128)(2,1)S(1)}, bf16[64,8,128]{2,1,0:T(8,128)(2,1)S(1)}, u32[]{:S(2)}, u32[]{:S(2)}) %collective-permute-start) | collective-permute-done | bytes 131104 | tf_op jit(solution)/shard_map/ppermute | solution.py:508
  29.4 0.0 collective-permute-start.3
  29.4 0.9 %collective-permute-done.1.refs_1_ = bf16[64,8,128]{2,1,0:T(8,128)(2,1)S(1)} collective-permute-done((bf16[64,8,128]{2,1,0:T(8,128)(2,1)S(1)}, bf16[64,8,128]{2,1,0:T(8,128)(2,1)S(1)}, u32[]{:S(2)}, u32[]{:S(2)}) %collective-permute-start.1) | collective-permute-done | bytes 131104 | tf_op jit(solution)/shard_map/ppermute | solution.py:508
  30.3 0.2 collective-permute-start.4
  30.5 0.6 %collective-permute-done.2.refs_2_ = bf16[64,8,128]{2,1,0:T(8,128)(2,1)S(1)} collective-permute-done((bf16[64,8,128]{2,1,0:T(8,128)(2,1)S(1)}, bf16[64,8,128]{2,1,0:T(8,128)(2,1)S(1)}, u32[]{:S(2)}, u32[]{:S(2)}) %collective-permute-start.2) | collective-permute-done | bytes 131104 | tf_op jit(solution)/shard_map/ppermute | solution.py:508
  31.1 0.0 collective-permute-start.5
  31.1 0.0 collective-permute-done.6.refs_7_
  31.1 0.0 collective-permute-done.3.refs_4_
  31.1 0.4 collective-permute-done.4.refs_5_
  31.6 0.8 %collective-permute-done.5.refs_6_ = bf16[32,8,128]{2,1,0:T(8,128)(2,1)S(1)} collective-permute-done((bf16[32,8,128]{2,1,0:T(8,128)(2,1)S(1)}, bf16[32,8,128]{2,1,0:T(8,128)(2,1)S(1)}, u32[]{:S(2)}, u32[]{:S(2)}) %collective-permute-start.5) | collective-permute-done | bytes 65568 | tf_op jit(solution)/shard_map/ppermute | solution.py:514
  32.4 3.0 %wave.1 = (bf16[32,8,128]{2,1,0:T(8,128)(2,1)S(1)}, bf16[32,8,128]{2,1,0:T(8,128)(2,1)S(1)}, bf16[32,8,128]{2,1,0:T(8,128)(2,1)S(1)}, bf16[32,8,128]{2,1,0:T(8,128)(2,1)S(1)}) custom-call(bf16[64,8,128]{2,1,0:T(8,128)(2,1)S(1)} %collective-permute-done.refs_0_, bf16[64,8,128]{2,1,0:T(8,128)(2,1)S(1)} %collective-permute-done.1.refs_1_, ...), custom_call_target="tpu_custom_call" | custom-call | tf_op jit(solution)/shard_map/wave/pallas_call | solution.py:370
  35.4 1.3 %collective-permute-start.7 = (bf16[32,8,128]{2,1,0:T(8,128)(2,1)S(1)}, bf16[32,8,128]{2,1,0:T(8,128)(2,1)S(1)}, u32[]{:S(2)}, u32[]{:S(2)}) collective-permute-start(bf16[32,8,128]{2,1,0:T(8,128)(2,1)S(1)} %get-tuple-element.37), channel_id=1, source_target_pairs={{0,6},{1,7},{2,4},{3,5},{4,2},{5,3},{6,0},{7,1},{8,14},{9,15},{10,... | collective-permute-start | bytes 196616 | tf_op jit(solution)/shard_map/ppermute | solution.py:508
  36.7 1.0 %collective-permute-start.8 = (bf16[32,8,128]{2,1,0:T(8,128)(2,1)S(1)}, bf16[32,8,128]{2,1,0:T(8,128)(2,1)S(1)}, u32[]{:S(2)}, u32[]{:S(2)}) collective-permute-start(bf16[32,8,128]{2,1,0:T(8,128)(2,1)S(1)} %get-tuple-element.38), channel_id=1, source_target_pairs={{0,4},{1,5},{2,6},{3,7},{4,0},{5,1},{6,2},{7,3},{8,12},{9,13},{10,... | collective-permute-start | bytes 196616 | tf_op jit(solution)/shard_map/ppermute | solution.py:508
  37.7 1.2 %collective-permute-start.9 = (bf16[32,8,128]{2,1,0:T(8,128)(2,1)S(1)}, bf16[32,8,128]{2,1,0:T(8,128)(2,1)S(1)}, u32[]{:S(2)}, u32[]{:S(2)}) collective-permute-start(bf16[32,8,128]{2,1,0:T(8,128)(2,1)S(1)} %get-tuple-element.39), channel_id=1, source_target_pairs={{0,2},{1,3},{2,0},{3,1},{4,6},{5,7},{6,4},{7,5},{8,10},{9,11},{10,... | collective-permute-start | bytes 196616 | tf_op jit(solution)/shard_map/ppermute | solution.py:508
  38.9 2.4 %collective-permute-done.7.refs_0_ = bf16[32,8,128]{2,1,0:T(8,128)(2,1)S(1)} collective-permute-done((bf16[32,8,128]{2,1,0:T(8,128)(2,1)S(1)}, bf16[32,8,128]{2,1,0:T(8,128)(2,1)S(1)}, u32[]{:S(2)}, u32[]{:S(2)}) %collective-permute-start.7) | collective-permute-done | bytes 65568 | tf_op jit(solution)/shard_map/ppermute | solution.py:508
  41.3 0.1 collective-permute-done.8.refs_1_
  41.4 0.7 %collective-permute-done.9.refs_2_ = bf16[32,8,128]{2,1,0:T(8,128)(2,1)S(1)} collective-permute-done((bf16[32,8,128]{2,1,0:T(8,128)(2,1)S(1)}, bf16[32,8,128]{2,1,0:T(8,128)(2,1)S(1)}, u32[]{:S(2)}, u32[]{:S(2)}) %collective-permute-start.9) | collective-permute-done | bytes 65568 | tf_op jit(solution)/shard_map/ppermute | solution.py:508
  42.1 1.0 %stack.1 = (f32[8,8,8,128]{3,2,1,0:T(8,128)S(1)}, bf16[8,8,8,128]{3,2,1,0:T(8,128)(2,1)S(1)}) custom-call(s32[1,128]{1,0:T(1,128)S(1)} %get-tuple-element.28.facts_ref, bf16[32,8,128]{2,1,0:T(8,128)(2,1)S(1)} %collective-permute-done.7.refs_0_, bf16[32,8,128]{2,1,0:T(8,128)(2,1)S(1)} %collective-permute-done.8.refs_1_, ...), custom_call_target="tpu_custom_call" | custom-call | tf_op jit(solution)/shard_map/stack/pallas_call | solution.py:571
  43.1 0.1 collective-permute-start.10
  43.2 1.3 %collective-permute-done.10.other_ref = bf16[8,8,8,128]{3,2,1,0:T(8,128)(2,1)S(1)} collective-permute-done((bf16[8,8,8,128]{3,2,1,0:T(8,128)(2,1)S(1)}, bf16[8,8,8,128]{3,2,1,0:T(8,128)(2,1)S(1)}, u32[]{:S(2)}, u32[]{:S(2)}) %collective-permute-start.10) | collective-permute-done | bytes 131104 | tf_op jit(solution)/shard_map/ppermute | solution.py:514
  44.6 10.5 %all_to_all.10.sums_ref = bf16[8,8,8,128]{3,2,1,0:T(8,128)(2,1)S(1)} all-to-all(bf16[8,8,8,128]{3,2,1,0:T(8,128)(2,1)S(1)} %join.1), channel_id=1, replica_groups={{0,2,4,6,8,10,12,14},{1,3,5,7,9,11,13,15},{16,18,20,22,24,26,28,30},{17..., dimensions={0} | all-to-all | bytes 262144 | tf_op jit(solution)/shard_map/all_to_all | solution.py:595
  55.1 0.7 %finish.1 = f32[4,8,8,128]{3,2,1,0:T(8,128)} custom-call(bf16[8,8,8,128]{3,2,1,0:T(8,128)(2,1)S(1)} %all_to_all.10.sums_ref), custom_call_target="tpu_custom_call" | custom-call | tf_op jit(solution)/shard_map/finish/pallas_call | solution.py:599
  (4 shorter events, 0.0 us)
Async XLA Ops:
  3.1 7.5 %copy-start = (bf16[1,32,32,128]{3,2,1,0:T(8,128)(2,1)S(1)}, bf16[1,32,32,128]{3,2,1,0:T(8,128)(2,1)}, u32[]{:S(2)}) copy-start(bf16[1,32,32,128]{3,2,1,0:T(8,128)(2,1)} %param.18) | copy-start | bytes 786436
  3.2 7.5 %copy-start.1 = (bf16[1,32,32,128]{3,2,1,0:T(8,128)(2,1)S(1)}, bf16[1,32,32,128]{3,2,1,0:T(8,128)(2,1)}, u32[]{:S(2)}) copy-start(bf16[1,32,32,128]{3,2,1,0:T(8,128)(2,1)} %param.19) | copy-start | bytes 786436
  3.2 18.1 %all-to-all-start = ((bf16[16,9,8,128]{3,2,1,0:T(8,128)(2,1)}), bf16[16,9,8,128]{3,2,1,0:T(8,128)(2,1)S(1)}, u32[]{:S(2)}, u32[]{:S(2)}) async-start(bf16[16,9,8,128]{3,2,1,0:T(8,128)(2,1)} %prepare.1), calls=%async_computation | async-start | bytes 589824 | tf_op jit(solution)/shard_map/all_to_all | solution.py:532
  22.0 7.3 %collective-permute-start = (bf16[64,8,128]{2,1,0:T(8,128)(2,1)S(1)}, bf16[64,8,128]{2,1,0:T(8,128)(2,1)S(1)}, u32[]{:S(2)}, u32[]{:S(2)}) collective-permute-start(bf16[64,8,128]{2,1,0:T(8,128)(2,1)S(1)} %get-tuple-element.29), channel_id=1, source_target_pairs={{0,6},{1,7},{2,4},{3,5},{4,2},{5,3},{6,0},{7,1},{8,14},{9,15},{10,... | collective-permute-start | bytes 393224 | tf_op jit(solution)/shard_map/ppermute | solution.py:508
  22.9 7.5 %collective-permute-start.1 = (bf16[64,8,128]{2,1,0:T(8,128)(2,1)S(1)}, bf16[64,8,128]{2,1,0:T(8,128)(2,1)S(1)}, u32[]{:S(2)}, u32[]{:S(2)}) collective-permute-start(bf16[64,8,128]{2,1,0:T(8,128)(2,1)S(1)} %get-tuple-element.30), channel_id=1, source_target_pairs={{0,4},{1,5},{2,6},{3,7},{4,0},{5,1},{6,2},{7,3},{8,12},{9,13},{10,... | collective-permute-start | bytes 393224 | tf_op jit(solution)/shard_map/ppermute | solution.py:508
  23.2 7.9 %collective-permute-start.2 = (bf16[64,8,128]{2,1,0:T(8,128)(2,1)S(1)}, bf16[64,8,128]{2,1,0:T(8,128)(2,1)S(1)}, u32[]{:S(2)}, u32[]{:S(2)}) collective-permute-start(bf16[64,8,128]{2,1,0:T(8,128)(2,1)S(1)} %get-tuple-element.31), channel_id=1, source_target_pairs={{0,2},{1,3},{2,0},{3,1},{4,6},{5,7},{6,4},{7,5},{8,10},{9,11},{10,... | collective-permute-start | bytes 393224 | tf_op jit(solution)/shard_map/ppermute | solution.py:508
  25.6 5.5 %collective-permute-start.6 = (bf16[32,8,128]{2,1,0:T(8,128)(2,1)S(1)}, bf16[32,8,128]{2,1,0:T(8,128)(2,1)S(1)}, u32[]{:S(2)}, u32[]{:S(2)}) collective-permute-start(bf16[32,8,128]{2,1,0:T(8,128)(2,1)S(1)} %get-tuple-element.33), channel_id=1, source_target_pairs={{0,1},{1,0},{2,3},{3,2},{4,5},{5,4},{6,7},{7,6},{8,9},{9,8},{10,11... | collective-permute-start | bytes 196616 | tf_op jit(solution)/shard_map/ppermute | solution.py:514
  29.4 1.8 %collective-permute-start.3 = (bf16[32,8,128]{2,1,0:T(8,128)(2,1)S(1)}, bf16[32,8,128]{2,1,0:T(8,128)(2,1)S(1)}, u32[]{:S(2)}, u32[]{:S(2)}) collective-permute-start(bf16[32,8,128]{2,1,0:T(8,128)(2,1)S(1)} %slice.12), channel_id=1, source_target_pairs={{0,1},{1,0},{2,3},{3,2},{4,5},{5,4},{6,7},{7,6},{8,9},{9,8},{10,11... | collective-permute-start | bytes 196616 | tf_op jit(solution)/shard_map/ppermute | solution.py:514
  30.3 1.3 %collective-permute-start.4 = (bf16[32,8,128]{2,1,0:T(8,128)(2,1)S(1)}, bf16[32,8,128]{2,1,0:T(8,128)(2,1)S(1)}, u32[]{:S(2)}, u32[]{:S(2)}) collective-permute-start(bf16[32,8,128]{2,1,0:T(8,128)(2,1)S(1)} %slice.13), channel_id=1, source_target_pairs={{0,1},{1,0},{2,3},{3,2},{4,5},{5,4},{6,7},{7,6},{8,9},{9,8},{10,11... | collective-permute-start | bytes 196616 | tf_op jit(solution)/shard_map/ppermute | solution.py:514
  31.1 1.3 %collective-permute-start.5 = (bf16[32,8,128]{2,1,0:T(8,128)(2,1)S(1)}, bf16[32,8,128]{2,1,0:T(8,128)(2,1)S(1)}, u32[]{:S(2)}, u32[]{:S(2)}) collective-permute-start(bf16[32,8,128]{2,1,0:T(8,128)(2,1)S(1)} %slice.14), channel_id=1, source_target_pairs={{0,1},{1,0},{2,3},{3,2},{4,5},{5,4},{6,7},{7,6},{8,9},{9,8},{10,11... | collective-permute-start | bytes 196616 | tf_op jit(solution)/shard_map/ppermute | solution.py:514
  35.4 5.9 %collective-permute-start.7 = (bf16[32,8,128]{2,1,0:T(8,128)(2,1)S(1)}, bf16[32,8,128]{2,1,0:T(8,128)(2,1)S(1)}, u32[]{:S(2)}, u32[]{:S(2)}) collective-permute-start(bf16[32,8,128]{2,1,0:T(8,128)(2,1)S(1)} %get-tuple-element.37), channel_id=1, source_target_pairs={{0,6},{1,7},{2,4},{3,5},{4,2},{5,3},{6,0},{7,1},{8,14},{9,15},{10,... | collective-permute-start | bytes 196616 | tf_op jit(solution)/shard_map/ppermute | solution.py:508
  36.7 4.7 %collective-permute-start.8 = (bf16[32,8,128]{2,1,0:T(8,128)(2,1)S(1)}, bf16[32,8,128]{2,1,0:T(8,128)(2,1)S(1)}, u32[]{:S(2)}, u32[]{:S(2)}) collective-permute-start(bf16[32,8,128]{2,1,0:T(8,128)(2,1)S(1)} %get-tuple-element.38), channel_id=1, source_target_pairs={{0,4},{1,5},{2,6},{3,7},{4,0},{5,1},{6,2},{7,3},{8,12},{9,13},{10,... | collective-permute-start | bytes 196616 | tf_op jit(solution)/shard_map/ppermute | solution.py:508
  37.7 4.4 %collective-permute-start.9 = (bf16[32,8,128]{2,1,0:T(8,128)(2,1)S(1)}, bf16[32,8,128]{2,1,0:T(8,128)(2,1)S(1)}, u32[]{:S(2)}, u32[]{:S(2)}) collective-permute-start(bf16[32,8,128]{2,1,0:T(8,128)(2,1)S(1)} %get-tuple-element.39), channel_id=1, source_target_pairs={{0,2},{1,3},{2,0},{3,1},{4,6},{5,7},{6,4},{7,5},{8,10},{9,11},{10,... | collective-permute-start | bytes 196616 | tf_op jit(solution)/shard_map/ppermute | solution.py:508
  43.1 1.4 %collective-permute-start.10 = (bf16[8,8,8,128]{3,2,1,0:T(8,128)(2,1)S(1)}, bf16[8,8,8,128]{3,2,1,0:T(8,128)(2,1)S(1)}, u32[]{:S(2)}, u32[]{:S(2)}) collective-permute-start(bf16[8,8,8,128]{3,2,1,0:T(8,128)(2,1)S(1)} %get-tuple-element.42), channel_id=1, source_target_pairs={{0,1},{1,0},{2,3},{3,2},{4,5},{5,4},{6,7},{7,6},{8,9},{9,8},{10,11... | collective-permute-start | bytes 393224 | tf_op jit(solution)/shard_map/ppermute | solution.py:514

commit v12 on v11

--- a/solution.py
+++ b/solution.py
@@ -533,7 +533,6 @@
 
     if not split:
         started = start(wave_prev[0], wave_now[0])
-        pieces, started = lax.optimization_barrier((pieces, started))
     *picked, facts = pl.pallas_call(
         functools.partial(pick_kernel, slots, near),
         out_shape=(

time: 56.1 us -> 55.9 us (level)
  blocking collectives: 10.5 us -> 28.5 us
  waiting for transfers between devices: 21 us -> 10.4 us
  starting transfers between devices: 14.9 us -> 7.38 us
    all_to_all x0 -> x1, blocking collectives: none -> 17.9 us  [per_device(): pieces = lax.all_to_all(sent, 'shot', 0, 0, tiled=True)]
    all_to_all x1 -> x0, waiting for transfers between devices: 9.92 us -> none  [per_device(): pieces = lax.all_to_all(sent, 'shot', 0, 0, tiled=True)]
    all_to_all x1 -> x0, starting transfers between devices: 7.5 us -> none  [per_device(): pieces = lax.all_to_all(sent, 'shot', 0, 0, tiled=True)]
    ppermute x5, waiting for transfers between devices: 2.55 us -> 1.91 us  [across(): return lax.ppermute(value, 'shot', [(i, i ^ 1) for i in range(count)])]
  transfers between devices with their start and end apart: 12 -> 11, of which waited for: 10 -> 8; matrix products, arithmetic and copies ran while one was open for 0% -> 0% of each run, Pallas kernels for 1% -> 1%
where the time goes in v12:
time: 55.9 us; the launch traced here: 55.6 us
  blocking collectives  28.5 us (51%)
  waiting for transfers between devices  10.4 us (19%)
  Pallas kernels  7.97 us (14%)
  starting transfers between devices  7.38 us (13%)
  between operations  1.4 us (3%)
    all_to_all x1, blocking collectives, per_device(): pieces = lax.all_to_all(sent, 'shot', 0, 0, tiled=True)  17.9 us
    all_to_all x1, blocking collectives, per_device(): lax.all_to_all(joined, 'shot', 0, 0, tiled=True, axis_index_groups=[list(...  10.5 us
    ppermute x6, waiting for transfers between devices, swap(): lax.ppermute(values[k], 'shot', [(i, i ^ 2 * k) for i in range(count)])  8.48 us
    ppermute x6, starting transfers between devices, swap(): lax.ppermute(values[k], 'shot', [(i, i ^ 2 * k) for i in range(count)])  7.11 us
    pallas_call x1, Pallas kernels, wave(): pl.pallas_call(functools.partial(wave_kernel, near), out_shape=(out,) * (...  3.01 us
    ppermute x5, waiting for transfers between devices, across(): return lax.ppermute(value, 'shot', [(i, i ^ 1) for i in range(count)])  1.91 us
    pallas_call x1, Pallas kernels, per_device(): pl.pallas_call(prepare_kernel, out_shape=jax.ShapeDtypeStruct((count, 2 *...  1.84 us
  transfers between devices with their start and end apart: 11, of which 8 were waited for; matrix products, arithmetic and copies ran while one was open for 0% of the time, Pallas kernels for 1%

profile of v12, /device:TPU:0, one launch (start us, length us, event | category | flops | bytes accessed | tf_op | source)
XLA Modules:
  0.0 55.6 jit_solution(1485766494477520358)
XLA Ops:
  1.3 1.8 %prepare.1 = bf16[16,9,8,128]{3,2,1,0:T(8,128)(2,1)} custom-call(s32[1]{0:T(128)S(6)} %copy.11.row_ref, s32[1]{0:T(128)S(6)} %copy.12.col_ref, s32[4]{0:T(128)} %ids_hbm.1, s32[4,8,8]{2,1,0:T(8,128)} %floor_hbm.1, bf16[4,8,8,128]{3,2,1,0:T(8,128)(2,1)} %p_hbm.1, bf16[4,8,8,128]{3,2,1,0:T(8,128)(2,1)} %s_hbm.1, bf16[4,8,8,128]{3,2,1,0:T(8,128)(2,1)} %rho_hbm.1, ...), custom_call_target="tpu_custom_call" | custom-call | tf_op jit(solution)/shard_map/prepare/pallas_call | solution.py:516
  3.1 17.9 %all_to_all.10 = bf16[16,9,8,128]{3,2,1,0:T(8,128)(2,1)S(1)} all-to-all(bf16[16,9,8,128]{3,2,1,0:T(8,128)(2,1)} %prepare.1), channel_id=1, replica_groups=mesh['grp'=2,'shot'=16,'depth'=1] {'shot'}, dimensions={0} | all-to-all | bytes 589824 | tf_op jit(solution)/shard_map/all_to_all | solution.py:532
  21.1 0.0 copy-start.1
  21.1 0.8 %pick.1 = (bf16[64,8,128]{2,1,0:T(8,128)(2,1)S(1)}, bf16[64,8,128]{2,1,0:T(8,128)(2,1)S(1)}, bf16[64,8,128]{2,1,0:T(8,128)(2,1)S(1)}, bf16[32,8,128]{2,1,0:T(8,1...) custom-call(bf16[144,8,128]{2,1,0:T(8,128)(2,1)S(1)} %bitcast.3), custom_call_target="tpu_custom_call" | custom-call | tf_op jit(solution)/shard_map/pick/pallas_call | solution.py:536
  21.9 0.0 copy-start
  21.9 0.8 %collective-permute-start = (bf16[64,8,128]{2,1,0:T(8,128)(2,1)S(1)}, bf16[64,8,128]{2,1,0:T(8,128)(2,1)S(1)}, u32[]{:S(2)}, u32[]{:S(2)}) collective-permute-start(bf16[64,8,128]{2,1,0:T(8,128)(2,1)S(1)} %get-tuple-element.21), channel_id=1, source_target_pairs={{0,6},{1,7},{2,4},{3,5},{4,2},{5,3},{6,0},{7,1},{8,14},{9,15},{10,... | collective-permute-start | bytes 393224 | tf_op jit(solution)/shard_map/ppermute | solution.py:508
  22.7 0.3 collective-permute-start.1
  23.1 2.4 %collective-permute-start.2 = (bf16[64,8,128]{2,1,0:T(8,128)(2,1)S(1)}, bf16[64,8,128]{2,1,0:T(8,128)(2,1)S(1)}, u32[]{:S(2)}, u32[]{:S(2)}) collective-permute-start(bf16[64,8,128]{2,1,0:T(8,128)(2,1)S(1)} %get-tuple-element.23), channel_id=1, source_target_pairs={{0,2},{1,3},{2,0},{3,1},{4,6},{5,7},{6,4},{7,5},{8,10},{9,11},{10,... | collective-permute-start | bytes 393224 | tf_op jit(solution)/shard_map/ppermute | solution.py:508
  25.5 0.0 collective-permute-start.6
  25.5 3.8 %collective-permute-done.refs_0_ = bf16[64,8,128]{2,1,0:T(8,128)(2,1)S(1)} collective-permute-done((bf16[64,8,128]{2,1,0:T(8,128)(2,1)S(1)}, bf16[64,8,128]{2,1,0:T(8,128)(2,1)S(1)}, u32[]{:S(2)}, u32[]{:S(2)}) %collective-permute-start) | collective-permute-done | bytes 131104 | tf_op jit(solution)/shard_map/ppermute | solution.py:508
  29.2 0.0 collective-permute-start.3
  29.3 0.9 %collective-permute-done.1.refs_1_ = bf16[64,8,128]{2,1,0:T(8,128)(2,1)S(1)} collective-permute-done((bf16[64,8,128]{2,1,0:T(8,128)(2,1)S(1)}, bf16[64,8,128]{2,1,0:T(8,128)(2,1)S(1)}, u32[]{:S(2)}, u32[]{:S(2)}) %collective-permute-start.1) | collective-permute-done | bytes 131104 | tf_op jit(solution)/shard_map/ppermute | solution.py:508
  30.2 0.2 collective-permute-start.4
  30.4 0.6 %collective-permute-done.2.refs_2_ = bf16[64,8,128]{2,1,0:T(8,128)(2,1)S(1)} collective-permute-done((bf16[64,8,128]{2,1,0:T(8,128)(2,1)S(1)}, bf16[64,8,128]{2,1,0:T(8,128)(2,1)S(1)}, u32[]{:S(2)}, u32[]{:S(2)}) %collective-permute-start.2) | collective-permute-done | bytes 131104 | tf_op jit(solution)/shard_map/ppermute | solution.py:508
  31.0 0.0 collective-permute-start.5
  31.0 0.0 copy-done.1
  31.0 0.0 copy-done
  31.0 0.6 %start.1 = (f32[32,4,8,128]{3,2,1,0:T(8,128)S(1)}, f32[32,4,8,128]{3,2,1,0:T(8,128)S(1)}, f32[32,4,8,128]{3,2,1,0:T(8,128)S(1)}) custom-call(bf16[32,32,128]{2,1,0:T(8,128)(2,1)S(1)} %bitcast.4, bf16[32,32,128]{2,1,0:T(8,128)(2,1)S(1)} %bitcast.5), custom_call_target="tpu_custom_call" | custom-call | flops 2621440 | bytes 2097152 | tf_op jit(solution)/shard_map/start/pallas_call | solution.py:260
  31.6 0.0 collective-permute-done.6.refs_7_
  31.6 0.0 collective-permute-done.3.refs_4_
  31.6 0.0 collective-permute-done.4.refs_5_
  31.7 0.6 %collective-permute-done.5.refs_6_ = bf16[32,8,128]{2,1,0:T(8,128)(2,1)S(1)} collective-permute-done((bf16[32,8,128]{2,1,0:T(8,128)(2,1)S(1)}, bf16[32,8,128]{2,1,0:T(8,128)(2,1)S(1)}, u32[]{:S(2)}, u32[]{:S(2)}) %collective-permute-start.5) | collective-permute-done | bytes 65568 | tf_op jit(solution)/shard_map/ppermute | solution.py:514
  32.2 3.0 %wave.1 = (bf16[32,8,128]{2,1,0:T(8,128)(2,1)S(1)}, bf16[32,8,128]{2,1,0:T(8,128)(2,1)S(1)}, bf16[32,8,128]{2,1,0:T(8,128)(2,1)S(1)}, bf16[32,8,128]{2,1,0:T(8,128)(2,1)S(1)}) custom-call(bf16[64,8,128]{2,1,0:T(8,128)(2,1)S(1)} %collective-permute-done.refs_0_, bf16[64,8,128]{2,1,0:T(8,128)(2,1)S(1)} %collective-permute-done.1.refs_1_, ...), custom_call_target="tpu_custom_call" | custom-call | tf_op jit(solution)/shard_map/wave/pallas_call | solution.py:370
  35.2 1.3 %collective-permute-start.7 = (bf16[32,8,128]{2,1,0:T(8,128)(2,1)S(1)}, bf16[32,8,128]{2,1,0:T(8,128)(2,1)S(1)}, u32[]{:S(2)}, u32[]{:S(2)}) collective-permute-start(bf16[32,8,128]{2,1,0:T(8,128)(2,1)S(1)} %get-tuple-element.29), channel_id=1, source_target_pairs={{0,6},{1,7},{2,4},{3,5},{4,2},{5,3},{6,0},{7,1},{8,14},{9,15},{10,... | collective-permute-start | bytes 196616 | tf_op jit(solution)/shard_map/ppermute | solution.py:508
  36.5 1.0 %collective-permute-start.8 = (bf16[32,8,128]{2,1,0:T(8,128)(2,1)S(1)}, bf16[32,8,128]{2,1,0:T(8,128)(2,1)S(1)}, u32[]{:S(2)}, u32[]{:S(2)}) collective-permute-start(bf16[32,8,128]{2,1,0:T(8,128)(2,1)S(1)} %get-tuple-element.30), channel_id=1, source_target_pairs={{0,4},{1,5},{2,6},{3,7},{4,0},{5,1},{6,2},{7,3},{8,12},{9,13},{10,... | collective-permute-start | bytes 196616 | tf_op jit(solution)/shard_map/ppermute | solution.py:508
  37.6 1.2 %collective-permute-start.9 = (bf16[32,8,128]{2,1,0:T(8,128)(2,1)S(1)}, bf16[32,8,128]{2,1,0:T(8,128)(2,1)S(1)}, u32[]{:S(2)}, u32[]{:S(2)}) collective-permute-start(bf16[32,8,128]{2,1,0:T(8,128)(2,1)S(1)} %get-tuple-element.31), channel_id=1, source_target_pairs={{0,2},{1,3},{2,0},{3,1},{4,6},{5,7},{6,4},{7,5},{8,10},{9,11},{10,... | collective-permute-start | bytes 196616 | tf_op jit(solution)/shard_map/ppermute | solution.py:508
  38.8 2.4 %collective-permute-done.7.refs_0_ = bf16[32,8,128]{2,1,0:T(8,128)(2,1)S(1)} collective-permute-done((bf16[32,8,128]{2,1,0:T(8,128)(2,1)S(1)}, bf16[32,8,128]{2,1,0:T(8,128)(2,1)S(1)}, u32[]{:S(2)}, u32[]{:S(2)}) %collective-permute-start.7) | collective-permute-done | bytes 65568 | tf_op jit(solution)/shard_map/ppermute | solution.py:508
  41.2 0.1 collective-permute-done.8.refs_1_
  41.3 0.7 %collective-permute-done.9.refs_2_ = bf16[32,8,128]{2,1,0:T(8,128)(2,1)S(1)} collective-permute-done((bf16[32,8,128]{2,1,0:T(8,128)(2,1)S(1)}, bf16[32,8,128]{2,1,0:T(8,128)(2,1)S(1)}, u32[]{:S(2)}, u32[]{:S(2)}) %collective-permute-start.9) | collective-permute-done | bytes 65568 | tf_op jit(solution)/shard_map/ppermute | solution.py:508
  42.0 1.0 %stack.1 = (f32[8,8,8,128]{3,2,1,0:T(8,128)S(1)}, bf16[8,8,8,128]{3,2,1,0:T(8,128)(2,1)S(1)}) custom-call(s32[1,128]{1,0:T(1,128)S(1)} %get-tuple-element.20.facts_ref, bf16[32,8,128]{2,1,0:T(8,128)(2,1)S(1)} %collective-permute-done.7.refs_0_, bf16[32,8,128]{2,1,0:T(8,128)(2,1)S(1)} %collective-permute-done.8.refs_1_, ...), custom_call_target="tpu_custom_call" | custom-call | tf_op jit(solution)/shard_map/stack/pallas_call | solution.py:570
  43.0 0.1 collective-permute-start.10
  43.1 1.3 %collective-permute-done.10.other_ref = bf16[8,8,8,128]{3,2,1,0:T(8,128)(2,1)S(1)} collective-permute-done((bf16[8,8,8,128]{3,2,1,0:T(8,128)(2,1)S(1)}, bf16[8,8,8,128]{3,2,1,0:T(8,128)(2,1)S(1)}, u32[]{:S(2)}, u32[]{:S(2)}) %collective-permute-start.10) | collective-permute-done | bytes 131104 | tf_op jit(solution)/shard_map/ppermute | solution.py:514
  44.4 10.5 %all_to_all.11.sums_ref = bf16[8,8,8,128]{3,2,1,0:T(8,128)(2,1)S(1)} all-to-all(bf16[8,8,8,128]{3,2,1,0:T(8,128)(2,1)S(1)} %join.1), channel_id=1, replica_groups={{0,2,4,6,8,10,12,14},{1,3,5,7,9,11,13,15},{16,18,20,22,24,26,28,30},{17..., dimensions={0} | all-to-all | bytes 262144 | tf_op jit(solution)/shard_map/all_to_all | solution.py:594
  55.0 0.7 %finish.1 = f32[4,8,8,128]{3,2,1,0:T(8,128)} custom-call(bf16[8,8,8,128]{3,2,1,0:T(8,128)(2,1)S(1)} %all_to_all.11.sums_ref), custom_call_target="tpu_custom_call" | custom-call | tf_op jit(solution)/shard_map/finish/pallas_call | solution.py:598
  (4 shorter events, 0.0 us)
Async XLA Ops:
  21.1 9.9 %copy-start.1 = (bf16[1,32,32,128]{3,2,1,0:T(8,128)(2,1)S(1)}, bf16[1,32,32,128]{3,2,1,0:T(8,128)(2,1)}, u32[]{:S(2)}) copy-start(bf16[1,32,32,128]{3,2,1,0:T(8,128)(2,1)} %param.19) | copy-start | bytes 786436
  21.9 9.1 %copy-start = (bf16[1,32,32,128]{3,2,1,0:T(8,128)(2,1)S(1)}, bf16[1,32,32,128]{3,2,1,0:T(8,128)(2,1)}, u32[]{:S(2)}) copy-start(bf16[1,32,32,128]{3,2,1,0:T(8,128)(2,1)} %param.18) | copy-start | bytes 786436
  21.9 7.3 %collective-permute-start = (bf16[64,8,128]{2,1,0:T(8,128)(2,1)S(1)}, bf16[64,8,128]{2,1,0:T(8,128)(2,1)S(1)}, u32[]{:S(2)}, u32[]{:S(2)}) collective-permute-start(bf16[64,8,128]{2,1,0:T(8,128)(2,1)S(1)} %get-tuple-element.21), channel_id=1, source_target_pairs={{0,6},{1,7},{2,4},{3,5},{4,2},{5,3},{6,0},{7,1},{8,14},{9,15},{10,... | collective-permute-start | bytes 393224 | tf_op jit(solution)/shard_map/ppermute | solution.py:508
  22.7 7.5 %collective-permute-start.1 = (bf16[64,8,128]{2,1,0:T(8,128)(2,1)S(1)}, bf16[64,8,128]{2,1,0:T(8,128)(2,1)S(1)}, u32[]{:S(2)}, u32[]{:S(2)}) collective-permute-start(bf16[64,8,128]{2,1,0:T(8,128)(2,1)S(1)} %get-tuple-element.22), channel_id=1, source_target_pairs={{0,4},{1,5},{2,6},{3,7},{4,0},{5,1},{6,2},{7,3},{8,12},{9,13},{10,... | collective-permute-start | bytes 393224 | tf_op jit(solution)/shard_map/ppermute | solution.py:508
  23.1 7.9 %collective-permute-start.2 = (bf16[64,8,128]{2,1,0:T(8,128)(2,1)S(1)}, bf16[64,8,128]{2,1,0:T(8,128)(2,1)S(1)}, u32[]{:S(2)}, u32[]{:S(2)}) collective-permute-start(bf16[64,8,128]{2,1,0:T(8,128)(2,1)S(1)} %get-tuple-element.23), channel_id=1, source_target_pairs={{0,2},{1,3},{2,0},{3,1},{4,6},{5,7},{6,4},{7,5},{8,10},{9,11},{10,... | collective-permute-start | bytes 393224 | tf_op jit(solution)/shard_map/ppermute | solution.py:508
  25.5 6.2 %collective-permute-start.6 = (bf16[32,8,128]{2,1,0:T(8,128)(2,1)S(1)}, bf16[32,8,128]{2,1,0:T(8,128)(2,1)S(1)}, u32[]{:S(2)}, u32[]{:S(2)}) collective-permute-start(bf16[32,8,128]{2,1,0:T(8,128)(2,1)S(1)} %get-tuple-element.25), channel_id=1, source_target_pairs={{0,1},{1,0},{2,3},{3,2},{4,5},{5,4},{6,7},{7,6},{8,9},{9,8},{10,11... | collective-permute-start | bytes 196616 | tf_op jit(solution)/shard_map/ppermute | solution.py:514
  29.2 2.4 %collective-permute-start.3 = (bf16[32,8,128]{2,1,0:T(8,128)(2,1)S(1)}, bf16[32,8,128]{2,1,0:T(8,128)(2,1)S(1)}, u32[]{:S(2)}, u32[]{:S(2)}) collective-permute-start(bf16[32,8,128]{2,1,0:T(8,128)(2,1)S(1)} %slice.12), channel_id=1, source_target_pairs={{0,1},{1,0},{2,3},{3,2},{4,5},{5,4},{6,7},{7,6},{8,9},{9,8},{10,11... | collective-permute-start | bytes 196616 | tf_op jit(solution)/shard_map/ppermute | solution.py:514
  30.2 1.5 %collective-permute-start.4 = (bf16[32,8,128]{2,1,0:T(8,128)(2,1)S(1)}, bf16[32,8,128]{2,1,0:T(8,128)(2,1)S(1)}, u32[]{:S(2)}, u32[]{:S(2)}) collective-permute-start(bf16[32,8,128]{2,1,0:T(8,128)(2,1)S(1)} %slice.13), channel_id=1, source_target_pairs={{0,1},{1,0},{2,3},{3,2},{4,5},{5,4},{6,7},{7,6},{8,9},{9,8},{10,11... | collective-permute-start | bytes 196616 | tf_op jit(solution)/shard_map/ppermute | solution.py:514
  31.0 1.3 %collective-permute-start.5 = (bf16[32,8,128]{2,1,0:T(8,128)(2,1)S(1)}, bf16[32,8,128]{2,1,0:T(8,128)(2,1)S(1)}, u32[]{:S(2)}, u32[]{:S(2)}) collective-permute-start(bf16[32,8,128]{2,1,0:T(8,128)(2,1)S(1)} %slice.14), channel_id=1, source_target_pairs={{0,1},{1,0},{2,3},{3,2},{4,5},{5,4},{6,7},{7,6},{8,9},{9,8},{10,11... | collective-permute-start | bytes 196616 | tf_op jit(solution)/shard_map/ppermute | solution.py:514
  35.2 5.9 %collective-permute-start.7 = (bf16[32,8,128]{2,1,0:T(8,128)(2,1)S(1)}, bf16[32,8,128]{2,1,0:T(8,128)(2,1)S(1)}, u32[]{:S(2)}, u32[]{:S(2)}) collective-permute-start(bf16[32,8,128]{2,1,0:T(8,128)(2,1)S(1)} %get-tuple-element.29), channel_id=1, source_target_pairs={{0,6},{1,7},{2,4},{3,5},{4,2},{5,3},{6,0},{7,1},{8,14},{9,15},{10,... | collective-permute-start | bytes 196616 | tf_op jit(solution)/shard_map/ppermute | solution.py:508
  36.5 4.7 %collective-permute-start.8 = (bf16[32,8,128]{2,1,0:T(8,128)(2,1)S(1)}, bf16[32,8,128]{2,1,0:T(8,128)(2,1)S(1)}, u32[]{:S(2)}, u32[]{:S(2)}) collective-permute-start(bf16[32,8,128]{2,1,0:T(8,128)(2,1)S(1)} %get-tuple-element.30), channel_id=1, source_target_pairs={{0,4},{1,5},{2,6},{3,7},{4,0},{5,1},{6,2},{7,3},{8,12},{9,13},{10,... | collective-permute-start | bytes 196616 | tf_op jit(solution)/shard_map/ppermute | solution.py:508
  37.6 4.4 %collective-permute-start.9 = (bf16[32,8,128]{2,1,0:T(8,128)(2,1)S(1)}, bf16[32,8,128]{2,1,0:T(8,128)(2,1)S(1)}, u32[]{:S(2)}, u32[]{:S(2)}) collective-permute-start(bf16[32,8,128]{2,1,0:T(8,128)(2,1)S(1)} %get-tuple-element.31), channel_id=1, source_target_pairs={{0,2},{1,3},{2,0},{3,1},{4,6},{5,7},{6,4},{7,5},{8,10},{9,11},{10,... | collective-permute-start | bytes 196616 | tf_op jit(solution)/shard_map/ppermute | solution.py:508
  43.0 1.4 %collective-permute-start.10 = (bf16[8,8,8,128]{3,2,1,0:T(8,128)(2,1)S(1)}, bf16[8,8,8,128]{3,2,1,0:T(8,128)(2,1)S(1)}, u32[]{:S(2)}, u32[]{:S(2)}) collective-permute-start(bf16[8,8,8,128]{3,2,1,0:T(8,128)(2,1)S(1)} %get-tuple-element.34), channel_id=1, source_target_pairs={{0,1},{1,0},{2,3},{3,2},{4,5},{5,4},{6,7},{7,6},{8,9},{9,8},{10,11... | collective-permute-start | bytes 393224 | tf_op jit(solution)/shard_map/ppermute | solution.py:514

commit v13 on v11

--- a/solution.py
+++ b/solution.py
@@ -423,7 +423,7 @@
             total[r, index] = jnp.zeros(total.shape[2:], total.dtype)
         return carry
 
-    lax.fori_loop(0, total.shape[1], clear, 0, unroll=8)
+    lax.fori_loop(0, total.shape[1], clear, 0, unroll=32)
     copy.wait()
     for k, terms_ref in enumerate(terms_refs):
         shot = FACTS * (me ^ 2 * k)

time: 56.1 us -> 56.1 us (level)
  no operation moved by 1% of the time
where the time goes in v13:
time: 56.1 us; the launch traced here: 55.8 us
  waiting for transfers between devices  21 us (37%)
  starting transfers between devices  14.9 us (27%)
  blocking collectives  10.5 us (19%)
  Pallas kernels  7.97 us (14%)
  between operations  1.4 us (2%)
    all_to_all x1, blocking collectives, per_device(): lax.all_to_all(joined, 'shot', 0, 0, tiled=True, axis_index_groups=[list(...  10.5 us
    all_to_all x1, waiting for transfers between devices, per_device(): pieces = lax.all_to_all(sent, 'shot', 0, 0, tiled=True)  9.92 us
    ppermute x6, waiting for transfers between devices, swap(): lax.ppermute(values[k], 'shot', [(i, i ^ 2 * k) for i in range(count)])  8.48 us
    all_to_all x1, starting transfers between devices, per_device(): pieces = lax.all_to_all(sent, 'shot', 0, 0, tiled=True)  7.5 us
    ppermute x6, starting transfers between devices, swap(): lax.ppermute(values[k], 'shot', [(i, i ^ 2 * k) for i in range(count)])  7.11 us
    pallas_call x1, Pallas kernels, wave(): pl.pallas_call(functools.partial(wave_kernel, near), out_shape=(out,) * (...  3.01 us
    ppermute x5, waiting for transfers between devices, across(): return lax.ppermute(value, 'shot', [(i, i ^ 1) for i in range(count)])  2.55 us
    pallas_call x1, Pallas kernels, per_device(): pl.pallas_call(prepare_kernel, out_shape=jax.ShapeDtypeStruct((count, 2 *...  1.84 us
  transfers between devices with their start and end apart: 12, of which 10 were waited for; matrix products, arithmetic and copies ran while one was open for 0% of the time, Pallas kernels for 1%

profile of v13, /device:TPU:0, one launch (start us, length us, event | category | flops | bytes accessed | tf_op | source)
XLA Modules:
  0.0 55.8 jit_solution(3482260692663166783)
XLA Ops:
  1.3 1.8 %prepare.1 = bf16[16,9,8,128]{3,2,1,0:T(8,128)(2,1)} custom-call(s32[1]{0:T(128)S(6)} %copy.11.row_ref, s32[1]{0:T(128)S(6)} %copy.12.col_ref, s32[4]{0:T(128)} %ids_hbm.1, s32[4,8,8]{2,1,0:T(8,128)} %floor_hbm.1, bf16[4,8,8,128]{3,2,1,0:T(8,128)(2,1)} %p_hbm.1, bf16[4,8,8,128]{3,2,1,0:T(8,128)(2,1)} %s_hbm.1, bf16[4,8,8,128]{3,2,1,0:T(8,128)(2,1)} %rho_hbm.1, ...), custom_call_target="tpu_custom_call" | custom-call | tf_op jit(solution)/shard_map/prepare/pallas_call | solution.py:516
  3.1 0.0 copy-start
  3.2 0.0 copy-start.1
  3.2 7.5 %all-to-all-start = ((bf16[16,9,8,128]{3,2,1,0:T(8,128)(2,1)}), bf16[16,9,8,128]{3,2,1,0:T(8,128)(2,1)S(1)}, u32[]{:S(2)}, u32[]{:S(2)}) async-start(bf16[16,9,8,128]{3,2,1,0:T(8,128)(2,1)} %prepare.1), calls=%async_computation | async-start | bytes 589824 | tf_op jit(solution)/shard_map/all_to_all | solution.py:532
  10.7 0.0 copy-done
  10.7 0.0 copy-done.1
  10.7 0.6 %start.1 = (f32[32,4,8,128]{3,2,1,0:T(8,128)S(1)}, f32[32,4,8,128]{3,2,1,0:T(8,128)S(1)}, f32[32,4,8,128]{3,2,1,0:T(8,128)S(1)}) custom-call(bf16[32,32,128]{2,1,0:T(8,128)(2,1)S(1)} %bitcast.4, bf16[32,32,128]{2,1,0:T(8,128)(2,1)S(1)} %bitcast.5), custom_call_target="tpu_custom_call" | custom-call | flops 2621440 | bytes 2097152 | tf_op jit(solution)/shard_map/start/pallas_call | solution.py:260
  11.3 9.9 %all-to-all-done = bf16[16,9,8,128]{3,2,1,0:T(8,128)(2,1)S(1)} async-done(((bf16[16,9,8,128]{3,2,1,0:T(8,128)(2,1)}), bf16[16,9,8,128]{3,2,1,0:T(8,128)(2,1)S(1)}, u32[]{:S(2)}, u32[]{:S(2)}) %all-to-all-start) | async-done | bytes 294944 | tf_op jit(solution)/shard_map/all_to_all | solution.py:532
  21.2 0.8 %pick.1 = (bf16[64,8,128]{2,1,0:T(8,128)(2,1)S(1)}, bf16[64,8,128]{2,1,0:T(8,128)(2,1)S(1)}, bf16[64,8,128]{2,1,0:T(8,128)(2,1)S(1)}, bf16[32,8,128]{2,1,0:T(8,1...) custom-call(bf16[144,8,128]{2,1,0:T(8,128)(2,1)S(1)} %bitcast.3), custom_call_target="tpu_custom_call" | custom-call | tf_op jit(solution)/shard_map/pick/pallas_call | solution.py:537
  22.0 0.8 %collective-permute-start = (bf16[64,8,128]{2,1,0:T(8,128)(2,1)S(1)}, bf16[64,8,128]{2,1,0:T(8,128)(2,1)S(1)}, u32[]{:S(2)}, u32[]{:S(2)}) collective-permute-start(bf16[64,8,128]{2,1,0:T(8,128)(2,1)S(1)} %get-tuple-element.29), channel_id=1, source_target_pairs={{0,6},{1,7},{2,4},{3,5},{4,2},{5,3},{6,0},{7,1},{8,14},{9,15},{10,... | collective-permute-start | bytes 393224 | tf_op jit(solution)/shard_map/ppermute | solution.py:508
  22.9 0.3 collective-permute-start.1
  23.2 2.4 %collective-permute-start.2 = (bf16[64,8,128]{2,1,0:T(8,128)(2,1)S(1)}, bf16[64,8,128]{2,1,0:T(8,128)(2,1)S(1)}, u32[]{:S(2)}, u32[]{:S(2)}) collective-permute-start(bf16[64,8,128]{2,1,0:T(8,128)(2,1)S(1)} %get-tuple-element.31), channel_id=1, source_target_pairs={{0,2},{1,3},{2,0},{3,1},{4,6},{5,7},{6,4},{7,5},{8,10},{9,11},{10,... | collective-permute-start | bytes 393224 | tf_op jit(solution)/shard_map/ppermute | solution.py:508
  25.6 0.0 collective-permute-start.6
  25.6 3.8 %collective-permute-done.refs_0_ = bf16[64,8,128]{2,1,0:T(8,128)(2,1)S(1)} collective-permute-done((bf16[64,8,128]{2,1,0:T(8,128)(2,1)S(1)}, bf16[64,8,128]{2,1,0:T(8,128)(2,1)S(1)}, u32[]{:S(2)}, u32[]{:S(2)}) %collective-permute-start) | collective-permute-done | bytes 131104 | tf_op jit(solution)/shard_map/ppermute | solution.py:508
  29.4 0.0 collective-permute-start.3
  29.4 0.9 %collective-permute-done.1.refs_1_ = bf16[64,8,128]{2,1,0:T(8,128)(2,1)S(1)} collective-permute-done((bf16[64,8,128]{2,1,0:T(8,128)(2,1)S(1)}, bf16[64,8,128]{2,1,0:T(8,128)(2,1)S(1)}, u32[]{:S(2)}, u32[]{:S(2)}) %collective-permute-start.1) | collective-permute-done | bytes 131104 | tf_op jit(solution)/shard_map/ppermute | solution.py:508
  30.3 0.2 collective-permute-start.4
  30.5 0.6 %collective-permute-done.2.refs_2_ = bf16[64,8,128]{2,1,0:T(8,128)(2,1)S(1)} collective-permute-done((bf16[64,8,128]{2,1,0:T(8,128)(2,1)S(1)}, bf16[64,8,128]{2,1,0:T(8,128)(2,1)S(1)}, u32[]{:S(2)}, u32[]{:S(2)}) %collective-permute-start.2) | collective-permute-done | bytes 131104 | tf_op jit(solution)/shard_map/ppermute | solution.py:508
  31.1 0.0 collective-permute-start.5
  31.1 0.0 collective-permute-done.6.refs_7_
  31.1 0.0 collective-permute-done.3.refs_4_
  31.1 0.4 collective-permute-done.4.refs_5_
  31.6 0.8 %collective-permute-done.5.refs_6_ = bf16[32,8,128]{2,1,0:T(8,128)(2,1)S(1)} collective-permute-done((bf16[32,8,128]{2,1,0:T(8,128)(2,1)S(1)}, bf16[32,8,128]{2,1,0:T(8,128)(2,1)S(1)}, u32[]{:S(2)}, u32[]{:S(2)}) %collective-permute-start.5) | collective-permute-done | bytes 65568 | tf_op jit(solution)/shard_map/ppermute | solution.py:514
  32.4 3.0 %wave.1 = (bf16[32,8,128]{2,1,0:T(8,128)(2,1)S(1)}, bf16[32,8,128]{2,1,0:T(8,128)(2,1)S(1)}, bf16[32,8,128]{2,1,0:T(8,128)(2,1)S(1)}, bf16[32,8,128]{2,1,0:T(8,128)(2,1)S(1)}) custom-call(bf16[64,8,128]{2,1,0:T(8,128)(2,1)S(1)} %collective-permute-done.refs_0_, bf16[64,8,128]{2,1,0:T(8,128)(2,1)S(1)} %collective-permute-done.1.refs_1_, ...), custom_call_target="tpu_custom_call" | custom-call | tf_op jit(solution)/shard_map/wave/pallas_call | solution.py:370
  35.4 1.3 %collective-permute-start.7 = (bf16[32,8,128]{2,1,0:T(8,128)(2,1)S(1)}, bf16[32,8,128]{2,1,0:T(8,128)(2,1)S(1)}, u32[]{:S(2)}, u32[]{:S(2)}) collective-permute-start(bf16[32,8,128]{2,1,0:T(8,128)(2,1)S(1)} %get-tuple-element.37), channel_id=1, source_target_pairs={{0,6},{1,7},{2,4},{3,5},{4,2},{5,3},{6,0},{7,1},{8,14},{9,15},{10,... | collective-permute-start | bytes 196616 | tf_op jit(solution)/shard_map/ppermute | solution.py:508
  36.7 1.0 %collective-permute-start.8 = (bf16[32,8,128]{2,1,0:T(8,128)(2,1)S(1)}, bf16[32,8,128]{2,1,0:T(8,128)(2,1)S(1)}, u32[]{:S(2)}, u32[]{:S(2)}) collective-permute-start(bf16[32,8,128]{2,1,0:T(8,128)(2,1)S(1)} %get-tuple-element.38), channel_id=1, source_target_pairs={{0,4},{1,5},{2,6},{3,7},{4,0},{5,1},{6,2},{7,3},{8,12},{9,13},{10,... | collective-permute-start | bytes 196616 | tf_op jit(solution)/shard_map/ppermute | solution.py:508
  37.7 1.2 %collective-permute-start.9 = (bf16[32,8,128]{2,1,0:T(8,128)(2,1)S(1)}, bf16[32,8,128]{2,1,0:T(8,128)(2,1)S(1)}, u32[]{:S(2)}, u32[]{:S(2)}) collective-permute-start(bf16[32,8,128]{2,1,0:T(8,128)(2,1)S(1)} %get-tuple-element.39), channel_id=1, source_target_pairs={{0,2},{1,3},{2,0},{3,1},{4,6},{5,7},{6,4},{7,5},{8,10},{9,11},{10,... | collective-permute-start | bytes 196616 | tf_op jit(solution)/shard_map/ppermute | solution.py:508
  38.9 2.4 %collective-permute-done.7.refs_0_ = bf16[32,8,128]{2,1,0:T(8,128)(2,1)S(1)} collective-permute-done((bf16[32,8,128]{2,1,0:T(8,128)(2,1)S(1)}, bf16[32,8,128]{2,1,0:T(8,128)(2,1)S(1)}, u32[]{:S(2)}, u32[]{:S(2)}) %collective-permute-start.7) | collective-permute-done | bytes 65568 | tf_op jit(solution)/shard_map/ppermute | solution.py:508
  41.3 0.1 collective-permute-done.8.refs_1_
  41.4 0.7 %collective-permute-done.9.refs_2_ = bf16[32,8,128]{2,1,0:T(8,128)(2,1)S(1)} collective-permute-done((bf16[32,8,128]{2,1,0:T(8,128)(2,1)S(1)}, bf16[32,8,128]{2,1,0:T(8,128)(2,1)S(1)}, u32[]{:S(2)}, u32[]{:S(2)}) %collective-permute-start.9) | collective-permute-done | bytes 65568 | tf_op jit(solution)/shard_map/ppermute | solution.py:508
  42.1 1.0 %stack.1 = (f32[8,8,8,128]{3,2,1,0:T(8,128)S(1)}, bf16[8,8,8,128]{3,2,1,0:T(8,128)(2,1)S(1)}) custom-call(s32[1,128]{1,0:T(1,128)S(1)} %get-tuple-element.28.facts_ref, bf16[32,8,128]{2,1,0:T(8,128)(2,1)S(1)} %collective-permute-done.7.refs_0_, bf16[32,8,128]{2,1,0:T(8,128)(2,1)S(1)} %collective-permute-done.8.refs_1_, ...), custom_call_target="tpu_custom_call" | custom-call | tf_op jit(solution)/shard_map/stack/pallas_call | solution.py:571
  43.1 0.1 collective-permute-start.10
  43.2 1.3 %collective-permute-done.10.other_ref = bf16[8,8,8,128]{3,2,1,0:T(8,128)(2,1)S(1)} collective-permute-done((bf16[8,8,8,128]{3,2,1,0:T(8,128)(2,1)S(1)}, bf16[8,8,8,128]{3,2,1,0:T(8,128)(2,1)S(1)}, u32[]{:S(2)}, u32[]{:S(2)}) %collective-permute-start.10) | collective-permute-done | bytes 131104 | tf_op jit(solution)/shard_map/ppermute | solution.py:514
  44.6 10.5 %all_to_all.10.sums_ref = bf16[8,8,8,128]{3,2,1,0:T(8,128)(2,1)S(1)} all-to-all(bf16[8,8,8,128]{3,2,1,0:T(8,128)(2,1)S(1)} %join.1), channel_id=1, replica_groups={{0,2,4,6,8,10,12,14},{1,3,5,7,9,11,13,15},{16,18,20,22,24,26,28,30},{17..., dimensions={0} | all-to-all | bytes 262144 | tf_op jit(solution)/shard_map/all_to_all | solution.py:595
  55.1 0.7 %finish.1 = f32[4,8,8,128]{3,2,1,0:T(8,128)} custom-call(bf16[8,8,8,128]{3,2,1,0:T(8,128)(2,1)S(1)} %all_to_all.10.sums_ref), custom_call_target="tpu_custom_call" | custom-call | tf_op jit(solution)/shard_map/finish/pallas_call | solution.py:599
  (4 shorter events, 0.0 us)
Async XLA Ops:
  3.1 7.5 %copy-start = (bf16[1,32,32,128]{3,2,1,0:T(8,128)(2,1)S(1)}, bf16[1,32,32,128]{3,2,1,0:T(8,128)(2,1)}, u32[]{:S(2)}) copy-start(bf16[1,32,32,128]{3,2,1,0:T(8,128)(2,1)} %param.18) | copy-start | bytes 786436
  3.2 7.5 %copy-start.1 = (bf16[1,32,32,128]{3,2,1,0:T(8,128)(2,1)S(1)}, bf16[1,32,32,128]{3,2,1,0:T(8,128)(2,1)}, u32[]{:S(2)}) copy-start(bf16[1,32,32,128]{3,2,1,0:T(8,128)(2,1)} %param.19) | copy-start | bytes 786436
  3.2 18.1 %all-to-all-start = ((bf16[16,9,8,128]{3,2,1,0:T(8,128)(2,1)}), bf16[16,9,8,128]{3,2,1,0:T(8,128)(2,1)S(1)}, u32[]{:S(2)}, u32[]{:S(2)}) async-start(bf16[16,9,8,128]{3,2,1,0:T(8,128)(2,1)} %prepare.1), calls=%async_computation | async-start | bytes 589824 | tf_op jit(solution)/shard_map/all_to_all | solution.py:532
  22.0 7.3 %collective-permute-start = (bf16[64,8,128]{2,1,0:T(8,128)(2,1)S(1)}, bf16[64,8,128]{2,1,0:T(8,128)(2,1)S(1)}, u32[]{:S(2)}, u32[]{:S(2)}) collective-permute-start(bf16[64,8,128]{2,1,0:T(8,128)(2,1)S(1)} %get-tuple-element.29), channel_id=1, source_target_pairs={{0,6},{1,7},{2,4},{3,5},{4,2},{5,3},{6,0},{7,1},{8,14},{9,15},{10,... | collective-permute-start | bytes 393224 | tf_op jit(solution)/shard_map/ppermute | solution.py:508
  22.9 7.5 %collective-permute-start.1 = (bf16[64,8,128]{2,1,0:T(8,128)(2,1)S(1)}, bf16[64,8,128]{2,1,0:T(8,128)(2,1)S(1)}, u32[]{:S(2)}, u32[]{:S(2)}) collective-permute-start(bf16[64,8,128]{2,1,0:T(8,128)(2,1)S(1)} %get-tuple-element.30), channel_id=1, source_target_pairs={{0,4},{1,5},{2,6},{3,7},{4,0},{5,1},{6,2},{7,3},{8,12},{9,13},{10,... | collective-permute-start | bytes 393224 | tf_op jit(solution)/shard_map/ppermute | solution.py:508
  23.2 7.9 %collective-permute-start.2 = (bf16[64,8,128]{2,1,0:T(8,128)(2,1)S(1)}, bf16[64,8,128]{2,1,0:T(8,128)(2,1)S(1)}, u32[]{:S(2)}, u32[]{:S(2)}) collective-permute-start(bf16[64,8,128]{2,1,0:T(8,128)(2,1)S(1)} %get-tuple-element.31), channel_id=1, source_target_pairs={{0,2},{1,3},{2,0},{3,1},{4,6},{5,7},{6,4},{7,5},{8,10},{9,11},{10,... | collective-permute-start | bytes 393224 | tf_op jit(solution)/shard_map/ppermute | solution.py:508
  25.6 5.5 %collective-permute-start.6 = (bf16[32,8,128]{2,1,0:T(8,128)(2,1)S(1)}, bf16[32,8,128]{2,1,0:T(8,128)(2,1)S(1)}, u32[]{:S(2)}, u32[]{:S(2)}) collective-permute-start(bf16[32,8,128]{2,1,0:T(8,128)(2,1)S(1)} %get-tuple-element.33), channel_id=1, source_target_pairs={{0,1},{1,0},{2,3},{3,2},{4,5},{5,4},{6,7},{7,6},{8,9},{9,8},{10,11... | collective-permute-start | bytes 196616 | tf_op jit(solution)/shard_map/ppermute | solution.py:514
  29.4 1.8 %collective-permute-start.3 = (bf16[32,8,128]{2,1,0:T(8,128)(2,1)S(1)}, bf16[32,8,128]{2,1,0:T(8,128)(2,1)S(1)}, u32[]{:S(2)}, u32[]{:S(2)}) collective-permute-start(bf16[32,8,128]{2,1,0:T(8,128)(2,1)S(1)} %slice.12), channel_id=1, source_target_pairs={{0,1},{1,0},{2,3},{3,2},{4,5},{5,4},{6,7},{7,6},{8,9},{9,8},{10,11... | collective-permute-start | bytes 196616 | tf_op jit(solution)/shard_map/ppermute | solution.py:514
  30.3 1.3 %collective-permute-start.4 = (bf16[32,8,128]{2,1,0:T(8,128)(2,1)S(1)}, bf16[32,8,128]{2,1,0:T(8,128)(2,1)S(1)}, u32[]{:S(2)}, u32[]{:S(2)}) collective-permute-start(bf16[32,8,128]{2,1,0:T(8,128)(2,1)S(1)} %slice.13), channel_id=1, source_target_pairs={{0,1},{1,0},{2,3},{3,2},{4,5},{5,4},{6,7},{7,6},{8,9},{9,8},{10,11... | collective-permute-start | bytes 196616 | tf_op jit(solution)/shard_map/ppermute | solution.py:514
  31.1 1.3 %collective-permute-start.5 = (bf16[32,8,128]{2,1,0:T(8,128)(2,1)S(1)}, bf16[32,8,128]{2,1,0:T(8,128)(2,1)S(1)}, u32[]{:S(2)}, u32[]{:S(2)}) collective-permute-start(bf16[32,8,128]{2,1,0:T(8,128)(2,1)S(1)} %slice.14), channel_id=1, source_target_pairs={{0,1},{1,0},{2,3},{3,2},{4,5},{5,4},{6,7},{7,6},{8,9},{9,8},{10,11... | collective-permute-start | bytes 196616 | tf_op jit(solution)/shard_map/ppermute | solution.py:514
  35.4 5.9 %collective-permute-start.7 = (bf16[32,8,128]{2,1,0:T(8,128)(2,1)S(1)}, bf16[32,8,128]{2,1,0:T(8,128)(2,1)S(1)}, u32[]{:S(2)}, u32[]{:S(2)}) collective-permute-start(bf16[32,8,128]{2,1,0:T(8,128)(2,1)S(1)} %get-tuple-element.37), channel_id=1, source_target_pairs={{0,6},{1,7},{2,4},{3,5},{4,2},{5,3},{6,0},{7,1},{8,14},{9,15},{10,... | collective-permute-start | bytes 196616 | tf_op jit(solution)/shard_map/ppermute | solution.py:508
  36.7 4.7 %collective-permute-start.8 = (bf16[32,8,128]{2,1,0:T(8,128)(2,1)S(1)}, bf16[32,8,128]{2,1,0:T(8,128)(2,1)S(1)}, u32[]{:S(2)}, u32[]{:S(2)}) collective-permute-start(bf16[32,8,128]{2,1,0:T(8,128)(2,1)S(1)} %get-tuple-element.38), channel_id=1, source_target_pairs={{0,4},{1,5},{2,6},{3,7},{4,0},{5,1},{6,2},{7,3},{8,12},{9,13},{10,... | collective-permute-start | bytes 196616 | tf_op jit(solution)/shard_map/ppermute | solution.py:508
  37.7 4.4 %collective-permute-start.9 = (bf16[32,8,128]{2,1,0:T(8,128)(2,1)S(1)}, bf16[32,8,128]{2,1,0:T(8,128)(2,1)S(1)}, u32[]{:S(2)}, u32[]{:S(2)}) collective-permute-start(bf16[32,8,128]{2,1,0:T(8,128)(2,1)S(1)} %get-tuple-element.39), channel_id=1, source_target_pairs={{0,2},{1,3},{2,0},{3,1},{4,6},{5,7},{6,4},{7,5},{8,10},{9,11},{10,... | collective-permute-start | bytes 196616 | tf_op jit(solution)/shard_map/ppermute | solution.py:508
  43.1 1.4 %collective-permute-start.10 = (bf16[8,8,8,128]{3,2,1,0:T(8,128)(2,1)S(1)}, bf16[8,8,8,128]{3,2,1,0:T(8,128)(2,1)S(1)}, u32[]{:S(2)}, u32[]{:S(2)}) collective-permute-start(bf16[8,8,8,128]{3,2,1,0:T(8,128)(2,1)S(1)} %get-tuple-element.42), channel_id=1, source_target_pairs={{0,1},{1,0},{2,3},{3,2},{4,5},{5,4},{6,7},{7,6},{8,9},{9,8},{10,11... | collective-permute-start | bytes 393224 | tf_op jit(solution)/shard_map/ppermute | solution.py:514
